TPU v7x, 32 devices: a whole 2x2x4 slice. The times are simulated.
32 devices in a mesh: seq: 8 (over z, x), head: 4 (over y, core).
Axes of the slice: x: 2, y: 2, z: 4, core: 2. Of those that a mesh axis runs over, the one named last changes fastest.
Arguments:
- tokens: float32 [4096, 1024], P(('seq', 'head')), may hold values from -6 to 6
- w_query: float32 [2, 1024, 1024], P(None, ('seq', 'head')), may hold values from -0.1875 to 0.1875
- w_key: float32 [2, 1024, 1024], P(None, ('seq', 'head')), may hold values from -0.1875 to 0.1875
- w_value: float32 [2, 1024, 1024], P(None, ('seq', 'head')), may hold values from -0.1875 to 0.1875
- w_out: float32 [2, 1024, 1024], P(None, ('seq', 'head')), may hold values from -1.5 to 1.5
- w_gate: float32 [2, 1024, 2816], P(None, ('seq', 'head')), may hold values from -0.1875 to 0.1875
- w_up: float32 [2, 1024, 2816], P(None, ('seq', 'head')), may hold values from -0.1875 to 0.1875
- w_down: float32 [2, 2816, 1024], P(None, ('seq', 'head')), may hold values from -0.109375 to 0.109375
- gain_attn: float32 [2, 1024], P(None, ('seq', 'head')), may hold values from 0.1 to 1.9
- gain_ffn: float32 [2, 1024], P(None, ('seq', 'head')), may hold values from 0.1 to 1.9
- variate_bias: float32 [2, 2, 16], replicated, may hold values from -3 to 3
- doc_starts: int32 [6], replicated, may hold values from 0 to 4095, as said below
- variate_ids: int32 [4096], replicated, may hold values from 0 to 7
- time_ids: int32 [4096], P(('seq', 'head')), may hold values from 0 to 511
- cotangent: float32 [4096, 1024], P(('seq', 'head')), may hold values from -6 to 6
Outputs:
- output: float32 [4096, 1024], P(('seq', 'head'))
- grad_tokens: float32 [4096, 1024], P(('seq', 'head'))
- grad_w_query: float32 [2, 1024, 1024], P(None, ('seq', 'head'))
- grad_w_key: float32 [2, 1024, 1024], P(None, ('seq', 'head'))
- grad_w_value: float32 [2, 1024, 1024], P(None, ('seq', 'head'))
- grad_w_out: float32 [2, 1024, 1024], P(None, ('seq', 'head'))
- grad_w_gate: float32 [2, 1024, 2816], P(None, ('seq', 'head'))
- grad_w_up: float32 [2, 1024, 2816], P(None, ('seq', 'head'))
- grad_w_down: float32 [2, 2816, 1024], P(None, ('seq', 'head'))
- grad_gain_attn: float32 [2, 1024], P(None, ('seq', 'head'))
- grad_gain_ffn: float32 [2, 1024], P(None, ('seq', 'head'))
- grad_variate_bias: float32 [2, 2, 16], replicated
Inputs may be any that keep to these rules, and one draw needn't show every extreme that they name: `doc_starts`: strictly increasing with the first entry 0. The first three starts lie among the first 512 tokens, the last three among the last 512 tokens, so that the third document runs from the first 512 tokens into the last 512.
All inputs are finite; a program needn't handle non-finite values.
Results may differ from a plain program's by a relative error of at most 0.04.
Values may be sent and summed in bfloat16 or wider, within the bound.
No kernel may reach another device: no remote copies, remote signals or barrier semaphores. Data moves between devices by JAX's collectives and lax.ppermute only.
A program may use at most 320 MiB of HBM per device.

v0:
```python
import math

import jax
import jax.numpy as jnp
from jax import lax
from jax.sharding import PartitionSpec as P

D = 1024
HEADS = 16
HD = 64
LAYERS = 2


NORM_EPS = 1e-05
FLOOR_SCORE = -1e30


def rms_parts(values, gain_vec):
    inverse = lax.rsqrt(jnp.mean(values * values, axis=-1, keepdims=True) + NORM_EPS)
    return (values * inverse * gain_vec, inverse)


def rms_back(values, inverse, gain_vec, upstream):
    scaled = values * inverse
    inner = upstream * gain_vec
    gain_grad = jnp.sum(upstream * scaled, axis=0)
    value_grad = inverse * (inner - scaled * jnp.mean(inner * scaled, axis=-1, keepdims=True))
    return (value_grad, gain_grad)


def rotate(values, cosines, sines):
    half_dim = values.shape[-1] // 2
    former = values[..., :half_dim]
    latter = values[..., half_dim:]
    return jnp.concatenate(
        [former * cosines - latter * sines, latter * cosines + former * sines], axis=-1
    )


def cross_dot(left, right):
    return jnp.einsum("tc,td->cd", left, right, preferred_element_type=jnp.float32)


def back_dot(left, right):
    return jnp.einsum("td,cd->tc", left, right, preferred_element_type=jnp.float32)


def on_device(
    tokens,
    w_query,
    w_key,
    w_value,
    w_out,
    w_gate,
    w_up,
    w_down,
    gain_attn,
    gain_ffn,
    variate_bias,
    doc_starts,
    variate_ids,
    time_ids,
    cotangent,
):
    groups = lax.axis_size("head")
    tok_rows = tokens.shape[0]
    all_rows = variate_ids.shape[0]
    seq_rows = tok_rows * groups
    local_heads = HEADS // groups
    head_width = local_heads * HD
    head_start = lax.axis_index("head") * local_heads
    first_row = lax.axis_index("seq") * seq_rows
    positions = jnp.arange(all_rows, dtype=jnp.int32)
    doc_ids = jnp.sum((doc_starts[None, :] <= positions[:, None]).astype(jnp.int32), axis=1)
    query_docs = lax.dynamic_slice_in_dim(doc_ids, first_row, seq_rows)
    query_vars = lax.dynamic_slice_in_dim(variate_ids, first_row, seq_rows)
    key_block = math.gcd(all_rows, 512)
    block_count = all_rows // key_block
    key_docs = doc_ids.reshape(block_count, key_block)
    key_vars = variate_ids.reshape(block_count, key_block)
    half_dim = HD // 2
    frequency = jnp.exp(jnp.arange(half_dim).astype(jnp.float32) * (-2.0 * math.log(10000.0) / HD))
    angles = time_ids.astype(jnp.float32)[:, None] * frequency[None, :]
    cosines = jnp.cos(angles)[:, None, :]
    sines = jnp.sin(angles)[:, None, :]
    score_scale = 1.0 / math.sqrt(HD)
    stacks = (w_query, w_key, w_value, w_out, w_gate, w_up, w_down, gain_attn, gain_ffn)

    def local_weights(layer_index):
        return tuple((member[layer_index].astype(jnp.bfloat16) for member in stacks))

    def block_scores(queries, keys_blk, docs_blk, vars_blk, bias_pair):
        scores = (
            jnp.einsum("qhd,khd->hqk", queries, keys_blk, preferred_element_type=jnp.float32)
            * score_scale
        )
        same_var = query_vars[:, None] == vars_blk[None, :]
        scores = scores + jnp.where(
            same_var[None], bias_pair[0][:, None, None], bias_pair[1][:, None, None]
        )
        allowed = query_docs[:, None] == docs_blk[None, :]
        return (jnp.where(allowed[None], scores, FLOOR_SCORE), same_var)

    stream = tokens
    saved = []
    for layer_index in range(LAYERS):
        own_part = local_weights(layer_index)
        fetched = (
            lax.all_gather(own_part[0], ("seq", "head"), axis=0, tiled=True),
            lax.all_gather(own_part[1], ("seq", "head"), axis=0, tiled=True),
            lax.all_gather(own_part[2], ("seq", "head"), axis=0, tiled=True),
            lax.all_gather(own_part[3], ("seq", "head"), axis=0, tiled=True),
            lax.all_gather(own_part[4], ("seq", "head"), axis=0, tiled=True),
            lax.all_gather(own_part[5], ("seq", "head"), axis=0, tiled=True),
            lax.all_gather(own_part[6], ("seq", "head"), axis=0, tiled=True),
            lax.all_gather(own_part[7], ("seq", "head"), axis=0, tiled=True),
            lax.all_gather(own_part[8], ("seq", "head"), axis=0, tiled=True),
        )
        (
            query_matrix,
            key_matrix,
            value_matrix,
            output_matrix,
            gate_matrix,
            upward_matrix,
            down_matrix,
            attention_gain,
            feedforward_gain,
        ) = fetched
        normed, inverse_one = rms_parts(stream, attention_gain.astype(jnp.float32))
        normed = normed.astype(jnp.bfloat16)
        query_lin = jnp.dot(normed, query_matrix, preferred_element_type=jnp.float32)
        key_lin = jnp.dot(normed, key_matrix, preferred_element_type=jnp.float32)
        value_low = jnp.dot(normed, value_matrix, preferred_element_type=jnp.float32).astype(
            jnp.bfloat16
        )
        query_low = (
            rotate(query_lin.reshape(tok_rows, HEADS, HD), cosines, sines)
            .reshape(tok_rows, D)
            .astype(jnp.bfloat16)
        )
        key_low = (
            rotate(key_lin.reshape(tok_rows, HEADS, HD), cosines, sines)
            .reshape(tok_rows, D)
            .astype(jnp.bfloat16)
        )
        query_heads, key_heads, value_heads = (
            lax.all_to_all(query_low, "head", split_axis=1, concat_axis=0, tiled=True),
            lax.all_to_all(key_low, "head", split_axis=1, concat_axis=0, tiled=True),
            lax.all_to_all(value_low, "head", split_axis=1, concat_axis=0, tiled=True),
        )
        keys_all, values_all = (
            lax.all_gather(key_heads, "seq", axis=0, tiled=True),
            lax.all_gather(value_heads, "seq", axis=0, tiled=True),
        )
        bias_pair = lax.dynamic_slice_in_dim(variate_bias[layer_index], head_start, local_heads, 1)
        queries = query_heads.reshape(seq_rows, local_heads, HD)
        key_blocks = keys_all.reshape(block_count, key_block, local_heads, HD)
        value_blocks = values_all.reshape(block_count, key_block, local_heads, HD)

        def max_step(carry, inputs):
            running_max, running_total = carry
            keys_blk, docs_blk, vars_blk = inputs
            scores, same_var = block_scores(queries, keys_blk, docs_blk, vars_blk, bias_pair)
            new_max = jnp.maximum(running_max, jnp.max(scores, axis=-1))
            running_total = running_total * jnp.exp(running_max - new_max) + jnp.sum(
                jnp.exp(scores - new_max[..., None]), axis=-1
            )
            return ((new_max, running_total), None)

        start_max = jnp.full((local_heads, seq_rows), FLOOR_SCORE, jnp.float32)
        start_total = jnp.zeros((local_heads, seq_rows), jnp.float32)
        (final_max, final_total), unused = lax.scan(
            max_step, (start_max, start_total), (key_blocks, key_docs, key_vars)
        )
        log_total = final_max + jnp.log(final_total)

        def value_step(plain_sum, inputs):
            keys_blk, values_blk, docs_blk, vars_blk = inputs
            scores, same_var = block_scores(queries, keys_blk, docs_blk, vars_blk, bias_pair)
            probs_low = jnp.exp(scores - log_total[..., None]).astype(jnp.bfloat16)
            plain_sum = plain_sum + jnp.einsum(
                "hqk,khd->qhd", probs_low, values_blk, preferred_element_type=jnp.float32
            )
            return (plain_sum, None)

        start_out = jnp.zeros((seq_rows, local_heads, HD), jnp.float32)
        plain_out, unused = lax.scan(
            value_step, start_out, (key_blocks, value_blocks, key_docs, key_vars)
        )
        attended = plain_out.reshape(seq_rows, head_width).astype(jnp.bfloat16)
        mixed = lax.all_to_all(attended, "head", split_axis=0, concat_axis=1, tiled=True)
        middle = stream + jnp.dot(mixed, output_matrix, preferred_element_type=jnp.float32)
        normed_ffn, inverse_two = rms_parts(middle, feedforward_gain.astype(jnp.float32))
        normed_ffn = normed_ffn.astype(jnp.bfloat16)
        gate_lin = jnp.dot(normed_ffn, gate_matrix, preferred_element_type=jnp.float32)
        upward_lin = jnp.dot(normed_ffn, upward_matrix, preferred_element_type=jnp.float32)
        hidden = (jax.nn.silu(gate_lin) * upward_lin).astype(jnp.bfloat16)
        kept_weights = None
        saved.append(
            (
                stream,
                inverse_one,
                normed,
                queries,
                key_blocks,
                value_blocks,
                log_total,
                plain_out,
                mixed,
                middle,
                inverse_two,
                normed_ffn,
                gate_lin,
                upward_lin,
                hidden,
                bias_pair,
                kept_weights,
            )
        )
        stream = middle + jnp.dot(hidden, down_matrix, preferred_element_type=jnp.float32)
    upstream = cotangent
    layer_grads = [None] * LAYERS
    bias_parts = [None] * LAYERS
    for layer_index in reversed(range(LAYERS)):
        (
            stream_in,
            inverse_one,
            normed,
            queries,
            key_blocks,
            value_blocks,
            log_total,
            plain_out,
            mixed,
            middle,
            inverse_two,
            normed_ffn,
            gate_lin,
            upward_lin,
            hidden,
            bias_pair,
            kept_weights,
        ) = saved[layer_index]
        own_part = local_weights(layer_index)
        fetched = (
            lax.all_gather(own_part[0], ("seq", "head"), axis=0, tiled=True),
            lax.all_gather(own_part[1], ("seq", "head"), axis=0, tiled=True),
            lax.all_gather(own_part[2], ("seq", "head"), axis=0, tiled=True),
            lax.all_gather(own_part[3], ("seq", "head"), axis=0, tiled=True),
            lax.all_gather(own_part[4], ("seq", "head"), axis=0, tiled=True),
            lax.all_gather(own_part[5], ("seq", "head"), axis=0, tiled=True),
            lax.all_gather(own_part[6], ("seq", "head"), axis=0, tiled=True),
            lax.all_gather(own_part[7], ("seq", "head"), axis=0, tiled=True),
            lax.all_gather(own_part[8], ("seq", "head"), axis=0, tiled=True),
        )
        (
            query_matrix,
            key_matrix,
            value_matrix,
            output_matrix,
            gate_matrix,
            upward_matrix,
            down_matrix,
            attention_gain,
            feedforward_gain,
        ) = fetched
        upstream_low = upstream.astype(jnp.bfloat16)
        grad_down = cross_dot(hidden, upstream_low)
        grad_hidden = back_dot(upstream_low, down_matrix)
        sigmoid_gate = jax.nn.sigmoid(gate_lin)
        grad_gate = (
            grad_hidden * upward_lin * (sigmoid_gate * (1.0 + gate_lin * (1.0 - sigmoid_gate)))
        ).astype(jnp.bfloat16)
        grad_upward = (grad_hidden * (gate_lin * sigmoid_gate)).astype(jnp.bfloat16)
        grad_gate_matrix = cross_dot(normed_ffn, grad_gate)
        grad_upward_matrix = cross_dot(normed_ffn, grad_upward)
        grad_normed_ffn = back_dot(grad_gate, gate_matrix) + back_dot(grad_upward, upward_matrix)
        norm_grad, grad_ffn_gain = rms_back(
            middle, inverse_two, feedforward_gain.astype(jnp.float32), grad_normed_ffn
        )
        grad_middle = upstream + norm_grad
        middle_low = grad_middle.astype(jnp.bfloat16)
        grad_output_matrix = cross_dot(mixed, middle_low)
        grad_mixed = back_dot(middle_low, output_matrix).astype(jnp.bfloat16)
        grad_heads_low = lax.all_to_all(grad_mixed, "head", split_axis=1, concat_axis=0, tiled=True)
        out_grad = grad_heads_low.reshape(seq_rows, local_heads, HD)
        row_dot = jnp.sum(out_grad.astype(jnp.float32) * plain_out, axis=-1).T

        def grad_step(carry, inputs):
            query_grad, same_grad, other_grad = carry
            keys_blk, values_blk, docs_blk, vars_blk = inputs
            scores, same_var = block_scores(queries, keys_blk, docs_blk, vars_blk, bias_pair)
            probability = jnp.exp(scores - log_total[..., None])
            probs_low = probability.astype(jnp.bfloat16)
            prob_grad = jnp.einsum(
                "qhd,khd->hqk", out_grad, values_blk, preferred_element_type=jnp.float32
            )
            score_grad = (probability * (prob_grad - row_dot[..., None])).astype(jnp.bfloat16)
            query_grad = query_grad + jnp.einsum(
                "hqk,khd->qhd", score_grad, keys_blk, preferred_element_type=jnp.float32
            )
            key_part = jnp.einsum(
                "hqk,qhd->khd", score_grad, queries, preferred_element_type=jnp.float32
            )
            value_part = jnp.einsum(
                "hqk,qhd->khd", probs_low, out_grad, preferred_element_type=jnp.float32
            )
            wide_grad = score_grad.astype(jnp.float32)
            same_grad = same_grad + jnp.sum(jnp.where(same_var[None], wide_grad, 0.0), axis=(1, 2))
            other_grad = other_grad + jnp.sum(
                jnp.where(same_var[None], 0.0, wide_grad), axis=(1, 2)
            )
            return ((query_grad, same_grad, other_grad), (key_part, value_part))

        start_query = jnp.zeros((seq_rows, local_heads, HD), jnp.float32)
        start_bias = jnp.zeros((local_heads,), jnp.float32)
        (query_grad, same_grad, other_grad), (key_parts, value_parts) = lax.scan(
            grad_step,
            (start_query, start_bias, start_bias),
            (key_blocks, value_blocks, key_docs, key_vars),
        )
        key_own, value_own = (
            lax.psum_scatter(
                key_parts.reshape(all_rows, head_width).astype(jnp.bfloat16),
                "seq",
                scatter_dimension=0,
                tiled=True,
            ).astype(jnp.float32),
            lax.psum_scatter(
                value_parts.reshape(all_rows, head_width).astype(jnp.bfloat16),
                "seq",
                scatter_dimension=0,
                tiled=True,
            ).astype(jnp.float32),
        )
        query_low = (query_grad * score_scale).reshape(seq_rows, head_width).astype(jnp.bfloat16)
        key_low = (key_own * score_scale).astype(jnp.bfloat16)
        value_low = value_own.astype(jnp.bfloat16)
        query_tok, key_tok, value_tok = (
            lax.all_to_all(query_low, "head", split_axis=0, concat_axis=1, tiled=True),
            lax.all_to_all(key_low, "head", split_axis=0, concat_axis=1, tiled=True),
            lax.all_to_all(value_low, "head", split_axis=0, concat_axis=1, tiled=True),
        )
        query_pre = (
            rotate(query_tok.astype(jnp.float32).reshape(tok_rows, HEADS, HD), cosines, -sines)
            .reshape(tok_rows, D)
            .astype(jnp.bfloat16)
        )
        key_pre = (
            rotate(key_tok.astype(jnp.float32).reshape(tok_rows, HEADS, HD), cosines, -sines)
            .reshape(tok_rows, D)
            .astype(jnp.bfloat16)
        )
        grad_query_matrix = cross_dot(normed, query_pre)
        grad_key_matrix = cross_dot(normed, key_pre)
        grad_value_matrix = cross_dot(normed, value_tok)
        grad_normed = (
            back_dot(query_pre, query_matrix)
            + back_dot(key_pre, key_matrix)
            + back_dot(value_tok, value_matrix)
        )
        input_grad, grad_attention_gain = rms_back(
            stream_in, inverse_one, attention_gain.astype(jnp.float32), grad_normed
        )
        upstream = grad_middle + input_grad
        bias_local = jnp.stack([same_grad, other_grad])
        bias_parts[layer_index] = lax.dynamic_update_slice(
            jnp.zeros((2, HEADS), jnp.float32), bias_local, (0, head_start)
        )
        layer_grads[layer_index] = (
            lax.psum_scatter(grad_query_matrix, ("seq", "head"), scatter_dimension=0, tiled=True),
            lax.psum_scatter(grad_key_matrix, ("seq", "head"), scatter_dimension=0, tiled=True),
            lax.psum_scatter(grad_value_matrix, ("seq", "head"), scatter_dimension=0, tiled=True),
            lax.psum_scatter(grad_output_matrix, ("seq", "head"), scatter_dimension=0, tiled=True),
            lax.psum_scatter(grad_gate_matrix, ("seq", "head"), scatter_dimension=0, tiled=True),
            lax.psum_scatter(grad_upward_matrix, ("seq", "head"), scatter_dimension=0, tiled=True),
            lax.psum_scatter(grad_down, ("seq", "head"), scatter_dimension=0, tiled=True),
            lax.psum_scatter(grad_attention_gain, ("seq", "head"), scatter_dimension=0, tiled=True),
            lax.psum_scatter(grad_ffn_gain, ("seq", "head"), scatter_dimension=0, tiled=True),
        )
    bias_total = lax.psum(jnp.stack(bias_parts), ("seq", "head"))
    stacked = [
        jnp.stack([layer_grads[layer_index][member_index] for layer_index in range(LAYERS)])
        for member_index in range(9)
    ]
    return (
        stream,
        upstream,
        stacked[0],
        stacked[1],
        stacked[2],
        stacked[3],
        stacked[4],
        stacked[5],
        stacked[6],
        stacked[7],
        stacked[8],
        bias_total,
    )


def solution(mesh):
    placed = (
        P(("seq", "head"), None),
        P(None, ("seq", "head"), None),
        P(None, ("seq", "head"), None),
        P(None, ("seq", "head"), None),
        P(None, ("seq", "head"), None),
        P(None, ("seq", "head"), None),
        P(None, ("seq", "head"), None),
        P(None, ("seq", "head"), None),
        P(None, ("seq", "head")),
        P(None, ("seq", "head")),
        P(),
        P(),
        P(),
        P(("seq", "head")),
        P(("seq", "head"), None),
    )
    return jax.shard_map(
        on_device,
        mesh=mesh,
        in_specs=placed,
        out_specs=(
            P(("seq", "head"), None),
            P(("seq", "head"), None),
            P(None, ("seq", "head"), None),
            P(None, ("seq", "head"), None),
            P(None, ("seq", "head"), None),
            P(None, ("seq", "head"), None),
            P(None, ("seq", "head"), None),
            P(None, ("seq", "head"), None),
            P(None, ("seq", "head"), None),
            P(None, ("seq", "head")),
            P(None, ("seq", "head")),
            P(),
        ),
        check_vma=False,
    )
```

profile of v0, /device:TPU:0, one launch (start us, length us, event | category | flops | bytes accessed | tf_op | source)
XLA Modules:
  0.0 3697.5 jit_solution(4262591401622500615)
XLA Ops:
  73.2 56.2 %all-gather.47.cloned.1.call-done = bf16[1,1024,1024]{2,1,0:T(8,128)(2,1)} async-done(((bf16[1,32,1024]{2,1,0:T(8,128)(2,1)}), bf16[1,1024,1024]{2,1,0:T(8,128)(2,1)}) %all-gather.47.cloned.1.call-update) | async-done | bytes 2097168 | tf_op jit(solution)/shard_map/all_gather | solution.py:110
  252.9 67.3 %while.86 = (s32[]{:T(128)}, f32[4,512]{1,0:T(4,128)S(1)}, f32[4,512]{1,0:T(4,128)S(1)}, s32[512]{0:T(512)S(1)}, s32[8,512]{1,0:T(8,128)S(1)}, /*index=5*/bf16[8...) while((s32[]{:T(128)}, f32[4,512]{1,0:T(4,128)S(1)}, ...), condition=%wide.region_5.6_spmd.clone, body=%wide.region_2.5_spmd.clone.sunk | while | flops 146286592 | bytes 10609416 | solution.py:173
  419.6 66.1 %all-gather.55.cloned.1.call-done = bf16[1,1024,2816]{2,1,0:T(8,128)(2,1)} async-done(((bf16[1,32,2816]{2,1,0:T(8,128)(2,1)}), bf16[1,1024,2816]{2,1,0:T(8,128)(2,1)}) %all-gather.55.cloned.1.call-update) | async-done | bytes 5767184 | tf_op jit(solution)/shard_map/all_gather | solution.py:114
  490.7 64.8 %all-gather.57.cloned.1.call-done = bf16[1,2816,1024]{2,1,0:T(8,128)(2,1)} async-done(((bf16[1,88,1024]{2,1,0:T(8,128)(2,1)}), bf16[1,2816,1024]{2,1,0:T(8,128)(2,1)}) %all-gather.57.cloned.1.call-update) | async-done | bytes 5767184 | tf_op jit(solution)/shard_map/all_gather | solution.py:115
  616.1 55.6 %all-gather.63.cloned.1.call-done = bf16[1,1024,1024]{2,1,0:T(8,128)(2,1)} async-done(((bf16[1,32,1024]{2,1,0:T(8,128)(2,1)}), bf16[1,1024,1024]{2,1,0:T(8,128)(2,1)}) %all-gather.63.cloned.1.call-update) | async-done | bytes 2097168 | tf_op jit(solution)/shard_map/all_gather | solution.py:109
  794.7 66.7 %while.88 = (s32[]{:T(128)}, f32[4,512]{1,0:T(4,128)S(1)}, f32[4,512]{1,0:T(4,128)S(1)}, s32[512]{0:T(512)S(1)}, s32[8,512]{1,0:T(8,128)S(1)}, /*index=5*/bf16[8...) while((s32[]{:T(128)}, f32[4,512]{1,0:T(4,128)S(1)}, ...), condition=%wide.region_13.14_spmd.clone, body=%wide.region_10.13_spmd.clone.sunk | while | flops 146286592 | bytes 10609416 | solution.py:173
  959.5 67.1 %all-gather.69.cloned.1.call-done = bf16[1,1024,2816]{2,1,0:T(8,128)(2,1)} async-done(((bf16[1,32,2816]{2,1,0:T(8,128)(2,1)}), bf16[1,1024,2816]{2,1,0:T(8,128)(2,1)}) %all-gather.69.cloned.1.call-update) | async-done | bytes 5767184 | tf_op jit(solution)/shard_map/all_gather | solution.py:114
  1031.3 64.9 %all-gather.67.cloned.1.call-done = bf16[1,1024,2816]{2,1,0:T(8,128)(2,1)} async-done(((bf16[1,32,2816]{2,1,0:T(8,128)(2,1)}), bf16[1,1024,2816]{2,1,0:T(8,128)(2,1)}) %all-gather.67.cloned.1.call-update) | async-done | bytes 5767184 | tf_op jit(solution)/shard_map/all_gather | solution.py:113
  1124.2 99.4 %while.90 = (s32[]{:T(128)}, f32[512,4,64]{0,2,1:T(8,128)S(1)}, f32[4]{0:T(128)S(1)}, f32[4]{0:T(128)S(1)}, bf16[8,512,4,64]{1,3,2,0:T(8,128)(2,1)}, /*index=5*/...) while((s32[]{:T(128)}, f32[512,4,64]{0,2,1:T(8,128)S(1)}, ...), condition=%wide.region_22.23_spmd.clone, body=%wide.region_19.22_spmd.clone.sunk | while | flops 691798016 | bytes 24423360 | solution.py:318
  1301.0 65.2 %reduce-scatter.21.cloned.1.call-done = bf16[512,256]{0,1:T(8,128)(2,1)} async-done(((bf16[4096,256]{0,1:T(8,128)(2,1)}), bf16[512,256]{0,1:T(8,128)(2,1)}) %reduce-scatter.21.cloned.1.call-update) | async-done | bytes 262160 | tf_op jit(solution)/shard_map/reduce_scatter | solution.py:330
  1407.5 91.0 %while.91 = (s32[]{:T(128)}, f32[512,4,64]{0,2,1:T(8,128)S(1)}, f32[4]{0:T(128)S(1)}, f32[4]{0:T(128)S(1)}, bf16[8,512,4,64]{1,3,2,0:T(8,128)(2,1)}, /*index=5*/...) while((s32[]{:T(128)}, f32[512,4,64]{0,2,1:T(8,128)S(1)}, ...), condition=%wide.region_31.32_spmd.clone, body=%wide.region_28.31_spmd.clone.sunk | while | flops 691798016 | bytes 24423360 | solution.py:318
  1783.6 139.2 %reduce-scatter.39.cloned.1.call-done = f32[32,1024]{1,0:T(8,128)} async-done(((f32[1024,1024]{1,0:T(8,128)}), f32[32,1024]{1,0:T(8,128)}) %reduce-scatter.39.cloned.1.call-update) | async-done | bytes 131088 | tf_op jit(solution)/shard_map/reduce_scatter | solution.py:375
  1924.5 138.1 %reduce-scatter.37.cloned.1.call-done = f32[32,1024]{1,0:T(8,128)} async-done(((f32[1024,1024]{1,0:T(8,128)}), f32[32,1024]{1,0:T(8,128)}) %reduce-scatter.37.cloned.1.call-update) | async-done | bytes 131088 | tf_op jit(solution)/shard_map/reduce_scatter | solution.py:374
  2062.6 139.6 %reduce-scatter.35.cloned.1.call-done = f32[32,1024]{1,0:T(8,128)} async-done(((f32[1024,1024]{1,0:T(8,128)}), f32[32,1024]{1,0:T(8,128)}) %reduce-scatter.35.cloned.1.call-update) | async-done | bytes 131088 | tf_op jit(solution)/shard_map/reduce_scatter | solution.py:374
  2203.9 137.7 %reduce-scatter.33.cloned.1.call-done = f32[32,1024]{1,0:T(8,128)} async-done(((f32[1024,1024]{1,0:T(8,128)}), f32[32,1024]{1,0:T(8,128)}) %reduce-scatter.33.cloned.1.call-update) | async-done | bytes 131088 | tf_op jit(solution)/shard_map/reduce_scatter | solution.py:373
  2341.6 139.5 %reduce-scatter.31.cloned.1.call-done = f32[32,1024]{1,0:T(8,128)} async-done(((f32[1024,1024]{1,0:T(8,128)}), f32[32,1024]{1,0:T(8,128)}) %reduce-scatter.31.cloned.1.call-update) | async-done | bytes 131088 | tf_op jit(solution)/shard_map/reduce_scatter | solution.py:373
  2482.8 137.8 %reduce-scatter.29.cloned.1.call-done = f32[32,1024]{1,0:T(8,128)} async-done(((f32[1024,1024]{1,0:T(8,128)}), f32[32,1024]{1,0:T(8,128)}) %reduce-scatter.29.cloned.1.call-update) | async-done | bytes 131088 | tf_op jit(solution)/shard_map/reduce_scatter | solution.py:372
  2620.6 139.3 %reduce-scatter.27.cloned.1.call-done = f32[32,1024]{1,0:T(8,128)} async-done(((f32[1024,1024]{1,0:T(8,128)}), f32[32,1024]{1,0:T(8,128)}) %reduce-scatter.27.cloned.1.call-update) | async-done | bytes 131088 | tf_op jit(solution)/shard_map/reduce_scatter | solution.py:372
  2761.6 151.1 %reduce-scatter.53.cloned.1.call-done = f32[88,1024]{1,0:T(8,128)} async-done(((f32[2816,1024]{1,0:T(8,128)}), f32[88,1024]{1,0:T(8,128)}) %reduce-scatter.53.cloned.1.call-update) | async-done | bytes 360464 | tf_op jit(solution)/shard_map/reduce_scatter | solution.py:378
  2912.7 155.3 %reduce-scatter.51.cloned.1.call-done = f32[88,1024]{1,0:T(8,128)} async-done(((f32[2816,1024]{1,0:T(8,128)}), f32[88,1024]{1,0:T(8,128)}) %reduce-scatter.51.cloned.1.call-update) | async-done | bytes 360464 | tf_op jit(solution)/shard_map/reduce_scatter | solution.py:378
  3070.1 152.9 %reduce-scatter.49.cloned.1.call-done = f32[32,2816]{1,0:T(8,128)} async-done(((f32[1024,2816]{1,0:T(8,128)}), f32[32,2816]{1,0:T(8,128)}) %reduce-scatter.49.cloned.1.call-update) | async-done | bytes 360464 | tf_op jit(solution)/shard_map/reduce_scatter | solution.py:377
  3223.0 155.4 %reduce-scatter.47.cloned.1.call-done = f32[32,2816]{1,0:T(8,128)} async-done(((f32[1024,2816]{1,0:T(8,128)}), f32[32,2816]{1,0:T(8,128)}) %reduce-scatter.47.cloned.1.call-update) | async-done | bytes 360464 | tf_op jit(solution)/shard_map/reduce_scatter | solution.py:377
  3380.4 153.0 %reduce-scatter.45.cloned.1.call-done = f32[32,2816]{1,0:T(8,128)} async-done(((f32[1024,2816]{1,0:T(8,128)}), f32[32,2816]{1,0:T(8,128)}) %reduce-scatter.45.cloned.1.call-update) | async-done | bytes 360464 | tf_op jit(solution)/shard_map/reduce_scatter | solution.py:376
  3533.4 155.1 %reduce-scatter.43.cloned.1.call-done = f32[32,2816]{1,0:T(8,128)} async-done(((f32[1024,2816]{1,0:T(8,128)}), f32[32,2816]{1,0:T(8,128)}) %reduce-scatter.43.cloned.1.call-update) | async-done | bytes 360464 | tf_op jit(solution)/shard_map/reduce_scatter | solution.py:376
  (899 shorter events, 1409.3 us)
Async XLA Ops:
  12.3 226.6 %all-gather.39.cloned.1.call-start = ((), (), s32[]{:S(2)}) async-start(), calls=%async_computation.35 | async-start | bytes 2359296 | tf_op jit(solution)/shard_map/all_gather | solution.py:153
  201.9 283.8 %all-gather.55.cloned.1.call-start = ((), (), s32[]{:S(2)}) async-start(), calls=%async_computation.61 | async-start | bytes 5947392 | tf_op jit(solution)/shard_map/all_gather | solution.py:114
  202.8 352.7 %all-gather.57.cloned.1.call-start = ((), (), s32[]{:S(2)}) async-start(), calls=%async_computation.62 | async-start | bytes 5947392 | tf_op jit(solution)/shard_map/all_gather | solution.py:115
  203.7 409.9 %all-gather.61.cloned.1.call-start = ((), (), s32[]{:S(2)}) async-start(), calls=%async_computation.64 | async-start | bytes 2162688 | tf_op jit(solution)/shard_map/all_gather | solution.py:110
  204.3 467.4 %all-gather.63.cloned.1.call-start = ((), (), s32[]{:S(2)}) async-start(), calls=%async_computation.65 | async-start | bytes 2162688 | tf_op jit(solution)/shard_map/all_gather | solution.py:109
  374.1 355.6 %all-gather.59.cloned.1.call-start = ((), (), s32[]{:S(2)}) async-start(), calls=%async_computation.63 | async-start | bytes 2162688 | tf_op jit(solution)/shard_map/all_gather | solution.py:111
  374.7 405.9 %all-gather.43.cloned.1.call-start = ((), (), s32[]{:S(2)}) async-start(), calls=%async_computation.37 | async-start | bytes 2359296 | tf_op jit(solution)/shard_map/all_gather | solution.py:153
  741.5 215.6 %all-gather.65.cloned.1.call-start = ((), (), s32[]{:S(2)}) async-start(), calls=%async_computation.66 | async-start | bytes 2162688 | tf_op jit(solution)/shard_map/all_gather | solution.py:112
  742.1 284.5 %all-gather.69.cloned.1.call-start = ((), (), s32[]{:S(2)}) async-start(), calls=%async_computation.68 | async-start | bytes 5947392 | tf_op jit(solution)/shard_map/all_gather | solution.py:114
  746.8 349.3 %all-gather.67.cloned.1.call-start = ((), (), s32[]{:S(2)}) async-start(), calls=%async_computation.67 | async-start | bytes 5947392 | tf_op jit(solution)/shard_map/all_gather | solution.py:113
  1508.7 275.0 %reduce-scatter.41.cloned.1.call-start = ((), (), s32[]{:S(2)}) async-start(), calls=%async_computation.49 | async-start | bytes 4325376 | tf_op jit(solution)/shard_map/reduce_scatter | solution.py:375
  1511.6 411.3 %reduce-scatter.39.cloned.1.call-start = ((), (), s32[]{:S(2)}) async-start(), calls=%async_computation.48 | async-start | bytes 4325376 | tf_op jit(solution)/shard_map/reduce_scatter | solution.py:375
  1514.4 548.2 %reduce-scatter.37.cloned.1.call-start = ((), (), s32[]{:S(2)}) async-start(), calls=%async_computation.47 | async-start | bytes 4325376 | tf_op jit(solution)/shard_map/reduce_scatter | solution.py:374
  1517.3 685.0 %reduce-scatter.35.cloned.1.call-start = ((), (), s32[]{:S(2)}) async-start(), calls=%async_computation.46 | async-start | bytes 4325376 | tf_op jit(solution)/shard_map/reduce_scatter | solution.py:374
  1582.5 759.1 %reduce-scatter.33.cloned.1.call-start = ((), (), s32[]{:S(2)}) async-start(), calls=%async_computation.45 | async-start | bytes 4325376 | tf_op jit(solution)/shard_map/reduce_scatter | solution.py:373
  1645.9 835.2 %reduce-scatter.31.cloned.1.call-start = ((), (), s32[]{:S(2)}) async-start(), calls=%async_computation.44 | async-start | bytes 4325376 | tf_op jit(solution)/shard_map/reduce_scatter | solution.py:373
  1655.9 964.6 %reduce-scatter.29.cloned.1.call-start = ((), (), s32[]{:S(2)}) async-start(), calls=%async_computation.43 | async-start | bytes 4325376 | tf_op jit(solution)/shard_map/reduce_scatter | solution.py:372
  1658.7 1101.2 %reduce-scatter.27.cloned.1.call-start = ((), (), s32[]{:S(2)}) async-start(), calls=%async_computation.42 | async-start | bytes 4325376 | tf_op jit(solution)/shard_map/reduce_scatter | solution.py:372
  1661.6 1251.1 %reduce-scatter.53.cloned.1.call-start = ((), (), s32[]{:S(2)}) async-start(), calls=%async_computation.55 | async-start | bytes 11894784 | tf_op jit(solution)/shard_map/reduce_scatter | solution.py:378
  1667.7 1400.4 %reduce-scatter.51.cloned.1.call-start = ((), (), s32[]{:S(2)}) async-start(), calls=%async_computation.54 | async-start | bytes 11894784 | tf_op jit(solution)/shard_map/reduce_scatter | solution.py:378
  1674.8 1548.2 %reduce-scatter.49.cloned.1.call-start = ((), (), s32[]{:S(2)}) async-start(), calls=%async_computation.53 | async-start | bytes 11894784 | tf_op jit(solution)/shard_map/reduce_scatter | solution.py:377
  1681.9 1696.5 %reduce-scatter.47.cloned.1.call-start = ((), (), s32[]{:S(2)}) async-start(), calls=%async_computation.52 | async-start | bytes 11894784 | tf_op jit(solution)/shard_map/reduce_scatter | solution.py:377
  1689.0 1844.5 %reduce-scatter.45.cloned.1.call-start = ((), (), s32[]{:S(2)}) async-start(), calls=%async_computation.51 | async-start | bytes 11894784 | tf_op jit(solution)/shard_map/reduce_scatter | solution.py:376
  1696.1 1992.5 %reduce-scatter.43.cloned.1.call-start = ((), (), s32[]{:S(2)}) async-start(), calls=%async_computation.50 | async-start | bytes 11894784 | tf_op jit(solution)/shard_map/reduce_scatter | solution.py:376
  (109 other events, 4668.5 us)
Sparse Core Ops, SparseCore 0:
  349.7 66.2 all-gather.52
  419.5 66.2 all-gather.54
  489.2 66.2 all-gather.56
  833.1 65.7 all-gather.70
  960.4 66.1 all-gather.68
  1029.9 66.2 all-gather.66
  1228.8 66.8 reduce-scatter.18
  1299.1 67.0 reduce-scatter.20
  1503.7 66.2 reduce-scatter.24
  1573.5 67.1 reduce-scatter.22
  1642.9 140.6 reduce-scatter.40
  1785.8 137.0 reduce-scatter.38
  1925.1 137.4 reduce-scatter.36
  2064.7 137.4 reduce-scatter.34
  2204.3 137.1 reduce-scatter.32
  2343.8 137.1 reduce-scatter.30
  2483.3 137.1 reduce-scatter.28
  2622.7 137.1 reduce-scatter.26
  2762.2 150.4 reduce-scatter.52
  2915.1 152.9 reduce-scatter.50
  3070.2 152.7 reduce-scatter.48
  3225.3 153.0 reduce-scatter.46
  3380.7 152.6 reduce-scatter.44
  3535.6 152.9 reduce-scatter.42
  (12 shorter events, 637.0 us)
where the time goes:
time: 3710 us; the launch traced here: 3700 us
  waiting for transfers between devices  2840 us (77%)
  matrix products  452 us (12%)
  blocking collectives  135 us (4%)
  local copies, waits for them, and re-layouts  110 us (3%)
  other arithmetic  109 us (3%)
  starting transfers between devices  37.7 us (1%)
    reduce_scatter x2, waiting for transfers between devices, on_device(): lax.psum_scatter(grad_upward_matrix, ('seq', 'head'), scatter_dimension=0...  308 us
    reduce_scatter x2, waiting for transfers between devices, on_device(): lax.psum_scatter(grad_gate_matrix, ('seq', 'head'), scatter_dimension=0,...  308 us
    reduce_scatter x2, waiting for transfers between devices, on_device(): lax.psum_scatter(grad_down, ('seq', 'head'), scatter_dimension=0, tiled=T...  306 us
    reduce_scatter x2, waiting for transfers between devices, on_device(): lax.psum_scatter(grad_value_matrix, ('seq', 'head'), scatter_dimension=0,...  278 us
    reduce_scatter x2, waiting for transfers between devices, on_device(): lax.psum_scatter(grad_query_matrix, ('seq', 'head'), scatter_dimension=0,...  277 us
    reduce_scatter x2, waiting for transfers between devices, on_device(): lax.psum_scatter(grad_key_matrix, ('seq', 'head'), scatter_dimension=0, t...  277 us
    reduce_scatter x2, waiting for transfers between devices, on_device(): lax.psum_scatter(grad_output_matrix, ('seq', 'head'), scatter_dimension=0...  163 us
    all_gather x2, waiting for transfers between devices, on_device(): lax.all_gather(own_part[5], ('seq', 'head'), axis=0, tiled=True)  133 us
  transfers between devices with their start and end apart: 46, of which 38 were waited for; matrix products, arithmetic and copies ran while one was open for 11% of the time, Pallas kernels for 0%

commit v1 on v0

v1 whole, which is shorter than its diff:
```python
import functools
import math

import jax
import jax.numpy as jnp
from jax import lax
from jax.experimental import pallas as pl
from jax.experimental.pallas import tpu as pltpu
from jax.sharding import PartitionSpec as P

D = 1024
HEADS = 16
HD = 64
LAYERS = 2
HALF_HEADS = HEADS // 2
VARIATES = 8
BLOCK = 256

NORM_EPS = 1e-05
FLOOR_SCORE = -1e30
LOW = jnp.bfloat16
BOTH = ("seq", "head")

Y_SWAP = [(0, 2), (2, 0), (1, 3), (3, 1)]
CORE_SWAP = [(0, 1), (1, 0), (2, 3), (3, 2)]
TRANSPOSE = [(0, 0), (1, 2), (2, 1), (3, 3)]
ANTI_TRANSPOSE = [(0, 2), (2, 3), (3, 1), (1, 0)]

NN = (((1,), (0,)), ((), ()))
NT = (((1,), (1,)), ((), ()))
TN = (((0,), (0,)), ((), ()))
TT = (((0,), (1,)), ((), ()))
VMEM_LIMIT = 56 * 1024 * 1024


def dot(left, right, dims):
    return lax.dot_general(left, right, dims, preferred_element_type=jnp.float32)


def forward_kernel(
    first_ref, q_ref, q_aug_ref, q_doc_ref, own_ref, sib_ref, k_aug_ref, k_doc_ref,
    out_ref, lse_ref, *, seq, width,
):
    tile = first_ref[0] + pl.program_id(0)
    sources = ((own_ref, HD), (sib_ref, 0))
    blocks = [(half, s) for half in range(2) for s in range(seq)]
    cols = q_ref.shape[-1]
    q_side = jnp.concatenate([q_ref[0, :HD, :], q_aug_ref[0]], axis=0).T

    def run(edge_tile):
        q_doc = q_doc_ref[0]
        top = jnp.full((cols, 1), FLOOR_SCORE, jnp.float32)
        total = jnp.zeros((cols, 1), jnp.float32)
        acc = jnp.zeros((cols, HD), jnp.float32)
        for start in range(0, len(blocks), width):
            group = blocks[start : start + width]
            parts = []
            for half, s in group:
                ref, low_row = sources[half]
                spot = half * seq + s
                k_side = jnp.concatenate([ref[s, low_row : low_row + HD, :], k_aug_ref[spot]], axis=0)
                score = dot(q_side, k_side, NN)
                if edge_tile or s in (0, seq - 1):
                    score = jnp.where(q_doc == k_doc_ref[spot], score, FLOOR_SCORE)
                parts.append(score)
            peak = functools.reduce(jnp.maximum, parts)
            fresh = jnp.maximum(top, jnp.max(peak, axis=-1, keepdims=True))
            shrink = jnp.exp(top - fresh)
            probs = [jnp.exp(part - fresh) for part in parts]
            total = total * shrink + jnp.sum(sum(probs[1:], probs[0]), axis=-1, keepdims=True)
            acc = acc * shrink
            for prob, (half, s) in zip(probs, group):
                ref, low_row = sources[half]
                values = ref[s, low_row + HD : low_row + 2 * HD, :]
                acc = acc + dot(prob.astype(LOW), values, NT)
            top = fresh
        result = acc / total
        lse = jnp.broadcast_to(top + jnp.log(total), (cols, HD))
        both = jnp.concatenate([result, lse], axis=1).T
        out_ref[0] = both[:HD]
        lse_ref[0] = both[HD : HD + 8]

    edge = jnp.logical_or(tile == 0, tile == seq - 1)
    pl.when(edge)(lambda: run(True))
    pl.when(jnp.logical_not(edge))(lambda: run(False))


def split_rows(row, rows):
    one = row.astype(LOW).astype(jnp.float32)
    two = (row - one).astype(LOW).astype(jnp.float32)
    three = row - one - two
    pad = jnp.zeros((rows - 3, row.shape[-1]), jnp.float32)
    return jnp.concatenate([one, two, three, pad], axis=0).astype(LOW)


def backward_kernel(
    first_ref, q_ref, q_aug_ref, q_doc_ref, lse_ref, out_ref, grad_ref,
    own_ref, sib_ref, k_aug_ref, k_doc_ref,
    dq_ref, dkv_ref, dkv_acc, *, seq,
):
    step = pl.program_id(0)
    tile = first_ref[0] + step
    sources = ((own_ref, HD), (sib_ref, 0))
    cols = q_ref.shape[-1]

    @pl.when(step == 0)
    def _():
        dkv_acc[...] = jnp.zeros_like(dkv_acc)

    q_low = q_ref[0, :HD, :]
    g_low = grad_ref[0]
    row_dot = jnp.sum(g_low.astype(jnp.float32) * out_ref[0], axis=0, keepdims=True)
    aug = jnp.concatenate(
        [q_aug_ref[0, :32, :], split_rows(-lse_ref[0, :1, :], 16), q_aug_ref[0, 48:, :]], axis=0
    )
    q_side = jnp.concatenate([q_low, aug], axis=0).T
    g_side = jnp.concatenate([g_low, split_rows(-row_dot, HD)], axis=0).T
    ones = jnp.concatenate(
        [jnp.ones((16, cols), LOW), jnp.zeros((HD - 16, cols), LOW)], axis=0
    )

    def run(edge_tile):
        q_doc = q_doc_ref[0]
        dq = jnp.zeros((cols, 2 * HD), jnp.float32)
        for half in range(2):
            ref, low_row = sources[half]
            for s in range(seq):
                spot = half * seq + s
                k_side = jnp.concatenate([ref[s, low_row : low_row + HD, :], k_aug_ref[spot]], axis=0)
                v_side = jnp.concatenate([ref[s, low_row + HD : low_row + 2 * HD, :], ones], axis=0)
                prob = jnp.exp(dot(q_side, k_side, NN))
                if edge_tile or s in (0, seq - 1):
                    prob = jnp.where(q_doc == k_doc_ref[spot], prob, 0.0)
                score_grad = (prob * dot(g_side, v_side, NN)).astype(LOW)
                dq = dq + dot(score_grad, k_side, NT)
                dkv_acc[spot, :HD, :] += dot(q_low, score_grad, NN)
                dkv_acc[spot, HD:, :] += dot(g_low, prob.astype(LOW), NN)
        dq_ref[0] = dq.T

    edge = jnp.logical_or(tile == 0, tile == seq - 1)
    pl.when(edge)(lambda: run(True))
    pl.when(jnp.logical_not(edge))(lambda: run(False))

    @pl.when(step == pl.num_programs(0) - 1)
    def _():
        dkv_ref[...] = dkv_acc[...].astype(LOW)


def whole_spec(array):
    rank = array.ndim
    return pl.BlockSpec(array.shape, lambda i, first: (0,) * rank)


def tile_spec(shape):
    rank = len(shape)
    return pl.BlockSpec((1,) + tuple(shape[1:]), lambda i, first: (i,) + (0,) * (rank - 1))


def attention_forward(first, queries, q_aug, q_doc, own, sib, k_aug, k_doc):
    seq, cols, tiles = own.shape[0], own.shape[2], queries.shape[0]
    return pl.pallas_call(
        functools.partial(forward_kernel, seq=seq, width=4),
        grid_spec=pltpu.PrefetchScalarGridSpec(
            num_scalar_prefetch=1,
            grid=(tiles,),
            in_specs=[tile_spec(member.shape) for member in (queries, q_aug, q_doc)]
            + [whole_spec(member) for member in (own, sib, k_aug, k_doc)],
            out_specs=[tile_spec((tiles, HD, cols)), tile_spec((tiles, 8, cols))],
        ),
        out_shape=[
            jax.ShapeDtypeStruct((tiles, HD, cols), jnp.float32),
            jax.ShapeDtypeStruct((tiles, 8, cols), jnp.float32),
        ],
        compiler_params=pltpu.CompilerParams(vmem_limit_bytes=VMEM_LIMIT),
        name="attention_forward",
    )(first, queries, q_aug, q_doc, own, sib, k_aug, k_doc)


def attention_backward(first, queries, q_aug, q_doc, lse, out, grad, own, sib, k_aug, k_doc):
    seq, cols, tiles = own.shape[0], own.shape[2], queries.shape[0]
    dkv_shape = (2 * seq, 2 * HD, cols)
    return pl.pallas_call(
        functools.partial(backward_kernel, seq=seq),
        grid_spec=pltpu.PrefetchScalarGridSpec(
            num_scalar_prefetch=1,
            grid=(tiles,),
            in_specs=[
                tile_spec(member.shape) for member in (queries, q_aug, q_doc, lse, out, grad)
            ]
            + [whole_spec(member) for member in (own, sib, k_aug, k_doc)],
            out_specs=[
                tile_spec((tiles, 2 * HD, cols)),
                pl.BlockSpec(dkv_shape, lambda i, first: (0, 0, 0)),
            ],
            scratch_shapes=[pltpu.VMEM(dkv_shape, jnp.float32)],
        ),
        out_shape=[
            jax.ShapeDtypeStruct((tiles, 2 * HD, cols), jnp.float32),
            jax.ShapeDtypeStruct(dkv_shape, LOW),
        ],
        compiler_params=pltpu.CompilerParams(vmem_limit_bytes=VMEM_LIMIT),
        name="attention_backward",
    )(first, queries, q_aug, q_doc, lse, out, grad, own, sib, k_aug, k_doc)


def silu_parts(gate):
    sigmoid = 1.0 / (1.0 + jnp.exp(-gate))
    return sigmoid, gate * sigmoid


def ffn_forward_kernel(x_ref, w_ref, both_ref, hidden_ref, out_ref, *, unit_rows, down_rows, unit_steps):
    step = pl.program_id(0)
    groups = w_ref.shape[0]

    @pl.when(step < unit_steps)
    def _():
        for place in range(w_ref.shape[1] // unit_rows):
            matrix = w_ref[:, place * unit_rows : (place + 1) * unit_rows, :].reshape(-1, BLOCK)
            both = dot(x_ref[...], matrix, NN)
            both_ref[place] = both
            half = BLOCK // 2
            hidden = silu_parts(both[:, :half])[1] * both[:, half:]
            spot = step * (w_ref.shape[1] // unit_rows) + place
            hidden_ref[:, pl.ds(pl.multiple_of(spot * half, half), half)] = hidden.astype(LOW)

    @pl.when(step >= unit_steps)
    def _():
        for place in range(w_ref.shape[1] // down_rows):
            matrix = w_ref[:, place * down_rows : (place + 1) * down_rows, :].reshape(-1, BLOCK)
            out_ref[:, place * BLOCK : (place + 1) * BLOCK] = dot(hidden_ref[...], matrix, NN)


def ffn_backward_kernel(
    g_ref, w_ref, both_ref, grads_ref, inner_ref, hidden_grad, *, unit_rows, down_rows, down_steps
):
    step = pl.program_id(0)
    half = BLOCK // 2

    @pl.when(step == 0)
    def _():
        hidden_grad[...] = jnp.zeros_like(hidden_grad)
        inner_ref[...] = jnp.zeros_like(inner_ref)

    @pl.when(step < down_steps)
    def _():
        for place in range(w_ref.shape[1] // down_rows):
            matrix = w_ref[:, place * down_rows : (place + 1) * down_rows, :].reshape(-1, BLOCK)
            part = g_ref[:, place * BLOCK : (place + 1) * BLOCK]
            hidden_grad[...] += dot(part, matrix, NT)

    @pl.when(step >= down_steps)
    def _():
        count = w_ref.shape[1] // unit_rows
        total = inner_ref[...]
        for place in range(count):
            matrix = w_ref[:, place * unit_rows : (place + 1) * unit_rows, :].reshape(-1, BLOCK)
            spot = (step - down_steps) * count + place
            gate, upward = both_ref[place, :, :half], both_ref[place, :, half:]
            above = hidden_grad[:, pl.ds(pl.multiple_of(spot * half, half), half)]
            sigmoid, silu = silu_parts(gate)
            grad_gate = above * upward * (sigmoid * (1.0 + gate * (1.0 - sigmoid)))
            grads = jnp.concatenate([grad_gate, above * silu], axis=1).astype(LOW)
            grads_ref[place] = grads
            total = total + dot(grads, matrix, NT)
        inner_ref[...] = total


def ffn_sizes(packed_shape, cols_ff, unit_rows, down_rows):
    rows = 2 * down_rows
    return rows, 2 * cols_ff // BLOCK * unit_rows // rows, D // BLOCK * down_rows // rows


def ffn_forward(x, packed, cols_ff, unit_rows, down_rows):
    groups, tokens = packed.shape[0], x.shape[0]
    rows, unit_steps, down_steps = ffn_sizes(packed.shape, cols_ff, unit_rows, down_rows)
    per_unit, per_down = rows // unit_rows, rows // down_rows
    last = unit_steps - 1
    return pl.pallas_call(
        functools.partial(
            ffn_forward_kernel, unit_rows=unit_rows, down_rows=down_rows, unit_steps=unit_steps
        ),
        grid=(unit_steps + down_steps,),
        in_specs=[
            pl.BlockSpec(x.shape, lambda i: (0, 0)),
            pl.BlockSpec((groups, rows, BLOCK), lambda i: (0, i, 0)),
        ],
        out_specs=[
            pl.BlockSpec((per_unit, tokens, BLOCK), lambda i: (jnp.minimum(i, last), 0, 0)),
            pl.BlockSpec((tokens, cols_ff), lambda i: (0, 0)),
            pl.BlockSpec((tokens, per_down * BLOCK), lambda i: (0, jnp.maximum(i - unit_steps, 0))),
        ],
        out_shape=[
            jax.ShapeDtypeStruct((per_unit * unit_steps, tokens, BLOCK), jnp.float32),
            jax.ShapeDtypeStruct((tokens, cols_ff), LOW),
            jax.ShapeDtypeStruct((tokens, D), jnp.float32),
        ],
        compiler_params=pltpu.CompilerParams(vmem_limit_bytes=VMEM_LIMIT),
        name="ffn_forward",
    )(x, packed)


def ffn_backward(grad, packed, both, cols_ff, unit_rows, down_rows):
    groups, tokens = packed.shape[0], grad.shape[0]
    rows, unit_steps, down_steps = ffn_sizes(packed.shape, cols_ff, unit_rows, down_rows)
    per_unit, per_down = rows // unit_rows, rows // down_rows
    steps = unit_steps + down_steps
    unit_spec = pl.BlockSpec(
        (per_unit, tokens, BLOCK), lambda i: (jnp.maximum(i - down_steps, 0), 0, 0)
    )
    return pl.pallas_call(
        functools.partial(
            ffn_backward_kernel, unit_rows=unit_rows, down_rows=down_rows, down_steps=down_steps
        ),
        grid=(steps,),
        in_specs=[
            pl.BlockSpec(
                (tokens, per_down * BLOCK), lambda i: (0, jnp.minimum(i, down_steps - 1))
            ),
            pl.BlockSpec((groups, rows, BLOCK), lambda i: (0, (i + unit_steps) % steps, 0)),
            unit_spec,
        ],
        out_specs=[unit_spec, pl.BlockSpec((tokens, D), lambda i: (0, 0))],
        out_shape=[
            jax.ShapeDtypeStruct((per_unit * unit_steps, tokens, BLOCK), LOW),
            jax.ShapeDtypeStruct((tokens, D), jnp.float32),
        ],
        scratch_shapes=[pltpu.VMEM((tokens, cols_ff), jnp.float32)],
        compiler_params=pltpu.CompilerParams(vmem_limit_bytes=VMEM_LIMIT),
        name="ffn_backward",
    )(grad, packed, both)


def weight_grad_kernel(left_ref, right_ref, *refs, rows, kind):
    out_ref = refs[-1]
    for place in range(out_ref.shape[1] // rows):
        if kind == "blocks":
            grad = dot(left_ref[...], right_ref[place], NN)
        elif kind == "columns":
            grad = dot(left_ref[...], right_ref[:, place * BLOCK : (place + 1) * BLOCK], NN)
        else:
            grad = dot(left_ref[...], right_ref[place * BLOCK : (place + 1) * BLOCK, :], NT)
        out_ref[:, place * rows : (place + 1) * rows, :] = grad.reshape(-1, rows, BLOCK).astype(LOW)


def weight_grad(buffer, total_rows, left, right, kind, rows, start, per_step):
    tokens = left.shape[1]
    groups = left.shape[0] // rows
    if kind == "blocks":
        count = right.shape[0]
        right_spec = pl.BlockSpec((per_step, tokens, BLOCK), lambda i: (i, 0, 0))
    elif kind == "columns":
        count = right.shape[1] // BLOCK
        right_spec = pl.BlockSpec((tokens, per_step * BLOCK), lambda i: (0, i))
    else:
        count = right.shape[0] // BLOCK
        right_spec = pl.BlockSpec((per_step * BLOCK, tokens), lambda i: (i, 0))
    first = start // (per_step * rows)
    operands, specs = [left, right], [pl.BlockSpec(left.shape, lambda i: (0, 0)), right_spec]
    if buffer is not None:
        operands.append(buffer)
        specs.append(pl.BlockSpec(memory_space=pl.ANY))
    return pl.pallas_call(
        functools.partial(weight_grad_kernel, rows=rows, kind=kind),
        grid=(count // per_step,),
        in_specs=specs,
        out_specs=pl.BlockSpec((groups, per_step * rows, BLOCK), lambda i: (0, first + i, 0)),
        out_shape=jax.ShapeDtypeStruct((groups, total_rows, BLOCK), LOW),
        input_output_aliases={} if buffer is None else {2: 0},
        compiler_params=pltpu.CompilerParams(vmem_limit_bytes=VMEM_LIMIT),
        name="weight_grad_" + kind,
    )(*operands)


def on_device(
    tokens,
    w_query,
    w_key,
    w_value,
    w_out,
    w_gate,
    w_up,
    w_down,
    gain_attn,
    gain_ffn,
    variate_bias,
    doc_starts,
    variate_ids,
    time_ids,
    cotangent,
):
    seq = lax.axis_size("seq")
    spread = seq // HALF_HEADS
    tiles = seq // spread
    tok_rows = tokens.shape[0]
    cols = 2 * tok_rows
    all_rows = variate_ids.shape[0]
    w_rows = w_query.shape[1]
    d_rows = w_down.shape[1]
    padded = -(-d_rows // 16) * 16
    half_ff = 2 * seq * padded
    half_width = HALF_HEADS * HD
    split_heads = 2 * w_rows == HD
    here_seq = lax.axis_index("seq")
    here_y = lax.axis_index("head") // 2
    here_core = lax.axis_index("head") % 2
    head_slot = here_seq // spread
    my_head = 2 * head_slot + here_y
    first_tile = (here_seq % spread) * tiles
    first = jnp.reshape(first_tile, (1,)).astype(jnp.int32)
    row_groups = [
        [4 * s + 2 * y + core for s in range(seq) for core in range(2)] for y in range(2)
    ]
    y_zero = here_y == 0
    core_zero = here_core == 0

    def swap_y(value):
        return lax.ppermute(value, "head", Y_SWAP)

    def beside(value):
        return jnp.concatenate([value, swap_y(value)], axis=0)

    def fold(partial):
        sent = swap_y(partial[tok_rows:].astype(LOW))
        return partial[:tok_rows] + sent.astype(jnp.float32)

    def cross_rows(parts):
        straight = jnp.where(core_zero, parts[0], parts[1])
        crossed = jnp.where(core_zero, parts[1], parts[0])
        straight = lax.ppermute(straight, "head", TRANSPOSE)
        crossed = lax.ppermute(crossed, "head", ANTI_TRANSPOSE)
        return jnp.where(
            y_zero,
            jnp.concatenate([straight, crossed], axis=0),
            jnp.concatenate([crossed, straight], axis=0),
        )

    def cross_back(pair):
        low_part, high_part = pair[:w_rows], pair[w_rows:]
        straight = jnp.where(y_zero, low_part, high_part)
        crossed = jnp.where(y_zero, high_part, low_part)
        straight = lax.ppermute(straight, "head", TRANSPOSE)
        crossed = lax.ppermute(crossed, "head", [(b, a) for a, b in ANTI_TRANSPOSE])
        return jnp.stack(
            [
                jnp.where(core_zero, straight, crossed),
                jnp.where(core_zero, crossed, straight),
            ]
        ).astype(jnp.float32)

    def gather(part):
        return lax.all_gather(part, BOTH, axis=0, tiled=True, axis_index_groups=row_groups)

    def blocks_of(matrix):
        rows, n = matrix.shape
        return matrix.reshape(rows, n // BLOCK, BLOCK).transpose(1, 0, 2).reshape(-1, BLOCK)

    def from_blocks(packed, rows):
        groups, count = packed.shape[0], packed.shape[1] // rows
        parts = packed.reshape(groups, count, rows, BLOCK).transpose(0, 2, 1, 3)
        return parts.reshape(groups * rows, count * BLOCK)

    def scatter(packed):
        part = lax.psum_scatter(
            packed.reshape(-1, packed.shape[-1]),
            BOTH,
            scatter_dimension=0,
            tiled=True,
            axis_index_groups=row_groups,
        )
        return part

    def split_qkv(query, key, value):
        stacked = jnp.stack([query, key, value], axis=0).reshape(3, w_rows, HALF_HEADS, 2, HD)
        return stacked.transpose(3, 1, 2, 0, 4).reshape(2, w_rows, 3 * half_width)

    def join_qkv(parts):
        parts = parts.reshape(2, w_rows, HALF_HEADS, 3, HD)
        return parts.transpose(3, 1, 2, 0, 4).reshape(3, w_rows, D)

    def split_units(gate, upward):
        def halves(matrix):
            parts = matrix.reshape(w_rows, seq, 2, 2, d_rows).transpose(2, 0, 1, 3, 4)
            parts = jnp.pad(parts, ((0, 0),) * 4 + ((0, padded - d_rows),))
            return parts.reshape(2, w_rows, -1, 1, BLOCK // 2)

        both = jnp.concatenate([halves(gate), halves(upward)], axis=3)
        return both.reshape(2, w_rows, 2 * half_ff)

    def join_units(parts):
        parts = parts.reshape(2, w_rows, -1, 2, BLOCK // 2)

        def joined(half):
            half = half.reshape(2, w_rows, seq, 2, padded)[..., :d_rows]
            return half.transpose(1, 2, 0, 3, 4).reshape(w_rows, 4 * seq * d_rows)

        return joined(parts[:, :, :, 0]), joined(parts[:, :, :, 1])

    def whole_out(part):
        matrix = lax.all_gather(part, BOTH, axis=0, tiled=True).reshape(HALF_HEADS, 2, HD, D)
        return lax.dynamic_index_in_dim(matrix, here_y, 1, keepdims=False).reshape(half_width, D)

    def whole_out_back(grad):
        spaced = lax.dynamic_update_slice_in_dim(
            jnp.zeros((HALF_HEADS, 2, HD, D), LOW),
            grad.astype(LOW).reshape(HALF_HEADS, 1, HD, D),
            here_y,
            1,
        )
        return lax.psum_scatter(spaced.reshape(D, D), BOTH, scatter_dimension=0, tiled=True)

    pair_rows = 2 * w_rows
    unit_end = 2 * half_ff // BLOCK * pair_rows
    ffn_end = unit_end + D // BLOCK * padded
    out_end = ffn_end + (D // BLOCK * w_rows if split_heads else 0)
    qkv_end = out_end + 3 * half_width // BLOCK * pair_rows
    layer_weights = []
    for layer in range(LAYERS):
        scale_attn = gain_attn[layer][:, None]
        scale_ffn = gain_ffn[layer][:, None]
        qkv_parts = split_qkv(
            (w_query[layer] * scale_attn).astype(LOW),
            (w_key[layer] * scale_attn).astype(LOW),
            (w_value[layer] * scale_attn).astype(LOW),
        )
        units_part = cross_rows(
            split_units(
                (w_gate[layer] * scale_ffn).astype(LOW), (w_up[layer] * scale_ffn).astype(LOW)
            )
        )
        out_part = w_out[layer].astype(LOW)
        down_part = jnp.pad(w_down[layer].astype(LOW), ((0, padded - d_rows), (0, 0)))
        qkv_matrix = gather(cross_rows(qkv_parts))
        members = [blocks_of(units_part), blocks_of(down_part)]
        if split_heads:
            members.append(blocks_of(out_part))
        packed = gather(jnp.concatenate(members, axis=0)).reshape(2 * seq, -1, BLOCK)
        if split_heads:
            out_matrix = from_blocks(packed[:, ffn_end:], w_rows)
        else:
            out_matrix = whole_out(out_part)
        layer_weights.append((qkv_matrix, out_matrix, packed))

    def placed_ids(ids):
        ids = ids.reshape(seq, 2, 2, tok_rows)
        ids = jnp.where(y_zero, ids, ids[:, ::-1])
        ids = jnp.where(core_zero, ids, ids[:, :, ::-1])
        return ids.transpose(2, 0, 1, 3).reshape(2 * seq, cols)

    def my_tiles(value):
        if spread == 1:
            return value
        return lax.dynamic_slice_in_dim(value, first_tile, tiles, 0)

    positions = jnp.arange(all_rows, dtype=jnp.int32)
    doc_ids = jnp.sum((doc_starts[None, :] <= positions[:, None]).astype(jnp.int32), axis=1)
    docs = placed_ids(doc_ids)
    variates = placed_ids(variate_ids)
    k_doc = docs[:, None, :]
    q_doc = my_tiles(docs[:seq])[:, :, None]
    q_variates = my_tiles(variates[:seq])
    extra_row = jnp.arange(HD, dtype=jnp.int32)[None, :, None]

    def one_hot(ids):
        return ids[:, None, :] == extra_row % VARIATES

    ones_row = (extra_row == 16) | (extra_row == 17) | ((extra_row >= 32) & (extra_row < 35))
    k_aug = jnp.where(one_hot(variates) & (extra_row < 16) | ones_row, 1.0, 0.0).astype(LOW)

    def query_extra(layer):
        same, other = variate_bias[layer, 0, my_head], variate_bias[layer, 1, my_head]
        gap = same - other
        gap_lead, other_lead = (part.astype(LOW).astype(jnp.float32) for part in (gap, other))
        gap_part = jnp.where(extra_row < VARIATES, gap_lead, gap - gap_lead)
        other_part = jnp.where(extra_row == 16, other_lead, other - other_lead)
        spread_gap = jnp.where(one_hot(q_variates), gap_part, 0.0)
        tail = jnp.where(extra_row < 18, other_part, 0.0)
        return jnp.where(extra_row < 16, spread_gap, tail).astype(LOW)

    q_augs = [query_extra(layer) for layer in range(LAYERS)]
    q_onehots = (q_variates[:, None, :] == jnp.arange(VARIATES, dtype=jnp.int32)[:, None]).astype(
        jnp.float32
    )

    def normalize(values):
        inverse = lax.rsqrt(jnp.mean(values * values, axis=-1, keepdims=True) + NORM_EPS)
        return values * inverse, inverse

    def normalize_back(scaled, inverse, inner):
        return inverse * (inner - scaled * jnp.mean(inner * scaled, axis=-1, keepdims=True))

    half_dim = HD // 2
    frequency = jnp.exp(jnp.arange(half_dim).astype(jnp.float32) * (-2.0 * math.log(10000.0) / HD))
    times = beside(time_ids.astype(jnp.float32))
    angles = frequency[:, None] * times[None, :]
    cosines, sines = jnp.cos(angles), jnp.sin(angles)
    start_scaled, start_inverse = normalize(tokens)
    start_normed = beside(start_scaled.astype(LOW))
    start_normed, k_aug, k_doc, q_doc, cosines, sines, *q_augs = lax.optimization_barrier(
        (start_normed, k_aug, k_doc, q_doc, cosines, sines, *q_augs)
    )

    def rotate(values, sines):
        former, latter = values[:, :half_dim], values[:, half_dim:]
        return jnp.concatenate(
            [former * cosines - latter * sines, latter * cosines + former * sines], axis=1
        )

    def to_heads(value):
        if spread > 1:
            value = jnp.repeat(value, spread, axis=0)
        return lax.all_to_all(value, "seq", split_axis=0, concat_axis=0, tiled=True)

    def from_heads(value, whole):
        if spread > 1 and not whole:
            value = lax.dynamic_update_slice_in_dim(
                jnp.zeros((seq,) + value.shape[1:], value.dtype), value, first_tile, 0
            )
        value = lax.all_to_all(value, "seq", split_axis=0, concat_axis=0, tiled=True)
        if spread > 1:
            value = value.reshape((HALF_HEADS, spread) + value.shape[1:])
            value = jnp.sum(value.astype(jnp.float32), axis=1).astype(LOW)
        return value

    stream = tokens
    saved = []
    for layer in range(LAYERS):
        qkv_matrix, out_matrix, packed = layer_weights[layer]
        if layer == 0:
            scaled_one, inverse_one, normed = start_scaled, start_inverse, start_normed
        else:
            scaled_one, inverse_one = normalize(stream)
            normed = beside(scaled_one.astype(LOW))
        projected = dot(qkv_matrix, normed, TT).reshape(HALF_HEADS, 3 * HD, cols)
        query = rotate(projected[:, :HD], sines) * (1.0 / math.sqrt(HD))
        key = rotate(projected[:, HD : 2 * HD], sines)
        sent = jnp.concatenate([query, key, projected[:, 2 * HD :]], axis=1).astype(LOW)
        own = to_heads(sent)
        sib = lax.ppermute(own[:, HD:], "head", CORE_SWAP)
        queries = my_tiles(own)
        q_aug = q_augs[layer]
        out, lse = attention_forward(first, queries, q_aug, q_doc, own, sib, k_aug, k_doc)
        attended = from_heads(out.astype(LOW), False).reshape(half_width, cols)
        middle = stream + fold(dot(attended, out_matrix, TN))
        scaled_two, inverse_two = normalize(middle)
        normed_ffn = beside(scaled_two.astype(LOW))
        both, hidden, partial = ffn_forward(normed_ffn, packed, half_ff, pair_rows, padded)
        saved.append(
            (
                scaled_one, inverse_one, normed, own, sib, queries, q_aug, out, lse, attended,
                scaled_two, inverse_two, normed_ffn, both, hidden,
            )
        )
        stream = middle + fold(partial)

    upstream = cotangent
    layer_grads = [{} for unused in range(LAYERS)]
    bias_parts = [None] * LAYERS
    buffer, sent_last = None, None
    qkv_grad = None

    for layer in reversed(range(LAYERS)):
        qkv_matrix, out_matrix, packed = layer_weights[layer]
        (
            scaled_one, inverse_one, normed, own, sib, queries, q_aug, out, lse, attended,
            scaled_two, inverse_two, normed_ffn, both, hidden,
        ) = saved[layer]
        upstream_low = beside(upstream.astype(LOW))
        grad_units, partial = ffn_backward(upstream_low, packed, both, half_ff, pair_rows, padded)
        inner = fold(partial)
        total_rows = qkv_end if layer < LAYERS - 1 else out_end
        buffer = weight_grad(
            buffer, total_rows, normed_ffn.T, grad_units, "blocks", pair_rows, 0, 2 * padded // pair_rows
        )
        buffer = weight_grad(
            buffer, total_rows, hidden.T, upstream_low, "columns", padded, unit_end, 2
        )
        grad_middle = upstream + normalize_back(scaled_two, inverse_two, inner)
        middle_low = beside(grad_middle.astype(LOW))
        grad_attended = dot(out_matrix, middle_low, NT).astype(LOW)
        if split_heads:
            buffer = weight_grad(
                buffer, total_rows, attended, middle_low, "columns", w_rows, ffn_end, D // BLOCK
            )
        else:
            layer_grads[layer]["out"] = whole_out_back(dot(attended, middle_low, NN))
        if sent_last is not None:
            buffer, sent_last = lax.optimization_barrier((buffer, sent_last))
            layer_grads[layer + 1]["sent"] = sent_last
        buffer, grad_attended = lax.optimization_barrier((buffer, grad_attended))
        sent_last = scatter(buffer)
        out_grad = my_tiles(to_heads(grad_attended.reshape(HALF_HEADS, HD, cols)))
        grad_q, grad_kv = attention_backward(
            first, queries, q_aug, q_doc, lse, out, out_grad, own, sib, k_aug, k_doc
        )
        same_grad = jnp.sum(grad_q[:, HD : HD + VARIATES] * q_onehots)
        all_grad = jnp.sum(grad_q[:, HD + 16])
        crossed = lax.ppermute(grad_kv[seq:], "head", CORE_SWAP)
        grad_kv = (grad_kv[:seq].astype(jnp.float32) + crossed.astype(jnp.float32)).astype(LOW)
        grad_q = (grad_q[:, :HD] * (1.0 / math.sqrt(HD))).astype(LOW)
        if spread > 1:
            grad_q = lax.dynamic_update_slice_in_dim(
                jnp.zeros((seq, HD, cols), LOW), grad_q, first_tile, 0
            )
        grad_heads = from_heads(jnp.concatenate([grad_q, grad_kv], axis=1), True)
        grad_heads = jnp.concatenate(
            [
                rotate(grad_heads[:, :HD].astype(jnp.float32), -sines).astype(LOW),
                rotate(grad_heads[:, HD : 2 * HD].astype(jnp.float32), -sines).astype(LOW),
                grad_heads[:, 2 * HD :],
            ],
            axis=1,
        ).reshape(3 * half_width, cols)
        bias_parts[layer] = jnp.stack([same_grad, all_grad - same_grad])
        if layer > 0:
            buffer = weight_grad(
                None, qkv_end, normed.T, grad_heads, "rows", pair_rows, out_end, 2
            )
        else:
            qkv_grad = dot(normed, grad_heads, TT).astype(LOW)
            qkv_grad, grad_heads, *bias_parts = lax.optimization_barrier(
                (qkv_grad, grad_heads, *bias_parts)
            )
            qkv_grad, sent_last = lax.optimization_barrier((qkv_grad, sent_last))
            layer_grads[0]["sent"] = sent_last
            qkv_grad = scatter(qkv_grad)
        inner = fold(dot(grad_heads, qkv_matrix, TT))
        upstream = grad_middle + normalize_back(scaled_one, inverse_one, inner)

    bias_local = lax.dynamic_update_slice(
        jnp.zeros((LAYERS, 2, HEADS), jnp.float32), jnp.stack(bias_parts)[:, :, None], (0, 0, my_head)
    )
    bias_total = bias_local
    for axis, size in (("head", 4), ("seq", seq)):
        hop = 1
        while hop < size:
            swap = [(place, place ^ hop) for place in range(size)]
            bias_total = bias_total + lax.ppermute(bias_total, axis, swap)
            hop *= 2

    finished = []
    for layer in range(LAYERS):
        sent = layer_grads[layer]["sent"]
        if layer < LAYERS - 1:
            above = sent[out_end:]
            layer_grads[layer + 1]["qkv"] = from_blocks(above[None], pair_rows)
        units_part = from_blocks(sent[None, :unit_end], pair_rows)
        gate_grad, up_grad = join_units(cross_back(units_part))
        down_grad = from_blocks(sent[None, unit_end:ffn_end], padded)[:d_rows].astype(jnp.float32)
        if split_heads:
            out_grad = from_blocks(sent[None, ffn_end:out_end], w_rows)
        else:
            out_grad = layer_grads[layer]["out"]
        qkv_part = qkv_grad if layer == 0 else layer_grads[layer]["qkv"]
        qkv_grads = join_qkv(cross_back(qkv_part))
        gain_one = sum(
            jnp.sum(qkv_grads[place] * member[layer], axis=1)
            for place, member in enumerate((w_query, w_key, w_value))
        )
        gain_two = jnp.sum(gate_grad * w_gate[layer] + up_grad * w_up[layer], axis=1)
        scale_attn = gain_attn[layer][:, None]
        scale_ffn = gain_ffn[layer][:, None]
        finished.append(
            (
                qkv_grads[0] * scale_attn,
                qkv_grads[1] * scale_attn,
                qkv_grads[2] * scale_attn,
                out_grad.astype(jnp.float32),
                gate_grad * scale_ffn,
                up_grad * scale_ffn,
                down_grad,
                gain_one,
                gain_two,
            )
        )
    stacked = [jnp.stack([finished[layer][place] for layer in range(LAYERS)]) for place in range(9)]
    return (stream, upstream, *stacked, bias_total)


def solution(mesh):
    rows = P(BOTH, None)
    middle = P(None, BOTH, None)
    gains = P(None, BOTH)
    return jax.shard_map(
        on_device,
        mesh=mesh,
        in_specs=(rows,) + (middle,) * 7 + (gains,) * 2 + (P(),) * 3 + (P(BOTH), rows),
        out_specs=(rows, rows) + (middle,) * 7 + (gains,) * 2 + (P(),),
        check_vma=False,
    )
```

time: 3710 us -> 840 us (0.23)
  waiting for transfers between devices: 2840 us -> 289 us
  matrix products: 452 us -> 19.4 us
  Pallas kernels: 0 us -> 179 us
  other arithmetic: 109 us -> 65 us
  starting transfers between devices: 37.7 us -> 77.5 us
    reduce_scatter x18 -> x3, waiting for transfers between devices: 2140 us -> 70.6 us  [scatter(): lax.psum_scatter(packed.reshape(-1, packed.shape[-1]), BOTH, scatter_dime...]
    all_gather x18 -> x4, waiting for transfers between devices: 656 us -> 71.9 us  [gather(): lax.all_gather(part, BOTH, axis=0, tiled=True, axis_index_groups=row_groups)]
    dot_general x154 -> x9, matrix products: 452 us -> 19.4 us  [dot(): lax.dot_general(left, right, dims, preferred_element_type=jnp.float32)]
    pallas_call x0 -> x15, Pallas kernels: none -> 179 us  [the longest x2 77.2 us: attention_backward(): pl.pallas_call(functools.partial(backward_kernel, seq=seq), grid_spec=plt...]
    unnamed x2 -> x0, blocking collectives: 82.3 us -> none
    ppermute x0 -> x42, waiting for transfers between devices: none -> 81 us  [the longest x17 63.8 us: swap_y(): return lax.ppermute(value, 'head', Y_SWAP)]
    ppermute x0 -> x42, starting transfers between devices: none -> 55.9 us  [the longest x17 21.3 us: swap_y(): return lax.ppermute(value, 'head', Y_SWAP)]
    all_to_all x6 -> x3, blocking collectives: 52.6 us -> 98.1 us  [to_heads(): return lax.all_to_all(value, 'seq', split_axis=0, concat_axis=0, tiled=True)]
  transfers between devices with their start and end apart: 46 -> 54, of which waited for: 38 -> 29; matrix products, arithmetic and copies ran while one was open for 11% -> 16% of each run, Pallas kernels for 0% -> 19%
where the time goes in v1:
time: 840 us; the launch traced here: 829 us
  waiting for transfers between devices  289 us (34%)
  Pallas kernels  179 us (21%)
  blocking collectives  98.1 us (12%)
  starting transfers between devices  77.5 us (9%)
  local copies, waits for them, and re-layouts  75.4 us (9%)
  other arithmetic  65 us (8%)
  between operations  24.5 us (3%)
  matrix products  19.4 us (2%)
    all_to_all x3, blocking collectives, to_heads(): return lax.all_to_all(value, 'seq', split_axis=0, concat_axis=0, tiled=True)  98.1 us
    pallas_call x2, Pallas kernels, attention_backward(): pl.pallas_call(functools.partial(backward_kernel, seq=seq), grid_spec=plt...  77.2 us
    all_gather x4, waiting for transfers between devices, gather(): lax.all_gather(part, BOTH, axis=0, tiled=True, axis_index_groups=row_groups)  71.9 us
    reduce_scatter x3, waiting for transfers between devices, scatter(): lax.psum_scatter(packed.reshape(-1, packed.shape[-1]), BOTH, scatter_dime...  70.6 us
    all_to_all x4, waiting for transfers between devices, from_heads(): lax.all_to_all(value, 'seq', split_axis=0, concat_axis=0, tiled=True)  64.6 us
    ppermute x17, waiting for transfers between devices, swap_y(): return lax.ppermute(value, 'head', Y_SWAP)  63.8 us
    pallas_call x2, Pallas kernels, attention_forward(): pl.pallas_call(functools.partial(forward_kernel, seq=seq, width=4), grid_...  37.1 us
    pallas_call x7, Pallas kernels, weight_grad(): pl.pallas_call(functools.partial(weight_grad_kernel, rows=rows, kind=kind...  28.2 us
  transfers between devices with their start and end apart: 54, of which 29 were waited for; matrix products, arithmetic and copies ran while one was open for 16% of the time, Pallas kernels for 19%

profile of v1, /device:TPU:0, one launch (start us, length us, event | category | flops | bytes accessed | tf_op | source)
XLA Modules:
  0.0 828.8 jit_solution(9500804296055274530)
XLA Ops:
  75.9 44.9 %all_to_all.40.q_ref.own_ref = bf16[8,192,256]{2,1,0:T(8,128)(2,1)S(1)} all-to-all(bf16[8,192,256]{2,1,0:T(8,128)(2,1)S(1)} %pad_maximum_fusion), channel_id=1, replica_groups=mesh['seq'=8,'head'=4] {'seq'}, dimensions={0} | all-to-all | bytes 1572864 | tf_op jit(solution)/shard_map/all_to_all | solution.py:611
  124.6 18.7 %attention_forward.2 = (f32[8,64,256]{2,1,0:T(8,128)}, f32[8,8,256]{2,1,0:T(8,128)}) custom-call(s32[1]{0:T(128)} %constant.88.clone.1.first_ref, bf16[8,192,256]{2,1,0:T(8,128)(2,1)} %copy-done, bf16[8,64,256]{2,1,0:T(8,128)(2,1)} %get-tuple-element.53.q_aug_ref, s32[8,256,1]{2,1,0:T(8,128)} %copy.159.q_doc_ref, bf16[8,192,256]{2,1,0:T(8,128)(2,1)} %copy-done, ...), custom_call_target="tpu_custom_call" | custom-call | tf_op jit(solution)/shard_map/attention_forward/pallas_call | solution.py:161
  148.5 30.4 %all-gather.7.cloned.1.call-done = bf16[20480,256]{1,0:T(8,128)(2,1)} async-done(((bf16[1280,256]{1,0:T(8,128)(2,1)}), bf16[20480,256]{1,0:T(8,128)(2,1)}) %all-gather.7.cloned.1.call-update) | async-done | bytes 10485776 | tf_op jit(solution)/shard_map/all_gather | solution.py:451
  183.5 7.0 collective-permute-done.7
  192.3 6.2 collective-permute-done.8
  199.6 9.2 %ffn_forward.2 = (f32[12,256,256]{2,1,0:T(8,128)}, bf16[256,1536]{1,0:T(8,128)(2,1)}, f32[256,1024]{1,0:T(8,128)}) custom-call(bf16[256,1024]{1,0:T(8,128)(2,1)} %get-tuple-element.185.x_ref, bf16[16,1280,256]{2,1,0:T(8,128)(2,1)} %bitcast.217), custom_call_target="tpu_custom_call" | custom-call | tf_op jit(solution)/shard_map/ffn_forward/pallas_call | solution.py:278
  219.5 6.2 all-gather.9.cloned.1.call-done
  228.9 41.1 %all_to_all.41.q_ref.own_ref = bf16[8,192,256]{2,1,0:T(8,128)(2,1)S(1)} all-to-all(bf16[8,192,256]{2,1,0:T(8,128)(2,1)S(1)} %pad_maximum_fusion.1), channel_id=1, replica_groups=mesh['seq'=8,'head'=4] {'seq'}, dimensions={0} | all-to-all | bytes 1572864 | tf_op jit(solution)/shard_map/all_to_all | solution.py:611
  272.8 18.4 %attention_forward.3 = (f32[8,64,256]{2,1,0:T(8,128)}, f32[8,8,256]{2,1,0:T(8,128)}) custom-call(s32[1]{0:T(128)} %constant.88.clone.1.first_ref, bf16[8,192,256]{2,1,0:T(8,128)(2,1)} %copy-done.1, bf16[8,64,256]{2,1,0:T(8,128)(2,1)} %get-tuple-element.59.q_aug_ref, s32[8,256,1]{2,1,0:T(8,128)} %copy.159.q_doc_ref, bf16[8,192,256]{2,1,0:T(8,128)(2,1)} %copy-done.1, ...), custom_call_target="tpu_custom_call" | custom-call | tf_op jit(solution)/shard_map/attention_forward/pallas_call | solution.py:161
  296.5 35.3 %all-gather.11.cloned.1.call-done = bf16[20480,256]{1,0:T(8,128)(2,1)} async-done(((bf16[1280,256]{1,0:T(8,128)(2,1)}), bf16[20480,256]{1,0:T(8,128)(2,1)}) %all-gather.11.cloned.1.call-update) | async-done | bytes 10485776 | tf_op jit(solution)/shard_map/all_gather | solution.py:451
  339.2 7.0 collective-permute-done.16
  357.9 9.1 %ffn_forward.3 = (f32[12,256,256]{2,1,0:T(8,128)}, bf16[256,1536]{1,0:T(8,128)(2,1)}, f32[256,1024]{1,0:T(8,128)}) custom-call(bf16[256,1024]{1,0:T(8,128)(2,1)} %get-tuple-element.187.x_ref, bf16[16,1280,256]{2,1,0:T(8,128)(2,1)} %bitcast.220), custom_call_target="tpu_custom_call" | custom-call | tf_op jit(solution)/shard_map/ffn_forward/pallas_call | solution.py:278
  367.0 9.4 %ffn_backward.2 = (bf16[12,256,256]{2,1,0:T(8,128)(2,1)}, f32[256,1024]{1,0:T(8,128)}) custom-call(bf16[256,1024]{1,0:T(8,128)(2,1)} %pad_maximum_fusion.12.g_ref.right_ref, bf16[16,1280,256]{2,1,0:T(8,128)(2,1)} %bitcast.221, f32[12,256,256]{2,1,0:T(8,128)} %get-tuple-element.62.both_ref), custom_call_target="tpu_custom_call" | custom-call | tf_op jit(solution)/shard_map/ffn_backward/pallas_call | solution.py:310
  379.7 7.1 collective-permute-done.20
  414.8 12.1 %all_to_all.42.grad_ref = bf16[8,64,256]{2,1,0:T(8,128)(2,1)} all-to-all(bf16[8,64,256]{2,1,0:T(8,128)(2,1)S(1)} %bitcast.271), channel_id=1, replica_groups=mesh['seq'=8,'head'=4] {'seq'}, dimensions={0} | all-to-all | bytes 524288 | tf_op jit(solution)/shard_map/all_to_all | solution.py:611
  426.9 38.6 %attention_backward.2 = (f32[8,128,256]{2,1,0:T(8,128)}, bf16[16,128,256]{2,1,0:T(8,128)(2,1)}) custom-call(s32[1]{0:T(128)} %constant.88.clone.1.first_ref, bf16[8,192,256]{2,1,0:T(8,128)(2,1)} %copy-done.1, bf16[8,64,256]{2,1,0:T(8,128)(2,1)} %get-tuple-element.59.q_aug_ref, s32[8,256,1]{2,1,0:T(8,128)} %copy.159.q_doc_ref, ...), custom_call_target="tpu_custom_call" | custom-call | tf_op jit(solution)/shard_map/attention_backward/pallas_call | solution.py:182
  474.3 33.5 %all-to-all-done.5 = bf16[8,192,256]{2,1,0:T(8,128)(2,1)} async-done(((bf16[8,192,256]{2,1,0:T(8,128)(2,1)}), bf16[8,192,256]{2,1,0:T(8,128)(2,1)}, u32[]{:S(2)}, u32[]{:S(2)}) %all-to-all-start.5) | async-done | bytes 786464 | tf_op jit(solution)/shard_map/all_to_all | solution.py:618
  513.5 6.9 collective-permute-done.23
  522.1 6.2 collective-permute-done.24
  529.2 9.3 %ffn_backward.3 = (bf16[12,256,256]{2,1,0:T(8,128)(2,1)}, f32[256,1024]{1,0:T(8,128)}) custom-call(bf16[256,1024]{1,0:T(8,128)(2,1)} %pad_maximum_fusion.14.g_ref.right_ref, bf16[16,1280,256]{2,1,0:T(8,128)(2,1)} %bitcast.218, f32[12,256,256]{2,1,0:T(8,128)} %get-tuple-element.70.both_ref), custom_call_target="tpu_custom_call" | custom-call | tf_op jit(solution)/shard_map/ffn_backward/pallas_call | solution.py:310
  588.8 38.6 %attention_backward.3 = (f32[8,128,256]{2,1,0:T(8,128)}, bf16[16,128,256]{2,1,0:T(8,128)(2,1)}) custom-call(s32[1]{0:T(128)} %constant.88.clone.1.first_ref, bf16[8,192,256]{2,1,0:T(8,128)(2,1)} %copy-done, bf16[8,64,256]{2,1,0:T(8,128)(2,1)} %get-tuple-element.53.q_aug_ref, s32[8,256,1]{2,1,0:T(8,128)} %copy.159.q_doc_ref, ...), custom_call_target="tpu_custom_call" | custom-call | tf_op jit(solution)/shard_map/attention_backward/pallas_call | solution.py:182
  649.0 31.0 %all-to-all-done.7 = bf16[8,192,256]{2,1,0:T(8,128)(2,1)} async-done(((bf16[8,192,256]{2,1,0:T(8,128)(2,1)}), bf16[8,192,256]{2,1,0:T(8,128)(2,1)}, u32[]{:S(2)}, u32[]{:S(2)}) %all-to-all-start.7) | async-done | bytes 786464 | tf_op jit(solution)/shard_map/all_to_all | solution.py:618
  711.1 25.5 %reduce-scatter.6.cloned.1.call-done = bf16[1664,256]{1,0:T(8,128)(2,1)} async-done(((bf16[26624,256]{1,0:T(8,128)(2,1)}), bf16[1664,256]{1,0:T(8,128)(2,1)}) %reduce-scatter.6.cloned.1.call-update) | async-done | bytes 851984 | tf_op jit(solution)/shard_map/reduce_scatter | solution.py:463
  761.1 45.1 %reduce-scatter.8.cloned.1.call-done = bf16[64,1536]{1,0:T(8,128)(2,1)} async-done(((bf16[1024,1536]{1,0:T(8,128)(2,1)}), bf16[64,1536]{1,0:T(8,128)(2,1)}) %reduce-scatter.8.cloned.1.call-update) | async-done | bytes 196624 | tf_op jit(solution)/shard_map/reduce_scatter | solution.py:463
  (567 shorter events, 307.5 us)
Async XLA Ops:
  7.2 65.5 %all-gather.5.cloned.1.call-start = ((), (), s32[]{:S(2)}) async-start(), calls=%async_computation.11 | async-start | bytes 3342336 | tf_op jit(solution)/shard_map/all_gather | solution.py:451
  21.6 157.4 %all-gather.7.cloned.1.call-start = ((), (), s32[]{:S(2)}) async-start(), calls=%async_computation.12 | async-start | bytes 11141120 | tf_op jit(solution)/shard_map/all_gather | solution.py:451
  27.2 16.7 %collective-permute-start.5 = (bf16[32,3072]{1,0:T(8,128)(2,1)}, bf16[32,3072]{1,0:T(8,128)(2,1)S(1)}, u32[]{:S(2)}, u32[]{:S(2)}) collective-permute-start(bf16[32,3072]{1,0:T(8,128)(2,1)} %select_n.341), channel_id=1, source_target_pairs={{0,0},{1,2},{2,1},{3,3},{4,4},{5,6},{6,5},{7,7},{8,8},{9,10},{10,9... | collective-permute-start | bytes 589832 | tf_op jit(solution)/shard_map/ppermute | solution.py:429
  29.8 14.2 %collective-permute-start.6 = (bf16[32,3072]{1,0:T(8,128)(2,1)}, bf16[32,3072]{1,0:T(8,128)(2,1)}, u32[]{:S(2)}, u32[]{:S(2)}) collective-permute-start(bf16[32,3072]{1,0:T(8,128)(2,1)} %select_n.343), channel_id=1, source_target_pairs={{0,2},{2,3},{3,1},{1,0},{4,6},{6,7},{7,5},{5,4},{8,10},{10,11},{11... | collective-permute-start | bytes 589832 | tf_op jit(solution)/shard_map/ppermute | solution.py:430
  49.0 176.6 %all-gather.9.cloned.1.call-start = ((), (), s32[]{:S(2)}) async-start(), calls=%async_computation.13 | async-start | bytes 3342336 | tf_op jit(solution)/shard_map/all_gather | solution.py:451
  59.2 272.5 %all-gather.11.cloned.1.call-start = ((), (), s32[]{:S(2)}) async-start(), calls=%async_computation.14 | async-start | bytes 11141120 | tf_op jit(solution)/shard_map/all_gather | solution.py:451
  60.7 11.9 %collective-permute-start.2 = (bf16[128,1024]{1,0:T(8,128)(2,1)S(1)}, bf16[128,1024]{1,0:T(8,128)(2,1)S(1)}, u32[]{:S(2)}, u32[]{:S(2)}) collective-permute-start(bf16[128,1024]{1,0:T(8,128)(2,1)S(1)} %multiply_convert_fusion.9), channel_id=1, source_target_pairs={{0,2},{2,0},{1,3},{3,1},{4,6},{6,4},{5,7},{7,5},{8,10},{10,8},{9,1... | collective-permute-start | bytes 786440 | tf_op jit(solution)/shard_map/ppermute | solution.py:417
  145.1 36.3 %all-to-all-start.1 = ((bf16[8,64,256]{2,1,0:T(8,128)(2,1)}), bf16[8,64,256]{2,1,0:T(8,128)(2,1)S(1)}, u32[]{:S(2)}, u32[]{:S(2)}) async-start(bf16[8,64,256]{2,1,0:T(8,128)(2,1)} %convert_element_type.312), calls=%async_computation.1 | async-start | bytes 524288 | tf_op jit(solution)/shard_map/all_to_all | solution.py:618
  293.0 42.2 %all-to-all-start.3 = ((bf16[8,64,256]{2,1,0:T(8,128)(2,1)}), bf16[8,64,256]{2,1,0:T(8,128)(2,1)S(1)}, u32[]{:S(2)}, u32[]{:S(2)}) async-start(bf16[8,64,256]{2,1,0:T(8,128)(2,1)} %convert_element_type.324), calls=%async_computation.3 | async-start | bytes 524288 | tf_op jit(solution)/shard_map/all_to_all | solution.py:618
  296.4 278.4 %reduce-scatter.4.cloned.1.call-start = ((), (), s32[]{:S(2)}) async-start(), calls=%async_computation.15 | async-start | bytes 11141120 | tf_op jit(solution)/shard_map/reduce_scatter | solution.py:463
  338.6 13.2 %collective-permute-start.19 = (bf16[128,1024]{1,0:T(8,128)(2,1)S(1)}, bf16[128,1024]{1,0:T(8,128)(2,1)S(1)}, u32[]{:S(2)}, u32[]{:S(2)}) collective-permute-start(bf16[128,1024]{1,0:T(8,128)(2,1)S(1)} %convert_element_type.332), channel_id=1, source_target_pairs={{0,2},{2,0},{1,3},{3,1},{4,6},{6,4},{5,7},{7,5},{8,10},{10,8},{9,1... | collective-permute-start | bytes 786440 | tf_op jit(solution)/shard_map/ppermute | solution.py:417
  346.5 10.3 %collective-permute-start.17 = (bf16[128,1024]{1,0:T(8,128)(2,1)S(1)}, bf16[128,1024]{1,0:T(8,128)(2,1)S(1)}, u32[]{:S(2)}, u32[]{:S(2)}) collective-permute-start(bf16[128,1024]{1,0:T(8,128)(2,1)S(1)} %multiply_convert_fusion.6), channel_id=1, source_target_pairs={{0,2},{2,0},{1,3},{3,1},{4,6},{6,4},{5,7},{7,5},{8,10},{10,8},{9,1... | collective-permute-start | bytes 786440 | tf_op jit(solution)/shard_map/ppermute | solution.py:417
  377.5 9.3 %collective-permute-start.20 = (bf16[128,1024]{1,0:T(8,128)(2,1)S(1)}, bf16[128,1024]{1,0:T(8,128)(2,1)S(1)}, u32[]{:S(2)}, u32[]{:S(2)}) collective-permute-start(bf16[128,1024]{1,0:T(8,128)(2,1)S(1)} %slice.787), channel_id=1, source_target_pairs={{0,2},{2,0},{1,3},{3,1},{4,6},{6,4},{5,7},{7,5},{8,10},{10,8},{9,1... | collective-permute-start | bytes 786440 | tf_op jit(solution)/shard_map/ppermute | solution.py:417
  379.1 11.8 %collective-permute-start.18 = (bf16[128,1024]{1,0:T(8,128)(2,1)S(1)}, bf16[128,1024]{1,0:T(8,128)(2,1)S(1)}, u32[]{:S(2)}, u32[]{:S(2)}) collective-permute-start(bf16[128,1024]{1,0:T(8,128)(2,1)S(1)} %slice.788), channel_id=1, source_target_pairs={{0,2},{2,0},{1,3},{3,1},{4,6},{6,4},{5,7},{7,5},{8,10},{10,8},{9,1... | collective-permute-start | bytes 786440 | tf_op jit(solution)/shard_map/ppermute | solution.py:417
  392.1 15.2 %collective-permute-start.21 = (bf16[128,1024]{1,0:T(8,128)(2,1)S(1)}, bf16[128,1024]{1,0:T(8,128)(2,1)}, u32[]{:S(2)}, u32[]{:S(2)}) collective-permute-start(bf16[128,1024]{1,0:T(8,128)(2,1)S(1)} %get-tuple-element.148), channel_id=1, source_target_pairs={{0,2},{2,0},{1,3},{3,1},{4,6},{6,4},{5,7},{7,5},{8,10},{10,8},{9,1... | collective-permute-start | bytes 786440 | tf_op jit(solution)/shard_map/ppermute | solution.py:417
  469.8 38.1 %all-to-all-start.5 = ((bf16[8,192,256]{2,1,0:T(8,128)(2,1)}), bf16[8,192,256]{2,1,0:T(8,128)(2,1)}, u32[]{:S(2)}, u32[]{:S(2)}) async-start(bf16[8,192,256]{2,1,0:T(8,128)(2,1)} %pad_maximum_fusion.2), calls=%async_computation.5 | async-start | bytes 1572864 | tf_op jit(solution)/shard_map/all_to_all | solution.py:618
  474.0 262.6 %reduce-scatter.6.cloned.1.call-start = ((), (), s32[]{:S(2)}) async-start(), calls=%async_computation.16 | async-start | bytes 14483456 | tf_op jit(solution)/shard_map/reduce_scatter | solution.py:463
  548.7 19.6 %collective-permute-start.26 = (bf16[128,1024]{1,0:T(8,128)(2,1)S(1)}, bf16[128,1024]{1,0:T(8,128)(2,1)}, u32[]{:S(2)}, u32[]{:S(2)}) collective-permute-start(bf16[128,1024]{1,0:T(8,128)(2,1)S(1)} %get-tuple-element.144), channel_id=1, source_target_pairs={{0,2},{2,0},{1,3},{3,1},{4,6},{6,4},{5,7},{7,5},{8,10},{10,8},{9,1... | collective-permute-start | bytes 786440 | tf_op jit(solution)/shard_map/ppermute | solution.py:417
  574.9 13.2 %all-to-all-start.6 = ((bf16[8,64,256]{2,1,0:T(8,128)(2,1)}), bf16[8,64,256]{2,1,0:T(8,128)(2,1)S(1)}, u32[]{:S(2)}, u32[]{:S(2)}) async-start(bf16[8,64,256]{2,1,0:T(8,128)(2,1)} %bitcast.52), calls=%async_computation.7 | async-start | bytes 524288 | tf_op jit(solution)/shard_map/all_to_all | solution.py:611
  628.8 10.2 %collective-permute-start.35 = (bf16[32,3072]{1,0:T(8,128)(2,1)S(1)}, bf16[32,3072]{1,0:T(8,128)(2,1)}, u32[]{:S(2)}, u32[]{:S(2)}) collective-permute-start(bf16[32,3072]{1,0:T(8,128)(2,1)S(1)} %bitcast.276), channel_id=1, source_target_pairs={{0,0},{1,2},{2,1},{3,3},{4,4},{5,6},{6,5},{7,7},{8,8},{9,10},{10,9... | collective-permute-start | bytes 589832 | tf_op jit(solution)/shard_map/ppermute | solution.py:441
  634.0 46.0 %all-to-all-start.7 = ((bf16[8,192,256]{2,1,0:T(8,128)(2,1)}), bf16[8,192,256]{2,1,0:T(8,128)(2,1)}, u32[]{:S(2)}, u32[]{:S(2)}) async-start(bf16[8,192,256]{2,1,0:T(8,128)(2,1)} %pad_maximum_fusion.3), calls=%async_computation.8 | async-start | bytes 1572864 | tf_op jit(solution)/shard_map/all_to_all | solution.py:618
  638.8 167.4 %reduce-scatter.8.cloned.1.call-start = ((), (), s32[]{:S(2)}) async-start(), calls=%async_computation.17 | async-start | bytes 3342336 | tf_op jit(solution)/shard_map/reduce_scatter | solution.py:463
  737.8 16.6 %collective-permute-start.33 = (bf16[32,3072]{1,0:T(8,128)(2,1)S(1)}, bf16[32,3072]{1,0:T(8,128)(2,1)S(1)}, u32[]{:S(2)}, u32[]{:S(2)}) collective-permute-start(bf16[32,3072]{1,0:T(8,128)(2,1)S(1)} %bitcast.274), channel_id=1, source_target_pairs={{0,0},{1,2},{2,1},{3,3},{4,4},{5,6},{6,5},{7,7},{8,8},{9,10},{10,9... | collective-permute-start | bytes 589832 | tf_op jit(solution)/shard_map/ppermute | solution.py:441
  738.5 15.9 %collective-permute-start.34 = (bf16[32,3072]{1,0:T(8,128)(2,1)S(1)}, bf16[32,3072]{1,0:T(8,128)(2,1)S(1)}, u32[]{:S(2)}, u32[]{:S(2)}) collective-permute-start(bf16[32,3072]{1,0:T(8,128)(2,1)S(1)} %bitcast.275), channel_id=1, source_target_pairs={{2,0},{3,2},{1,3},{0,1},{6,4},{7,6},{5,7},{4,5},{10,8},{11,10},{9,... | collective-permute-start | bytes 589832 | tf_op jit(solution)/shard_map/ppermute | solution.py:442
  (109 other events, 718.7 us)
Sparse Core Ops, SparseCore 0:
  21.7 47.6 all-gather.4
  72.3 106.6 all-gather.6
  181.3 44.3 all-gather.8
  228.3 103.3 all-gather.10
  414.0 132.4 reduce-scatter.3
  575.0 161.5 reduce-scatter.5
  741.5 64.6 reduce-scatter.7

commit v2 on v1

v2 whole, which is shorter than its diff:
```python
import functools
import math

import jax
import jax.numpy as jnp
from jax import lax
from jax.experimental import pallas as pl
from jax.experimental.pallas import tpu as pltpu
from jax.sharding import PartitionSpec as P

D = 1024
HEADS = 16
HD = 64
LAYERS = 2
VARIATES = 8
BLOCK = 256

NORM_EPS = 1e-05
FLOOR_SCORE = -1e30
LOW = jnp.bfloat16
BOTH = ("seq", "head")

QUARTERS = 4
QUARTER_HEADS = HEADS // QUARTERS
Q_TILE = 256
Y_SWAP = [(place, place ^ 2) for place in range(4)]
CORE_SWAP = [(place, place ^ 1) for place in range(4)]

NN = (((1,), (0,)), ((), ()))
NT = (((1,), (1,)), ((), ()))
TN = (((0,), (0,)), ((), ()))
TT = (((0,), (1,)), ((), ()))
VMEM_LIMIT = 56 * 1024 * 1024


def cost(flops, operands, results, transcendentals=0):
    moved = sum(member.size * member.dtype.itemsize for member in [*operands, *results])
    return pl.CostEstimate(flops=flops, bytes_accessed=moved, transcendentals=transcendentals)


def dot(left, right, dims):
    return lax.dot_general(left, right, dims, preferred_element_type=jnp.float32)


def forward_kernel(q_ref, q_aug_ref, own_ref, sib_ref, k_aug_ref, out_ref, lse_ref, *, width):
    blocks = own_ref.shape[0]
    sources = ((own_ref, HD), (sib_ref, 0))
    spots = [(half, block) for half in range(2) for block in range(blocks)]
    cols = q_ref.shape[-1]
    q_side = jnp.concatenate([q_ref[0, :HD, :], q_aug_ref[0]], axis=0).T
    top = jnp.full((cols, 1), FLOOR_SCORE, jnp.float32)
    total = jnp.zeros((cols, 1), jnp.float32)
    acc = jnp.zeros((cols, HD), jnp.float32)
    for start in range(0, len(spots), width):
        group = spots[start : start + width]
        parts = []
        for half, block in group:
            ref, low_row = sources[half]
            extra = k_aug_ref[half * blocks + block]
            k_side = jnp.concatenate([ref[block, low_row : low_row + HD, :], extra], axis=0)
            parts.append(dot(q_side, k_side, NN))
        peak = functools.reduce(jnp.maximum, parts)
        fresh = jnp.maximum(top, jnp.max(peak, axis=-1, keepdims=True))
        shrink = jnp.exp(top - fresh)
        probs = [jnp.exp(part - fresh) for part in parts]
        total = total * shrink + jnp.sum(sum(probs[1:], probs[0]), axis=-1, keepdims=True)
        acc = acc * shrink
        for prob, (half, block) in zip(probs, group):
            ref, low_row = sources[half]
            values = ref[block, low_row + HD : low_row + 2 * HD, :]
            acc = acc + dot(prob.astype(LOW), values, NT)
        top = fresh
    result = acc / total
    lse = jnp.broadcast_to(top + jnp.log(total), (cols, HD))
    both = jnp.concatenate([result, lse], axis=1).T
    out_ref[0] = both[:HD].astype(LOW)
    lse_ref[0] = both[HD : HD + 8]


def split_rows(row, rows):
    one = row.astype(LOW).astype(jnp.float32)
    two = (row - one).astype(LOW).astype(jnp.float32)
    three = row - one - two
    pad = jnp.zeros((rows - 3, row.shape[-1]), jnp.float32)
    return jnp.concatenate([one, two, three, pad], axis=0).astype(LOW)


def backward_kernel(
    q_ref, q_aug_ref, lse_ref, out_ref, grad_ref, own_ref, sib_ref, k_aug_ref, dq_ref, dkv_ref, dkv_acc
):
    step = pl.program_id(0)
    blocks = own_ref.shape[0]
    sources = ((own_ref, HD), (sib_ref, 0))
    cols, key_cols = q_ref.shape[-1], own_ref.shape[-1]

    @pl.when(step == 0)
    def _():
        dkv_acc[...] = jnp.zeros_like(dkv_acc)

    q_low = q_ref[0, :HD, :]
    g_low = grad_ref[0]
    row_dot = jnp.sum(
        g_low.astype(jnp.float32) * out_ref[0].astype(jnp.float32), axis=0, keepdims=True
    )
    aug = jnp.concatenate(
        [q_aug_ref[0, :32, :], split_rows(-lse_ref[0, :1, :], 16), q_aug_ref[0, 48:, :]], axis=0
    )
    q_side = jnp.concatenate([q_low, aug], axis=0).T
    g_side = jnp.concatenate([g_low, split_rows(-row_dot, HD)], axis=0).T
    ones = jnp.concatenate(
        [jnp.ones((16, key_cols), LOW), jnp.zeros((HD - 16, key_cols), LOW)], axis=0
    )
    dq = jnp.zeros((cols, 2 * HD), jnp.float32)
    for half in range(2):
        ref, low_row = sources[half]
        for block in range(blocks):
            spot = half * blocks + block
            k_side = jnp.concatenate(
                [ref[block, low_row : low_row + HD, :], k_aug_ref[spot]], axis=0
            )
            v_side = jnp.concatenate([ref[block, low_row + HD : low_row + 2 * HD, :], ones], axis=0)
            prob = jnp.exp(dot(q_side, k_side, NN))
            score_grad = (prob * dot(g_side, v_side, NN)).astype(LOW)
            dq = dq + dot(score_grad, k_side, NT)
            dkv_acc[spot, :HD, :] += dot(q_low, score_grad, NN)
            dkv_acc[spot, HD:, :] += dot(g_low, prob.astype(LOW), NN)
    dq_ref[0] = dq.T

    @pl.when(step == pl.num_programs(0) - 1)
    def _():
        dkv_ref[...] = dkv_acc[...].astype(LOW)


def whole_spec(array):
    rank = array.ndim
    return pl.BlockSpec(array.shape, lambda i: (0,) * rank)


def tile_spec(rows, cols):
    cuts = cols // Q_TILE
    return pl.BlockSpec((1, rows, Q_TILE), lambda i: (i // cuts, 0, i % cuts))


def attention_forward(queries, q_aug, own, sib, k_aug):
    tiles, unused, cols = queries.shape
    pairs = 2 * tiles * own.shape[0] * cols * cols
    results = [
        jax.ShapeDtypeStruct((tiles, HD, cols), LOW),
        jax.ShapeDtypeStruct((tiles, 8, cols), jnp.float32),
    ]
    return pl.pallas_call(
        functools.partial(forward_kernel, width=2),
        grid=(tiles * cols // Q_TILE,),
        in_specs=[tile_spec(3 * HD, cols), tile_spec(HD, cols)]
        + [whole_spec(member) for member in (own, sib, k_aug)],
        out_specs=[tile_spec(HD, cols), tile_spec(8, cols)],
        out_shape=results,
        cost_estimate=cost(16 * HD * pairs, [queries, own, sib], results, pairs),
        compiler_params=pltpu.CompilerParams(vmem_limit_bytes=VMEM_LIMIT),
        name="attention_forward",
    )(queries, q_aug, own, sib, k_aug)


def attention_backward(queries, q_aug, lse, out, grad, own, sib, k_aug):
    tiles, unused, cols = queries.shape
    dkv_shape = (2 * own.shape[0], 2 * HD, cols)
    pairs = 2 * tiles * own.shape[0] * cols * cols
    results = [
        jax.ShapeDtypeStruct((tiles, 2 * HD, cols), jnp.float32),
        jax.ShapeDtypeStruct(dkv_shape, LOW),
    ]
    return pl.pallas_call(
        backward_kernel,
        grid=(tiles * cols // Q_TILE,),
        in_specs=[tile_spec(3 * HD, cols), tile_spec(HD, cols), tile_spec(8, cols)]
        + [tile_spec(HD, cols)] * 2
        + [whole_spec(member) for member in (own, sib, k_aug)],
        out_specs=[tile_spec(2 * HD, cols), pl.BlockSpec(dkv_shape, lambda i: (0, 0, 0))],
        out_shape=results,
        cost_estimate=cost(32 * HD * pairs, [queries, own, sib], results, pairs),
        scratch_shapes=[pltpu.VMEM(dkv_shape, jnp.float32)],
        compiler_params=pltpu.CompilerParams(vmem_limit_bytes=VMEM_LIMIT),
        name="attention_backward",
    )(queries, q_aug, lse, out, grad, own, sib, k_aug)


def silu_parts(gate):
    sigmoid = 1.0 / (1.0 + jnp.exp(-gate))
    return sigmoid, gate * sigmoid


def ffn_forward_kernel(x_ref, w_ref, both_ref, hidden_ref, out_ref, *, unit_rows, down_rows, unit_steps):
    step = pl.program_id(0)
    groups = w_ref.shape[0]

    @pl.when(step < unit_steps)
    def _():
        for place in range(w_ref.shape[1] // unit_rows):
            matrix = w_ref[:, place * unit_rows : (place + 1) * unit_rows, :].reshape(-1, BLOCK)
            both = dot(x_ref[...], matrix, NN)
            both_ref[place] = both
            half = BLOCK // 2
            hidden = silu_parts(both[:, :half])[1] * both[:, half:]
            spot = step * (w_ref.shape[1] // unit_rows) + place
            hidden_ref[:, pl.ds(pl.multiple_of(spot * half, half), half)] = hidden.astype(LOW)

    @pl.when(step >= unit_steps)
    def _():
        for place in range(w_ref.shape[1] // down_rows):
            matrix = w_ref[:, place * down_rows : (place + 1) * down_rows, :].reshape(-1, BLOCK)
            out_ref[:, place * BLOCK : (place + 1) * BLOCK] = dot(hidden_ref[...], matrix, NN)


def ffn_backward_kernel(
    g_ref, w_ref, both_ref, grads_ref, inner_ref, hidden_grad, *, unit_rows, down_rows, down_steps
):
    step = pl.program_id(0)
    half = BLOCK // 2

    @pl.when(step == 0)
    def _():
        hidden_grad[...] = jnp.zeros_like(hidden_grad)
        inner_ref[...] = jnp.zeros_like(inner_ref)

    @pl.when(step < down_steps)
    def _():
        for place in range(w_ref.shape[1] // down_rows):
            matrix = w_ref[:, place * down_rows : (place + 1) * down_rows, :].reshape(-1, BLOCK)
            part = g_ref[:, place * BLOCK : (place + 1) * BLOCK]
            hidden_grad[...] += dot(part, matrix, NT)

    @pl.when(step >= down_steps)
    def _():
        count = w_ref.shape[1] // unit_rows
        total = inner_ref[...]
        for place in range(count):
            matrix = w_ref[:, place * unit_rows : (place + 1) * unit_rows, :].reshape(-1, BLOCK)
            spot = (step - down_steps) * count + place
            gate, upward = both_ref[place, :, :half], both_ref[place, :, half:]
            above = hidden_grad[:, pl.ds(pl.multiple_of(spot * half, half), half)]
            sigmoid, silu = silu_parts(gate)
            grad_gate = above * upward * (sigmoid * (1.0 + gate * (1.0 - sigmoid)))
            grads = jnp.concatenate([grad_gate, above * silu], axis=1).astype(LOW)
            grads_ref[place] = grads
            total = total + dot(grads, matrix, NT)
        inner_ref[...] = total


def ffn_sizes(packed_shape, cols_ff, unit_rows, down_rows):
    rows = D // BLOCK * down_rows
    return rows, 2 * cols_ff // BLOCK * unit_rows // rows, D // BLOCK * down_rows // rows


def ffn_forward(x, packed, cols_ff, unit_rows, down_rows):
    groups, tokens = packed.shape[0], x.shape[0]
    rows, unit_steps, down_steps = ffn_sizes(packed.shape, cols_ff, unit_rows, down_rows)
    per_unit, per_down = rows // unit_rows, rows // down_rows
    last = unit_steps - 1
    results = [
        jax.ShapeDtypeStruct((per_unit * unit_steps, tokens, BLOCK), jnp.float32),
        jax.ShapeDtypeStruct((tokens, cols_ff), LOW),
        jax.ShapeDtypeStruct((tokens, D), jnp.float32),
    ]
    return pl.pallas_call(
        functools.partial(
            ffn_forward_kernel, unit_rows=unit_rows, down_rows=down_rows, unit_steps=unit_steps
        ),
        grid=(unit_steps + down_steps,),
        in_specs=[
            pl.BlockSpec(x.shape, lambda i: (0, 0)),
            pl.BlockSpec((groups, rows, BLOCK), lambda i: (0, i, 0)),
        ],
        out_specs=[
            pl.BlockSpec((per_unit, tokens, BLOCK), lambda i: (jnp.minimum(i, last), 0, 0)),
            pl.BlockSpec((tokens, cols_ff), lambda i: (0, 0)),
            pl.BlockSpec((tokens, per_down * BLOCK), lambda i: (0, jnp.maximum(i - unit_steps, 0))),
        ],
        out_shape=results,
        cost_estimate=cost(6 * tokens * D * cols_ff, [x, packed], results),
        compiler_params=pltpu.CompilerParams(vmem_limit_bytes=VMEM_LIMIT),
        name="ffn_forward",
    )(x, packed)


def ffn_backward(grad, packed, both, cols_ff, unit_rows, down_rows):
    groups, tokens = packed.shape[0], grad.shape[0]
    rows, unit_steps, down_steps = ffn_sizes(packed.shape, cols_ff, unit_rows, down_rows)
    per_unit, per_down = rows // unit_rows, rows // down_rows
    steps = unit_steps + down_steps
    results = [
        jax.ShapeDtypeStruct((per_unit * unit_steps, tokens, BLOCK), LOW),
        jax.ShapeDtypeStruct((tokens, D), jnp.float32),
    ]
    unit_spec = pl.BlockSpec(
        (per_unit, tokens, BLOCK), lambda i: (jnp.maximum(i - down_steps, 0), 0, 0)
    )
    return pl.pallas_call(
        functools.partial(
            ffn_backward_kernel, unit_rows=unit_rows, down_rows=down_rows, down_steps=down_steps
        ),
        grid=(steps,),
        in_specs=[
            pl.BlockSpec(
                (tokens, per_down * BLOCK), lambda i: (0, jnp.minimum(i, down_steps - 1))
            ),
            pl.BlockSpec((groups, rows, BLOCK), lambda i: (0, (i + unit_steps) % steps, 0)),
            unit_spec,
        ],
        out_specs=[unit_spec, pl.BlockSpec((tokens, D), lambda i: (0, 0))],
        out_shape=results,
        cost_estimate=cost(6 * tokens * D * cols_ff, [grad, packed, both], results),
        scratch_shapes=[pltpu.VMEM((tokens, cols_ff), jnp.float32)],
        compiler_params=pltpu.CompilerParams(vmem_limit_bytes=VMEM_LIMIT),
        name="ffn_backward",
    )(grad, packed, both)


def weight_grad_kernel(left_ref, right_ref, *refs, rows, kind):
    out_ref = refs[-1]
    for place in range(out_ref.shape[1] // rows):
        if kind == "blocks":
            grad = dot(left_ref[...], right_ref[place], NN)
        elif kind == "columns":
            grad = dot(left_ref[...], right_ref[:, place * BLOCK : (place + 1) * BLOCK], NN)
        else:
            grad = dot(left_ref[...], right_ref[place * BLOCK : (place + 1) * BLOCK, :], NT)
        out_ref[:, place * rows : (place + 1) * rows, :] = grad.reshape(-1, rows, BLOCK).astype(LOW)


def weight_grad(buffer, total_rows, left, right, kind, rows, start, per_step):
    tokens = left.shape[1]
    groups = left.shape[0] // rows
    if kind == "blocks":
        count = right.shape[0]
        right_spec = pl.BlockSpec((per_step, tokens, BLOCK), lambda i: (i, 0, 0))
    elif kind == "columns":
        count = right.shape[1] // BLOCK
        right_spec = pl.BlockSpec((tokens, per_step * BLOCK), lambda i: (0, i))
    else:
        count = right.shape[0] // BLOCK
        right_spec = pl.BlockSpec((per_step * BLOCK, tokens), lambda i: (i, 0))
    first = start // (per_step * rows)
    operands, specs = [left, right], [pl.BlockSpec(left.shape, lambda i: (0, 0)), right_spec]
    if buffer is not None:
        operands.append(buffer)
        specs.append(pl.BlockSpec(memory_space=pl.ANY))
    return pl.pallas_call(
        functools.partial(weight_grad_kernel, rows=rows, kind=kind),
        grid=(count // per_step,),
        in_specs=specs,
        out_specs=pl.BlockSpec((groups, per_step * rows, BLOCK), lambda i: (0, first + i, 0)),
        out_shape=jax.ShapeDtypeStruct((groups, total_rows, BLOCK), LOW),
        input_output_aliases={} if buffer is None else {2: 0},
        cost_estimate=cost(2 * left.size * count * BLOCK, [left, left, right], []),
        compiler_params=pltpu.CompilerParams(vmem_limit_bytes=VMEM_LIMIT),
        name="weight_grad_" + kind,
    )(*operands)


def put_qkv(came_ref, place_ref, start, outs, layer, weights, gain_ref, gain_out_ref):
    for quarter in range(QUARTERS):
        part = came_ref[place_ref[quarter], :, start : start + 3 * QUARTER_HEADS * HD]
        part = part.astype(jnp.float32)
        for slot in range(QUARTER_HEADS):
            column = HD * (QUARTERS * slot + quarter)
            for which, out_ref in enumerate(outs):
                first = (3 * slot + which) * HD
                out_ref[layer, :, column : column + HD] = part[:, first : first + HD]
    gain_grad = 0.0
    for out_ref, weight_ref in zip(outs, weights):
        grad = out_ref[layer]
        gain_grad = gain_grad + jnp.sum(grad * weight_ref[layer], axis=1, keepdims=True)
        out_ref[layer] = grad * gain_ref[layer]
    gain_out_ref[layer] = jnp.broadcast_to(gain_grad, gain_out_ref.shape[1:])


def put_units(came_ref, place_ref, start, outs, layer, weights, gain_ref, gain_out_ref, d_rows, padded, planes):
    half = BLOCK // 2
    for quarter in range(QUARTERS):
        part = came_ref[place_ref[quarter], :, start : start + 4 * planes * padded]
        part = part.astype(jnp.float32)
        for plane in range(planes):
            for core in range(2):
                column = d_rows * (8 * plane + 2 * quarter + core)
                unit, end = (2 * plane + core) * padded, (2 * plane + core) * padded + d_rows
                while unit < end:
                    stop = min(end, (unit // half + 1) * half)
                    for which, out_ref in enumerate(outs):
                        first = unit // half * BLOCK + which * half + unit % half
                        out_ref[layer, :, column : column + stop - unit] = part[
                            :, first : first + stop - unit
                        ]
                    column, unit = column + stop - unit, stop
    gain_grad = 0.0
    for out_ref, weight_ref in zip(outs, weights):
        grad = out_ref[layer]
        gain_grad = gain_grad + jnp.sum(grad * weight_ref[layer], axis=1, keepdims=True)
        out_ref[layer] = grad * gain_ref[layer]
    gain_out_ref[layer] = jnp.broadcast_to(gain_grad, gain_out_ref.shape[1:])


def finish_kernel(place_ref, *refs, ends, w_rows, d_rows, padded, planes, with_out):
    came_ref, *sums = refs[: 1 + LAYERS]
    weights, gains = refs[1 + LAYERS : 6 + LAYERS], refs[6 + LAYERS : 8 + LAYERS]
    outs = refs[8 + LAYERS :]
    units_width = 4 * planes * padded
    for layer in range(LAYERS):
        put_units(
            came_ref, place_ref, layer * units_width, outs[4:6], layer, weights[3:], gains[1],
            outs[8], d_rows, padded, planes,
        )
        if layer > 0:
            start = LAYERS * units_width + (layer - 1) * 3 * QUARTER_HEADS * HD
            put_qkv(came_ref, place_ref, start, outs[:3], layer, weights[:3], gains[0], outs[7])
        for block in range(D // BLOCK):
            lanes = slice(block * BLOCK, (block + 1) * BLOCK)
            rows = sums[layer][ends[0] + block * padded : ends[0] + (block + 1) * padded, :]
            outs[6][layer, :, lanes] = rows.astype(jnp.float32)[:d_rows]
            if with_out:
                rows = sums[layer][ends[1] + block * w_rows : ends[1] + (block + 1) * w_rows, :]
                outs[3][layer, :, lanes] = rows.astype(jnp.float32)


def finish_first_kernel(place_ref, came_ref, *refs):
    weights, gain_ref, outs, gain_out_ref = refs[:3], refs[3], refs[8:11], refs[11]
    for layer in range(1, LAYERS):
        for have_ref, out_ref in zip(refs[4:8], refs[8:]):
            out_ref[layer] = have_ref[layer]
    put_qkv(came_ref, place_ref, 0, outs, 0, weights, gain_ref, gain_out_ref)


def in_vmem(count):
    return [pl.BlockSpec(memory_space=pltpu.VMEM)] * count


def finish_gradients(place, came, sums, weights, gains, d_shape, ends, planes, with_out):
    layers, w_rows, unused = weights[0].shape
    d_rows = d_shape[1]
    padded = -(-d_rows // 16) * 16
    shapes = [weights[0].shape] * 4 + [weights[3].shape] * 2 + [d_shape] + [(layers, w_rows, 128)] * 2
    return pl.pallas_call(
        functools.partial(
            finish_kernel, ends=ends, w_rows=w_rows, d_rows=d_rows, padded=padded, planes=planes,
            with_out=with_out,
        ),
        in_specs=[pl.BlockSpec(memory_space=pltpu.SMEM)] + in_vmem(8 + LAYERS),
        out_specs=in_vmem(9),
        out_shape=[jax.ShapeDtypeStruct(shape, jnp.float32) for shape in shapes],
        compiler_params=pltpu.CompilerParams(vmem_limit_bytes=VMEM_LIMIT),
        name="finish_gradients",
    )(place, came, *sums, *weights, *gains)


def finish_first(place, came, weights, gain, grads, gain_grad):
    results = [*grads, gain_grad]
    return pl.pallas_call(
        finish_first_kernel,
        in_specs=[pl.BlockSpec(memory_space=pltpu.SMEM)] + in_vmem(9),
        out_specs=in_vmem(4),
        out_shape=[jax.ShapeDtypeStruct(member.shape, jnp.float32) for member in results],
        compiler_params=pltpu.CompilerParams(vmem_limit_bytes=VMEM_LIMIT),
        name="finish_first",
    )(place, came, *weights, gain, *results)


def on_device(
    tokens,
    w_query,
    w_key,
    w_value,
    w_out,
    w_gate,
    w_up,
    w_down,
    gain_attn,
    gain_ffn,
    variate_bias,
    doc_starts,
    variate_ids,
    time_ids,
    cotangent,
):
    seq = lax.axis_size("seq")
    planes = seq // 2
    spread = planes // QUARTER_HEADS
    tiles = planes // spread
    tok_rows = tokens.shape[0]
    cols = 4 * tok_rows
    all_rows = variate_ids.shape[0]
    w_rows = w_query.shape[1]
    d_rows = w_down.shape[1]
    padded = -(-d_rows // 16) * 16
    quarter_ff = 2 * planes * padded
    quarter_width = QUARTER_HEADS * HD
    split_heads = 2 * w_rows == HD
    here_seq, here_head = lax.axis_index("seq"), lax.axis_index("head")
    here_plane, here_lo = here_seq // 2, here_seq % 2
    here_y, here_core = here_head // 2, here_head % 2
    my_quarter = 2 * here_lo + here_y
    my_head = QUARTERS * (here_plane // spread) + my_quarter
    first_tile = (here_plane % spread) * tiles
    devices = [
        (plane, lo, y, core)
        for plane in range(planes)
        for lo in range(2)
        for y in range(2)
        for core in range(2)
    ]

    def place_of(plane, lo, y, core):
        return 8 * plane + 4 * lo + 2 * y + core

    row_groups = [
        [place_of(plane, lo, y, core) for plane in range(planes) for core in range(2)]
        for lo in range(2)
        for y in range(2)
    ]
    plane_groups = [[2 * plane + lo for plane in range(planes)] for lo in range(2)]
    x_swap = [(place, place ^ 1) for place in range(seq)]
    corner_swap = [
        (place_of(plane, lo, y, core), place_of(plane, 1 - lo, 1 - y, core))
        for plane, lo, y, core in devices
    ]

    def neighbours(across_y, across_x, across_both):
        return (
            lax.ppermute(across_y, "head", Y_SWAP),
            lax.ppermute(across_x, "seq", x_swap),
            lax.ppermute(across_both, BOTH, corner_swap),
        )

    def beside(value):
        return jnp.concatenate([value, *neighbours(value, value, value)], axis=0)

    def fold(partial):
        low = partial[tok_rows:].astype(LOW).reshape(3, tok_rows, -1)
        parts = neighbours(low[0], low[1], low[2])
        return partial[:tok_rows] + sum(part.astype(jnp.float32) for part in parts)

    def flip(pair, bit):
        return jnp.where(bit == 0, pair[0], pair[1]), jnp.where(bit == 0, pair[1], pair[0])

    def xor_order(grid, high, low):
        rows = [flip(row, low) for row in grid]
        first, second = zip(*[flip(column, high) for column in zip(*rows)])
        return [list(first), list(second)]

    def cross_rows(parts):
        grid = xor_order([[parts[0], parts[1]], [parts[2], parts[3]]], here_y, here_core)
        came = [[None, None], [None, None]]
        for high in range(2):
            for low in range(2):
                hops = [
                    (place_of(plane, lo, y, core), place_of(plane, y ^ high, core ^ low, lo))
                    for plane, lo, y, core in devices
                ]
                came[high][low] = lax.ppermute(grid[high][low], BOTH, hops)
        came = xor_order(came, here_lo, here_y)
        return jnp.concatenate([*came[0], *came[1]], axis=0)

    def cross_back(rows):
        parts = [rows[place * w_rows : (place + 1) * w_rows] for place in range(4)]
        grid = xor_order([parts[:2], parts[2:]], here_lo, here_y)
        came = [[None, None], [None, None]]
        for high in range(2):
            for low in range(2):
                hops = [
                    (place_of(plane, lo, y, core), place_of(plane, core, lo ^ high, y ^ low))
                    for plane, lo, y, core in devices
                ]
                came[high][low] = lax.ppermute(grid[high][low], BOTH, hops)
        return jnp.stack([*came[0], *came[1]])

    device_groups = [[8 * plane + place for place in range(8)] for plane in range(planes)]

    def plane_exchange(value):
        return lax.all_to_all(
            value, BOTH, split_axis=0, concat_axis=0, tiled=True, axis_index_groups=device_groups
        )

    def cross_rows_at_once(parts):
        zeros = jnp.zeros_like(parts)
        sent = jnp.stack(
            [jnp.where(here_lo == core, parts, zeros) for core in range(2)], axis=1
        )
        came = plane_exchange(sent.reshape(8, *parts.shape[1:]))
        came = jnp.where(here_core == 0, came[:4], came[4:])
        return came.reshape(-1, parts.shape[-1])

    def cross_back_at_once(rows):
        parts = rows.reshape(4, w_rows, -1)
        zeros = jnp.zeros_like(parts)
        sent = [jnp.where(here_core == lo, parts, zeros) for lo in range(2)]
        return plane_exchange(jnp.concatenate(sent, axis=0))

    def gather(part):
        return lax.all_gather(part, BOTH, axis=0, tiled=True, axis_index_groups=row_groups)

    def blocks_of(matrix):
        rows, n = matrix.shape
        return matrix.reshape(rows, n // BLOCK, BLOCK).transpose(1, 0, 2).reshape(-1, BLOCK)

    def from_blocks(packed, rows):
        groups, count = packed.shape[0], packed.shape[1] // rows
        parts = packed.reshape(groups, count, rows, BLOCK).transpose(0, 2, 1, 3)
        return parts.reshape(groups * rows, count * BLOCK)

    def scatter(packed):
        part = lax.psum_scatter(
            packed.reshape(-1, packed.shape[-1]),
            BOTH,
            scatter_dimension=0,
            tiled=True,
            axis_index_groups=row_groups,
        )
        return part

    def split_qkv(query, key, value):
        stacked = jnp.stack([query, key, value], axis=0)
        stacked = stacked.reshape(3, w_rows, QUARTER_HEADS, QUARTERS, HD)
        return stacked.transpose(3, 1, 2, 0, 4).reshape(QUARTERS, w_rows, 3 * quarter_width)

    def join_qkv(parts):
        parts = parts.reshape(QUARTERS, w_rows, QUARTER_HEADS, 3, HD)
        return parts.transpose(3, 1, 2, 0, 4).reshape(3, w_rows, D)

    def split_units(gate, upward):
        def quarters(matrix):
            parts = matrix.reshape(w_rows, planes, QUARTERS, 2, d_rows).transpose(2, 0, 1, 3, 4)
            parts = jnp.pad(parts, ((0, 0),) * 4 + ((0, padded - d_rows),))
            return parts.reshape(QUARTERS, w_rows, -1, 1, BLOCK // 2)

        both = jnp.concatenate([quarters(gate), quarters(upward)], axis=3)
        return both.reshape(QUARTERS, w_rows, 2 * quarter_ff)

    def join_units(parts):
        parts = parts.reshape(QUARTERS, w_rows, -1, 2, BLOCK // 2)

        def joined(part):
            part = part.reshape(QUARTERS, w_rows, planes, 2, padded)[..., :d_rows]
            return part.transpose(1, 2, 0, 3, 4).reshape(w_rows, 4 * seq * d_rows)

        return joined(parts[:, :, :, 0]), joined(parts[:, :, :, 1])

    def whole_out(part):
        matrix = lax.all_gather(part, BOTH, axis=0, tiled=True).reshape(QUARTER_HEADS, QUARTERS, HD, D)
        return lax.dynamic_index_in_dim(matrix, my_quarter, 1, keepdims=False).reshape(quarter_width, D)

    def whole_out_back(grad):
        spaced = lax.dynamic_update_slice_in_dim(
            jnp.zeros((QUARTER_HEADS, QUARTERS, HD, D), LOW),
            grad.astype(LOW).reshape(QUARTER_HEADS, 1, HD, D),
            my_quarter,
            1,
        )
        return lax.psum_scatter(spaced.reshape(D, D), BOTH, scatter_dimension=0, tiled=True)

    def normalize(values):
        inverse = lax.rsqrt(jnp.mean(values * values, axis=-1, keepdims=True) + NORM_EPS)
        return values * inverse, inverse

    def normalize_back(scaled, inverse, inner):
        return inverse * (inner - scaled * jnp.mean(inner * scaled, axis=-1, keepdims=True))

    def scaled_qkv(layer):
        scale = gain_attn[layer][:, None]
        return split_qkv(
            *((member[layer] * scale).astype(LOW) for member in (w_query, w_key, w_value))
        )

    def attention_part(layer, qkv_rows):
        if not split_heads:
            return qkv_rows
        return jnp.concatenate([qkv_rows, blocks_of(w_out[layer].astype(LOW))], axis=1)

    def attention_matrices(layer, part):
        whole = gather(part)
        if split_heads:
            out_matrix = from_blocks(
                whole[:, 3 * quarter_width :].reshape(2 * planes, -1, BLOCK), w_rows
            )
        else:
            out_matrix = whole_out(w_out[layer].astype(LOW))
        return whole[:, : 3 * quarter_width], out_matrix

    first_part = attention_part(0, cross_rows_at_once(scaled_qkv(0)))
    first_part, tokens, cotangent, time_ids, w_query, w_key, w_value, w_gate, w_up = (
        lax.optimization_barrier(
            (first_part, tokens, cotangent, time_ids, w_query, w_key, w_value, w_gate, w_up)
        )
    )
    attention_weights = [attention_matrices(0, first_part)]
    start_scaled, start_inverse = normalize(tokens)
    start_normed = beside(start_scaled.astype(LOW))

    group_rows = 4 * w_rows
    unit_end = 2 * quarter_ff // BLOCK * group_rows
    ffn_end = unit_end + D // BLOCK * padded
    out_end = ffn_end + (D // BLOCK * w_rows if split_heads else 0)
    qkv_end = out_end + 3 * quarter_width // BLOCK * group_rows

    def units_parts(layer):
        scale = gain_ffn[layer][:, None]
        return split_units((w_gate[layer] * scale).astype(LOW), (w_up[layer] * scale).astype(LOW))

    def ffn_part(layer, units_rows):
        down_part = jnp.pad(w_down[layer].astype(LOW), ((0, padded - d_rows), (0, 0)))
        return jnp.concatenate([blocks_of(units_rows), blocks_of(down_part)], axis=0)

    later_weights = [units_parts(layer) for layer in range(LAYERS)]
    later_weights += [scaled_qkv(layer) for layer in range(1, LAYERS)]
    later_widths = [member.shape[-1] for member in later_weights]
    later_weights = jnp.concatenate(later_weights, axis=-1)

    def cut(whole):
        parts, start = [], 0
        for width in later_widths:
            parts.append(whole[..., start : start + width])
            start += width
        return parts

    ffn_weights = []

    def placed_ids(ids):
        ids = ids.reshape(planes, 2, 2, 2, tok_rows)
        ids = jnp.where(here_lo == 0, ids, ids[:, ::-1])
        ids = jnp.where(here_y == 0, ids, ids[:, :, ::-1])
        ids = jnp.where(here_core == 0, ids, ids[:, :, :, ::-1])
        return ids.transpose(3, 0, 1, 2, 4).reshape(2 * planes, cols)

    def my_tiles(value):
        if spread == 1:
            return value
        return lax.dynamic_slice_in_dim(value, first_tile, tiles, 0)

    positions = jnp.arange(all_rows, dtype=jnp.int32)
    doc_ids = jnp.sum((doc_starts[None, :] <= positions[:, None]).astype(jnp.int32), axis=1)
    docs = placed_ids(doc_ids)
    variates = placed_ids(variate_ids)
    q_docs, q_variates = my_tiles(docs[:planes]), my_tiles(variates[:planes])
    extra_row = jnp.arange(HD, dtype=jnp.int32)[None, :, None]

    def one_hot(ids):
        return ids[:, None, :] == extra_row % VARIATES

    def is_doc(ids):
        return ids[:, None, :] == extra_row - 24

    doc_row = (extra_row >= 24) & (extra_row < 32)
    ones_row = (extra_row == 16) | (extra_row == 17) | ((extra_row >= 32) & (extra_row < 35))
    k_hits = one_hot(variates) & (extra_row < 16) | is_doc(docs) & doc_row | ones_row
    k_aug = jnp.where(k_hits, 1.0, 0.0).astype(LOW)

    def query_extra(layer):
        same, other = variate_bias[layer, 0, my_head], variate_bias[layer, 1, my_head]
        gap = same - other
        gap_lead, other_lead = (part.astype(LOW).astype(jnp.float32) for part in (gap, other))
        gap_part = jnp.where(extra_row < VARIATES, gap_lead, gap - gap_lead)
        other_part = jnp.where(extra_row == 16, other_lead, other - other_lead)
        spread_gap = jnp.where(one_hot(q_variates), gap_part, 0.0)
        shut = jnp.where(doc_row & ~is_doc(q_docs), FLOOR_SCORE, 0.0)
        tail = jnp.where(extra_row < 18, other_part, shut)
        return jnp.where(extra_row < 16, spread_gap, tail).astype(LOW)

    q_augs = [query_extra(layer) for layer in range(LAYERS)]
    q_onehots = (q_variates[:, None, :] == jnp.arange(VARIATES, dtype=jnp.int32)[:, None]).astype(
        jnp.float32
    )

    half_dim = HD // 2
    frequency = jnp.exp(jnp.arange(half_dim).astype(jnp.float32) * (-2.0 * math.log(10000.0) / HD))
    times = beside(time_ids.astype(jnp.float32))
    angles = frequency[:, None] * times[None, :]
    cosines, sines = jnp.cos(angles), jnp.sin(angles)
    start_normed, later_weights, k_aug, cosines, sines, *q_augs = lax.optimization_barrier(
        (start_normed, later_weights, k_aug, cosines, sines, *q_augs)
    )

    def rotate(values, sines):
        former, latter = values[:, :half_dim], values[:, half_dim:]
        return jnp.concatenate(
            [former * cosines - latter * sines, latter * cosines + former * sines], axis=1
        )

    def to_heads(value):
        if spread > 1:
            value = jnp.repeat(value, spread, axis=0)
        return lax.all_to_all(
            value, "seq", split_axis=0, concat_axis=0, tiled=True, axis_index_groups=plane_groups
        )

    def all_blocks(value):
        if spread == 1:
            return value
        zeros = jnp.zeros((planes,) + value.shape[1:], value.dtype)
        return lax.dynamic_update_slice_in_dim(zeros, value, first_tile, 0)

    def from_heads(value):
        value = lax.all_to_all(
            value, "seq", split_axis=0, concat_axis=0, tiled=True, axis_index_groups=plane_groups
        )
        if spread > 1:
            value = value.reshape((QUARTER_HEADS, spread) + value.shape[1:])
            value = jnp.sum(value.astype(jnp.float32), axis=1).astype(LOW)
        return value

    stream = tokens
    saved = []
    for layer in range(LAYERS):
        qkv_matrix, out_matrix = attention_weights[layer]
        if layer == 0:
            scaled_one, inverse_one, normed = start_scaled, start_inverse, start_normed
        else:
            scaled_one, inverse_one = normalize(stream)
            normed = beside(scaled_one.astype(LOW))
        projected = dot(qkv_matrix, normed, TT).reshape(QUARTER_HEADS, 3 * HD, cols)
        query = rotate(projected[:, :HD], sines) * (1.0 / math.sqrt(HD))
        key = rotate(projected[:, HD : 2 * HD], sines)
        sent = jnp.concatenate([query, key, projected[:, 2 * HD :]], axis=1).astype(LOW)
        if layer == 0:
            sent, later_weights = lax.optimization_barrier((sent, later_weights))
            later_weights = cross_rows(later_weights)
        own = to_heads(sent)
        own, later_weights = lax.optimization_barrier((own, later_weights))
        packed = gather(ffn_part(layer, cut(later_weights)[layer])).reshape(2 * planes, -1, BLOCK)
        ffn_weights.append(packed)
        sib = lax.ppermute(own[:, HD:], "head", CORE_SWAP)
        queries = my_tiles(own)
        q_aug = q_augs[layer]
        out, lse = attention_forward(queries, q_aug, own, sib, k_aug)
        if layer == 0:
            out, cotangent = lax.optimization_barrier((out, cotangent))
            last_grad_low = beside(cotangent.astype(LOW))
        attended = from_heads(all_blocks(out)).reshape(quarter_width, cols)
        if layer == 0:
            attended, last_grad_low = lax.optimization_barrier((attended, last_grad_low))
        middle = stream + fold(dot(attended, out_matrix, TN))
        scaled_two, inverse_two = normalize(middle)
        normed_ffn = beside(scaled_two.astype(LOW))
        if layer < LAYERS - 1:
            next_part = attention_part(layer + 1, cut(later_weights)[LAYERS + layer])
            normed_ffn, next_part = lax.optimization_barrier((normed_ffn, next_part))
            attention_weights.append(attention_matrices(layer + 1, next_part))
        both, hidden, partial = ffn_forward(normed_ffn, packed, quarter_ff, group_rows, padded)
        saved.append(
            (
                scaled_one, inverse_one, normed, own, sib, queries, q_aug, out, lse, attended,
                scaled_two, inverse_two, normed_ffn, both, hidden,
            )
        )
        if layer < LAYERS - 1:
            stream = middle + fold(partial)
        else:
            last_middle, last_partial = middle, partial

    upstream = cotangent
    whole_grads, ffn_sums = [None] * LAYERS, [None] * LAYERS
    bias_parts = [None] * LAYERS
    buffer, sent_last = None, None
    qkv_grad = None

    for layer in reversed(range(LAYERS)):
        (qkv_matrix, out_matrix), packed = attention_weights[layer], ffn_weights[layer]
        (
            scaled_one, inverse_one, normed, own, sib, queries, q_aug, out, lse, attended,
            scaled_two, inverse_two, normed_ffn, both, hidden,
        ) = saved[layer]
        upstream_low = beside(upstream.astype(LOW)) if layer < LAYERS - 1 else last_grad_low
        grad_units, partial = ffn_backward(upstream_low, packed, both, quarter_ff, group_rows, padded)
        inner = fold(partial)
        total_rows = qkv_end if layer < LAYERS - 1 else out_end
        buffer = weight_grad(
            buffer, total_rows, normed_ffn.T, grad_units, "blocks", group_rows, 0, 4 * padded // group_rows
        )
        inner, buffer = lax.optimization_barrier((inner, buffer))
        buffer = weight_grad(
            buffer, total_rows, hidden.T, upstream_low, "columns", padded, unit_end, D // BLOCK
        )
        grad_middle = upstream + normalize_back(scaled_two, inverse_two, inner)
        middle_low = beside(grad_middle.astype(LOW))
        middle_low, buffer = lax.optimization_barrier((middle_low, buffer))
        grad_attended = dot(out_matrix, middle_low, NT).astype(LOW)
        if split_heads:
            buffer = weight_grad(
                buffer, total_rows, attended, middle_low, "columns", w_rows, ffn_end, D // BLOCK
            )
        else:
            whole_grads[layer] = whole_out_back(dot(attended, middle_low, NN))
        if sent_last is not None:
            buffer, sent_last = lax.optimization_barrier((buffer, sent_last))
            ffn_sums[layer + 1] = sent_last
        out_grad = my_tiles(to_heads(grad_attended.reshape(QUARTER_HEADS, HD, cols)))
        buffer, out_grad = lax.optimization_barrier((buffer, out_grad))
        if layer == 0:
            sent_last = scatter(buffer)
        grad_q, grad_kv = attention_backward(
            queries, q_aug, lse, out, out_grad, own, sib, k_aug
        )
        same_grad = jnp.sum(grad_q[:, HD : HD + VARIATES] * q_onehots)
        all_grad = jnp.sum(grad_q[:, HD + 16])
        crossed = lax.ppermute(grad_kv[planes:], "head", CORE_SWAP)
        grad_kv = (grad_kv[:planes].astype(jnp.float32) + crossed.astype(jnp.float32)).astype(LOW)
        grad_q = (grad_q[:, :HD] * (1.0 / math.sqrt(HD))).astype(LOW)
        if layer == LAYERS - 1:
            grad_kv, last_partial = lax.optimization_barrier((grad_kv, last_partial))
            stream = last_middle + fold(last_partial)
        grad_heads = from_heads(jnp.concatenate([all_blocks(grad_q), grad_kv], axis=1))
        if layer > 0:
            grad_heads, buffer, stream = lax.optimization_barrier((grad_heads, buffer, stream))
            sent_last = scatter(buffer)
        grad_heads = jnp.concatenate(
            [
                rotate(grad_heads[:, :HD].astype(jnp.float32), -sines).astype(LOW),
                rotate(grad_heads[:, HD : 2 * HD].astype(jnp.float32), -sines).astype(LOW),
                grad_heads[:, 2 * HD :],
            ],
            axis=1,
        ).reshape(3 * quarter_width, cols)
        bias_parts[layer] = jnp.stack([same_grad, all_grad - same_grad])
        if layer > 0:
            buffer = weight_grad(
                None, qkv_end, normed.T, grad_heads, "rows", group_rows, out_end, 1
            )
        else:
            qkv_grad = dot(normed, grad_heads, TT).astype(LOW)
            qkv_grad, grad_heads = lax.optimization_barrier((qkv_grad, grad_heads))
            qkv_grad, sent_last = lax.optimization_barrier((qkv_grad, sent_last))
            ffn_sums[0] = sent_last
            qkv_sum = scatter(qkv_grad)
        partial = dot(grad_heads, qkv_matrix, TT)
        if layer > 0:
            inner = fold(partial)
            inner, buffer = lax.optimization_barrier((inner, buffer))
        else:
            qkv_sum, partial = lax.optimization_barrier((qkv_sum, partial))
            inner = fold(partial)
        upstream = grad_middle + normalize_back(scaled_one, inverse_one, inner)

    bias_local = lax.dynamic_update_slice(
        jnp.zeros((LAYERS, 2, HEADS), jnp.float32), jnp.stack(bias_parts)[:, :, None], (0, 0, my_head)
    )
    bias_total = bias_local
    for axis, size in (("head", 4), ("seq", seq)):
        hop = 1
        while hop < size:
            swap = [(place, place ^ hop) for place in range(size)]
            bias_total = bias_total + lax.ppermute(bias_total, axis, swap)
            hop *= 2

    later_sums = [from_blocks(member[None, :unit_end], group_rows) for member in ffn_sums]
    later_sums += [from_blocks(member[None, out_end:], group_rows) for member in ffn_sums[:-1]]
    quarters = jnp.arange(QUARTERS, dtype=jnp.int32)
    weights = (w_query, w_key, w_value, w_gate, w_up)
    gains = (gain_attn[:, :, None], gain_ffn[:, :, None])
    *grads, gain_one, gain_two = finish_gradients(
        quarters ^ (2 * here_y + here_core), cross_back(jnp.concatenate(later_sums, axis=1)), ffn_sums,
        weights, gains, w_down.shape, (unit_end, ffn_end), planes, split_heads,
    )
    if not split_heads:
        grads[3] = jnp.stack(whole_grads).astype(jnp.float32)
    *grads[:3], gain_one = finish_first(
        2 * quarters + here_lo, cross_back_at_once(qkv_sum), weights[:3], gains[0], grads[:3], gain_one
    )
    return (stream, upstream, *grads, gain_one[:, :, 0], gain_two[:, :, 0], bias_total)


def solution(mesh):
    rows = P(BOTH, None)
    middle = P(None, BOTH, None)
    gains = P(None, BOTH)
    return jax.shard_map(
        on_device,
        mesh=mesh,
        in_specs=(rows,) + (middle,) * 7 + (gains,) * 2 + (P(),) * 3 + (P(BOTH), rows),
        out_specs=(rows, rows) + (middle,) * 7 + (gains,) * 2 + (P(),),
        check_vma=False,
    )
```

time: 840 us -> 716 us (0.85)
  blocking collectives: 98.1 us -> 0 us
  starting transfers between devices: 77.5 us -> 123 us
  local copies, waits for them, and re-layouts: 75.4 us -> 50.2 us
  Pallas kernels: 179 us -> 160 us
  waiting for transfers between devices: 289 us -> 277 us
    all_to_all x3 -> x0, blocking collectives: 98.1 us -> none  [to_heads(): return lax.all_to_all(value, 'seq', split_axis=0, concat_axis=0, tiled=True)]
    ppermute x35 -> x61, waiting for transfers between devices: 75.4 us -> 154 us  [the longest x17 73.3 us: neighbours(): lax.ppermute(across_x, 'seq', x_swap)]
    all_gather x4, waiting for transfers between devices: 71.9 us -> 0.05 us  [gather(): lax.all_gather(part, BOTH, axis=0, tiled=True, axis_index_groups=row_groups)]
    reduce_scatter x3, waiting for transfers between devices: 70.6 us -> 9.6 us  [scatter(): lax.psum_scatter(packed.reshape(-1, packed.shape[-1]), BOTH, scatter_dime...]
    all_to_all x5 -> x10, waiting for transfers between devices: 65.8 us -> 102 us  [the longest x4 55.6 us: from_heads(): lax.all_to_all(value, 'seq', split_axis=0, concat_axis=0, tiled=True, axi...]
    ppermute x35 -> x61, starting transfers between devices: 51 us -> 73.7 us  [the longest x17 32.2 us: neighbours(): lax.ppermute(across_x, 'seq', x_swap)]
    all_to_all x5 -> x10, starting transfers between devices: 20.9 us -> 38.2 us  [the longest x4 15.6 us: to_heads(): lax.all_to_all(value, 'seq', split_axis=0, concat_axis=0, tiled=True, axi...]
    pallas_call x4 -> x6, Pallas kernels: 114 us -> 102 us  [the longest x2 60.2 us: attention_backward(): pl.pallas_call(backward_kernel, grid=(tiles * cols // Q_TILE,), in_specs=...]
  transfers between devices with their start and end apart: 54 -> 85, of which waited for: 29 -> 54; matrix products, arithmetic and copies ran while one was open for 16% -> 12% of each run, Pallas kernels for 19% -> 16%
where the time goes in v2:
time: 716 us; the launch traced here: 710 us
  waiting for transfers between devices  277 us (39%)
  Pallas kernels  160 us (22%)
  starting transfers between devices  123 us (17%)
  other arithmetic  62.1 us (9%)
  local copies, waits for them, and re-layouts  50.2 us (7%)
  between operations  24.3 us (3%)
  matrix products  14.2 us (2%)
    ppermute x17, waiting for transfers between devices, neighbours(): lax.ppermute(across_x, 'seq', x_swap)  73.3 us
    ppermute x17, waiting for transfers between devices, neighbours(): lax.ppermute(across_both, BOTH, corner_swap)  60.7 us
    pallas_call x2, Pallas kernels, attention_backward(): pl.pallas_call(backward_kernel, grid=(tiles * cols // Q_TILE,), in_specs=...  60.2 us
    all_to_all x4, waiting for transfers between devices, from_heads(): lax.all_to_all(value, 'seq', split_axis=0, concat_axis=0, tiled=True, axi...  55.6 us
    all_to_all x4, waiting for transfers between devices, to_heads(): lax.all_to_all(value, 'seq', split_axis=0, concat_axis=0, tiled=True, axi...  45.9 us
    pallas_call x2, Pallas kernels, attention_forward(): pl.pallas_call(functools.partial(forward_kernel, width=2), grid=(tiles *...  34.4 us
    ppermute x17, starting transfers between devices, neighbours(): lax.ppermute(across_x, 'seq', x_swap)  32.2 us
    pallas_call x7, Pallas kernels, weight_grad(): pl.pallas_call(functools.partial(weight_grad_kernel, rows=rows, kind=kind...  25.8 us
  transfers between devices with their start and end apart: 85, of which 54 were waited for; matrix products, arithmetic and copies ran while one was open for 12% of the time, Pallas kernels for 16%

profile of v2, /device:TPU:0, one launch (start us, length us, event | category | flops | bytes accessed | tf_op | source)
XLA Modules:
  0.0 710.0 jit_solution(2395811565064008911)
XLA Ops:
  52.1 6.7 collective-permute-done
  84.6 14.3 %all-to-all-done.1.q_ref.own_ref = bf16[4,192,512]{2,1,0:T(8,128)(2,1)S(1)} async-done(((bf16[4,192,512]{2,1,0:T(8,128)(2,1)}), bf16[4,192,512]{2,1,0:T(8,128)(2,1)S(1)}, u32[]{:S(2)}, u32[]{:S(2)}) %all-to-all-start.1) | async-done | bytes 786464 | tf_op jit(solution)/shard_map/all_to_all | solution.py:788
  103.0 17.2 %attention_forward.2 = (bf16[4,64,512]{2,1,0:T(8,128)(2,1)}, f32[4,8,512]{2,1,0:T(8,128)}) custom-call(bf16[4,192,512]{2,1,0:T(8,128)(2,1)} %copy-done.16, bf16[4,64,512]{2,1,0:T(8,128)(2,1)} %get-tuple-element.113.q_aug_ref, bf16[4,192,512]{2,1,0:T(8,128)(2,1)} %copy-done.16, bf16[4,128,512]{2,1,0:T(8,128)(2,1)} %copy-done.61, ...), custom_call_target="tpu_custom_call" | custom-call | flops 8589934592 | bytes 2424832 | tf_op jit(solution)/shard_map/attention_forward/pallas_call | solution.py:151
  148.0 6.6 collective-permute-done.16
  175.6 7.9 %ffn_forward.2 = (f32[6,512,256]{2,1,0:T(8,128)}, bf16[512,768]{1,0:T(8,128)(2,1)}, f32[512,1024]{1,0:T(8,128)}) custom-call(bf16[512,1024]{1,0:T(8,128)(2,1)} %pad_maximum_fusion.2.x_ref, bf16[8,1152,256]{2,1,0:T(8,128)(2,1)} %bitcast.203), custom_call_target="tpu_custom_call" | custom-call | flops 2415919104 | bytes 11796480 | tf_op jit(solution)/shard_map/ffn_forward/pallas_call | solution.py:264
  188.9 6.7 collective-permute-done.22
  205.1 6.6 collective-permute-done.25
  225.4 18.6 %all-to-all-done.3.q_ref.own_ref = bf16[4,192,512]{2,1,0:T(8,128)(2,1)S(1)} async-done(((bf16[4,192,512]{2,1,0:T(8,128)(2,1)}), bf16[4,192,512]{2,1,0:T(8,128)(2,1)S(1)}, u32[]{:S(2)}, u32[]{:S(2)}) %all-to-all-start.3) | async-done | bytes 786464 | tf_op jit(solution)/shard_map/all_to_all | solution.py:788
  250.9 17.2 %attention_forward.3 = (bf16[4,64,512]{2,1,0:T(8,128)(2,1)}, f32[4,8,512]{2,1,0:T(8,128)}) custom-call(bf16[4,192,512]{2,1,0:T(8,128)(2,1)} %copy-done.17, bf16[4,64,512]{2,1,0:T(8,128)(2,1)} %get-tuple-element.125.q_aug_ref, bf16[4,192,512]{2,1,0:T(8,128)(2,1)} %copy-done.17, bf16[4,128,512]{2,1,0:T(8,128)(2,1)} %copy-done.62, ...), custom_call_target="tpu_custom_call" | custom-call | flops 8589934592 | bytes 2424832 | tf_op jit(solution)/shard_map/attention_forward/pallas_call | solution.py:151
  272.2 16.0 %all-to-all-done.4 = bf16[4,64,512]{2,1,0:T(8,128)(2,1)S(1)} async-done(((bf16[4,64,512]{2,1,0:T(8,128)(2,1)}), bf16[4,64,512]{2,1,0:T(8,128)(2,1)S(1)}, u32[]{:S(2)}, u32[]{:S(2)}) %all-to-all-start.4) | async-done | bytes 262176 | tf_op jit(solution)/shard_map/all_to_all | solution.py:799
  292.4 6.6 collective-permute-done.29
  307.7 6.6 collective-permute-done.32
  320.2 7.8 %ffn_forward.3 = (f32[6,512,256]{2,1,0:T(8,128)}, bf16[512,768]{1,0:T(8,128)(2,1)}, f32[512,1024]{1,0:T(8,128)}) custom-call(bf16[512,1024]{1,0:T(8,128)(2,1)} %get-tuple-element.291.x_ref, bf16[8,1152,256]{2,1,0:T(8,128)(2,1)} %bitcast.205), custom_call_target="tpu_custom_call" | custom-call | flops 2415919104 | bytes 11796480 | tf_op jit(solution)/shard_map/ffn_forward/pallas_call | solution.py:264
  328.1 8.1 %ffn_backward.2 = (bf16[6,512,256]{2,1,0:T(8,128)(2,1)}, f32[512,1024]{1,0:T(8,128)}) custom-call(bf16[512,1024]{1,0:T(8,128)(2,1)} %pad_maximum_fusion.1.g_ref.right_ref, bf16[8,1152,256]{2,1,0:T(8,128)(2,1)} %bitcast.206, f32[6,512,256]{2,1,0:T(8,128)} %get-tuple-element.130.both_ref), custom_call_target="tpu_custom_call" | custom-call | flops 2415919104 | bytes 12582912 | tf_op jit(solution)/shard_map/ffn_backward/pallas_call | solution.py:297
  379.6 6.7 all-to-all-done.5.grad_ref
  387.0 30.0 %attention_backward.2 = (f32[4,128,512]{2,1,0:T(8,128)}, bf16[8,128,512]{2,1,0:T(8,128)(2,1)}) custom-call(bf16[4,192,512]{2,1,0:T(8,128)(2,1)} %copy-done.17, bf16[4,64,512]{2,1,0:T(8,128)(2,1)} %get-tuple-element.125.q_aug_ref, f32[4,8,512]{2,1,0:T(8,128)} %get-tuple-element.126.lse_ref, bf16[4,64,512]{2,1,0:T(8,128)(2,1)} %get-tuple-element.127.out_ref, ...), custom_call_target="tpu_custom_call" | custom-call | flops 17179869184 | bytes 4194304 | tf_op jit(solution)/shard_map/attention_backward/pallas_call | solution.py:172
  430.4 6.6 collective-permute-done.42
  470.2 6.6 collective-permute-done.48
  482.6 8.1 %ffn_backward.3 = (bf16[6,512,256]{2,1,0:T(8,128)(2,1)}, f32[512,1024]{1,0:T(8,128)}) custom-call(bf16[512,1024]{1,0:T(8,128)(2,1)} %pad_maximum_fusion.6.g_ref.right_ref, bf16[8,1152,256]{2,1,0:T(8,128)(2,1)} %bitcast.204, f32[6,512,256]{2,1,0:T(8,128)} %get-tuple-element.148.both_ref), custom_call_target="tpu_custom_call" | custom-call | flops 2415919104 | bytes 12582912 | tf_op jit(solution)/shard_map/ffn_backward/pallas_call | solution.py:297
  533.7 6.3 all-to-all-done.7.grad_ref
  540.7 30.2 %attention_backward.3 = (f32[4,128,512]{2,1,0:T(8,128)}, bf16[8,128,512]{2,1,0:T(8,128)(2,1)}) custom-call(bf16[4,192,512]{2,1,0:T(8,128)(2,1)} %copy-done.16, bf16[4,64,512]{2,1,0:T(8,128)(2,1)} %get-tuple-element.113.q_aug_ref, f32[4,8,512]{2,1,0:T(8,128)} %get-tuple-element.153.lse_ref, bf16[4,64,512]{2,1,0:T(8,128)(2,1)} %get-tuple-element.117.out_ref, ...), custom_call_target="tpu_custom_call" | custom-call | flops 17179869184 | bytes 4194304 | tf_op jit(solution)/shard_map/attention_backward/pallas_call | solution.py:172
  580.1 32.3 %all-to-all-done.8 = bf16[4,192,512]{2,1,0:T(8,128)(2,1)S(1)} async-done(((bf16[4,192,512]{2,1,0:T(8,128)(2,1)}), bf16[4,192,512]{2,1,0:T(8,128)(2,1)S(1)}, u32[]{:S(2)}, u32[]{:S(2)}) %all-to-all-start.8) | async-done | bytes 786464 | tf_op jit(solution)/shard_map/all_to_all | solution.py:799
  616.0 9.6 %reduce-scatter.6.cloned.1.call-done.refs_1_ = bf16[1664,256]{1,0:T(8,128)(2,1)} async-done(((bf16[13312,256]{1,0:T(8,128)(2,1)}), bf16[1664,256]{1,0:T(8,128)(2,1)}) %reduce-scatter.6.cloned.1.call-update) | async-done | bytes 851984 | tf_op jit(solution)/shard_map/reduce_scatter | solution.py:609
  686.2 8.2 %collective-permute-done.57 = bf16[128,1024]{1,0:T(8,128)(2,1)} collective-permute-done((bf16[128,1024]{1,0:T(8,128)(2,1)}, bf16[128,1024]{1,0:T(8,128)(2,1)}, u32[]{:S(2)}, u32[]{:S(2)}) %collective-permute-start.57) | collective-permute-done | bytes 262176 | tf_op jit(solution)/shard_map/ppermute | solution.py:528
  (542 shorter events, 394.1 us)
Async XLA Ops:
  18.3 41.8 %all-gather.5.cloned.1.call-start = ((), (), s32[]{:S(2)}) async-start(), calls=%async_computation.13 | async-start | bytes 2359296 | tf_op jit(solution)/shard_map/all_gather | solution.py:597
  29.9 22.2 %collective-permute-start.2 = (bf16[128,1024]{1,0:T(8,128)(2,1)}, bf16[128,1024]{1,0:T(8,128)(2,1)}, u32[]{:S(2)}, u32[]{:S(2)}) collective-permute-start(bf16[128,1024]{1,0:T(8,128)(2,1)} %multiply_convert_fusion.5), channel_id=1, source_target_pairs={{0,6},{1,7},{2,4},{3,5},{4,2},{5,3},{6,0},{7,1},{8,14},{9,15},{10,... | collective-permute-start | bytes 786440 | tf_op jit(solution)/shard_map/ppermute | solution.py:529
  32.8 19.3 %collective-permute-start.1 = (bf16[128,1024]{1,0:T(8,128)(2,1)}, bf16[128,1024]{1,0:T(8,128)(2,1)}, u32[]{:S(2)}, u32[]{:S(2)}) collective-permute-start(bf16[128,1024]{1,0:T(8,128)(2,1)} %multiply_convert_fusion.5), channel_id=1, source_target_pairs={{0,4},{4,0},{8,12},{12,8},{16,20},{20,16},{24,28},{28,24},{1,5},{5... | collective-permute-start | bytes 786440 | tf_op jit(solution)/shard_map/ppermute | solution.py:528
  33.3 18.3 %collective-permute-start.5 = (f32[128]{0:T(128)S(1)}, f32[128]{0:T(128)S(1)}, u32[]{:S(2)}, u32[]{:S(2)}) collective-permute-start(f32[128]{0:T(128)S(1)} %convert_element_type.283), channel_id=1, source_target_pairs={{0,6},{1,7},{2,4},{3,5},{4,2},{5,3},{6,0},{7,1},{8,14},{9,15},{10,... | collective-permute-start | bytes 1544 | tf_op jit(solution)/shard_map/ppermute | solution.py:529
  34.8 17.0 %collective-permute-start.4 = (f32[128]{0:T(128)S(1)}, f32[128]{0:T(128)S(1)}, u32[]{:S(2)}, u32[]{:S(2)}) collective-permute-start(f32[128]{0:T(128)S(1)} %convert_element_type.283), channel_id=1, source_target_pairs={{0,4},{4,0},{8,12},{12,8},{16,20},{20,16},{24,28},{28,24},{1,5},{5... | collective-permute-start | bytes 1544 | tf_op jit(solution)/shard_map/ppermute | solution.py:528
  34.9 16.9 %collective-permute-start.3 = (f32[128]{0:T(128)S(1)}, f32[128]{0:T(128)S(1)}, u32[]{:S(2)}, u32[]{:S(2)}) collective-permute-start(f32[128]{0:T(128)S(1)} %convert_element_type.283), channel_id=1, source_target_pairs={{0,2},{1,3},{2,0},{3,1},{4,6},{5,7},{6,4},{7,5},{8,10},{9,11},{10,... | collective-permute-start | bytes 1544 | tf_op jit(solution)/shard_map/ppermute | solution.py:527
  73.6 25.3 %all-to-all-start.1 = ((bf16[4,192,512]{2,1,0:T(8,128)(2,1)}), bf16[4,192,512]{2,1,0:T(8,128)(2,1)S(1)}, u32[]{:S(2)}, u32[]{:S(2)}) async-start(bf16[4,192,512]{2,1,0:T(8,128)(2,1)} %pad_maximum_fusion.12), calls=%async_computation.1 | async-start | bytes 1572864 | tf_op jit(solution)/shard_map/all_to_all | solution.py:788
  78.5 97.1 %all-gather.9.cloned.1.call-start = ((), (), s32[]{:S(2)}) async-start(), calls=%async_computation.15 | async-start | bytes 5308416 | tf_op jit(solution)/shard_map/all_gather | solution.py:597
  121.3 14.6 %collective-permute-start.12 = (bf16[128,1024]{1,0:T(8,128)(2,1)S(1)}, bf16[128,1024]{1,0:T(8,128)(2,1)}, u32[]{:S(2)}, u32[]{:S(2)}) collective-permute-start(bf16[128,1024]{1,0:T(8,128)(2,1)S(1)} %convert_element_type.294), channel_id=1, source_target_pairs={{0,4},{4,0},{8,12},{12,8},{16,20},{20,16},{24,28},{28,24},{1,5},{5... | collective-permute-start | bytes 786440 | tf_op jit(solution)/shard_map/ppermute | solution.py:528
  123.9 20.0 %all-to-all-start.2 = ((bf16[4,64,512]{2,1,0:T(8,128)(2,1)}), bf16[4,64,512]{2,1,0:T(8,128)(2,1)S(1)}, u32[]{:S(2)}, u32[]{:S(2)}) async-start(bf16[4,64,512]{2,1,0:T(8,128)(2,1)} %get-tuple-element.117.out_ref), calls=%async_computation.2 | async-start | bytes 524288 | tf_op jit(solution)/shard_map/all_to_all | solution.py:799
  127.3 77.8 %all-gather.7.cloned.1.call-start = ((), (), s32[]{:S(2)}) async-start(), calls=%async_computation.14 | async-start | bytes 2359296 | tf_op jit(solution)/shard_map/all_gather | solution.py:597
  160.1 14.5 %collective-permute-start.18 = (bf16[128,1024]{1,0:T(8,128)(2,1)S(1)}, bf16[128,1024]{1,0:T(8,128)(2,1)S(1)}, u32[]{:S(2)}, u32[]{:S(2)}) collective-permute-start(bf16[128,1024]{1,0:T(8,128)(2,1)S(1)} %multiply_convert_fusion.4), channel_id=1, source_target_pairs={{0,4},{4,0},{8,12},{12,8},{16,20},{20,16},{24,28},{28,24},{1,5},{5... | collective-permute-start | bytes 786440 | tf_op jit(solution)/shard_map/ppermute | solution.py:528
  201.9 14.6 %collective-permute-start.24 = (bf16[128,1024]{1,0:T(8,128)(2,1)S(1)}, bf16[128,1024]{1,0:T(8,128)(2,1)S(1)}, u32[]{:S(2)}, u32[]{:S(2)}) collective-permute-start(bf16[128,1024]{1,0:T(8,128)(2,1)S(1)} %multiply_convert_fusion.3), channel_id=1, source_target_pairs={{0,4},{4,0},{8,12},{12,8},{16,20},{20,16},{24,28},{28,24},{1,5},{5... | collective-permute-start | bytes 786440 | tf_op jit(solution)/shard_map/ppermute | solution.py:528
  220.2 23.8 %all-to-all-start.3 = ((bf16[4,192,512]{2,1,0:T(8,128)(2,1)}), bf16[4,192,512]{2,1,0:T(8,128)(2,1)S(1)}, u32[]{:S(2)}, u32[]{:S(2)}) async-start(bf16[4,192,512]{2,1,0:T(8,128)(2,1)} %pad_maximum_fusion.13), calls=%async_computation.3 | async-start | bytes 1572864 | tf_op jit(solution)/shard_map/all_to_all | solution.py:788
  223.7 96.5 %all-gather.11.cloned.1.call-start = ((), (), s32[]{:S(2)}) async-start(), calls=%async_computation.16 | async-start | bytes 5308416 | tf_op jit(solution)/shard_map/all_gather | solution.py:597
  268.1 20.1 %all-to-all-start.4 = ((bf16[4,64,512]{2,1,0:T(8,128)(2,1)}), bf16[4,64,512]{2,1,0:T(8,128)(2,1)S(1)}, u32[]{:S(2)}, u32[]{:S(2)}) async-start(bf16[4,64,512]{2,1,0:T(8,128)(2,1)} %get-tuple-element.127.out_ref), calls=%async_computation.4 | async-start | bytes 524288 | tf_op jit(solution)/shard_map/all_to_all | solution.py:799
  421.3 24.2 %all-to-all-start.6 = ((bf16[4,192,512]{2,1,0:T(8,128)(2,1)}), bf16[4,192,512]{2,1,0:T(8,128)(2,1)S(1)}, u32[]{:S(2)}, u32[]{:S(2)}) async-start(bf16[4,192,512]{2,1,0:T(8,128)(2,1)} %pad_maximum_fusion.14), calls=%async_computation.6 | async-start | bytes 1572864 | tf_op jit(solution)/shard_map/all_to_all | solution.py:799
  424.8 108.9 %reduce-scatter.4.cloned.1.call-start = ((), (), s32[]{:S(2)}) async-start(), calls=%async_computation.17 | async-start | bytes 5898240 | tf_op jit(solution)/shard_map/reduce_scatter | solution.py:609
  427.2 14.6 %collective-permute-start.41 = (bf16[128,1024]{1,0:T(8,128)(2,1)S(1)}, bf16[128,1024]{1,0:T(8,128)(2,1)S(1)}, u32[]{:S(2)}, u32[]{:S(2)}) collective-permute-start(bf16[128,1024]{1,0:T(8,128)(2,1)S(1)} %get-tuple-element.289), channel_id=1, source_target_pairs={{0,4},{4,0},{8,12},{12,8},{16,20},{20,16},{24,28},{28,24},{1,5},{5... | collective-permute-start | bytes 786440 | tf_op jit(solution)/shard_map/ppermute | solution.py:528
  530.9 94.7 %reduce-scatter.6.cloned.1.call-start = ((), (), s32[]{:S(2)}) async-start(), calls=%async_computation.18 | async-start | bytes 7667712 | tf_op jit(solution)/shard_map/reduce_scatter | solution.py:609
  575.1 37.3 %all-to-all-start.8 = ((bf16[4,192,512]{2,1,0:T(8,128)(2,1)}), bf16[4,192,512]{2,1,0:T(8,128)(2,1)S(1)}, u32[]{:S(2)}, u32[]{:S(2)}) async-start(bf16[4,192,512]{2,1,0:T(8,128)(2,1)} %pad_maximum_fusion.15), calls=%async_computation.9 | async-start | bytes 1572864 | tf_op jit(solution)/shard_map/all_to_all | solution.py:799
  578.6 97.4 %reduce-scatter.8.cloned.1.call-start = ((), (), s32[]{:S(2)}) async-start(), calls=%async_computation.19 | async-start | bytes 1769472 | tf_op jit(solution)/shard_map/reduce_scatter | solution.py:609
  679.2 15.2 %collective-permute-start.57 = (bf16[128,1024]{1,0:T(8,128)(2,1)}, bf16[128,1024]{1,0:T(8,128)(2,1)}, u32[]{:S(2)}, u32[]{:S(2)}) collective-permute-start(bf16[128,1024]{1,0:T(8,128)(2,1)} %get-tuple-element.280), channel_id=1, source_target_pairs={{0,4},{4,0},{8,12},{12,8},{16,20},{20,16},{24,28},{28,24},{1,5},{5... | collective-permute-start | bytes 786440 | tf_op jit(solution)/shard_map/ppermute | solution.py:528
  682.2 15.7 %all-to-all-start.9 = ((bf16[8,32,768]{2,1,0:T(8,128)(2,1)}), bf16[8,32,768]{2,1,0:T(8,128)(2,1)S(1)}, u32[]{:S(2)}, u32[]{:S(2)}) async-start(bf16[8,32,768]{2,1,0:T(8,128)(2,1)} %pad_maximum_fusion.22), calls=%async_computation.12 | async-start | bytes 786432 | tf_op jit(solution)/shard_map/all_to_all | solution.py:577
  (130 other events, 1226.6 us)
Sparse Core Ops, SparseCore 0:
  27.8 30.8 all-gather.4
  100.3 55.8 all-gather.8
  175.7 26.8 all-gather.6
  248.2 55.5 all-gather.10
  445.6 58.3 reduce-scatter.3
  540.1 85.4 reduce-scatter.5
  627.9 35.6 reduce-scatter.7

commit v3 on v2

--- a/solution.py
+++ b/solution.py
@@ -22,7 +22,6 @@
 
 QUARTERS = 4
 QUARTER_HEADS = HEADS // QUARTERS
-Q_TILE = 256
 Y_SWAP = [(place, place ^ 2) for place in range(4)]
 CORE_SWAP = [(place, place ^ 1) for place in range(4)]
 
@@ -42,7 +41,7 @@
     return lax.dot_general(left, right, dims, preferred_element_type=jnp.float32)
 
 
-def forward_kernel(q_ref, q_aug_ref, own_ref, sib_ref, k_aug_ref, out_ref, lse_ref, *, width):
+def forward_kernel(flip_ref, q_ref, q_aug_ref, own_ref, sib_ref, k_aug_ref, out_ref, lse_ref):
     blocks = own_ref.shape[0]
     sources = ((own_ref, HD), (sib_ref, 0))
     spots = [(half, block) for half in range(2) for block in range(blocks)]
@@ -51,29 +50,33 @@
     top = jnp.full((cols, 1), FLOOR_SCORE, jnp.float32)
     total = jnp.zeros((cols, 1), jnp.float32)
     acc = jnp.zeros((cols, HD), jnp.float32)
-    for start in range(0, len(spots), width):
-        group = spots[start : start + width]
-        parts = []
-        for half, block in group:
-            ref, low_row = sources[half]
-            extra = k_aug_ref[half * blocks + block]
-            k_side = jnp.concatenate([ref[block, low_row : low_row + HD, :], extra], axis=0)
-            parts.append(dot(q_side, k_side, NN))
-        peak = functools.reduce(jnp.maximum, parts)
-        fresh = jnp.maximum(top, jnp.max(peak, axis=-1, keepdims=True))
+
+    def scores(half, block):
+        ref, low_row = sources[half]
+        extra = k_aug_ref[half * blocks + block]
+        k_side = jnp.concatenate([ref[block, low_row : low_row + HD, :], extra], axis=0)
+        return dot(q_side, k_side, NN)
+
+    following = scores(*spots[0])
+    for number, (half, block) in enumerate(spots):
+        part = following
+        if number + 1 < len(spots):
+            following = scores(*spots[number + 1])
+        fresh = jnp.maximum(top, jnp.max(part, axis=-1, keepdims=True))
         shrink = jnp.exp(top - fresh)
-        probs = [jnp.exp(part - fresh) for part in parts]
-        total = total * shrink + jnp.sum(sum(probs[1:], probs[0]), axis=-1, keepdims=True)
-        acc = acc * shrink
-        for prob, (half, block) in zip(probs, group):
-            ref, low_row = sources[half]
-            values = ref[block, low_row + HD : low_row + 2 * HD, :]
-            acc = acc + dot(prob.astype(LOW), values, NT)
+        prob = jnp.exp(part - fresh)
+        total = total * shrink + jnp.sum(prob, axis=-1, keepdims=True)
+        ref, low_row = sources[half]
+        values = ref[block, low_row + HD : low_row + 2 * HD, :]
+        acc = acc * shrink + dot(prob.astype(LOW), values, NT)
         top = fresh
     result = acc / total
     lse = jnp.broadcast_to(top + jnp.log(total), (cols, HD))
     both = jnp.concatenate([result, lse], axis=1).T
-    out_ref[0] = both[:HD].astype(LOW)
+    piece = out_ref.shape[-1]
+    for place in range(cols // piece):
+        part = both[:HD, place * piece : (place + 1) * piece]
+        out_ref[0, place ^ flip_ref[0]] = part.astype(LOW)
     lse_ref[0] = both[HD : HD + 8]
 
 
@@ -86,7 +89,8 @@
 
 
 def backward_kernel(
-    q_ref, q_aug_ref, lse_ref, out_ref, grad_ref, own_ref, sib_ref, k_aug_ref, dq_ref, dkv_ref, dkv_acc
+    flip_ref, q_ref, q_aug_ref, lse_ref, out_ref, grad_ref, own_ref, sib_ref, k_aug_ref,
+    dq_ref, dkv_ref, dkv_acc,
 ):
     step = pl.program_id(0)
     blocks = own_ref.shape[0]
@@ -98,10 +102,10 @@
         dkv_acc[...] = jnp.zeros_like(dkv_acc)
 
     q_low = q_ref[0, :HD, :]
-    g_low = grad_ref[0]
-    row_dot = jnp.sum(
-        g_low.astype(jnp.float32) * out_ref[0].astype(jnp.float32), axis=0, keepdims=True
-    )
+    places = range(grad_ref.shape[1])
+    g_low = jnp.concatenate([grad_ref[0, place ^ flip_ref[0]] for place in places], axis=1)
+    out = jnp.concatenate([out_ref[0, place ^ flip_ref[0]] for place in places], axis=1)
+    row_dot = jnp.sum(g_low.astype(jnp.float32) * out.astype(jnp.float32), axis=0, keepdims=True)
     aug = jnp.concatenate(
         [q_aug_ref[0, :32, :], split_rows(-lse_ref[0, :1, :], 16), q_aug_ref[0, 48:, :]], axis=0
     )
@@ -111,19 +115,26 @@
         [jnp.ones((16, key_cols), LOW), jnp.zeros((HD - 16, key_cols), LOW)], axis=0
     )
     dq = jnp.zeros((cols, 2 * HD), jnp.float32)
-    for half in range(2):
+    spots = [(half, block) for half in range(2) for block in range(blocks)]
+
+    def products(half, block):
         ref, low_row = sources[half]
-        for block in range(blocks):
-            spot = half * blocks + block
-            k_side = jnp.concatenate(
-                [ref[block, low_row : low_row + HD, :], k_aug_ref[spot]], axis=0
-            )
-            v_side = jnp.concatenate([ref[block, low_row + HD : low_row + 2 * HD, :], ones], axis=0)
-            prob = jnp.exp(dot(q_side, k_side, NN))
-            score_grad = (prob * dot(g_side, v_side, NN)).astype(LOW)
-            dq = dq + dot(score_grad, k_side, NT)
-            dkv_acc[spot, :HD, :] += dot(q_low, score_grad, NN)
-            dkv_acc[spot, HD:, :] += dot(g_low, prob.astype(LOW), NN)
+        k_side = jnp.concatenate(
+            [ref[block, low_row : low_row + HD, :], k_aug_ref[half * blocks + block]], axis=0
+        )
+        v_side = jnp.concatenate([ref[block, low_row + HD : low_row + 2 * HD, :], ones], axis=0)
+        return k_side, dot(q_side, k_side, NN), dot(g_side, v_side, NN)
+
+    following = products(*spots[0])
+    for spot in range(len(spots)):
+        k_side, score, prob_grad = following
+        if spot + 1 < len(spots):
+            following = products(*spots[spot + 1])
+        prob = jnp.exp(score)
+        score_grad = (prob * prob_grad).astype(LOW)
+        dq = dq + dot(score_grad, k_side, NT)
+        dkv_acc[spot, :HD, :] += dot(q_low, score_grad, NN)
+        dkv_acc[spot, HD:, :] += dot(g_low, prob.astype(LOW), NN)
     dq_ref[0] = dq.T
 
     @pl.when(step == pl.num_programs(0) - 1)
@@ -131,37 +142,44 @@
         dkv_ref[...] = dkv_acc[...].astype(LOW)
 
 
-def whole_spec(array):
-    rank = array.ndim
-    return pl.BlockSpec(array.shape, lambda i: (0,) * rank)
+def whole_spec(shape):
+    rank = len(shape)
+    return pl.BlockSpec(shape, lambda i, flip: (0,) * rank)
 
 
 def tile_spec(rows, cols):
-    cuts = cols // Q_TILE
-    return pl.BlockSpec((1, rows, Q_TILE), lambda i: (i // cuts, 0, i % cuts))
-
-
-def attention_forward(queries, q_aug, own, sib, k_aug):
+    return pl.BlockSpec((1, rows, cols), lambda i, flip: (i, 0, 0))
+
+
+def owner_spec(shape):
+    return pl.BlockSpec((1, *shape[1:]), lambda i, flip: (i, 0, 0, 0))
+
+
+def attention_forward(flip, queries, q_aug, own, sib, k_aug):
     tiles, unused, cols = queries.shape
     pairs = 2 * tiles * own.shape[0] * cols * cols
+    out_shape = (tiles, 4, HD, cols // 4)
     results = [
-        jax.ShapeDtypeStruct((tiles, HD, cols), LOW),
+        jax.ShapeDtypeStruct(out_shape, LOW),
         jax.ShapeDtypeStruct((tiles, 8, cols), jnp.float32),
     ]
     return pl.pallas_call(
-        functools.partial(forward_kernel, width=2),
-        grid=(tiles * cols // Q_TILE,),
-        in_specs=[tile_spec(3 * HD, cols), tile_spec(HD, cols)]
-        + [whole_spec(member) for member in (own, sib, k_aug)],
-        out_specs=[tile_spec(HD, cols), tile_spec(8, cols)],
+        forward_kernel,
+        grid_spec=pltpu.PrefetchScalarGridSpec(
+            num_scalar_prefetch=1,
+            grid=(tiles,),
+            in_specs=[tile_spec(3 * HD, cols), tile_spec(HD, cols)]
+            + [whole_spec(member.shape) for member in (own, sib, k_aug)],
+            out_specs=[owner_spec(out_shape), tile_spec(8, cols)],
+        ),
         out_shape=results,
         cost_estimate=cost(16 * HD * pairs, [queries, own, sib], results, pairs),
         compiler_params=pltpu.CompilerParams(vmem_limit_bytes=VMEM_LIMIT),
         name="attention_forward",
-    )(queries, q_aug, own, sib, k_aug)
-
-
-def attention_backward(queries, q_aug, lse, out, grad, own, sib, k_aug):
+    )(flip, queries, q_aug, own, sib, k_aug)
+
+
+def attention_backward(flip, queries, q_aug, lse, out, grad, own, sib, k_aug):
     tiles, unused, cols = queries.shape
     dkv_shape = (2 * own.shape[0], 2 * HD, cols)
     pairs = 2 * tiles * own.shape[0] * cols * cols
@@ -171,17 +189,20 @@
     ]
     return pl.pallas_call(
         backward_kernel,
-        grid=(tiles * cols // Q_TILE,),
-        in_specs=[tile_spec(3 * HD, cols), tile_spec(HD, cols), tile_spec(8, cols)]
-        + [tile_spec(HD, cols)] * 2
-        + [whole_spec(member) for member in (own, sib, k_aug)],
-        out_specs=[tile_spec(2 * HD, cols), pl.BlockSpec(dkv_shape, lambda i: (0, 0, 0))],
+        grid_spec=pltpu.PrefetchScalarGridSpec(
+            num_scalar_prefetch=1,
+            grid=(tiles,),
+            in_specs=[tile_spec(3 * HD, cols), tile_spec(HD, cols), tile_spec(8, cols)]
+            + [owner_spec(out.shape)] * 2
+            + [whole_spec(member.shape) for member in (own, sib, k_aug)],
+            out_specs=[tile_spec(2 * HD, cols), whole_spec(dkv_shape)],
+            scratch_shapes=[pltpu.VMEM(dkv_shape, jnp.float32)],
+        ),
         out_shape=results,
         cost_estimate=cost(32 * HD * pairs, [queries, own, sib], results, pairs),
-        scratch_shapes=[pltpu.VMEM(dkv_shape, jnp.float32)],
         compiler_params=pltpu.CompilerParams(vmem_limit_bytes=VMEM_LIMIT),
         name="attention_backward",
-    )(queries, q_aug, lse, out, grad, own, sib, k_aug)
+    )(flip, queries, q_aug, lse, out, grad, own, sib, k_aug)
 
 
 def silu_parts(gate):
@@ -189,130 +210,178 @@
     return sigmoid, gate * sigmoid
 
 
-def ffn_forward_kernel(x_ref, w_ref, both_ref, hidden_ref, out_ref, *, unit_rows, down_rows, unit_steps):
-    step = pl.program_id(0)
-    groups = w_ref.shape[0]
-
-    @pl.when(step < unit_steps)
-    def _():
-        for place in range(w_ref.shape[1] // unit_rows):
-            matrix = w_ref[:, place * unit_rows : (place + 1) * unit_rows, :].reshape(-1, BLOCK)
-            both = dot(x_ref[...], matrix, NN)
-            both_ref[place] = both
-            half = BLOCK // 2
-            hidden = silu_parts(both[:, :half])[1] * both[:, half:]
-            spot = step * (w_ref.shape[1] // unit_rows) + place
-            hidden_ref[:, pl.ds(pl.multiple_of(spot * half, half), half)] = hidden.astype(LOW)
-
-    @pl.when(step >= unit_steps)
-    def _():
-        for place in range(w_ref.shape[1] // down_rows):
-            matrix = w_ref[:, place * down_rows : (place + 1) * down_rows, :].reshape(-1, BLOCK)
-            out_ref[:, place * BLOCK : (place + 1) * BLOCK] = dot(hidden_ref[...], matrix, NN)
-
-
-def ffn_backward_kernel(
-    g_ref, w_ref, both_ref, grads_ref, inner_ref, hidden_grad, *, unit_rows, down_rows, down_steps
+def put_parts(values, lanes, own_ref, *low_refs):
+    rows = own_ref.shape[0]
+    own_ref[:, lanes] = values[:rows]
+    for place, low_ref in enumerate(low_refs):
+        low_ref[:, lanes] = values[(place + 1) * rows : (place + 2) * rows].astype(LOW)
+
+
+def parts_of(tokens, lanes, index):
+    shape = (tokens // 4, D)
+    types = [jnp.float32, LOW, LOW, LOW]
+    return (
+        [jax.ShapeDtypeStruct(shape, kind) for kind in types],
+        [pl.BlockSpec((tokens // 4, lanes), index) for unused in types],
+    )
+
+
+def ffn_forward_kernel(
+    x_ref, unit_ref, down_ref, both_ref, hidden_ref, *out_refs, unit_rows, down_rows, unit_steps
 ):
     step = pl.program_id(0)
     half = BLOCK // 2
 
-    @pl.when(step == 0)
+    @pl.when(step < unit_steps)
     def _():
-        hidden_grad[...] = jnp.zeros_like(hidden_grad)
-        inner_ref[...] = jnp.zeros_like(inner_ref)
+        count = unit_ref.shape[1] // unit_rows
+        for place in range(count):
+            matrix = unit_ref[:, place * unit_rows : (place + 1) * unit_rows, :].reshape(-1, BLOCK)
+            both = dot(x_ref[...], matrix, NN)
+            both_ref[place] = both.astype(both_ref.dtype)
+            hidden = silu_parts(both[:, :half])[1] * both[:, half:]
+            spot = step * count + place
+            hidden_ref[:, pl.ds(pl.multiple_of(spot * half, half), half)] = hidden.astype(LOW)
+
+    @pl.when(step >= unit_steps)
+    def _():
+        for place in range(down_ref.shape[1] // down_rows):
+            matrix = down_ref[:, place * down_rows : (place + 1) * down_rows, :].reshape(-1, BLOCK)
+            lanes = slice(place * BLOCK, (place + 1) * BLOCK)
+            put_parts(dot(hidden_ref[...], matrix, NN), lanes, *out_refs)
+
+
+def ffn_backward_kernel(
+    g_ref, unit_ref, down_ref, both_ref, grads_ref, *refs, unit_rows, down_rows, down_steps
+):
+    part_refs, inner_ref, hidden_grad = refs[:4], refs[4], refs[5]
+    step = pl.program_id(0)
+    half = BLOCK // 2
 
     @pl.when(step < down_steps)
     def _():
-        for place in range(w_ref.shape[1] // down_rows):
-            matrix = w_ref[:, place * down_rows : (place + 1) * down_rows, :].reshape(-1, BLOCK)
+        total = 0.0
+        for place in range(down_ref.shape[1] // down_rows):
+            matrix = down_ref[:, place * down_rows : (place + 1) * down_rows, :].reshape(-1, BLOCK)
             part = g_ref[:, place * BLOCK : (place + 1) * BLOCK]
-            hidden_grad[...] += dot(part, matrix, NT)
+            total = total + dot(part, matrix, NT)
+
+        @pl.when(step == 0)
+        def _():
+            hidden_grad[...] = total
+
+        @pl.when(step > 0)
+        def _():
+            hidden_grad[...] += total
 
     @pl.when(step >= down_steps)
     def _():
-        count = w_ref.shape[1] // unit_rows
-        total = inner_ref[...]
+        count = unit_ref.shape[1] // unit_rows
+        total = 0.0
         for place in range(count):
-            matrix = w_ref[:, place * unit_rows : (place + 1) * unit_rows, :].reshape(-1, BLOCK)
+            matrix = unit_ref[:, place * unit_rows : (place + 1) * unit_rows, :].reshape(-1, BLOCK)
             spot = (step - down_steps) * count + place
-            gate, upward = both_ref[place, :, :half], both_ref[place, :, half:]
+            gate = both_ref[place, :, :half].astype(jnp.float32)
+            upward = both_ref[place, :, half:].astype(jnp.float32)
             above = hidden_grad[:, pl.ds(pl.multiple_of(spot * half, half), half)]
             sigmoid, silu = silu_parts(gate)
             grad_gate = above * upward * (sigmoid * (1.0 + gate * (1.0 - sigmoid)))
             grads = jnp.concatenate([grad_gate, above * silu], axis=1).astype(LOW)
             grads_ref[place] = grads
             total = total + dot(grads, matrix, NT)
-        inner_ref[...] = total
-
-
-def ffn_sizes(packed_shape, cols_ff, unit_rows, down_rows):
-    rows = D // BLOCK * down_rows
-    return rows, 2 * cols_ff // BLOCK * unit_rows // rows, D // BLOCK * down_rows // rows
+
+        @pl.when(step == down_steps)
+        def _():
+            inner_ref[...] = total
+
+        @pl.when(step > down_steps)
+        def _():
+            inner_ref[...] += total
+
+    @pl.when(step == pl.num_programs(0) - 1)
+    def _():
+        put_parts(inner_ref[...], slice(0, D), *part_refs)
+
+
+FFN_DOWNS = 4
+
+
+def ffn_units(cols_ff):
+    return max(count for count in (1, 2, 3) if 2 * cols_ff // BLOCK % count == 0)
+
+
+def ffn_specs(cols_ff, unit_rows, down_rows, groups, unit_step, down_step):
+    unit_blocks, down_blocks = 2 * cols_ff // BLOCK, D // BLOCK
+    units, downs = ffn_units(cols_ff) * unit_rows, FFN_DOWNS * down_rows
+    first_down = unit_blocks * unit_rows // downs
+    return (
+        unit_blocks // ffn_units(cols_ff),
+        down_blocks // FFN_DOWNS,
+        [
+            pl.BlockSpec((groups, units, BLOCK), lambda i: (0, unit_step(i), 0)),
+            pl.BlockSpec((groups, downs, BLOCK), lambda i: (0, first_down + down_step(i), 0)),
+        ],
+    )
 
 
 def ffn_forward(x, packed, cols_ff, unit_rows, down_rows):
-    groups, tokens = packed.shape[0], x.shape[0]
-    rows, unit_steps, down_steps = ffn_sizes(packed.shape, cols_ff, unit_rows, down_rows)
-    per_unit, per_down = rows // unit_rows, rows // down_rows
-    last = unit_steps - 1
+    tokens, unit_steps = x.shape[0], 2 * cols_ff // BLOCK // ffn_units(cols_ff)
+    unit_step = lambda i: jnp.minimum(i, unit_steps - 1)
+    down_step = lambda i: jnp.maximum(i - unit_steps, 0)
+    unit_steps, down_steps, specs = ffn_specs(
+        cols_ff, unit_rows, down_rows, packed.shape[0], unit_step, down_step
+    )
+    parts, part_specs = parts_of(tokens, FFN_DOWNS * BLOCK, lambda i: (0, down_step(i)))
     results = [
-        jax.ShapeDtypeStruct((per_unit * unit_steps, tokens, BLOCK), jnp.float32),
+        jax.ShapeDtypeStruct((2 * cols_ff // BLOCK, tokens, BLOCK), LOW),
         jax.ShapeDtypeStruct((tokens, cols_ff), LOW),
-        jax.ShapeDtypeStruct((tokens, D), jnp.float32),
+        *parts,
     ]
     return pl.pallas_call(
         functools.partial(
             ffn_forward_kernel, unit_rows=unit_rows, down_rows=down_rows, unit_steps=unit_steps
         ),
         grid=(unit_steps + down_steps,),
-        in_specs=[
-            pl.BlockSpec(x.shape, lambda i: (0, 0)),
-            pl.BlockSpec((groups, rows, BLOCK), lambda i: (0, i, 0)),
-        ],
+        in_specs=[pl.BlockSpec(x.shape, lambda i: (0, 0)), *specs],
         out_specs=[
-            pl.BlockSpec((per_unit, tokens, BLOCK), lambda i: (jnp.minimum(i, last), 0, 0)),
+            pl.BlockSpec((ffn_units(cols_ff), tokens, BLOCK), lambda i: (unit_step(i), 0, 0)),
             pl.BlockSpec((tokens, cols_ff), lambda i: (0, 0)),
-            pl.BlockSpec((tokens, per_down * BLOCK), lambda i: (0, jnp.maximum(i - unit_steps, 0))),
+            *part_specs,
         ],
         out_shape=results,
         cost_estimate=cost(6 * tokens * D * cols_ff, [x, packed], results),
         compiler_params=pltpu.CompilerParams(vmem_limit_bytes=VMEM_LIMIT),
         name="ffn_forward",
-    )(x, packed)
+    )(x, packed, packed)
 
 
 def ffn_backward(grad, packed, both, cols_ff, unit_rows, down_rows):
-    groups, tokens = packed.shape[0], grad.shape[0]
-    rows, unit_steps, down_steps = ffn_sizes(packed.shape, cols_ff, unit_rows, down_rows)
-    per_unit, per_down = rows // unit_rows, rows // down_rows
-    steps = unit_steps + down_steps
-    results = [
-        jax.ShapeDtypeStruct((per_unit * unit_steps, tokens, BLOCK), LOW),
-        jax.ShapeDtypeStruct((tokens, D), jnp.float32),
-    ]
-    unit_spec = pl.BlockSpec(
-        (per_unit, tokens, BLOCK), lambda i: (jnp.maximum(i - down_steps, 0), 0, 0)
-    )
+    tokens, down_steps = grad.shape[0], D // BLOCK // FFN_DOWNS
+    unit_step = lambda i: jnp.maximum(i - down_steps, 0)
+    down_step = lambda i: jnp.minimum(i, down_steps - 1)
+    unit_steps, down_steps, specs = ffn_specs(
+        cols_ff, unit_rows, down_rows, packed.shape[0], unit_step, down_step
+    )
+    unit_spec = pl.BlockSpec((ffn_units(cols_ff), tokens, BLOCK), lambda i: (unit_step(i), 0, 0))
+    parts, part_specs = parts_of(tokens, D, lambda i: (0, 0))
+    results = [jax.ShapeDtypeStruct((2 * cols_ff // BLOCK, tokens, BLOCK), LOW), *parts]
     return pl.pallas_call(
         functools.partial(
             ffn_backward_kernel, unit_rows=unit_rows, down_rows=down_rows, down_steps=down_steps
         ),
-        grid=(steps,),
+        grid=(unit_steps + down_steps,),
         in_specs=[
-            pl.BlockSpec(
-                (tokens, per_down * BLOCK), lambda i: (0, jnp.minimum(i, down_steps - 1))
-            ),
-            pl.BlockSpec((groups, rows, BLOCK), lambda i: (0, (i + unit_steps) % steps, 0)),
+            pl.BlockSpec((tokens, FFN_DOWNS * BLOCK), lambda i: (0, down_step(i))),
+            *specs,
             unit_spec,
         ],
-        out_specs=[unit_spec, pl.BlockSpec((tokens, D), lambda i: (0, 0))],
+        out_specs=[unit_spec, *part_specs],
         out_shape=results,
+        scratch_shapes=[pltpu.VMEM((tokens, D), jnp.float32), pltpu.VMEM((tokens, cols_ff), jnp.float32)],
         cost_estimate=cost(6 * tokens * D * cols_ff, [grad, packed, both], results),
-        scratch_shapes=[pltpu.VMEM((tokens, cols_ff), jnp.float32)],
         compiler_params=pltpu.CompilerParams(vmem_limit_bytes=VMEM_LIMIT),
         name="ffn_backward",
-    )(grad, packed, both)
+    )(grad, packed, packed, both)
 
 
 def weight_grad_kernel(left_ref, right_ref, *refs, rows, kind):
@@ -399,10 +468,10 @@
     gain_out_ref[layer] = jnp.broadcast_to(gain_grad, gain_out_ref.shape[1:])
 
 
-def finish_kernel(place_ref, *refs, ends, w_rows, d_rows, padded, planes, with_out):
+def finish_kernel(place_ref, *refs, unit_end, w_rows, d_rows, padded, planes, with_out):
     came_ref, *sums = refs[: 1 + LAYERS]
-    weights, gains = refs[1 + LAYERS : 6 + LAYERS], refs[6 + LAYERS : 8 + LAYERS]
-    outs = refs[8 + LAYERS :]
+    out_sums, refs = refs[1 + LAYERS : 2 * LAYERS], refs[2 * LAYERS :]
+    weights, gains, outs = refs[:5], refs[5:7], refs[7:]
     units_width = 4 * planes * padded
     for layer in range(LAYERS):
         put_units(
@@ -414,53 +483,58 @@
             put_qkv(came_ref, place_ref, start, outs[:3], layer, weights[:3], gains[0], outs[7])
         for block in range(D // BLOCK):
             lanes = slice(block * BLOCK, (block + 1) * BLOCK)
-            rows = sums[layer][ends[0] + block * padded : ends[0] + (block + 1) * padded, :]
+            rows = sums[layer][unit_end + block * padded : unit_end + (block + 1) * padded, :]
             outs[6][layer, :, lanes] = rows.astype(jnp.float32)[:d_rows]
-            if with_out:
-                rows = sums[layer][ends[1] + block * w_rows : ends[1] + (block + 1) * w_rows, :]
+            if with_out and layer > 0:
+                rows = out_sums[layer - 1][block * w_rows : (block + 1) * w_rows, :]
                 outs[3][layer, :, lanes] = rows.astype(jnp.float32)
 
 
-def finish_first_kernel(place_ref, came_ref, *refs):
-    weights, gain_ref, outs, gain_out_ref = refs[:3], refs[3], refs[8:11], refs[11]
+def finish_first_kernel(place_ref, came_ref, out_sum_ref, *refs, w_rows, with_out):
+    weights, gain_ref, have, outs = refs[:3], refs[3], refs[4:9], refs[9:]
     for layer in range(1, LAYERS):
-        for have_ref, out_ref in zip(refs[4:8], refs[8:]):
+        for have_ref, out_ref in zip(have, outs):
             out_ref[layer] = have_ref[layer]
-    put_qkv(came_ref, place_ref, 0, outs, 0, weights, gain_ref, gain_out_ref)
+    put_qkv(came_ref, place_ref, 0, outs[:3], 0, weights, gain_ref, outs[3])
+    if with_out:
+        for block in range(D // BLOCK):
+            rows = out_sum_ref[block * w_rows : (block + 1) * w_rows, :]
+            outs[4][0, :, block * BLOCK : (block + 1) * BLOCK] = rows.astype(jnp.float32)
 
 
 def in_vmem(count):
     return [pl.BlockSpec(memory_space=pltpu.VMEM)] * count
 
 
-def finish_gradients(place, came, sums, weights, gains, d_shape, ends, planes, with_out):
+def finish_gradients(
+    place, came, sums, out_sums, weights, gains, d_shape, unit_end, planes, with_out
+):
     layers, w_rows, unused = weights[0].shape
     d_rows = d_shape[1]
     padded = -(-d_rows // 16) * 16
     shapes = [weights[0].shape] * 4 + [weights[3].shape] * 2 + [d_shape] + [(layers, w_rows, 128)] * 2
     return pl.pallas_call(
         functools.partial(
-            finish_kernel, ends=ends, w_rows=w_rows, d_rows=d_rows, padded=padded, planes=planes,
+            finish_kernel, unit_end=unit_end, w_rows=w_rows, d_rows=d_rows, padded=padded, planes=planes,
             with_out=with_out,
         ),
-        in_specs=[pl.BlockSpec(memory_space=pltpu.SMEM)] + in_vmem(8 + LAYERS),
+        in_specs=[pl.BlockSpec(memory_space=pltpu.SMEM)] + in_vmem(7 + 2 * LAYERS),
         out_specs=in_vmem(9),
         out_shape=[jax.ShapeDtypeStruct(shape, jnp.float32) for shape in shapes],
         compiler_params=pltpu.CompilerParams(vmem_limit_bytes=VMEM_LIMIT),
         name="finish_gradients",
-    )(place, came, *sums, *weights, *gains)
-
-
-def finish_first(place, came, weights, gain, grads, gain_grad):
-    results = [*grads, gain_grad]
+    )(place, came, *sums, *out_sums, *weights, *gains)
+
+
+def finish_first(place, came, out_sum, weights, gain, grads, with_out):
     return pl.pallas_call(
-        finish_first_kernel,
-        in_specs=[pl.BlockSpec(memory_space=pltpu.SMEM)] + in_vmem(9),
-        out_specs=in_vmem(4),
-        out_shape=[jax.ShapeDtypeStruct(member.shape, jnp.float32) for member in results],
+        functools.partial(finish_first_kernel, w_rows=weights[0].shape[1], with_out=with_out),
+        in_specs=[pl.BlockSpec(memory_space=pltpu.SMEM)] + in_vmem(11),
+        out_specs=in_vmem(5),
+        out_shape=[jax.ShapeDtypeStruct(member.shape, jnp.float32) for member in grads],
         compiler_params=pltpu.CompilerParams(vmem_limit_bytes=VMEM_LIMIT),
         name="finish_first",
-    )(place, came, *weights, gain, *results)
+    )(place, came, out_sum, *weights, gain, *grads)
 
 
 def on_device(
@@ -532,10 +606,12 @@
     def beside(value):
         return jnp.concatenate([value, *neighbours(value, value, value)], axis=0)
 
-    def fold(partial):
+    def fold(own, *others):
+        return own + sum(part.astype(jnp.float32) for part in neighbours(*others))
+
+    def fold_whole(partial):
         low = partial[tok_rows:].astype(LOW).reshape(3, tok_rows, -1)
-        parts = neighbours(low[0], low[1], low[2])
-        return partial[:tok_rows] + sum(part.astype(jnp.float32) for part in parts)
+        return fold(partial[:tok_rows], low[0], low[1], low[2])
 
     def flip(pair, bit):
         return jnp.where(bit == 0, pair[0], pair[1]), jnp.where(bit == 0, pair[1], pair[0])
@@ -642,10 +718,6 @@
 
         return joined(parts[:, :, :, 0]), joined(parts[:, :, :, 1])
 
-    def whole_out(part):
-        matrix = lax.all_gather(part, BOTH, axis=0, tiled=True).reshape(QUARTER_HEADS, QUARTERS, HD, D)
-        return lax.dynamic_index_in_dim(matrix, my_quarter, 1, keepdims=False).reshape(quarter_width, D)
-
     def whole_out_back(grad):
         spaced = lax.dynamic_update_slice_in_dim(
             jnp.zeros((QUARTER_HEADS, QUARTERS, HD, D), LOW),
@@ -669,19 +741,13 @@
         )
 
     def attention_part(layer, qkv_rows):
-        if not split_heads:
-            return qkv_rows
-        return jnp.concatenate([qkv_rows, blocks_of(w_out[layer].astype(LOW))], axis=1)
-
-    def attention_matrices(layer, part):
+        blocks = blocks_of(w_out[layer].astype(LOW))
+        return jnp.concatenate([qkv_rows, blocks], axis=1)
+
+    def attention_matrices(part):
         whole = gather(part)
-        if split_heads:
-            out_matrix = from_blocks(
-                whole[:, 3 * quarter_width :].reshape(2 * planes, -1, BLOCK), w_rows
-            )
-        else:
-            out_matrix = whole_out(w_out[layer].astype(LOW))
-        return whole[:, : 3 * quarter_width], out_matrix
+        blocks = whole[:, 3 * quarter_width :].reshape(2 * planes, -1, BLOCK)
+        return whole[:, : 3 * quarter_width], from_blocks(blocks, w_rows)
 
     first_part = attention_part(0, cross_rows_at_once(scaled_qkv(0)))
     first_part, tokens, cotangent, time_ids, w_query, w_key, w_value, w_gate, w_up = (
@@ -689,7 +755,7 @@
             (first_part, tokens, cotangent, time_ids, w_query, w_key, w_value, w_gate, w_up)
         )
     )
-    attention_weights = [attention_matrices(0, first_part)]
+    attention_weights, out_weights = [attention_matrices(first_part)], []
     start_scaled, start_inverse = normalize(tokens)
     start_normed = beside(start_scaled.astype(LOW))
 
@@ -697,7 +763,6 @@
     unit_end = 2 * quarter_ff // BLOCK * group_rows
     ffn_end = unit_end + D // BLOCK * padded
     out_end = ffn_end + (D // BLOCK * w_rows if split_heads else 0)
-    qkv_end = out_end + 3 * quarter_width // BLOCK * group_rows
 
     def units_parts(layer):
         scale = gain_ffn[layer][:, None]
@@ -795,19 +860,65 @@
         zeros = jnp.zeros((planes,) + value.shape[1:], value.dtype)
         return lax.dynamic_update_slice_in_dim(zeros, value, first_tile, 0)
 
+    def over_spread(value):
+        if spread == 1:
+            return value
+        value = value.reshape((QUARTER_HEADS, spread) + value.shape[1:])
+        return jnp.sum(value.astype(jnp.float32), axis=1).astype(LOW)
+
     def from_heads(value):
+        return over_spread(
+            lax.all_to_all(
+                value, "seq", split_axis=0, concat_axis=0, tiled=True, axis_index_groups=plane_groups
+            )
+        )
+
+    chip_groups = [
+        [place_of(plane, lo, y, core) for plane in range(planes) for lo in range(2) for y in range(2)]
+        for core in range(2)
+    ]
+
+    def over_chips(value):
+        shape = value.shape
+        value = value.reshape(-1, *shape[2:])
         value = lax.all_to_all(
-            value, "seq", split_axis=0, concat_axis=0, tiled=True, axis_index_groups=plane_groups
-        )
-        if spread > 1:
-            value = value.reshape((QUARTER_HEADS, spread) + value.shape[1:])
-            value = jnp.sum(value.astype(jnp.float32), axis=1).astype(LOW)
-        return value
+            value, BOTH, split_axis=0, concat_axis=0, tiled=True, axis_index_groups=chip_groups
+        )
+        return value.reshape(shape)
+
+    chip_flips = jnp.reshape(my_quarter, (1,)).astype(jnp.int32)
+
+    def plane_order(value):
+        grid = [[value[:, 2 * lo + y] for y in range(2)] for lo in range(2)]
+        grid = xor_order(grid, here_lo, here_y)
+        return jnp.stack([*grid[0], *grid[1]])
+
+    def chip_order(value):
+        grid = xor_order([[value[0], value[1]], [value[2], value[3]]], here_lo, here_y)
+        return jnp.stack([*grid[0], *grid[1]], axis=1)
+
+    def share_for_out(middle_low, attended):
+        pieces = attended.reshape(4, quarter_width, tok_rows)
+        cuts = quarter_width // tok_rows
+
+        def joined(piece):
+            parts = [piece[cut * tok_rows : (cut + 1) * tok_rows] for cut in range(cuts)]
+            return jnp.concatenate([middle_low, *parts], axis=1)
+
+        came = neighbours(*(joined(piece) for piece in pieces[1:]))
+        tokens_low = jnp.concatenate([middle_low, *(part[:, :D] for part in came)], axis=0)
+
+        def results(part):
+            return jnp.concatenate(
+                [part[:, D + cut * tok_rows : D + (cut + 1) * tok_rows] for cut in range(cuts)], axis=0
+            )
+
+        return tokens_low, jnp.concatenate([pieces[0], *(results(part) for part in came)], axis=1)
 
     stream = tokens
     saved = []
     for layer in range(LAYERS):
-        qkv_matrix, out_matrix = attention_weights[layer]
+        qkv_matrix, out_quarter = attention_weights[layer]
         if layer == 0:
             scaled_one, inverse_one, normed = start_scaled, start_inverse, start_normed
         else:
@@ -819,29 +930,32 @@
         sent = jnp.concatenate([query, key, projected[:, 2 * HD :]], axis=1).astype(LOW)
         if layer == 0:
             sent, later_weights = lax.optimization_barrier((sent, later_weights))
-            later_weights = cross_rows(later_weights)
+            later_weights, cotangent = lax.optimization_barrier((cross_rows(later_weights), cotangent))
+            last_grad_low = beside(cotangent.astype(LOW))
         own = to_heads(sent)
-        own, later_weights = lax.optimization_barrier((own, later_weights))
-        packed = gather(ffn_part(layer, cut(later_weights)[layer])).reshape(2 * planes, -1, BLOCK)
+        next_part = ffn_part(layer, cut(later_weights)[layer])
+        own, next_part, last_grad_low = lax.optimization_barrier((own, next_part, last_grad_low))
+        packed = gather(next_part).reshape(2 * planes, -1, BLOCK)
         ffn_weights.append(packed)
+        own, out_quarter = lax.optimization_barrier((own, out_quarter))
+        out_parts = [out_quarter, *neighbours(out_quarter, out_quarter, out_quarter)]
         sib = lax.ppermute(own[:, HD:], "head", CORE_SWAP)
         queries = my_tiles(own)
         q_aug = q_augs[layer]
-        out, lse = attention_forward(queries, q_aug, own, sib, k_aug)
-        if layer == 0:
-            out, cotangent = lax.optimization_barrier((out, cotangent))
-            last_grad_low = beside(cotangent.astype(LOW))
-        attended = from_heads(all_blocks(out)).reshape(quarter_width, cols)
-        if layer == 0:
-            attended, last_grad_low = lax.optimization_barrier((attended, last_grad_low))
-        middle = stream + fold(dot(attended, out_matrix, TN))
+        out, lse = attention_forward(chip_flips, queries, q_aug, own, sib, k_aug)
+        out, *out_parts = lax.optimization_barrier((out, *out_parts))
+        out_matrix = jnp.concatenate(out_parts, axis=0)
+        out_weights.append(out_matrix)
+        attended = over_spread(over_chips(all_blocks(out))).reshape(QUARTER_HEADS, 4, HD, tok_rows)
+        attended = plane_order(attended).reshape(D, tok_rows)
+        middle = stream + dot(attended, out_matrix, TN)
         scaled_two, inverse_two = normalize(middle)
         normed_ffn = beside(scaled_two.astype(LOW))
         if layer < LAYERS - 1:
             next_part = attention_part(layer + 1, cut(later_weights)[LAYERS + layer])
             normed_ffn, next_part = lax.optimization_barrier((normed_ffn, next_part))
-            attention_weights.append(attention_matrices(layer + 1, next_part))
-        both, hidden, partial = ffn_forward(normed_ffn, packed, quarter_ff, group_rows, padded)
+            attention_weights.append(attention_matrices(next_part))
+        both, hidden, *parts = ffn_forward(normed_ffn, packed, quarter_ff, group_rows, padded)
         saved.append(
             (
                 scaled_one, inverse_one, normed, own, sib, queries, q_aug, out, lse, attended,
@@ -849,65 +963,65 @@
             )
         )
         if layer < LAYERS - 1:
-            stream = middle + fold(partial)
+            stream = middle + fold(*parts)
         else:
-            last_middle, last_partial = middle, partial
+            last_middle, last_parts = middle, parts
 
     upstream = cotangent
-    whole_grads, ffn_sums = [None] * LAYERS, [None] * LAYERS
+    whole_grads, ffn_sums, qkv_sums = [None] * LAYERS, [None] * LAYERS, [None] * LAYERS
     bias_parts = [None] * LAYERS
-    buffer, sent_last = None, None
-    qkv_grad = None
-
     for layer in reversed(range(LAYERS)):
-        (qkv_matrix, out_matrix), packed = attention_weights[layer], ffn_weights[layer]
+        qkv_matrix, unused = attention_weights[layer]
+        out_matrix, packed = out_weights[layer], ffn_weights[layer]
         (
             scaled_one, inverse_one, normed, own, sib, queries, q_aug, out, lse, attended,
             scaled_two, inverse_two, normed_ffn, both, hidden,
         ) = saved[layer]
         upstream_low = beside(upstream.astype(LOW)) if layer < LAYERS - 1 else last_grad_low
-        grad_units, partial = ffn_backward(upstream_low, packed, both, quarter_ff, group_rows, padded)
-        inner = fold(partial)
-        total_rows = qkv_end if layer < LAYERS - 1 else out_end
+        grad_units, *parts = ffn_backward(upstream_low, packed, both, quarter_ff, group_rows, padded)
+        inner = fold(*parts)
         buffer = weight_grad(
-            buffer, total_rows, normed_ffn.T, grad_units, "blocks", group_rows, 0, 4 * padded // group_rows
+            None, ffn_end, normed_ffn.T, grad_units, "blocks", group_rows, 0, 4 * padded // group_rows
         )
         inner, buffer = lax.optimization_barrier((inner, buffer))
         buffer = weight_grad(
-            buffer, total_rows, hidden.T, upstream_low, "columns", padded, unit_end, D // BLOCK
+            buffer, ffn_end, hidden.T, upstream_low, "columns", padded, unit_end, D // BLOCK
         )
         grad_middle = upstream + normalize_back(scaled_two, inverse_two, inner)
-        middle_low = beside(grad_middle.astype(LOW))
-        middle_low, buffer = lax.optimization_barrier((middle_low, buffer))
+        middle_low = grad_middle.astype(LOW)
         grad_attended = dot(out_matrix, middle_low, NT).astype(LOW)
-        if split_heads:
-            buffer = weight_grad(
-                buffer, total_rows, attended, middle_low, "columns", w_rows, ffn_end, D // BLOCK
+        grad_attended = chip_order(grad_attended.reshape(4, QUARTER_HEADS, HD, tok_rows))
+        if spread > 1:
+            grad_attended = jnp.repeat(grad_attended, spread, axis=0)
+        out_grad = my_tiles(over_chips(grad_attended))
+        buffer, out_grad, middle_low, attended = lax.optimization_barrier(
+            (buffer, out_grad, middle_low, attended)
+        )
+        if layer < LAYERS - 1:
+            buffer, qkv_sums[layer + 1] = lax.optimization_barrier((buffer, qkv_sums[layer + 1]))
+        ffn_sums[layer] = scatter(buffer)
+        middle_low, attended = share_for_out(middle_low, attended)
+        grad_q, grad_kv = attention_backward(
+            chip_flips, queries, q_aug, lse, out, out_grad, own, sib, k_aug
+        )
+        grad_kv, middle_low, attended = lax.optimization_barrier((grad_kv, middle_low, attended))
+        if not split_heads:
+            whole_grads[layer] = whole_out_back(dot(attended, middle_low, NN))
+        else:
+            out_blocks = weight_grad(
+                None, out_end - ffn_end, attended, middle_low, "columns", w_rows, 0, D // BLOCK
             )
-        else:
-            whole_grads[layer] = whole_out_back(dot(attended, middle_low, NN))
-        if sent_last is not None:
-            buffer, sent_last = lax.optimization_barrier((buffer, sent_last))
-            ffn_sums[layer + 1] = sent_last
-        out_grad = my_tiles(to_heads(grad_attended.reshape(QUARTER_HEADS, HD, cols)))
-        buffer, out_grad = lax.optimization_barrier((buffer, out_grad))
-        if layer == 0:
-            sent_last = scatter(buffer)
-        grad_q, grad_kv = attention_backward(
-            queries, q_aug, lse, out, out_grad, own, sib, k_aug
-        )
         same_grad = jnp.sum(grad_q[:, HD : HD + VARIATES] * q_onehots)
         all_grad = jnp.sum(grad_q[:, HD + 16])
         crossed = lax.ppermute(grad_kv[planes:], "head", CORE_SWAP)
         grad_kv = (grad_kv[:planes].astype(jnp.float32) + crossed.astype(jnp.float32)).astype(LOW)
         grad_q = (grad_q[:, :HD] * (1.0 / math.sqrt(HD))).astype(LOW)
         if layer == LAYERS - 1:
-            grad_kv, last_partial = lax.optimization_barrier((grad_kv, last_partial))
-            stream = last_middle + fold(last_partial)
+            grad_kv, *last_parts = lax.optimization_barrier((grad_kv, *last_parts))
+            stream = last_middle + fold(*last_parts)
         grad_heads = from_heads(jnp.concatenate([all_blocks(grad_q), grad_kv], axis=1))
-        if layer > 0:
-            grad_heads, buffer, stream = lax.optimization_barrier((grad_heads, buffer, stream))
-            sent_last = scatter(buffer)
+        if layer == LAYERS - 1:
+            grad_heads, stream = lax.optimization_barrier((grad_heads, stream))
         grad_heads = jnp.concatenate(
             [
                 rotate(grad_heads[:, :HD].astype(jnp.float32), -sines).astype(LOW),
@@ -917,23 +1031,20 @@
             axis=1,
         ).reshape(3 * quarter_width, cols)
         bias_parts[layer] = jnp.stack([same_grad, all_grad - same_grad])
+        partial = dot(grad_heads, qkv_matrix, TT)
+        qkv_grad = dot(normed, grad_heads, TT).astype(LOW)
+        qkv_grad, ffn_sums[layer] = lax.optimization_barrier((qkv_grad, ffn_sums[layer]))
+        if split_heads:
+            qkv_grad = jnp.concatenate([qkv_grad, out_blocks.reshape(-1, BLOCK)], axis=1)
         if layer > 0:
-            buffer = weight_grad(
-                None, qkv_end, normed.T, grad_heads, "rows", group_rows, out_end, 1
+            inner = fold_whole(partial)
+            inner, qkv_grad = lax.optimization_barrier((inner, qkv_grad))
+        qkv_sums[layer] = scatter(qkv_grad)
+        if layer == 0:
+            qkv_sums[0], partial, *bias_parts = lax.optimization_barrier(
+                (qkv_sums[0], partial, *bias_parts)
             )
-        else:
-            qkv_grad = dot(normed, grad_heads, TT).astype(LOW)
-            qkv_grad, grad_heads = lax.optimization_barrier((qkv_grad, grad_heads))
-            qkv_grad, sent_last = lax.optimization_barrier((qkv_grad, sent_last))
-            ffn_sums[0] = sent_last
-            qkv_sum = scatter(qkv_grad)
-        partial = dot(grad_heads, qkv_matrix, TT)
-        if layer > 0:
-            inner = fold(partial)
-            inner, buffer = lax.optimization_barrier((inner, buffer))
-        else:
-            qkv_sum, partial = lax.optimization_barrier((qkv_sum, partial))
-            inner = fold(partial)
+            inner = fold_whole(partial)
         upstream = grad_middle + normalize_back(scaled_one, inverse_one, inner)
 
     bias_local = lax.dynamic_update_slice(
@@ -948,19 +1059,24 @@
             hop *= 2
 
     later_sums = [from_blocks(member[None, :unit_end], group_rows) for member in ffn_sums]
-    later_sums += [from_blocks(member[None, out_end:], group_rows) for member in ffn_sums[:-1]]
+    out_sums = [member[:, 3 * quarter_width :] for member in qkv_sums]
+    qkv_sums = [member[:, : 3 * quarter_width] for member in qkv_sums]
+    if not split_heads:
+        out_sums = [member[:, :BLOCK] for member in qkv_sums]
+    later_sums = jnp.concatenate([*later_sums, *qkv_sums[1:]], axis=1)
     quarters = jnp.arange(QUARTERS, dtype=jnp.int32)
     weights = (w_query, w_key, w_value, w_gate, w_up)
     gains = (gain_attn[:, :, None], gain_ffn[:, :, None])
     *grads, gain_one, gain_two = finish_gradients(
-        quarters ^ (2 * here_y + here_core), cross_back(jnp.concatenate(later_sums, axis=1)), ffn_sums,
-        weights, gains, w_down.shape, (unit_end, ffn_end), planes, split_heads,
+        quarters ^ (2 * here_y + here_core), cross_back(later_sums), ffn_sums,
+        out_sums[1:], weights, gains, w_down.shape, unit_end, planes, split_heads,
+    )
+    *grads[:3], gain_one, grads[3] = finish_first(
+        2 * quarters + here_lo, cross_back_at_once(qkv_sums[0]), out_sums[0], weights[:3], gains[0],
+        [*grads[:3], gain_one, grads[3]], split_heads,
     )
     if not split_heads:
         grads[3] = jnp.stack(whole_grads).astype(jnp.float32)
-    *grads[:3], gain_one = finish_first(
-        2 * quarters + here_lo, cross_back_at_once(qkv_sum), weights[:3], gains[0], grads[:3], gain_one
-    )
     return (stream, upstream, *grads, gain_one[:, :, 0], gain_two[:, :, 0], bias_total)
 
 

time: 716 us -> 648 us (0.905)
  waiting for transfers between devices: 277 us -> 223 us
  Pallas kernels: 160 us -> 134 us
  starting transfers between devices: 123 us -> 133 us
    ppermute x17, waiting for transfers between devices: 73.3 us -> 39.1 us  [neighbours(): lax.ppermute(across_x, 'seq', x_swap)]
    all_to_all x0 -> x4, waiting for transfers between devices: none -> 32.8 us  [over_chips(): lax.all_to_all(value, BOTH, split_axis=0, concat_axis=0, tiled=True, axis...]
    all_to_all x4 -> x2, waiting for transfers between devices: 45.9 us -> 16.1 us  [to_heads(): lax.all_to_all(value, 'seq', split_axis=0, concat_axis=0, tiled=True, axi...]
    all_to_all x0 -> x4, starting transfers between devices: none -> 22.9 us  [over_chips(): lax.all_to_all(value, BOTH, split_axis=0, concat_axis=0, tiled=True, axis...]
    ppermute x17, starting transfers between devices: 32.2 us -> 11.9 us  [neighbours(): lax.ppermute(across_x, 'seq', x_swap)]
    pallas_call x6, Pallas kernels: 102 us -> 82.4 us  [the longest x2 45.8 us: attention_backward(): pl.pallas_call(backward_kernel, grid_spec=pltpu.PrefetchScalarGridSpec(nu...]
    all_to_all x4 -> x2, waiting for transfers between devices: 55.6 us -> 42.4 us  [from_heads(): lax.all_to_all(value, 'seq', split_axis=0, concat_axis=0, tiled=True, axi...]
    ppermute x17, starting transfers between devices: 10.3 us -> 21 us  [neighbours(): lax.ppermute(across_y, 'head', Y_SWAP)]
  transfers between devices with their start and end apart: 85 -> 86, of which waited for: 54 -> 47; matrix products, arithmetic and copies ran while one was open for 12% -> 14% of each run, Pallas kernels for 16% -> 18%
where the time goes in v3:
time: 648 us; the launch traced here: 642 us
  waiting for transfers between devices  223 us (34%)
  Pallas kernels  134 us (21%)
  starting transfers between devices  133 us (21%)
  other arithmetic  58.4 us (9%)
  local copies, waits for them, and re-layouts  53.3 us (8%)
  between operations  24.5 us (4%)
  matrix products  16.4 us (3%)
    ppermute x17, waiting for transfers between devices, neighbours(): lax.ppermute(across_both, BOTH, corner_swap)  54.3 us
    pallas_call x2, Pallas kernels, attention_backward(): pl.pallas_call(backward_kernel, grid_spec=pltpu.PrefetchScalarGridSpec(nu...  45.8 us
    all_to_all x2, waiting for transfers between devices, from_heads(): lax.all_to_all(value, 'seq', split_axis=0, concat_axis=0, tiled=True, axi...  42.4 us
    ppermute x17, waiting for transfers between devices, neighbours(): lax.ppermute(across_x, 'seq', x_swap)  39.1 us
    all_to_all x4, waiting for transfers between devices, over_chips(): lax.all_to_all(value, BOTH, split_axis=0, concat_axis=0, tiled=True, axis...  32.8 us
    pallas_call x2, Pallas kernels, attention_forward(): pl.pallas_call(forward_kernel, grid_spec=pltpu.PrefetchScalarGridSpec(num...  28.9 us
    ppermute x17, starting transfers between devices, neighbours(): lax.ppermute(across_both, BOTH, corner_swap)  28.4 us
    all_to_all x4, starting transfers between devices, over_chips(): lax.all_to_all(value, BOTH, split_axis=0, concat_axis=0, tiled=True, axis...  22.9 us
  transfers between devices with their start and end apart: 86, of which 47 were waited for; matrix products, arithmetic and copies ran while one was open for 14% of the time, Pallas kernels for 18%

profile of v3, /device:TPU:0, one launch (start us, length us, event | category | flops | bytes accessed | tf_op | source)
XLA Modules:
  0.0 642.5 jit_solution(2468382203833575126)
XLA Ops:
  13.1 5.2 all-to-all-start
  53.4 6.1 collective-permute-done
  106.7 14.4 %attention_forward.2 = (bf16[4,4,64,128]{3,2,1,0:T(8,128)(2,1)}, f32[4,8,512]{2,1,0:T(8,128)}) custom-call(s32[1]{0:T(128)} %bitcast.flip_ref, bf16[4,192,512]{2,1,0:T(8,128)(2,1)} %copy-done.12, bf16[4,64,512]{2,1,0:T(8,128)(2,1)} %get-tuple-element.154.q_aug_ref, bf16[4,192,512]{2,1,0:T(8,128)(2,1)} %copy-done.12, bf16[4,128,512]{2,1,0:T(8,128)(2,1)} %copy-done.62, ...), custom_call_target="tpu_custom_call" | custom-call | flops 8589934592 | bytes 2424832 | tf_op jit(solution)/shard_map/attention_forward/pallas_call | solution.py:166
  121.2 7.9 %collective-permute-done.16 = bf16[256,1024]{1,0:T(8,128)(2,1)S(1)} collective-permute-done((bf16[256,1024]{1,0:T(8,128)(2,1)S(1)}, bf16[256,1024]{1,0:T(8,128)(2,1)S(1)}, u32[]{:S(2)}, u32[]{:S(2)}) %collective-permute-start.16) | collective-permute-done | bytes 524320 | tf_op jit(solution)/shard_map/ppermute | solution.py:603
  129.9 6.0 all-to-all-start.2
  138.6 12.6 %all-to-all-done.2 = bf16[16,64,128]{2,1,0:T(8,128)(2,1)S(1)} async-done(((bf16[16,64,128]{2,1,0:T(8,128)(2,1)}), bf16[16,64,128]{2,1,0:T(8,128)(2,1)S(1)}, u32[]{:S(2)}, u32[]{:S(2)}) %all-to-all-start.2) | async-done | bytes 262176 | tf_op jit(solution)/shard_map/all_to_all | solution.py:884
  165.0 7.0 %ffn_forward.2 = (bf16[6,512,256]{2,1,0:T(8,128)(2,1)}, bf16[512,768]{1,0:T(8,128)(2,1)}, f32[128,1024]{1,0:T(8,128)}, bf16[128,1024]{1,0:T(8,128)(2,1)}, bf16[1...) custom-call(bf16[512,1024]{1,0:T(8,128)(2,1)} %pad_maximum_fusion.4.x_ref, bf16[8,1152,256]{2,1,0:T(8,128)(2,1)} %bitcast.290, ...), custom_call_target="tpu_custom_call" | custom-call | flops 2415919104 | bytes 9437184 | tf_op jit(solution)/shard_map/ffn_forward/pallas_call | solution.py:340
  175.6 6.7 %collective-permute-done.22 = bf16[128,1024]{1,0:T(8,128)(2,1)S(1)} collective-permute-done((bf16[128,1024]{1,0:T(8,128)(2,1)}, bf16[128,1024]{1,0:T(8,128)(2,1)S(1)}, u32[]{:S(2)}, u32[]{:S(2)}) %collective-permute-start.22) | collective-permute-done | bytes 262176 | tf_op jit(solution)/shard_map/ppermute | solution.py:603
  191.3 5.5 all-gather.7.cloned.1.call-done
  205.9 7.5 %all-to-all-start.3 = ((bf16[4,192,512]{2,1,0:T(8,128)(2,1)}), bf16[4,192,512]{2,1,0:T(8,128)(2,1)S(1)}, u32[]{:S(2)}, u32[]{:S(2)}) async-start(bf16[4,192,512]{2,1,0:T(8,128)(2,1)} %pad_maximum_fusion.15), calls=%async_computation.3 | async-start | bytes 1572864 | tf_op jit(solution)/shard_map/all_to_all | solution.py:853
  217.6 16.1 %all-to-all-done.3.q_ref.own_ref = bf16[4,192,512]{2,1,0:T(8,128)(2,1)S(1)} async-done(((bf16[4,192,512]{2,1,0:T(8,128)(2,1)}), bf16[4,192,512]{2,1,0:T(8,128)(2,1)S(1)}, u32[]{:S(2)}, u32[]{:S(2)}) %all-to-all-start.3) | async-done | bytes 786464 | tf_op jit(solution)/shard_map/all_to_all | solution.py:853
  238.9 14.5 %attention_forward.3 = (bf16[4,4,64,128]{3,2,1,0:T(8,128)(2,1)}, f32[4,8,512]{2,1,0:T(8,128)}) custom-call(s32[1]{0:T(128)} %bitcast.flip_ref, bf16[4,192,512]{2,1,0:T(8,128)(2,1)} %copy-done.13, bf16[4,64,512]{2,1,0:T(8,128)(2,1)} %get-tuple-element.173.q_aug_ref, bf16[4,192,512]{2,1,0:T(8,128)(2,1)} %copy-done.13, bf16[4,128,512]{2,1,0:T(8,128)(2,1)} %copy-done.63, ...), custom_call_target="tpu_custom_call" | custom-call | flops 8589934592 | bytes 2424832 | tf_op jit(solution)/shard_map/attention_forward/pallas_call | solution.py:166
  253.5 8.1 %collective-permute-done.29 = bf16[256,1024]{1,0:T(8,128)(2,1)S(1)} collective-permute-done((bf16[256,1024]{1,0:T(8,128)(2,1)S(1)}, bf16[256,1024]{1,0:T(8,128)(2,1)S(1)}, u32[]{:S(2)}, u32[]{:S(2)}) %collective-permute-start.29) | collective-permute-done | bytes 524320 | tf_op jit(solution)/shard_map/ppermute | solution.py:603
  270.4 11.7 %all-to-all-done.4 = bf16[16,64,128]{2,1,0:T(8,128)(2,1)S(1)} async-done(((bf16[16,64,128]{2,1,0:T(8,128)(2,1)}), bf16[16,64,128]{2,1,0:T(8,128)(2,1)S(1)}, u32[]{:S(2)}, u32[]{:S(2)}) %all-to-all-start.4) | async-done | bytes 262176 | tf_op jit(solution)/shard_map/all_to_all | solution.py:884
  288.0 5.7 collective-permute-done.32
  297.7 7.0 %ffn_forward.3 = (bf16[6,512,256]{2,1,0:T(8,128)(2,1)}, bf16[512,768]{1,0:T(8,128)(2,1)}, f32[128,1024]{1,0:T(8,128)}, bf16[128,1024]{1,0:T(8,128)(2,1)}, bf16[1...) custom-call(bf16[512,1024]{1,0:T(8,128)(2,1)} %get-tuple-element.355.x_ref, bf16[8,1152,256]{2,1,0:T(8,128)(2,1)} %bitcast.294, ...), custom_call_target="tpu_custom_call" | custom-call | flops 2415919104 | bytes 9437184 | tf_op jit(solution)/shard_map/ffn_forward/pallas_call | solution.py:340
  304.6 7.8 %ffn_backward.2 = (bf16[6,512,256]{2,1,0:T(8,128)(2,1)}, f32[128,1024]{1,0:T(8,128)}, bf16[128,1024]{1,0:T(8,128)(2,1)}, bf16[128,1024]{1,0:T(8,128)(2,1)}, bf16[128,1024]{1,0:T(8,128)(2,1)}) custom-call(bf16[512,1024]{1,0:T(8,128)(2,1)} %pad_maximum_fusion.3.g_ref.right_ref, bf16[8,1152,256]{2,1,0:T(8,128)(2,1)} %bitcast.296, ...), custom_call_target="tpu_custom_call" | custom-call | flops 2415919104 | bytes 10223616 | tf_op jit(solution)/shard_map/ffn_backward/pallas_call | solution.py:368
  332.9 8.5 %all-to-all-start.5 = ((bf16[16,64,128]{2,1,0:T(8,128)(2,1)}), bf16[16,64,128]{2,1,0:T(8,128)(2,1)S(1)}, u32[]{:S(2)}, u32[]{:S(2)}) async-start(bf16[16,64,128]{2,1,0:T(8,128)(2,1)} %bitcast.76), calls=%async_computation.5 | async-start | bytes 524288 | tf_op jit(solution)/shard_map/all_to_all | solution.py:884
  355.8 22.9 %attention_backward.2 = (f32[4,128,512]{2,1,0:T(8,128)}, bf16[8,128,512]{2,1,0:T(8,128)(2,1)}) custom-call(s32[1]{0:T(128)} %bitcast.flip_ref, bf16[4,192,512]{2,1,0:T(8,128)(2,1)} %copy-done.13, bf16[4,64,512]{2,1,0:T(8,128)(2,1)} %get-tuple-element.173.q_aug_ref, f32[4,8,512]{2,1,0:T(8,128)} %get-tuple-element.174.lse_ref, ...), custom_call_target="tpu_custom_call" | custom-call | flops 17179869184 | bytes 4194304 | tf_op jit(solution)/shard_map/attention_backward/pallas_call | solution.py:190
  404.6 13.9 %all-to-all-done.6 = bf16[4,192,512]{2,1,0:T(8,128)(2,1)S(1)} async-done(((bf16[4,192,512]{2,1,0:T(8,128)(2,1)}), bf16[4,192,512]{2,1,0:T(8,128)(2,1)S(1)}, u32[]{:S(2)}, u32[]{:S(2)}) %all-to-all-start.6) | async-done | bytes 786464 | tf_op jit(solution)/shard_map/all_to_all | solution.py:871
  444.8 6.6 %collective-permute-done.48 = bf16[128,1024]{1,0:T(8,128)(2,1)S(1)} collective-permute-done((bf16[128,1024]{1,0:T(8,128)(2,1)S(1)}, bf16[128,1024]{1,0:T(8,128)(2,1)S(1)}, u32[]{:S(2)}, u32[]{:S(2)}) %collective-permute-start.48) | collective-permute-done | bytes 262176 | tf_op jit(solution)/shard_map/ppermute | solution.py:603
  457.1 8.0 %ffn_backward.3 = (bf16[6,512,256]{2,1,0:T(8,128)(2,1)}, f32[128,1024]{1,0:T(8,128)}, bf16[128,1024]{1,0:T(8,128)(2,1)}, bf16[128,1024]{1,0:T(8,128)(2,1)}, bf16[128,1024]{1,0:T(8,128)(2,1)}) custom-call(bf16[512,1024]{1,0:T(8,128)(2,1)} %pad_maximum_fusion.8.g_ref.right_ref, bf16[8,1152,256]{2,1,0:T(8,128)(2,1)} %bitcast.292, ...), custom_call_target="tpu_custom_call" | custom-call | flops 2415919104 | bytes 10223616 | tf_op jit(solution)/shard_map/ffn_backward/pallas_call | solution.py:368
  502.0 22.9 %attention_backward.3 = (f32[4,128,512]{2,1,0:T(8,128)}, bf16[8,128,512]{2,1,0:T(8,128)(2,1)}) custom-call(s32[1]{0:T(128)} %bitcast.flip_ref, bf16[4,192,512]{2,1,0:T(8,128)(2,1)} %copy-done.12, bf16[4,64,512]{2,1,0:T(8,128)(2,1)} %get-tuple-element.154.q_aug_ref, f32[4,8,512]{2,1,0:T(8,128)} %get-tuple-element.222.lse_ref, ...), custom_call_target="tpu_custom_call" | custom-call | flops 17179869184 | bytes 4194304 | tf_op jit(solution)/shard_map/attention_backward/pallas_call | solution.py:190
  536.0 28.5 %all-to-all-done.8 = bf16[4,192,512]{2,1,0:T(8,128)(2,1)S(1)} async-done(((bf16[4,192,512]{2,1,0:T(8,128)(2,1)}), bf16[4,192,512]{2,1,0:T(8,128)(2,1)S(1)}, u32[]{:S(2)}, u32[]{:S(2)}) %all-to-all-start.8) | async-done | bytes 786464 | tf_op jit(solution)/shard_map/all_to_all | solution.py:871
  (588 shorter events, 356.7 us)
Async XLA Ops:
  18.3 42.5 %all-gather.5.cloned.1.call-start = ((), (), s32[]{:S(2)}) async-start(), calls=%async_computation.14 | async-start | bytes 2359296 | tf_op jit(solution)/shard_map/all_gather | solution.py:673
  30.1 23.3 %collective-permute-start.2 = (bf16[128,1024]{1,0:T(8,128)(2,1)}, bf16[128,1024]{1,0:T(8,128)(2,1)}, u32[]{:S(2)}, u32[]{:S(2)}) collective-permute-start(bf16[128,1024]{1,0:T(8,128)(2,1)} %multiply_convert_fusion.5), channel_id=1, source_target_pairs={{0,6},{1,7},{2,4},{3,5},{4,2},{5,3},{6,0},{7,1},{8,14},{9,15},{10,... | collective-permute-start | bytes 786440 | tf_op jit(solution)/shard_map/ppermute | solution.py:603
  33.0 20.4 %collective-permute-start.1 = (bf16[128,1024]{1,0:T(8,128)(2,1)}, bf16[128,1024]{1,0:T(8,128)(2,1)}, u32[]{:S(2)}, u32[]{:S(2)}) collective-permute-start(bf16[128,1024]{1,0:T(8,128)(2,1)} %multiply_convert_fusion.5), channel_id=1, source_target_pairs={{0,4},{4,0},{8,12},{12,8},{16,20},{20,16},{24,28},{28,24},{1,5},{5... | collective-permute-start | bytes 786440 | tf_op jit(solution)/shard_map/ppermute | solution.py:602
  75.1 26.4 %all-to-all-start.1 = ((bf16[4,192,512]{2,1,0:T(8,128)(2,1)}), bf16[4,192,512]{2,1,0:T(8,128)(2,1)S(1)}, u32[]{:S(2)}, u32[]{:S(2)}) async-start(bf16[4,192,512]{2,1,0:T(8,128)(2,1)} %pad_maximum_fusion.14), calls=%async_computation.1 | async-start | bytes 1572864 | tf_op jit(solution)/shard_map/all_to_all | solution.py:853
  79.9 85.0 %all-gather.9.cloned.1.call-start = ((), (), s32[]{:S(2)}) async-start(), calls=%async_computation.16 | async-start | bytes 5308416 | tf_op jit(solution)/shard_map/all_gather | solution.py:673
  103.9 25.2 %collective-permute-start.16 = (bf16[256,1024]{1,0:T(8,128)(2,1)S(1)}, bf16[256,1024]{1,0:T(8,128)(2,1)S(1)}, u32[]{:S(2)}, u32[]{:S(2)}) collective-permute-start(bf16[256,1024]{1,0:T(8,128)(2,1)S(1)} %bitcast.314), channel_id=1, source_target_pairs={{0,6},{1,7},{2,4},{3,5},{4,2},{5,3},{6,0},{7,1},{8,14},{9,15},{10,... | collective-permute-start | bytes 1572872 | tf_op jit(solution)/shard_map/ppermute | solution.py:603
  129.9 21.3 %all-to-all-start.2 = ((bf16[16,64,128]{2,1,0:T(8,128)(2,1)}), bf16[16,64,128]{2,1,0:T(8,128)(2,1)S(1)}, u32[]{:S(2)}, u32[]{:S(2)}) async-start(bf16[16,64,128]{2,1,0:T(8,128)(2,1)} %bitcast.347), calls=%async_computation.2 | async-start | bytes 524288 | tf_op jit(solution)/shard_map/all_to_all | solution.py:884
  135.9 60.9 %all-gather.7.cloned.1.call-start = ((), (), s32[]{:S(2)}) async-start(), calls=%async_computation.15 | async-start | bytes 2359296 | tf_op jit(solution)/shard_map/all_gather | solution.py:673
  205.9 27.8 %all-to-all-start.3 = ((bf16[4,192,512]{2,1,0:T(8,128)(2,1)}), bf16[4,192,512]{2,1,0:T(8,128)(2,1)S(1)}, u32[]{:S(2)}, u32[]{:S(2)}) async-start(bf16[4,192,512]{2,1,0:T(8,128)(2,1)} %pad_maximum_fusion.15), calls=%async_computation.3 | async-start | bytes 1572864 | tf_op jit(solution)/shard_map/all_to_all | solution.py:853
  213.5 84.2 %all-gather.11.cloned.1.call-start = ((), (), s32[]{:S(2)}) async-start(), calls=%async_computation.17 | async-start | bytes 5308416 | tf_op jit(solution)/shard_map/all_gather | solution.py:673
  237.5 24.1 %collective-permute-start.29 = (bf16[256,1024]{1,0:T(8,128)(2,1)S(1)}, bf16[256,1024]{1,0:T(8,128)(2,1)S(1)}, u32[]{:S(2)}, u32[]{:S(2)}) collective-permute-start(bf16[256,1024]{1,0:T(8,128)(2,1)S(1)} %bitcast.318), channel_id=1, source_target_pairs={{0,6},{1,7},{2,4},{3,5},{4,2},{5,3},{6,0},{7,1},{8,14},{9,15},{10,... | collective-permute-start | bytes 1572872 | tf_op jit(solution)/shard_map/ppermute | solution.py:603
  262.4 19.7 %all-to-all-start.4 = ((bf16[16,64,128]{2,1,0:T(8,128)(2,1)}), bf16[16,64,128]{2,1,0:T(8,128)(2,1)S(1)}, u32[]{:S(2)}, u32[]{:S(2)}) async-start(bf16[16,64,128]{2,1,0:T(8,128)(2,1)} %bitcast.348), calls=%async_computation.4 | async-start | bytes 524288 | tf_op jit(solution)/shard_map/all_to_all | solution.py:884
  341.4 94.7 %reduce-scatter.5.cloned.1.call-start = ((), (), s32[]{:S(2)}) async-start(), calls=%async_computation.18 | async-start | bytes 5308416 | tf_op jit(solution)/shard_map/reduce_scatter | solution.py:685
  352.3 26.5 %collective-permute-start.38 = (bf16[128,1280]{1,0:T(8,128)(2,1)S(1)}, bf16[128,1280]{1,0:T(8,128)(2,1)S(1)}, u32[]{:S(2)}, u32[]{:S(2)}) collective-permute-start(bf16[128,1280]{1,0:T(8,128)(2,1)S(1)} %get-tuple-element.411), channel_id=1, source_target_pairs={{0,6},{1,7},{2,4},{3,5},{4,2},{5,3},{6,0},{7,1},{8,14},{9,15},{10,... | collective-permute-start | bytes 983048 | tf_op jit(solution)/shard_map/ppermute | solution.py:603
  353.4 25.4 %collective-permute-start.37 = (bf16[128,1280]{1,0:T(8,128)(2,1)S(1)}, bf16[128,1280]{1,0:T(8,128)(2,1)S(1)}, u32[]{:S(2)}, u32[]{:S(2)}) collective-permute-start(bf16[128,1280]{1,0:T(8,128)(2,1)S(1)} %get-tuple-element.410), channel_id=1, source_target_pairs={{0,4},{4,0},{8,12},{12,8},{16,20},{20,16},{24,28},{28,24},{1,5},{5... | collective-permute-start | bytes 983048 | tf_op jit(solution)/shard_map/ppermute | solution.py:602
  354.6 24.2 %collective-permute-start.36 = (bf16[128,1280]{1,0:T(8,128)(2,1)S(1)}, bf16[128,1280]{1,0:T(8,128)(2,1)S(1)}, u32[]{:S(2)}, u32[]{:S(2)}) collective-permute-start(bf16[128,1280]{1,0:T(8,128)(2,1)S(1)} %get-tuple-element.409), channel_id=1, source_target_pairs={{0,2},{1,3},{2,0},{3,1},{4,6},{5,7},{6,4},{7,5},{8,10},{9,11},{10,... | collective-permute-start | bytes 983048 | tf_op jit(solution)/shard_map/ppermute | solution.py:601
  383.8 34.8 %all-to-all-start.6 = ((bf16[4,192,512]{2,1,0:T(8,128)(2,1)}), bf16[4,192,512]{2,1,0:T(8,128)(2,1)S(1)}, u32[]{:S(2)}, u32[]{:S(2)}) async-start(bf16[4,192,512]{2,1,0:T(8,128)(2,1)} %pad_maximum_fusion.16), calls=%async_computation.6 | async-start | bytes 1572864 | tf_op jit(solution)/shard_map/all_to_all | solution.py:871
  387.3 110.0 %reduce-scatter.7.cloned.1.call-start = ((), (), s32[]{:S(2)}) async-start(), calls=%async_computation.19 | async-start | bytes 2359296 | tf_op jit(solution)/shard_map/reduce_scatter | solution.py:685
  487.2 79.7 %reduce-scatter.9.cloned.1.call-start = ((), (), s32[]{:S(2)}) async-start(), calls=%async_computation.20 | async-start | bytes 5308416 | tf_op jit(solution)/shard_map/reduce_scatter | solution.py:685
  498.4 26.4 %collective-permute-start.54 = (bf16[128,1280]{1,0:T(8,128)(2,1)S(1)}, bf16[128,1280]{1,0:T(8,128)(2,1)S(1)}, u32[]{:S(2)}, u32[]{:S(2)}) collective-permute-start(bf16[128,1280]{1,0:T(8,128)(2,1)S(1)} %get-tuple-element.398), channel_id=1, source_target_pairs={{0,6},{1,7},{2,4},{3,5},{4,2},{5,3},{6,0},{7,1},{8,14},{9,15},{10,... | collective-permute-start | bytes 983048 | tf_op jit(solution)/shard_map/ppermute | solution.py:603
  499.6 25.4 %collective-permute-start.53 = (bf16[128,1280]{1,0:T(8,128)(2,1)S(1)}, bf16[128,1280]{1,0:T(8,128)(2,1)S(1)}, u32[]{:S(2)}, u32[]{:S(2)}) collective-permute-start(bf16[128,1280]{1,0:T(8,128)(2,1)S(1)} %get-tuple-element.397), channel_id=1, source_target_pairs={{0,4},{4,0},{8,12},{12,8},{16,20},{20,16},{24,28},{28,24},{1,5},{5... | collective-permute-start | bytes 983048 | tf_op jit(solution)/shard_map/ppermute | solution.py:602
  500.7 24.2 %collective-permute-start.52 = (bf16[128,1280]{1,0:T(8,128)(2,1)S(1)}, bf16[128,1280]{1,0:T(8,128)(2,1)S(1)}, u32[]{:S(2)}, u32[]{:S(2)}) collective-permute-start(bf16[128,1280]{1,0:T(8,128)(2,1)S(1)} %get-tuple-element.396), channel_id=1, source_target_pairs={{0,2},{1,3},{2,0},{3,1},{4,6},{5,7},{6,4},{7,5},{8,10},{9,11},{10,... | collective-permute-start | bytes 983048 | tf_op jit(solution)/shard_map/ppermute | solution.py:601
  529.9 34.6 %all-to-all-start.8 = ((bf16[4,192,512]{2,1,0:T(8,128)(2,1)}), bf16[4,192,512]{2,1,0:T(8,128)(2,1)S(1)}, u32[]{:S(2)}, u32[]{:S(2)}) async-start(bf16[4,192,512]{2,1,0:T(8,128)(2,1)} %pad_maximum_fusion.17), calls=%async_computation.9 | async-start | bytes 1572864 | tf_op jit(solution)/shard_map/all_to_all | solution.py:871
  533.4 69.6 %reduce-scatter.11.cloned.1.call-start = ((), (), s32[]{:S(2)}) async-start(), calls=%async_computation.21 | async-start | bytes 2359296 | tf_op jit(solution)/shard_map/reduce_scatter | solution.py:685
  (140 other events, 1311.3 us)
Sparse Core Ops, SparseCore 0:
  27.5 30.7 all-gather.4
  101.6 57.6 all-gather.8
  165.0 31.7 all-gather.6
  233.9 56.1 all-gather.10
  351.6 63.9 reduce-scatter.4
  439.4 33.8 reduce-scatter.6
  497.4 63.5 reduce-scatter.8
  568.8 34.1 reduce-scatter.10

commit v4 on v3

--- a/solution.py
+++ b/solution.py
@@ -226,9 +226,18 @@
     )
 
 
-def ffn_forward_kernel(
-    x_ref, unit_ref, down_ref, both_ref, hidden_ref, *out_refs, unit_rows, down_rows, unit_steps
-):
+def join_rows(x_ref, refs):
+    @pl.when(pl.program_id(0) == 0)
+    def _():
+        rows = refs[0].shape[0]
+        for place, ref in enumerate(refs):
+            x_ref[place * rows : (place + 1) * rows, :] = ref[...]
+
+
+def ffn_forward_kernel(*refs, unit_rows, down_rows, unit_steps):
+    unit_ref, down_ref, both_ref, hidden_ref = refs[4:8]
+    out_refs, x_ref = refs[8:12], refs[12]
+    join_rows(x_ref, refs[:4])
     step = pl.program_id(0)
     half = BLOCK // 2
 
@@ -251,10 +260,10 @@
             put_parts(dot(hidden_ref[...], matrix, NN), lanes, *out_refs)
 
 
-def ffn_backward_kernel(
-    g_ref, unit_ref, down_ref, both_ref, grads_ref, *refs, unit_rows, down_rows, down_steps
-):
-    part_refs, inner_ref, hidden_grad = refs[:4], refs[4], refs[5]
+def ffn_backward_kernel(*refs, unit_rows, down_rows, down_steps):
+    unit_ref, down_ref, both_ref, grads_ref = refs[4:8]
+    part_refs, inner_ref, hidden_grad, g_ref = refs[8:12], refs[12], refs[13], refs[14]
+    join_rows(g_ref, refs[:4])
     step = pl.program_id(0)
     half = BLOCK // 2
 
@@ -263,8 +272,8 @@
         total = 0.0
         for place in range(down_ref.shape[1] // down_rows):
             matrix = down_ref[:, place * down_rows : (place + 1) * down_rows, :].reshape(-1, BLOCK)
-            part = g_ref[:, place * BLOCK : (place + 1) * BLOCK]
-            total = total + dot(part, matrix, NT)
+            lanes = pl.ds(pl.multiple_of((step * FFN_DOWNS + place) * BLOCK, BLOCK), BLOCK)
+            total = total + dot(g_ref[:, lanes], matrix, NT)
 
         @pl.when(step == 0)
         def _():
@@ -324,8 +333,8 @@
     )
 
 
-def ffn_forward(x, packed, cols_ff, unit_rows, down_rows):
-    tokens, unit_steps = x.shape[0], 2 * cols_ff // BLOCK // ffn_units(cols_ff)
+def ffn_forward(rows, packed, cols_ff, unit_rows, down_rows):
+    tokens, unit_steps = 4 * rows[0].shape[0], 2 * cols_ff // BLOCK // ffn_units(cols_ff)
     unit_step = lambda i: jnp.minimum(i, unit_steps - 1)
     down_step = lambda i: jnp.maximum(i - unit_steps, 0)
     unit_steps, down_steps, specs = ffn_specs(
@@ -342,21 +351,22 @@
             ffn_forward_kernel, unit_rows=unit_rows, down_rows=down_rows, unit_steps=unit_steps
         ),
         grid=(unit_steps + down_steps,),
-        in_specs=[pl.BlockSpec(x.shape, lambda i: (0, 0)), *specs],
+        in_specs=[pl.BlockSpec(rows[0].shape, lambda i: (0, 0))] * 4 + specs,
         out_specs=[
             pl.BlockSpec((ffn_units(cols_ff), tokens, BLOCK), lambda i: (unit_step(i), 0, 0)),
             pl.BlockSpec((tokens, cols_ff), lambda i: (0, 0)),
             *part_specs,
         ],
         out_shape=results,
-        cost_estimate=cost(6 * tokens * D * cols_ff, [x, packed], results),
+        scratch_shapes=[pltpu.VMEM((tokens, D), LOW)],
+        cost_estimate=cost(6 * tokens * D * cols_ff, [*rows, packed], results),
         compiler_params=pltpu.CompilerParams(vmem_limit_bytes=VMEM_LIMIT),
         name="ffn_forward",
-    )(x, packed, packed)
-
-
-def ffn_backward(grad, packed, both, cols_ff, unit_rows, down_rows):
-    tokens, down_steps = grad.shape[0], D // BLOCK // FFN_DOWNS
+    )(*rows, packed, packed)
+
+
+def ffn_backward(rows, packed, both, cols_ff, unit_rows, down_rows):
+    tokens, down_steps = 4 * rows[0].shape[0], D // BLOCK // FFN_DOWNS
     unit_step = lambda i: jnp.maximum(i - down_steps, 0)
     down_step = lambda i: jnp.minimum(i, down_steps - 1)
     unit_steps, down_steps, specs = ffn_specs(
@@ -370,60 +380,90 @@
             ffn_backward_kernel, unit_rows=unit_rows, down_rows=down_rows, down_steps=down_steps
         ),
         grid=(unit_steps + down_steps,),
-        in_specs=[
-            pl.BlockSpec((tokens, FFN_DOWNS * BLOCK), lambda i: (0, down_step(i))),
-            *specs,
-            unit_spec,
-        ],
+        in_specs=[pl.BlockSpec(rows[0].shape, lambda i: (0, 0))] * 4 + [*specs, unit_spec],
         out_specs=[unit_spec, *part_specs],
         out_shape=results,
-        scratch_shapes=[pltpu.VMEM((tokens, D), jnp.float32), pltpu.VMEM((tokens, cols_ff), jnp.float32)],
-        cost_estimate=cost(6 * tokens * D * cols_ff, [grad, packed, both], results),
+        scratch_shapes=[
+            pltpu.VMEM((tokens, D), jnp.float32),
+            pltpu.VMEM((tokens, cols_ff), jnp.float32),
+            pltpu.VMEM((tokens, D), LOW),
+        ],
+        cost_estimate=cost(6 * tokens * D * cols_ff, [*rows, packed, both], results),
         compiler_params=pltpu.CompilerParams(vmem_limit_bytes=VMEM_LIMIT),
         name="ffn_backward",
-    )(grad, packed, packed, both)
-
-
-def weight_grad_kernel(left_ref, right_ref, *refs, rows, kind):
-    out_ref = refs[-1]
-    for place in range(out_ref.shape[1] // rows):
-        if kind == "blocks":
-            grad = dot(left_ref[...], right_ref[place], NN)
-        elif kind == "columns":
-            grad = dot(left_ref[...], right_ref[:, place * BLOCK : (place + 1) * BLOCK], NN)
-        else:
-            grad = dot(left_ref[...], right_ref[place * BLOCK : (place + 1) * BLOCK, :], NT)
+    )(*rows, packed, packed, both)
+
+
+def ffn_weight_grads_kernel(*refs, unit_rows, down_rows):
+    unit_grads_ref, hidden_ref, g_refs, out_ref, x_ref = refs[4], refs[5], refs[6:10], refs[10], refs[11]
+    step, last = pl.program_id(0), pl.num_programs(0) - 1
+
+    @pl.when(step == 0)
+    def _():
+        rows = refs[0].shape[0]
+        for place, ref in enumerate(refs[:4]):
+            x_ref[:, place * rows : (place + 1) * rows] = ref[...].T
+
+    @pl.when(step < last)
+    def _():
+        for place in range(out_ref.shape[1] // unit_rows):
+            grad = dot(x_ref[...], unit_grads_ref[place], NN)
+            grad = grad.reshape(-1, unit_rows, BLOCK).astype(LOW)
+            out_ref[:, place * unit_rows : (place + 1) * unit_rows, :] = grad
+
+    @pl.when(step == last)
+    def _():
+        hidden = hidden_ref[...].T
+        for place in range(out_ref.shape[1] // down_rows):
+            lanes = slice(place * BLOCK, (place + 1) * BLOCK)
+            right = jnp.concatenate([ref[:, lanes] for ref in g_refs], axis=0)
+            grad = dot(hidden, right, NN).reshape(-1, down_rows, BLOCK).astype(LOW)
+            out_ref[:, place * down_rows : (place + 1) * down_rows, :] = grad
+
+
+def ffn_weight_grads(rows, unit_grads, hidden, grad_rows, groups, unit_rows, down_rows):
+    tokens, cols_ff = hidden.shape
+    step_rows = D // BLOCK * down_rows
+    per_step = step_rows // unit_rows
+    steps = unit_grads.shape[0] // per_step
+    last = steps - 1
+    result = jax.ShapeDtypeStruct((groups, (steps + 1) * step_rows, BLOCK), LOW)
+    part_spec = pl.BlockSpec(rows[0].shape, lambda i: (0, 0))
+    return pl.pallas_call(
+        functools.partial(ffn_weight_grads_kernel, unit_rows=unit_rows, down_rows=down_rows),
+        grid=(steps + 1,),
+        in_specs=[part_spec] * 4
+        + [
+            pl.BlockSpec((per_step, tokens, BLOCK), lambda i: (jnp.minimum(i, last), 0, 0)),
+            pl.BlockSpec(hidden.shape, lambda i: (0, 0)),
+        ]
+        + [part_spec] * 4,
+        out_specs=pl.BlockSpec((groups, step_rows, BLOCK), lambda i: (0, i, 0)),
+        out_shape=result,
+        scratch_shapes=[pltpu.VMEM((D, tokens), LOW)],
+        cost_estimate=cost(6 * tokens * D * cols_ff, [*rows, unit_grads, hidden, *grad_rows], [result]),
+        compiler_params=pltpu.CompilerParams(vmem_limit_bytes=VMEM_LIMIT),
+        name="ffn_weight_grads",
+    )(*rows, unit_grads, hidden, *grad_rows)
+
+
+def out_grad_kernel(left_ref, right_ref, out_ref, *, rows):
+    for place in range(D // BLOCK):
+        grad = dot(left_ref[...], right_ref[:, place * BLOCK : (place + 1) * BLOCK], NN)
         out_ref[:, place * rows : (place + 1) * rows, :] = grad.reshape(-1, rows, BLOCK).astype(LOW)
 
 
-def weight_grad(buffer, total_rows, left, right, kind, rows, start, per_step):
-    tokens = left.shape[1]
-    groups = left.shape[0] // rows
-    if kind == "blocks":
-        count = right.shape[0]
-        right_spec = pl.BlockSpec((per_step, tokens, BLOCK), lambda i: (i, 0, 0))
-    elif kind == "columns":
-        count = right.shape[1] // BLOCK
-        right_spec = pl.BlockSpec((tokens, per_step * BLOCK), lambda i: (0, i))
-    else:
-        count = right.shape[0] // BLOCK
-        right_spec = pl.BlockSpec((per_step * BLOCK, tokens), lambda i: (i, 0))
-    first = start // (per_step * rows)
-    operands, specs = [left, right], [pl.BlockSpec(left.shape, lambda i: (0, 0)), right_spec]
-    if buffer is not None:
-        operands.append(buffer)
-        specs.append(pl.BlockSpec(memory_space=pl.ANY))
+def out_weight_grad(left, right, rows):
+    result = jax.ShapeDtypeStruct((left.shape[0] // rows, D // BLOCK * rows, BLOCK), LOW)
     return pl.pallas_call(
-        functools.partial(weight_grad_kernel, rows=rows, kind=kind),
-        grid=(count // per_step,),
-        in_specs=specs,
-        out_specs=pl.BlockSpec((groups, per_step * rows, BLOCK), lambda i: (0, first + i, 0)),
-        out_shape=jax.ShapeDtypeStruct((groups, total_rows, BLOCK), LOW),
-        input_output_aliases={} if buffer is None else {2: 0},
-        cost_estimate=cost(2 * left.size * count * BLOCK, [left, left, right], []),
+        functools.partial(out_grad_kernel, rows=rows),
+        in_specs=in_vmem(2),
+        out_specs=in_vmem(1)[0],
+        out_shape=result,
+        cost_estimate=cost(2 * left.size * D, [left, right], [result]),
         compiler_params=pltpu.CompilerParams(vmem_limit_bytes=VMEM_LIMIT),
-        name="weight_grad_" + kind,
-    )(*operands)
+        name="out_weight_grad",
+    )(left, right)
 
 
 def put_qkv(came_ref, place_ref, start, outs, layer, weights, gain_ref, gain_out_ref):
@@ -603,8 +643,11 @@
             lax.ppermute(across_both, BOTH, corner_swap),
         )
 
+    def beside_parts(value):
+        return [value, *neighbours(value, value, value)]
+
     def beside(value):
-        return jnp.concatenate([value, *neighbours(value, value, value)], axis=0)
+        return jnp.concatenate(beside_parts(value), axis=0)
 
     def fold(own, *others):
         return own + sum(part.astype(jnp.float32) for part in neighbours(*others))
@@ -762,7 +805,6 @@
     group_rows = 4 * w_rows
     unit_end = 2 * quarter_ff // BLOCK * group_rows
     ffn_end = unit_end + D // BLOCK * padded
-    out_end = ffn_end + (D // BLOCK * w_rows if split_heads else 0)
 
     def units_parts(layer):
         scale = gain_ffn[layer][:, None]
@@ -928,38 +970,50 @@
         query = rotate(projected[:, :HD], sines) * (1.0 / math.sqrt(HD))
         key = rotate(projected[:, HD : 2 * HD], sines)
         sent = jnp.concatenate([query, key, projected[:, 2 * HD :]], axis=1).astype(LOW)
+        sent, later_weights, cotangent = lax.optimization_barrier((sent, later_weights, cotangent))
         if layer == 0:
-            sent, later_weights = lax.optimization_barrier((sent, later_weights))
-            later_weights, cotangent = lax.optimization_barrier((cross_rows(later_weights), cotangent))
-            last_grad_low = beside(cotangent.astype(LOW))
+            later_weights, cotangent = lax.optimization_barrier(
+                (cross_rows(later_weights), cotangent)
+            )
+            last_grad_parts = beside_parts(cotangent.astype(LOW))
         own = to_heads(sent)
+        if layer == 0:
+            own, last_grad_parts = lax.optimization_barrier((own, last_grad_parts))
         next_part = ffn_part(layer, cut(later_weights)[layer])
-        own, next_part, last_grad_low = lax.optimization_barrier((own, next_part, last_grad_low))
+        own, next_part = lax.optimization_barrier((own, next_part))
         packed = gather(next_part).reshape(2 * planes, -1, BLOCK)
         ffn_weights.append(packed)
         own, out_quarter = lax.optimization_barrier((own, out_quarter))
-        out_parts = [out_quarter, *neighbours(out_quarter, out_quarter, out_quarter)]
+        halves = out_quarter.reshape(2, quarter_width // 2, D)
+        half = jnp.where(here_core == 0, halves[0], halves[1])
+        out_parts = neighbours(half, half, half)
         sib = lax.ppermute(own[:, HD:], "head", CORE_SWAP)
         queries = my_tiles(own)
         q_aug = q_augs[layer]
         out, lse = attention_forward(chip_flips, queries, q_aug, own, sib, k_aug)
         out, *out_parts = lax.optimization_barrier((out, *out_parts))
-        out_matrix = jnp.concatenate(out_parts, axis=0)
+        mine = jnp.stack(out_parts)
+        other = lax.ppermute(mine, "head", CORE_SWAP)
+        pairs = jnp.where(
+            here_core == 0, jnp.stack([mine, other], axis=1), jnp.stack([other, mine], axis=1)
+        )
+        out_matrix = jnp.concatenate([out_quarter, pairs.reshape(3 * quarter_width, D)], axis=0)
         out_weights.append(out_matrix)
         attended = over_spread(over_chips(all_blocks(out))).reshape(QUARTER_HEADS, 4, HD, tok_rows)
         attended = plane_order(attended).reshape(D, tok_rows)
+        attended, out_matrix = lax.optimization_barrier((attended, out_matrix))
         middle = stream + dot(attended, out_matrix, TN)
         scaled_two, inverse_two = normalize(middle)
-        normed_ffn = beside(scaled_two.astype(LOW))
+        normed_parts = beside_parts(scaled_two.astype(LOW))
         if layer < LAYERS - 1:
             next_part = attention_part(layer + 1, cut(later_weights)[LAYERS + layer])
-            normed_ffn, next_part = lax.optimization_barrier((normed_ffn, next_part))
+            normed_parts, next_part = lax.optimization_barrier((normed_parts, next_part))
             attention_weights.append(attention_matrices(next_part))
-        both, hidden, *parts = ffn_forward(normed_ffn, packed, quarter_ff, group_rows, padded)
+        both, hidden, *parts = ffn_forward(normed_parts, packed, quarter_ff, group_rows, padded)
         saved.append(
             (
                 scaled_one, inverse_one, normed, own, sib, queries, q_aug, out, lse, attended,
-                scaled_two, inverse_two, normed_ffn, both, hidden,
+                scaled_two, inverse_two, normed_parts, both, hidden,
             )
         )
         if layer < LAYERS - 1:
@@ -975,18 +1029,21 @@
         out_matrix, packed = out_weights[layer], ffn_weights[layer]
         (
             scaled_one, inverse_one, normed, own, sib, queries, q_aug, out, lse, attended,
-            scaled_two, inverse_two, normed_ffn, both, hidden,
+            scaled_two, inverse_two, normed_parts, both, hidden,
         ) = saved[layer]
-        upstream_low = beside(upstream.astype(LOW)) if layer < LAYERS - 1 else last_grad_low
-        grad_units, *parts = ffn_backward(upstream_low, packed, both, quarter_ff, group_rows, padded)
+        if layer < LAYERS - 1:
+            upstream_parts = beside_parts(upstream.astype(LOW))
+        else:
+            upstream_parts = last_grad_parts
+        grad_units, *parts = ffn_backward(upstream_parts, packed, both, quarter_ff, group_rows, padded)
         inner = fold(*parts)
-        buffer = weight_grad(
-            None, ffn_end, normed_ffn.T, grad_units, "blocks", group_rows, 0, 4 * padded // group_rows
+        buffer = ffn_weight_grads(
+            normed_parts, grad_units, hidden, upstream_parts, 2 * planes, group_rows, padded
         )
         inner, buffer = lax.optimization_barrier((inner, buffer))
-        buffer = weight_grad(
-            buffer, ffn_end, hidden.T, upstream_low, "columns", padded, unit_end, D // BLOCK
-        )
+        if layer < LAYERS - 1:
+            buffer, qkv_sums[layer + 1] = lax.optimization_barrier((buffer, qkv_sums[layer + 1]))
+        ffn_sums[layer] = scatter(buffer)
         grad_middle = upstream + normalize_back(scaled_two, inverse_two, inner)
         middle_low = grad_middle.astype(LOW)
         grad_attended = dot(out_matrix, middle_low, NT).astype(LOW)
@@ -994,12 +1051,7 @@
         if spread > 1:
             grad_attended = jnp.repeat(grad_attended, spread, axis=0)
         out_grad = my_tiles(over_chips(grad_attended))
-        buffer, out_grad, middle_low, attended = lax.optimization_barrier(
-            (buffer, out_grad, middle_low, attended)
-        )
-        if layer < LAYERS - 1:
-            buffer, qkv_sums[layer + 1] = lax.optimization_barrier((buffer, qkv_sums[layer + 1]))
-        ffn_sums[layer] = scatter(buffer)
+        out_grad, middle_low, attended = lax.optimization_barrier((out_grad, middle_low, attended))
         middle_low, attended = share_for_out(middle_low, attended)
         grad_q, grad_kv = attention_backward(
             chip_flips, queries, q_aug, lse, out, out_grad, own, sib, k_aug
@@ -1008,9 +1060,7 @@
         if not split_heads:
             whole_grads[layer] = whole_out_back(dot(attended, middle_low, NN))
         else:
-            out_blocks = weight_grad(
-                None, out_end - ffn_end, attended, middle_low, "columns", w_rows, 0, D // BLOCK
-            )
+            out_blocks = out_weight_grad(attended, middle_low, w_rows)
         same_grad = jnp.sum(grad_q[:, HD : HD + VARIATES] * q_onehots)
         all_grad = jnp.sum(grad_q[:, HD + 16])
         crossed = lax.ppermute(grad_kv[planes:], "head", CORE_SWAP)
@@ -1040,13 +1090,16 @@
             inner = fold_whole(partial)
             inner, qkv_grad = lax.optimization_barrier((inner, qkv_grad))
         qkv_sums[layer] = scatter(qkv_grad)
-        if layer == 0:
-            qkv_sums[0], partial, *bias_parts = lax.optimization_barrier(
-                (qkv_sums[0], partial, *bias_parts)
-            )
-            inner = fold_whole(partial)
-        upstream = grad_middle + normalize_back(scaled_one, inverse_one, inner)
-
+        if layer > 0:
+            upstream = grad_middle + normalize_back(scaled_one, inverse_one, inner)
+
+    later_sums = [from_blocks(member[None, :unit_end], group_rows) for member in ffn_sums]
+    out_sums = [member[:, 3 * quarter_width :] for member in qkv_sums]
+    qkv_sums = [member[:, : 3 * quarter_width] for member in qkv_sums]
+    if not split_heads:
+        out_sums = [member[:, :BLOCK] for member in qkv_sums]
+    later_sums = jnp.concatenate([*later_sums, *qkv_sums[1:]], axis=1)
+    came, *bias_parts = lax.optimization_barrier((cross_back(later_sums), *bias_parts))
     bias_local = lax.dynamic_update_slice(
         jnp.zeros((LAYERS, 2, HEADS), jnp.float32), jnp.stack(bias_parts)[:, :, None], (0, 0, my_head)
     )
@@ -1057,20 +1110,16 @@
             swap = [(place, place ^ hop) for place in range(size)]
             bias_total = bias_total + lax.ppermute(bias_total, axis, swap)
             hop *= 2
-
-    later_sums = [from_blocks(member[None, :unit_end], group_rows) for member in ffn_sums]
-    out_sums = [member[:, 3 * quarter_width :] for member in qkv_sums]
-    qkv_sums = [member[:, : 3 * quarter_width] for member in qkv_sums]
-    if not split_heads:
-        out_sums = [member[:, :BLOCK] for member in qkv_sums]
-    later_sums = jnp.concatenate([*later_sums, *qkv_sums[1:]], axis=1)
     quarters = jnp.arange(QUARTERS, dtype=jnp.int32)
     weights = (w_query, w_key, w_value, w_gate, w_up)
     gains = (gain_attn[:, :, None], gain_ffn[:, :, None])
     *grads, gain_one, gain_two = finish_gradients(
-        quarters ^ (2 * here_y + here_core), cross_back(later_sums), ffn_sums,
+        quarters ^ (2 * here_y + here_core), came, ffn_sums,
         out_sums[1:], weights, gains, w_down.shape, unit_end, planes, split_heads,
     )
+    qkv_sums[0], out_sums[0], partial = lax.optimization_barrier((qkv_sums[0], out_sums[0], partial))
+    inner = fold_whole(partial)
+    upstream = grad_middle + normalize_back(scaled_one, inverse_one, inner)
     *grads[:3], gain_one, grads[3] = finish_first(
         2 * quarters + here_lo, cross_back_at_once(qkv_sums[0]), out_sums[0], weights[:3], gains[0],
         [*grads[:3], gain_one, grads[3]], split_heads,

time: 648 us -> 615 us (0.949)
  waiting for transfers between devices: 223 us -> 175 us
  blocking collectives: 0 us -> 37.6 us
  starting transfers between devices: 133 us -> 117 us
  local copies, waits for them, and re-layouts: 53.3 us -> 44.2 us
    all_to_all x0 -> x2, blocking collectives: none -> 37.6 us  [over_chips(): lax.all_to_all(value, BOTH, split_axis=0, concat_axis=0, tiled=True, axis...]
    all_to_all x2, waiting for transfers between devices: 42.4 us -> 22.5 us  [from_heads(): lax.all_to_all(value, 'seq', split_axis=0, concat_axis=0, tiled=True, axi...]
    ppermute x17, waiting for transfers between devices: 54.3 us -> 34.4 us  [neighbours(): lax.ppermute(across_both, BOTH, corner_swap)]
    ppermute x17, waiting for transfers between devices: 6.92 us -> 22 us  [neighbours(): lax.ppermute(across_y, 'head', Y_SWAP)]
    all_to_all x4 -> x2, starting transfers between devices: 22.9 us -> 10.2 us  [over_chips(): lax.all_to_all(value, BOTH, split_axis=0, concat_axis=0, tiled=True, axis...]
    all_to_all x4 -> x2, waiting for transfers between devices: 32.8 us -> 23.5 us  [over_chips(): lax.all_to_all(value, BOTH, split_axis=0, concat_axis=0, tiled=True, axis...]
    ppermute x17, starting transfers between devices: 11.9 us -> 20.3 us  [neighbours(): lax.ppermute(across_x, 'seq', x_swap)]
    unnamed x157 -> x147, local copies, waits for them, and re-layouts: 17.3 us -> 9.34 us
  transfers between devices with their start and end apart: 86 -> 86, of which waited for: 47 -> 41; matrix products, arithmetic and copies ran while one was open for 14% -> 15% of each run, Pallas kernels for 18% -> 19%
where the time goes in v4:
time: 615 us; the launch traced here: 610 us
  waiting for transfers between devices  175 us (28%)
  Pallas kernels  131 us (21%)
  starting transfers between devices  117 us (19%)
  other arithmetic  63.7 us (10%)
  local copies, waits for them, and re-layouts  44.2 us (7%)
  blocking collectives  37.6 us (6%)
  between operations  24.6 us (4%)
  matrix products  16 us (3%)
    pallas_call x2, Pallas kernels, attention_backward(): pl.pallas_call(backward_kernel, grid_spec=pltpu.PrefetchScalarGridSpec(nu...  45.8 us
    all_to_all x2, blocking collectives, over_chips(): lax.all_to_all(value, BOTH, split_axis=0, concat_axis=0, tiled=True, axis...  37.6 us
    ppermute x17, waiting for transfers between devices, neighbours(): lax.ppermute(across_both, BOTH, corner_swap)  34.4 us
    ppermute x17, waiting for transfers between devices, neighbours(): lax.ppermute(across_x, 'seq', x_swap)  33.5 us
    pallas_call x2, Pallas kernels, attention_forward(): pl.pallas_call(forward_kernel, grid_spec=pltpu.PrefetchScalarGridSpec(num...  29.1 us
    ppermute x17, starting transfers between devices, neighbours(): lax.ppermute(across_both, BOTH, corner_swap)  24.8 us
    all_to_all x2, waiting for transfers between devices, over_chips(): lax.all_to_all(value, BOTH, split_axis=0, concat_axis=0, tiled=True, axis...  23.5 us
    all_to_all x2, waiting for transfers between devices, from_heads(): lax.all_to_all(value, 'seq', split_axis=0, concat_axis=0, tiled=True, axi...  22.5 us
  transfers between devices with their start and end apart: 86, of which 41 were waited for; matrix products, arithmetic and copies ran while one was open for 15% of the time, Pallas kernels for 19%

profile of v4, /device:TPU:0, one launch (start us, length us, event | category | flops | bytes accessed | tf_op | source)
XLA Modules:
  0.0 609.8 jit_solution(5669678299305208864)
XLA Ops:
  13.1 5.2 all-to-all-start
  56.9 6.1 collective-permute-done
  76.2 4.8 all-to-all-start.1
  107.9 14.5 %attention_forward.2 = (bf16[4,4,64,128]{3,2,1,0:T(8,128)(2,1)}, f32[4,8,512]{2,1,0:T(8,128)}) custom-call(s32[1]{0:T(128)} %bitcast.flip_ref, bf16[4,192,512]{2,1,0:T(8,128)(2,1)} %copy-done.20, bf16[4,64,512]{2,1,0:T(8,128)(2,1)} %get-tuple-element.168.q_aug_ref, bf16[4,192,512]{2,1,0:T(8,128)(2,1)} %copy-done.20, bf16[4,128,512]{2,1,0:T(8,128)(2,1)} %copy-done.67, ...), custom_call_target="tpu_custom_call" | custom-call | flops 8589934592 | bytes 2424832 | tf_op jit(solution)/shard_map/attention_forward/pallas_call | solution.py:166
  122.4 5.0 all-to-all-start.2
  129.8 11.9 %all-to-all-done.2 = bf16[16,64,128]{2,1,0:T(8,128)(2,1)S(1)} async-done(((bf16[16,64,128]{2,1,0:T(8,128)(2,1)}), bf16[16,64,128]{2,1,0:T(8,128)(2,1)S(1)}, u32[]{:S(2)}, u32[]{:S(2)}) %all-to-all-start.2) | async-done | bytes 262176 | tf_op jit(solution)/shard_map/all_to_all | solution.py:926
  160.5 7.1 %ffn_forward.2 = (bf16[6,512,256]{2,1,0:T(8,128)(2,1)}, bf16[512,768]{1,0:T(8,128)(2,1)}, f32[128,1024]{1,0:T(8,128)}, bf16[128,1024]{1,0:T(8,128)(2,1)}, bf16[1...) custom-call(bf16[128,1024]{1,0:T(8,128)(2,1)} %copy-done.16, bf16[128,1024]{1,0:T(8,128)(2,1)} %copy-done.26, ...), custom_call_target="tpu_custom_call" | custom-call | flops 2415919104 | bytes 9437184 | tf_op jit(solution)/shard_map/ffn_forward/pallas_call | solution.py:349
  171.1 6.9 %collective-permute-done.23 = bf16[128,1024]{1,0:T(8,128)(2,1)S(1)} collective-permute-done((bf16[128,1024]{1,0:T(8,128)(2,1)}, bf16[128,1024]{1,0:T(8,128)(2,1)S(1)}, u32[]{:S(2)}, u32[]{:S(2)}) %collective-permute-start.23) | collective-permute-done | bytes 262176 | tf_op jit(solution)/shard_map/ppermute | solution.py:643
  209.1 17.6 %all-to-all-done.3.q_ref.own_ref = bf16[4,192,512]{2,1,0:T(8,128)(2,1)} async-done(((bf16[4,192,512]{2,1,0:T(8,128)(2,1)}), bf16[4,192,512]{2,1,0:T(8,128)(2,1)}, u32[]{:S(2)}, u32[]{:S(2)}) %all-to-all-start.3) | async-done | bytes 786464 | tf_op jit(solution)/shard_map/all_to_all | solution.py:895
  233.0 14.6 %attention_forward.3 = (bf16[4,4,64,128]{3,2,1,0:T(8,128)(2,1)}, f32[4,8,512]{2,1,0:T(8,128)}) custom-call(s32[1]{0:T(128)} %bitcast.flip_ref, bf16[4,192,512]{2,1,0:T(8,128)(2,1)} %all-to-all-done.3.q_ref.own_ref, bf16[4,64,512]{2,1,0:T(8,128)(2,1)} %get-tuple-element.192.q_aug_ref, bf16[4,192,512]{2,1,0:T(8,128)(2,1)} %all-to-all-done.3.q_ref.own_ref, ...), custom_call_target="tpu_custom_call" | custom-call | flops 8589934592 | bytes 2424832 | tf_op jit(solution)/shard_map/attention_forward/pallas_call | solution.py:166
  247.6 5.2 all-to-all-start.4
  255.4 11.7 %all-to-all-done.4 = bf16[16,64,128]{2,1,0:T(8,128)(2,1)} async-done(((bf16[16,64,128]{2,1,0:T(8,128)(2,1)}), bf16[16,64,128]{2,1,0:T(8,128)(2,1)}, u32[]{:S(2)}, u32[]{:S(2)}) %all-to-all-start.4) | async-done | bytes 262176 | tf_op jit(solution)/shard_map/all_to_all | solution.py:926
  285.3 7.1 %ffn_forward.3 = (bf16[6,512,256]{2,1,0:T(8,128)(2,1)}, bf16[512,768]{1,0:T(8,128)(2,1)}, f32[128,1024]{1,0:T(8,128)}, bf16[128,1024]{1,0:T(8,128)(2,1)}, bf16[1...) custom-call(bf16[128,1024]{1,0:T(8,128)(2,1)} %copy-done.19, bf16[128,1024]{1,0:T(8,128)(2,1)} %copy-done.28, ...), custom_call_target="tpu_custom_call" | custom-call | flops 2415919104 | bytes 9437184 | tf_op jit(solution)/shard_map/ffn_forward/pallas_call | solution.py:349
  292.4 7.9 %ffn_backward.2 = (bf16[6,512,256]{2,1,0:T(8,128)(2,1)}, f32[128,1024]{1,0:T(8,128)}, bf16[128,1024]{1,0:T(8,128)(2,1)}, bf16[128,1024]{1,0:T(8,128)(2,1)}, bf16[128,1024]{1,0:T(8,128)(2,1)}) custom-call(bf16[128,1024]{1,0:T(8,128)(2,1)} %copy-done.9, bf16[128,1024]{1,0:T(8,128)(2,1)} %collective-permute-done.10.refs_1_.refs_7_, ...), custom_call_target="tpu_custom_call" | custom-call | flops 2415919104 | bytes 10223616 | tf_op jit(solution)/shard_map/ffn_backward/pallas_call | solution.py:378
  303.9 6.7 %ffn_weight_grads.2 = bf16[8,1152,256]{2,1,0:T(8,128)(2,1)} custom-call(bf16[128,1024]{1,0:T(8,128)(2,1)} %copy-done.19, bf16[128,1024]{1,0:T(8,128)(2,1)} %copy-done.28, bf16[128,1024]{1,0:T(8,128)(2,1)} %copy-done.29, bf16[128,1024]{1,0:T(8,128)(2,1)} %collective-permute-done.34.refs_3_, bf16[6,512,256]{2,1,0:T(8,128)(2,1)} %get-tuple-element.213.refs_4_, ...), custom_call_target="tpu_custom_call" | custom-call | flops 2415919104 | bytes 9175040 | tf_op jit(solution)/shard_map/ffn_weight_grads/pallas_call | solution.py:432
  317.3 19.4 %all_to_all.50 = bf16[16,64,128]{2,1,0:T(8,128)(2,1)} all-to-all(bf16[16,64,128]{2,1,0:T(8,128)(2,1)S(1)} %bitcast.345), channel_id=1, replica_groups={{0,2,4,6,8,10,12,14,16,18,20,22,24,26,28,30},{1,3,5,7,9,11,13,15,17,19,..., dimensions={0} | all-to-all | bytes 524288 | tf_op jit(solution)/shard_map/all_to_all | solution.py:926
  340.4 22.9 %attention_backward.2 = (f32[4,128,512]{2,1,0:T(8,128)}, bf16[8,128,512]{2,1,0:T(8,128)(2,1)}) custom-call(s32[1]{0:T(128)} %bitcast.flip_ref, bf16[4,192,512]{2,1,0:T(8,128)(2,1)} %all-to-all-done.3.q_ref.own_ref, bf16[4,64,512]{2,1,0:T(8,128)(2,1)} %get-tuple-element.192.q_aug_ref, f32[4,8,512]{2,1,0:T(8,128)} %get-tuple-element.193.lse_ref, ...), custom_call_target="tpu_custom_call" | custom-call | flops 17179869184 | bytes 4194304 | tf_op jit(solution)/shard_map/attention_backward/pallas_call | solution.py:190
  382.3 4.8 collective-permute-done.43
  418.3 4.8 collective-permute-done.48.refs_1_.refs_7_
  430.5 8.0 %ffn_backward.3 = (bf16[6,512,256]{2,1,0:T(8,128)(2,1)}, f32[128,1024]{1,0:T(8,128)}, bf16[128,1024]{1,0:T(8,128)(2,1)}, bf16[128,1024]{1,0:T(8,128)(2,1)}, bf16[128,1024]{1,0:T(8,128)(2,1)}) custom-call(bf16[128,1024]{1,0:T(8,128)(2,1)} %copy-done.10, bf16[128,1024]{1,0:T(8,128)(2,1)} %copy-done.30, bf16[128,1024]{1,0:T(8,128)(2,1)} %copy-done.31, ...), custom_call_target="tpu_custom_call" | custom-call | flops 2415919104 | bytes 10223616 | tf_op jit(solution)/shard_map/ffn_backward/pallas_call | solution.py:378
  442.0 6.7 %ffn_weight_grads.3 = bf16[8,1152,256]{2,1,0:T(8,128)(2,1)} custom-call(bf16[128,1024]{1,0:T(8,128)(2,1)} %copy-done.16, bf16[128,1024]{1,0:T(8,128)(2,1)} %copy-done.26, bf16[128,1024]{1,0:T(8,128)(2,1)} %copy-done.27, bf16[128,1024]{1,0:T(8,128)(2,1)} %collective-permute-done.20.refs_3_, bf16[6,512,256]{2,1,0:T(8,128)(2,1)} %get-tuple-element.243.refs_4_, ...), custom_call_target="tpu_custom_call" | custom-call | flops 2415919104 | bytes 9175040 | tf_op jit(solution)/shard_map/ffn_weight_grads/pallas_call | solution.py:432
  455.0 18.1 %all_to_all.51 = bf16[16,64,128]{2,1,0:T(8,128)(2,1)} all-to-all(bf16[16,64,128]{2,1,0:T(8,128)(2,1)S(1)} %bitcast.346), channel_id=1, replica_groups={{0,2,4,6,8,10,12,14,16,18,20,22,24,26,28,30},{1,3,5,7,9,11,13,15,17,19,..., dimensions={0} | all-to-all | bytes 524288 | tf_op jit(solution)/shard_map/all_to_all | solution.py:926
  476.8 22.9 %attention_backward.3 = (f32[4,128,512]{2,1,0:T(8,128)}, bf16[8,128,512]{2,1,0:T(8,128)(2,1)}) custom-call(s32[1]{0:T(128)} %bitcast.flip_ref, bf16[4,192,512]{2,1,0:T(8,128)(2,1)} %copy-done.20, bf16[4,64,512]{2,1,0:T(8,128)(2,1)} %get-tuple-element.168.q_aug_ref, f32[4,8,512]{2,1,0:T(8,128)} %get-tuple-element.246.lse_ref, ...), custom_call_target="tpu_custom_call" | custom-call | flops 17179869184 | bytes 4194304 | tf_op jit(solution)/shard_map/attention_backward/pallas_call | solution.py:190
  510.9 18.1 %all-to-all-done.8 = bf16[4,192,512]{2,1,0:T(8,128)(2,1)S(1)} async-done(((bf16[4,192,512]{2,1,0:T(8,128)(2,1)}), bf16[4,192,512]{2,1,0:T(8,128)(2,1)S(1)}, u32[]{:S(2)}, u32[]{:S(2)}) %all-to-all-start.8) | async-done | bytes 786464 | tf_op jit(solution)/shard_map/all_to_all | solution.py:913
  (580 shorter events, 327.3 us)
Async XLA Ops:
  18.3 45.9 %all-gather.5.cloned.1.call-start = ((), (), s32[]{:S(2)}) async-start(), calls=%async_computation.14 | async-start | bytes 2359296 | tf_op jit(solution)/shard_map/all_gather | solution.py:716
  30.7 26.2 %collective-permute-start.2 = (bf16[128,1024]{1,0:T(8,128)(2,1)}, bf16[128,1024]{1,0:T(8,128)(2,1)}, u32[]{:S(2)}, u32[]{:S(2)}) collective-permute-start(bf16[128,1024]{1,0:T(8,128)(2,1)} %multiply_convert_fusion.5), channel_id=1, source_target_pairs={{0,6},{1,7},{2,4},{3,5},{4,2},{5,3},{6,0},{7,1},{8,14},{9,15},{10,... | collective-permute-start | bytes 786440 | tf_op jit(solution)/shard_map/ppermute | solution.py:643
  33.6 23.3 %collective-permute-start.1 = (bf16[128,1024]{1,0:T(8,128)(2,1)}, bf16[128,1024]{1,0:T(8,128)(2,1)}, u32[]{:S(2)}, u32[]{:S(2)}) collective-permute-start(bf16[128,1024]{1,0:T(8,128)(2,1)} %multiply_convert_fusion.5), channel_id=1, source_target_pairs={{0,4},{4,0},{8,12},{12,8},{16,20},{20,16},{24,28},{28,24},{1,5},{5... | collective-permute-start | bytes 786440 | tf_op jit(solution)/shard_map/ppermute | solution.py:642
  34.7 21.1 %collective-permute-start.5 = (f32[128]{0:T(128)}, f32[128]{0:T(128)}, u32[]{:S(2)}, u32[]{:S(2)}) collective-permute-start(f32[128]{0:T(128)} %convert_element_type.262), channel_id=1, source_target_pairs={{0,6},{1,7},{2,4},{3,5},{4,2},{5,3},{6,0},{7,1},{8,14},{9,15},{10,... | collective-permute-start | bytes 1544 | tf_op jit(solution)/shard_map/ppermute | solution.py:643
  36.1 19.7 %collective-permute-start.4 = (f32[128]{0:T(128)}, f32[128]{0:T(128)}, u32[]{:S(2)}, u32[]{:S(2)}) collective-permute-start(f32[128]{0:T(128)} %convert_element_type.262), channel_id=1, source_target_pairs={{0,4},{4,0},{8,12},{12,8},{16,20},{20,16},{24,28},{28,24},{1,5},{5... | collective-permute-start | bytes 1544 | tf_op jit(solution)/shard_map/ppermute | solution.py:642
  36.2 19.7 %collective-permute-start.3 = (f32[128]{0:T(128)}, f32[128]{0:T(128)}, u32[]{:S(2)}, u32[]{:S(2)}) collective-permute-start(f32[128]{0:T(128)} %convert_element_type.262), channel_id=1, source_target_pairs={{0,2},{1,3},{2,0},{3,1},{4,6},{5,7},{6,4},{7,5},{8,10},{9,11},{10,... | collective-permute-start | bytes 1544 | tf_op jit(solution)/shard_map/ppermute | solution.py:641
  76.2 26.3 %all-to-all-start.1 = ((bf16[4,192,512]{2,1,0:T(8,128)(2,1)}), bf16[4,192,512]{2,1,0:T(8,128)(2,1)S(1)}, u32[]{:S(2)}, u32[]{:S(2)}) async-start(bf16[4,192,512]{2,1,0:T(8,128)(2,1)} %pad_maximum_fusion.12), calls=%async_computation.1 | async-start | bytes 1572864 | tf_op jit(solution)/shard_map/all_to_all | solution.py:895
  81.1 79.4 %all-gather.9.cloned.1.call-start = ((), (), s32[]{:S(2)}) async-start(), calls=%async_computation.16 | async-start | bytes 5308416 | tf_op jit(solution)/shard_map/all_gather | solution.py:716
  127.4 62.5 %all-gather.7.cloned.1.call-start = ((), (), s32[]{:S(2)}) async-start(), calls=%async_computation.15 | async-start | bytes 2359296 | tf_op jit(solution)/shard_map/all_gather | solution.py:716
  201.9 24.8 %all-to-all-start.3 = ((bf16[4,192,512]{2,1,0:T(8,128)(2,1)}), bf16[4,192,512]{2,1,0:T(8,128)(2,1)}, u32[]{:S(2)}, u32[]{:S(2)}) async-start(bf16[4,192,512]{2,1,0:T(8,128)(2,1)} %pad_maximum_fusion.14), calls=%async_computation.3 | async-start | bytes 1572864 | tf_op jit(solution)/shard_map/all_to_all | solution.py:895
  206.1 79.2 %all-gather.11.cloned.1.call-start = ((), (), s32[]{:S(2)}) async-start(), calls=%async_computation.17 | async-start | bytes 5308416 | tf_op jit(solution)/shard_map/all_gather | solution.py:716
  247.6 19.4 %all-to-all-start.4 = ((bf16[16,64,128]{2,1,0:T(8,128)(2,1)}), bf16[16,64,128]{2,1,0:T(8,128)(2,1)}, u32[]{:S(2)}, u32[]{:S(2)}) async-start(bf16[16,64,128]{2,1,0:T(8,128)(2,1)} %bitcast.361), calls=%async_computation.4 | async-start | bytes 524288 | tf_op jit(solution)/shard_map/all_to_all | solution.py:926
  252.8 156.9 %reduce-scatter.5.cloned.1.call-start = ((), (), s32[]{:S(2)}) async-start(), calls=%async_computation.18 | async-start | bytes 5308416 | tf_op jit(solution)/shard_map/reduce_scatter | solution.py:728
  336.8 26.5 %collective-permute-start.40 = (bf16[128,1280]{1,0:T(8,128)(2,1)S(1)}, bf16[128,1280]{1,0:T(8,128)(2,1)S(1)}, u32[]{:S(2)}, u32[]{:S(2)}) collective-permute-start(bf16[128,1280]{1,0:T(8,128)(2,1)S(1)} %get-tuple-element.433), channel_id=1, source_target_pairs={{0,6},{1,7},{2,4},{3,5},{4,2},{5,3},{6,0},{7,1},{8,14},{9,15},{10,... | collective-permute-start | bytes 983048 | tf_op jit(solution)/shard_map/ppermute | solution.py:643
  337.2 26.2 %collective-permute-start.39 = (bf16[128,1280]{1,0:T(8,128)(2,1)S(1)}, bf16[128,1280]{1,0:T(8,128)(2,1)S(1)}, u32[]{:S(2)}, u32[]{:S(2)}) collective-permute-start(bf16[128,1280]{1,0:T(8,128)(2,1)S(1)} %get-tuple-element.432), channel_id=1, source_target_pairs={{0,4},{4,0},{8,12},{12,8},{16,20},{20,16},{24,28},{28,24},{1,5},{5... | collective-permute-start | bytes 983048 | tf_op jit(solution)/shard_map/ppermute | solution.py:642
  339.8 23.6 %collective-permute-start.38 = (bf16[128,1280]{1,0:T(8,128)(2,1)S(1)}, bf16[128,1280]{1,0:T(8,128)(2,1)S(1)}, u32[]{:S(2)}, u32[]{:S(2)}) collective-permute-start(bf16[128,1280]{1,0:T(8,128)(2,1)S(1)} %get-tuple-element.431), channel_id=1, source_target_pairs={{0,2},{1,3},{2,0},{3,1},{4,6},{5,7},{6,4},{7,5},{8,10},{9,11},{10,... | collective-permute-start | bytes 983048 | tf_op jit(solution)/shard_map/ppermute | solution.py:641
  368.4 24.2 %all-to-all-start.6 = ((bf16[4,192,512]{2,1,0:T(8,128)(2,1)}), bf16[4,192,512]{2,1,0:T(8,128)(2,1)S(1)}, u32[]{:S(2)}, u32[]{:S(2)}) async-start(bf16[4,192,512]{2,1,0:T(8,128)(2,1)} %pad_maximum_fusion.16), calls=%async_computation.6 | async-start | bytes 1572864 | tf_op jit(solution)/shard_map/all_to_all | solution.py:913
  371.9 80.7 %reduce-scatter.7.cloned.1.call-start = ((), (), s32[]{:S(2)}) async-start(), calls=%async_computation.19 | async-start | bytes 2359296 | tf_op jit(solution)/shard_map/reduce_scatter | solution.py:728
  412.8 118.6 %reduce-scatter.9.cloned.1.call-start = ((), (), s32[]{:S(2)}) async-start(), calls=%async_computation.20 | async-start | bytes 5308416 | tf_op jit(solution)/shard_map/reduce_scatter | solution.py:728
  473.2 26.5 %collective-permute-start.56 = (bf16[128,1280]{1,0:T(8,128)(2,1)S(1)}, bf16[128,1280]{1,0:T(8,128)(2,1)S(1)}, u32[]{:S(2)}, u32[]{:S(2)}) collective-permute-start(bf16[128,1280]{1,0:T(8,128)(2,1)S(1)} %get-tuple-element.420), channel_id=1, source_target_pairs={{0,6},{1,7},{2,4},{3,5},{4,2},{5,3},{6,0},{7,1},{8,14},{9,15},{10,... | collective-permute-start | bytes 983048 | tf_op jit(solution)/shard_map/ppermute | solution.py:643
  473.8 26.0 %collective-permute-start.55 = (bf16[128,1280]{1,0:T(8,128)(2,1)S(1)}, bf16[128,1280]{1,0:T(8,128)(2,1)S(1)}, u32[]{:S(2)}, u32[]{:S(2)}) collective-permute-start(bf16[128,1280]{1,0:T(8,128)(2,1)S(1)} %get-tuple-element.419), channel_id=1, source_target_pairs={{0,4},{4,0},{8,12},{12,8},{16,20},{20,16},{24,28},{28,24},{1,5},{5... | collective-permute-start | bytes 983048 | tf_op jit(solution)/shard_map/ppermute | solution.py:642
  476.2 23.6 %collective-permute-start.54 = (bf16[128,1280]{1,0:T(8,128)(2,1)S(1)}, bf16[128,1280]{1,0:T(8,128)(2,1)S(1)}, u32[]{:S(2)}, u32[]{:S(2)}) collective-permute-start(bf16[128,1280]{1,0:T(8,128)(2,1)S(1)} %get-tuple-element.418), channel_id=1, source_target_pairs={{0,2},{1,3},{2,0},{3,1},{4,6},{5,7},{6,4},{7,5},{8,10},{9,11},{10,... | collective-permute-start | bytes 983048 | tf_op jit(solution)/shard_map/ppermute | solution.py:641
  504.8 24.2 %all-to-all-start.8 = ((bf16[4,192,512]{2,1,0:T(8,128)(2,1)}), bf16[4,192,512]{2,1,0:T(8,128)(2,1)S(1)}, u32[]{:S(2)}, u32[]{:S(2)}) async-start(bf16[4,192,512]{2,1,0:T(8,128)(2,1)} %pad_maximum_fusion.17), calls=%async_computation.9 | async-start | bytes 1572864 | tf_op jit(solution)/shard_map/all_to_all | solution.py:913
  508.3 68.9 %reduce-scatter.11.cloned.1.call-start = ((), (), s32[]{:S(2)}) async-start(), calls=%async_computation.21 | async-start | bytes 2359296 | tf_op jit(solution)/shard_map/reduce_scatter | solution.py:728
  (138 other events, 1264.1 us)
Sparse Core Ops, SparseCore 0:
  28.1 30.7 all-gather.4
  102.7 56.5 all-gather.8
  160.9 28.9 all-gather.6
  226.8 56.7 all-gather.10
  314.2 58.9 reduce-scatter.4
  412.9 33.8 reduce-scatter.6
  452.7 57.1 reduce-scatter.8
  533.2 33.7 reduce-scatter.10

commit v5 on v4

--- a/solution.py
+++ b/solution.py
@@ -30,6 +30,10 @@
 TN = (((0,), (0,)), ((), ()))
 TT = (((0,), (1,)), ((), ()))
 VMEM_LIMIT = 56 * 1024 * 1024
+
+
+def in_vmem(count):
+    return [pl.BlockSpec(memory_space=pltpu.VMEM)] * count
 
 
 def cost(flops, operands, results, transcendentals=0):
@@ -466,6 +470,94 @@
     )(left, right)
 
 
+def take_qkv(room_ref, layer, quarter, weights, gain_ref):
+    for slot in range(QUARTER_HEADS):
+        column = HD * (QUARTERS * slot + quarter)
+        for which, weight_ref in enumerate(weights):
+            first = (3 * slot + which) * HD
+            part = weight_ref[layer, :, column : column + HD] * gain_ref[layer]
+            room_ref[:, first : first + HD] = part
+
+
+def first_parts_kernel(lo_ref, *refs):
+    weights, gain_ref, out_ref, room_ref = refs[:3], refs[3], refs[4], refs[5]
+    for quarter in range(QUARTERS):
+        take_qkv(room_ref, 0, quarter, weights, gain_ref)
+        out_ref[2 * quarter + lo_ref[0]] = room_ref[...].astype(LOW)
+        out_ref[2 * quarter + 1 - lo_ref[0]] = jnp.zeros(room_ref.shape, LOW)
+
+
+def first_parts(lo, weights, gain):
+    w_rows, width = weights[0].shape[1], 3 * QUARTER_HEADS * HD
+    return pl.pallas_call(
+        first_parts_kernel,
+        in_specs=[pl.BlockSpec(memory_space=pltpu.SMEM)] + in_vmem(4),
+        out_specs=in_vmem(1)[0],
+        out_shape=jax.ShapeDtypeStruct((2 * QUARTERS, w_rows, width), LOW),
+        scratch_shapes=[pltpu.VMEM((w_rows, width), jnp.float32)],
+        compiler_params=pltpu.CompilerParams(vmem_limit_bytes=VMEM_LIMIT),
+        name="first_parts",
+    )(lo, *weights, gain)
+
+
+def unit_places(d_rows, padded, planes):
+    width = 2 * planes // 2 * padded
+    column = lax.broadcasted_iota(jnp.int32, (1, QUARTERS * width), 1)
+    quarter, rest = column // width, column % width
+    group, unit = rest // padded, rest % padded
+    source = d_rows * (8 * (group // 2) + 2 * quarter + group % 2) + unit
+    source = jnp.where(unit < d_rows, source, -1)
+    rows = lax.broadcasted_iota(jnp.int32, (4 * planes * d_rows, 1), 0)
+    return jnp.where(rows == source, 1.0, 0.0).astype(LOW)
+
+
+def later_parts_kernel(place_ref, *refs, d_rows, padded, planes):
+    weights, gains = refs[:5], refs[5:7]
+    outs, rows_ref, qkv_ref, all_ref = refs[7:11], refs[11], refs[12], refs[13]
+    half, cols_ff = BLOCK // 2, 2 * planes * padded
+    w_rows, width = weights[0].shape[1], cols_ff // 2
+    taken = 4 * planes * d_rows
+    pieces = [(layer, which, part) for layer in range(LAYERS) for which in range(2) for part in range(2)]
+    for number, (layer, which, part) in enumerate(pieces):
+        rows = weights[3 + which][layer, :, part * taken : (part + 1) * taken] * gains[1][layer]
+        rows_ref[number * w_rows : (number + 1) * w_rows, :] = rows
+    placed = dot(rows_ref[...].astype(LOW), unit_places(d_rows, padded, planes), NN)
+    for number, (layer, which, part) in enumerate(pieces):
+        rows = placed[number * w_rows : (number + 1) * w_rows].astype(LOW)
+        for quarter in range(QUARTERS):
+            for block in range(width // half):
+                first = layer * 2 * cols_ff + (part * (width // half) + block) * BLOCK + which * half
+                lane = quarter * width + block * half
+                all_ref[quarter, :, first : first + half] = rows[:, lane : lane + half]
+    for quarter in range(QUARTERS):
+        for layer in range(1, LAYERS):
+            take_qkv(qkv_ref, layer, quarter, weights[:3], gains[0])
+            first = LAYERS * 2 * cols_ff + (layer - 1) * qkv_ref.shape[1]
+            all_ref[quarter, :, first : first + qkv_ref.shape[1]] = qkv_ref[...].astype(LOW)
+    for place, out_ref in enumerate(outs):
+        out_ref[...] = all_ref[place ^ place_ref[0]]
+
+
+def later_parts(place, weights, gains, d_rows, planes):
+    w_rows = weights[0].shape[1]
+    padded = -(-d_rows // 16) * 16
+    cols_ff, width = 2 * planes * padded, 3 * QUARTER_HEADS * HD
+    whole = LAYERS * 2 * cols_ff + (LAYERS - 1) * width
+    return pl.pallas_call(
+        functools.partial(later_parts_kernel, d_rows=d_rows, padded=padded, planes=planes),
+        in_specs=[pl.BlockSpec(memory_space=pltpu.SMEM)] + in_vmem(7),
+        out_specs=in_vmem(4),
+        out_shape=[jax.ShapeDtypeStruct((w_rows, whole), LOW)] * QUARTERS,
+        scratch_shapes=[
+            pltpu.VMEM((4 * LAYERS * w_rows, 4 * planes * d_rows), jnp.float32),
+            pltpu.VMEM((w_rows, width), jnp.float32),
+            pltpu.VMEM((QUARTERS, w_rows, whole), LOW),
+        ],
+        compiler_params=pltpu.CompilerParams(vmem_limit_bytes=VMEM_LIMIT),
+        name="later_parts",
+    )(place, *weights, *gains)
+
+
 def put_qkv(came_ref, place_ref, start, outs, layer, weights, gain_ref, gain_out_ref):
     for quarter in range(QUARTERS):
         part = came_ref[place_ref[quarter], :, start : start + 3 * QUARTER_HEADS * HD]
@@ -480,7 +572,7 @@
         grad = out_ref[layer]
         gain_grad = gain_grad + jnp.sum(grad * weight_ref[layer], axis=1, keepdims=True)
         out_ref[layer] = grad * gain_ref[layer]
-    gain_out_ref[layer] = jnp.broadcast_to(gain_grad, gain_out_ref.shape[1:])
+    gain_out_ref[layer : layer + 1, :] = jnp.broadcast_to(gain_grad, (gain_grad.shape[0], 128)).T[:1]
 
 
 def put_units(came_ref, place_ref, start, outs, layer, weights, gain_ref, gain_out_ref, d_rows, padded, planes):
@@ -505,7 +597,7 @@
         grad = out_ref[layer]
         gain_grad = gain_grad + jnp.sum(grad * weight_ref[layer], axis=1, keepdims=True)
         out_ref[layer] = grad * gain_ref[layer]
-    gain_out_ref[layer] = jnp.broadcast_to(gain_grad, gain_out_ref.shape[1:])
+    gain_out_ref[layer : layer + 1, :] = jnp.broadcast_to(gain_grad, (gain_grad.shape[0], 128)).T[:1]
 
 
 def finish_kernel(place_ref, *refs, unit_end, w_rows, d_rows, padded, planes, with_out):
@@ -534,16 +626,12 @@
     weights, gain_ref, have, outs = refs[:3], refs[3], refs[4:9], refs[9:]
     for layer in range(1, LAYERS):
         for have_ref, out_ref in zip(have, outs):
-            out_ref[layer] = have_ref[layer]
+            out_ref[layer : layer + 1] = have_ref[layer : layer + 1]
     put_qkv(came_ref, place_ref, 0, outs[:3], 0, weights, gain_ref, outs[3])
     if with_out:
         for block in range(D // BLOCK):
             rows = out_sum_ref[block * w_rows : (block + 1) * w_rows, :]
             outs[4][0, :, block * BLOCK : (block + 1) * BLOCK] = rows.astype(jnp.float32)
-
-
-def in_vmem(count):
-    return [pl.BlockSpec(memory_space=pltpu.VMEM)] * count
 
 
 def finish_gradients(
@@ -552,7 +640,7 @@
     layers, w_rows, unused = weights[0].shape
     d_rows = d_shape[1]
     padded = -(-d_rows // 16) * 16
-    shapes = [weights[0].shape] * 4 + [weights[3].shape] * 2 + [d_shape] + [(layers, w_rows, 128)] * 2
+    shapes = [weights[0].shape] * 4 + [weights[3].shape] * 2 + [d_shape] + [(layers, w_rows)] * 2
     return pl.pallas_call(
         functools.partial(
             finish_kernel, unit_end=unit_end, w_rows=w_rows, d_rows=d_rows, padded=padded, planes=planes,
@@ -652,9 +740,9 @@
     def fold(own, *others):
         return own + sum(part.astype(jnp.float32) for part in neighbours(*others))
 
-    def fold_whole(partial):
+    def four_parts(partial):
         low = partial[tok_rows:].astype(LOW).reshape(3, tok_rows, -1)
-        return fold(partial[:tok_rows], low[0], low[1], low[2])
+        return partial[:tok_rows], low[0], low[1], low[2]
 
     def flip(pair, bit):
         return jnp.where(bit == 0, pair[0], pair[1]), jnp.where(bit == 0, pair[1], pair[0])
@@ -665,7 +753,6 @@
         return [list(first), list(second)]
 
     def cross_rows(parts):
-        grid = xor_order([[parts[0], parts[1]], [parts[2], parts[3]]], here_y, here_core)
         came = [[None, None], [None, None]]
         for high in range(2):
             for low in range(2):
@@ -673,7 +760,7 @@
                     (place_of(plane, lo, y, core), place_of(plane, y ^ high, core ^ low, lo))
                     for plane, lo, y, core in devices
                 ]
-                came[high][low] = lax.ppermute(grid[high][low], BOTH, hops)
+                came[high][low] = lax.ppermute(parts[2 * high + low], BOTH, hops)
         came = xor_order(came, here_lo, here_y)
         return jnp.concatenate([*came[0], *came[1]], axis=0)
 
@@ -697,14 +784,10 @@
             value, BOTH, split_axis=0, concat_axis=0, tiled=True, axis_index_groups=device_groups
         )
 
-    def cross_rows_at_once(parts):
-        zeros = jnp.zeros_like(parts)
-        sent = jnp.stack(
-            [jnp.where(here_lo == core, parts, zeros) for core in range(2)], axis=1
-        )
-        came = plane_exchange(sent.reshape(8, *parts.shape[1:]))
+    def cross_rows_at_once(sent):
+        came = plane_exchange(sent)
         came = jnp.where(here_core == 0, came[:4], came[4:])
-        return came.reshape(-1, parts.shape[-1])
+        return came.reshape(-1, sent.shape[-1])
 
     def cross_back_at_once(rows):
         parts = rows.reshape(4, w_rows, -1)
@@ -734,33 +817,6 @@
         )
         return part
 
-    def split_qkv(query, key, value):
-        stacked = jnp.stack([query, key, value], axis=0)
-        stacked = stacked.reshape(3, w_rows, QUARTER_HEADS, QUARTERS, HD)
-        return stacked.transpose(3, 1, 2, 0, 4).reshape(QUARTERS, w_rows, 3 * quarter_width)
-
-    def join_qkv(parts):
-        parts = parts.reshape(QUARTERS, w_rows, QUARTER_HEADS, 3, HD)
-        return parts.transpose(3, 1, 2, 0, 4).reshape(3, w_rows, D)
-
-    def split_units(gate, upward):
-        def quarters(matrix):
-            parts = matrix.reshape(w_rows, planes, QUARTERS, 2, d_rows).transpose(2, 0, 1, 3, 4)
-            parts = jnp.pad(parts, ((0, 0),) * 4 + ((0, padded - d_rows),))
-            return parts.reshape(QUARTERS, w_rows, -1, 1, BLOCK // 2)
-
-        both = jnp.concatenate([quarters(gate), quarters(upward)], axis=3)
-        return both.reshape(QUARTERS, w_rows, 2 * quarter_ff)
-
-    def join_units(parts):
-        parts = parts.reshape(QUARTERS, w_rows, -1, 2, BLOCK // 2)
-
-        def joined(part):
-            part = part.reshape(QUARTERS, w_rows, planes, 2, padded)[..., :d_rows]
-            return part.transpose(1, 2, 0, 3, 4).reshape(w_rows, 4 * seq * d_rows)
-
-        return joined(parts[:, :, :, 0]), joined(parts[:, :, :, 1])
-
     def whole_out_back(grad):
         spaced = lax.dynamic_update_slice_in_dim(
             jnp.zeros((QUARTER_HEADS, QUARTERS, HD, D), LOW),
@@ -777,12 +833,6 @@
     def normalize_back(scaled, inverse, inner):
         return inverse * (inner - scaled * jnp.mean(inner * scaled, axis=-1, keepdims=True))
 
-    def scaled_qkv(layer):
-        scale = gain_attn[layer][:, None]
-        return split_qkv(
-            *((member[layer] * scale).astype(LOW) for member in (w_query, w_key, w_value))
-        )
-
     def attention_part(layer, qkv_rows):
         blocks = blocks_of(w_out[layer].astype(LOW))
         return jnp.concatenate([qkv_rows, blocks], axis=1)
@@ -792,12 +842,12 @@
         blocks = whole[:, 3 * quarter_width :].reshape(2 * planes, -1, BLOCK)
         return whole[:, : 3 * quarter_width], from_blocks(blocks, w_rows)
 
-    first_part = attention_part(0, cross_rows_at_once(scaled_qkv(0)))
-    first_part, tokens, cotangent, time_ids, w_query, w_key, w_value, w_gate, w_up = (
-        lax.optimization_barrier(
-            (first_part, tokens, cotangent, time_ids, w_query, w_key, w_value, w_gate, w_up)
-        )
-    )
+    gains = (gain_attn[:, :, None], gain_ffn[:, :, None])
+    first_sent = first_parts(
+        jnp.reshape(here_lo, (1,)).astype(jnp.int32), (w_query, w_key, w_value), gains[0]
+    )
+    first_part = attention_part(0, cross_rows_at_once(first_sent))
+    first_part, time_ids, w_gate, w_up = lax.optimization_barrier((first_part, time_ids, w_gate, w_up))
     attention_weights, out_weights = [attention_matrices(first_part)], []
     start_scaled, start_inverse = normalize(tokens)
     start_normed = beside(start_scaled.astype(LOW))
@@ -806,18 +856,15 @@
     unit_end = 2 * quarter_ff // BLOCK * group_rows
     ffn_end = unit_end + D // BLOCK * padded
 
-    def units_parts(layer):
-        scale = gain_ffn[layer][:, None]
-        return split_units((w_gate[layer] * scale).astype(LOW), (w_up[layer] * scale).astype(LOW))
-
     def ffn_part(layer, units_rows):
         down_part = jnp.pad(w_down[layer].astype(LOW), ((0, padded - d_rows), (0, 0)))
         return jnp.concatenate([blocks_of(units_rows), blocks_of(down_part)], axis=0)
 
-    later_weights = [units_parts(layer) for layer in range(LAYERS)]
-    later_weights += [scaled_qkv(layer) for layer in range(1, LAYERS)]
-    later_widths = [member.shape[-1] for member in later_weights]
-    later_weights = jnp.concatenate(later_weights, axis=-1)
+    later_sent = later_parts(
+        jnp.reshape(2 * here_y + here_core, (1,)).astype(jnp.int32),
+        (w_query, w_key, w_value, w_gate, w_up), gains, d_rows, planes,
+    )
+    later_widths = [2 * quarter_ff] * LAYERS + [3 * quarter_width] * (LAYERS - 1)
 
     def cut(whole):
         parts, start = [], 0
@@ -879,8 +926,8 @@
     times = beside(time_ids.astype(jnp.float32))
     angles = frequency[:, None] * times[None, :]
     cosines, sines = jnp.cos(angles), jnp.sin(angles)
-    start_normed, later_weights, k_aug, cosines, sines, *q_augs = lax.optimization_barrier(
-        (start_normed, later_weights, k_aug, cosines, sines, *q_augs)
+    start_normed, later_sent, k_aug, cosines, sines, *q_augs = lax.optimization_barrier(
+        (start_normed, later_sent, k_aug, cosines, sines, *q_augs)
     )
 
     def rotate(values, sines):
@@ -938,6 +985,15 @@
     def chip_order(value):
         grid = xor_order([[value[0], value[1]], [value[2], value[3]]], here_lo, here_y)
         return jnp.stack([*grid[0], *grid[1]], axis=1)
+
+    def sum_everywhere(value):
+        for axis, size in (("head", 4), ("seq", seq)):
+            hop = 1
+            while hop < size:
+                swap = [(place, place ^ hop) for place in range(size)]
+                value = value + lax.ppermute(value, axis, swap)
+                hop *= 2
+        return value
 
     def share_for_out(middle_low, attended):
         pieces = attended.reshape(4, quarter_width, tok_rows)
@@ -970,11 +1026,9 @@
         query = rotate(projected[:, :HD], sines) * (1.0 / math.sqrt(HD))
         key = rotate(projected[:, HD : 2 * HD], sines)
         sent = jnp.concatenate([query, key, projected[:, 2 * HD :]], axis=1).astype(LOW)
-        sent, later_weights, cotangent = lax.optimization_barrier((sent, later_weights, cotangent))
         if layer == 0:
-            later_weights, cotangent = lax.optimization_barrier(
-                (cross_rows(later_weights), cotangent)
-            )
+            later_weights = cross_rows(later_sent)
+            sent, cotangent = lax.optimization_barrier((sent, cotangent))
             last_grad_parts = beside_parts(cotangent.astype(LOW))
         own = to_heads(sent)
         if layer == 0:
@@ -1070,8 +1124,16 @@
             grad_kv, *last_parts = lax.optimization_barrier((grad_kv, *last_parts))
             stream = last_middle + fold(*last_parts)
         grad_heads = from_heads(jnp.concatenate([all_blocks(grad_q), grad_kv], axis=1))
+        bias_parts[layer] = jnp.stack([same_grad, all_grad - same_grad])
         if layer == LAYERS - 1:
-            grad_heads, stream = lax.optimization_barrier((grad_heads, stream))
+            grad_heads, stream, bias_parts[layer] = lax.optimization_barrier(
+                (grad_heads, stream, bias_parts[layer])
+            )
+        if layer == 0:
+            later_sums = [from_blocks(member[None, :unit_end], group_rows) for member in ffn_sums]
+            later_sums += [member[:, : 3 * quarter_width] for member in qkv_sums[1:]]
+            came = cross_back(jnp.concatenate(later_sums, axis=1))
+            grad_heads, came = lax.optimization_barrier((grad_heads, came))
         grad_heads = jnp.concatenate(
             [
                 rotate(grad_heads[:, :HD].astype(jnp.float32), -sines).astype(LOW),
@@ -1080,15 +1142,14 @@
             ],
             axis=1,
         ).reshape(3 * quarter_width, cols)
-        bias_parts[layer] = jnp.stack([same_grad, all_grad - same_grad])
         partial = dot(grad_heads, qkv_matrix, TT)
         qkv_grad = dot(normed, grad_heads, TT).astype(LOW)
-        qkv_grad, ffn_sums[layer] = lax.optimization_barrier((qkv_grad, ffn_sums[layer]))
         if split_heads:
             qkv_grad = jnp.concatenate([qkv_grad, out_blocks.reshape(-1, BLOCK)], axis=1)
         if layer > 0:
-            inner = fold_whole(partial)
+            inner = fold(*four_parts(partial))
             inner, qkv_grad = lax.optimization_barrier((inner, qkv_grad))
+        qkv_grad, ffn_sums[layer] = lax.optimization_barrier((qkv_grad, ffn_sums[layer]))
         qkv_sums[layer] = scatter(qkv_grad)
         if layer > 0:
             upstream = grad_middle + normalize_back(scaled_one, inverse_one, inner)
@@ -1098,27 +1159,20 @@
     qkv_sums = [member[:, : 3 * quarter_width] for member in qkv_sums]
     if not split_heads:
         out_sums = [member[:, :BLOCK] for member in qkv_sums]
-    later_sums = jnp.concatenate([*later_sums, *qkv_sums[1:]], axis=1)
-    came, *bias_parts = lax.optimization_barrier((cross_back(later_sums), *bias_parts))
     bias_local = lax.dynamic_update_slice(
         jnp.zeros((LAYERS, 2, HEADS), jnp.float32), jnp.stack(bias_parts)[:, :, None], (0, 0, my_head)
     )
-    bias_total = bias_local
-    for axis, size in (("head", 4), ("seq", seq)):
-        hop = 1
-        while hop < size:
-            swap = [(place, place ^ hop) for place in range(size)]
-            bias_total = bias_total + lax.ppermute(bias_total, axis, swap)
-            hop *= 2
+    bias_total = sum_everywhere(bias_local)
     quarters = jnp.arange(QUARTERS, dtype=jnp.int32)
     weights = (w_query, w_key, w_value, w_gate, w_up)
-    gains = (gain_attn[:, :, None], gain_ffn[:, :, None])
     *grads, gain_one, gain_two = finish_gradients(
         quarters ^ (2 * here_y + here_core), came, ffn_sums,
         out_sums[1:], weights, gains, w_down.shape, unit_end, planes, split_heads,
     )
-    qkv_sums[0], out_sums[0], partial = lax.optimization_barrier((qkv_sums[0], out_sums[0], partial))
-    inner = fold_whole(partial)
+    qkv_sums[0], out_sums[0], gain_two, parts, grads = lax.optimization_barrier(
+        (qkv_sums[0], out_sums[0], gain_two, four_parts(partial), grads)
+    )
+    inner = fold(*parts)
     upstream = grad_middle + normalize_back(scaled_one, inverse_one, inner)
     *grads[:3], gain_one, grads[3] = finish_first(
         2 * quarters + here_lo, cross_back_at_once(qkv_sums[0]), out_sums[0], weights[:3], gains[0],
@@ -1126,7 +1180,7 @@
     )
     if not split_heads:
         grads[3] = jnp.stack(whole_grads).astype(jnp.float32)
-    return (stream, upstream, *grads, gain_one[:, :, 0], gain_two[:, :, 0], bias_total)
+    return (stream, upstream, *grads, gain_one, gain_two, bias_total)
 
 
 def solution(mesh):

time: 615 us -> 593 us (0.964)
  waiting for transfers between devices: 175 us -> 161 us
  local copies, waits for them, and re-layouts: 44.2 us -> 33.1 us
  other arithmetic: 63.7 us -> 54.7 us
  Pallas kernels: 131 us -> 139 us
    all_to_all x2, waiting for transfers between devices: 22.5 us -> 5.34 us  [from_heads(): lax.all_to_all(value, 'seq', split_axis=0, concat_axis=0, tiled=True, axi...]
    pallas_call x0 -> x2, Pallas kernels: none -> 7.9 us  [the longest x1 4.64 us: later_parts(): pl.pallas_call(functools.partial(later_parts_kernel, d_rows=d_rows, padde...]
    ppermute x17, waiting for transfers between devices: 22 us -> 14.8 us  [neighbours(): lax.ppermute(across_y, 'head', Y_SWAP)]
    squeeze x4 -> x0, local copies, waits for them, and re-layouts: 6.7 us -> none  [the longest x2 3.35 us: units_parts(): w_up[layer] * scale]
    all_to_all x2, waiting for transfers between devices: 0.01 us -> 6.54 us  [plane_exchange(): lax.all_to_all(value, BOTH, split_axis=0, concat_axis=0, tiled=True, axis...]
  transfers between devices with their start and end apart: 86 -> 86, of which waited for: 41 -> 48; matrix products, arithmetic and copies ran while one was open for 15% -> 14% of each run, Pallas kernels for 19% -> 20%
where the time goes in v5:
time: 593 us; the launch traced here: 582 us
  waiting for transfers between devices  161 us (27%)
  Pallas kernels  139 us (23%)
  starting transfers between devices  116 us (20%)
  other arithmetic  54.7 us (9%)
  blocking collectives  37.9 us (6%)
  local copies, waits for them, and re-layouts  33.1 us (6%)
  between operations  24.4 us (4%)
  matrix products  15.3 us (3%)
    pallas_call x2, Pallas kernels, attention_backward(): pl.pallas_call(backward_kernel, grid_spec=pltpu.PrefetchScalarGridSpec(nu...  45.9 us
    all_to_all x2, blocking collectives, over_chips(): lax.all_to_all(value, BOTH, split_axis=0, concat_axis=0, tiled=True, axis...  37.9 us
    ppermute x17, waiting for transfers between devices, neighbours(): lax.ppermute(across_x, 'seq', x_swap)  33.6 us
    pallas_call x2, Pallas kernels, attention_forward(): pl.pallas_call(forward_kernel, grid_spec=pltpu.PrefetchScalarGridSpec(num...  29.1 us
    ppermute x17, waiting for transfers between devices, neighbours(): lax.ppermute(across_both, BOTH, corner_swap)  28.7 us
    ppermute x17, starting transfers between devices, neighbours(): lax.ppermute(across_both, BOTH, corner_swap)  24 us
    all_to_all x2, waiting for transfers between devices, over_chips(): lax.all_to_all(value, BOTH, split_axis=0, concat_axis=0, tiled=True, axis...  23.8 us
    ppermute x17, starting transfers between devices, neighbours(): lax.ppermute(across_x, 'seq', x_swap)  20.6 us
  transfers between devices with their start and end apart: 86, of which 48 were waited for; matrix products, arithmetic and copies ran while one was open for 14% of the time, Pallas kernels for 20%

profile of v5, /device:TPU:0, one launch (start us, length us, event | category | flops | bytes accessed | tf_op | source)
XLA Modules:
  0.0 581.7 jit_solution(15064739081636555279)
XLA Ops:
  11.9 5.3 all-to-all-start
  18.2 6.5 %all-to-all-done = bf16[8,32,768]{2,1,0:T(8,128)(2,1)S(1)} async-done(((bf16[8,32,768]{2,1,0:T(8,128)(2,1)}), bf16[8,32,768]{2,1,0:T(8,128)(2,1)S(1)}, u32[]{:S(2)}, u32[]{:S(2)}) %all-to-all-start) | async-done | bytes 393248 | tf_op jit(solution)/shard_map/all_to_all | solution.py:783
  43.8 4.6 later_parts.1
  60.5 5.0 all-to-all-start.1
  90.3 14.5 %attention_forward.2 = (bf16[4,4,64,128]{3,2,1,0:T(8,128)(2,1)}, f32[4,8,512]{2,1,0:T(8,128)}) custom-call(s32[1]{0:T(128)} %bitcast.flip_ref, bf16[4,192,512]{2,1,0:T(8,128)(2,1)} %copy-done.17, bf16[4,64,512]{2,1,0:T(8,128)(2,1)} %get-tuple-element.174.q_aug_ref, bf16[4,192,512]{2,1,0:T(8,128)(2,1)} %copy-done.17, bf16[4,128,512]{2,1,0:T(8,128)(2,1)} %copy-done.68, ...), custom_call_target="tpu_custom_call" | custom-call | flops 8589934592 | bytes 2424832 | tf_op jit(solution)/shard_map/attention_forward/pallas_call | solution.py:170
  111.2 12.1 %all-to-all-done.2 = bf16[16,64,128]{2,1,0:T(8,128)(2,1)S(1)} async-done(((bf16[16,64,128]{2,1,0:T(8,128)(2,1)}), bf16[16,64,128]{2,1,0:T(8,128)(2,1)S(1)}, u32[]{:S(2)}, u32[]{:S(2)}) %all-to-all-start.2) | async-done | bytes 262176 | tf_op jit(solution)/shard_map/all_to_all | solution.py:973
  142.8 7.1 %ffn_forward.2 = (bf16[6,512,256]{2,1,0:T(8,128)(2,1)}, bf16[512,768]{1,0:T(8,128)(2,1)}, f32[128,1024]{1,0:T(8,128)}, bf16[128,1024]{1,0:T(8,128)(2,1)}, bf16[1...) custom-call(bf16[128,1024]{1,0:T(8,128)(2,1)} %copy-done.13, bf16[128,1024]{1,0:T(8,128)(2,1)} %copy-done.26, ...), custom_call_target="tpu_custom_call" | custom-call | flops 2415919104 | bytes 9437184 | tf_op jit(solution)/shard_map/ffn_forward/pallas_call | solution.py:353
  153.3 6.9 %collective-permute-done.23 = bf16[128,1024]{1,0:T(8,128)(2,1)S(1)} collective-permute-done((bf16[128,1024]{1,0:T(8,128)(2,1)}, bf16[128,1024]{1,0:T(8,128)(2,1)S(1)}, u32[]{:S(2)}, u32[]{:S(2)}) %collective-permute-start.23) | collective-permute-done | bytes 262176 | tf_op jit(solution)/shard_map/ppermute | solution.py:731
  175.1 4.6 collective-permute-done.25
  191.7 16.7 %all-to-all-done.3.q_ref.own_ref = bf16[4,192,512]{2,1,0:T(8,128)(2,1)} async-done(((bf16[4,192,512]{2,1,0:T(8,128)(2,1)}), bf16[4,192,512]{2,1,0:T(8,128)(2,1)}, u32[]{:S(2)}, u32[]{:S(2)}) %all-to-all-start.3) | async-done | bytes 786464 | tf_op jit(solution)/shard_map/all_to_all | solution.py:942
  214.7 14.5 %attention_forward.3 = (bf16[4,4,64,128]{3,2,1,0:T(8,128)(2,1)}, f32[4,8,512]{2,1,0:T(8,128)}) custom-call(s32[1]{0:T(128)} %bitcast.flip_ref, bf16[4,192,512]{2,1,0:T(8,128)(2,1)} %all-to-all-done.3.q_ref.own_ref, bf16[4,64,512]{2,1,0:T(8,128)(2,1)} %get-tuple-element.196.q_aug_ref, bf16[4,192,512]{2,1,0:T(8,128)(2,1)} %all-to-all-done.3.q_ref.own_ref, ...), custom_call_target="tpu_custom_call" | custom-call | flops 8589934592 | bytes 2424832 | tf_op jit(solution)/shard_map/attention_forward/pallas_call | solution.py:170
  229.3 5.7 all-to-all-start.4
  237.6 11.7 %all-to-all-done.4 = bf16[16,64,128]{2,1,0:T(8,128)(2,1)} async-done(((bf16[16,64,128]{2,1,0:T(8,128)(2,1)}), bf16[16,64,128]{2,1,0:T(8,128)(2,1)}, u32[]{:S(2)}, u32[]{:S(2)}) %all-to-all-start.4) | async-done | bytes 262176 | tf_op jit(solution)/shard_map/all_to_all | solution.py:973
  267.6 7.1 %ffn_forward.3 = (bf16[6,512,256]{2,1,0:T(8,128)(2,1)}, bf16[512,768]{1,0:T(8,128)(2,1)}, f32[128,1024]{1,0:T(8,128)}, bf16[128,1024]{1,0:T(8,128)(2,1)}, bf16[1...) custom-call(bf16[128,1024]{1,0:T(8,128)(2,1)} %copy-done.16, bf16[128,1024]{1,0:T(8,128)(2,1)} %copy-done.28, ...), custom_call_target="tpu_custom_call" | custom-call | flops 2415919104 | bytes 9437184 | tf_op jit(solution)/shard_map/ffn_forward/pallas_call | solution.py:353
  274.7 7.9 %ffn_backward.2 = (bf16[6,512,256]{2,1,0:T(8,128)(2,1)}, f32[128,1024]{1,0:T(8,128)}, bf16[128,1024]{1,0:T(8,128)(2,1)}, bf16[128,1024]{1,0:T(8,128)(2,1)}, bf16[128,1024]{1,0:T(8,128)(2,1)}) custom-call(bf16[128,1024]{1,0:T(8,128)(2,1)} %copy-done.9, bf16[128,1024]{1,0:T(8,128)(2,1)} %collective-permute-done.6.refs_1_.refs_7_, ...), custom_call_target="tpu_custom_call" | custom-call | flops 2415919104 | bytes 10223616 | tf_op jit(solution)/shard_map/ffn_backward/pallas_call | solution.py:382
  286.1 6.8 %ffn_weight_grads.2 = bf16[8,1152,256]{2,1,0:T(8,128)(2,1)} custom-call(bf16[128,1024]{1,0:T(8,128)(2,1)} %copy-done.16, bf16[128,1024]{1,0:T(8,128)(2,1)} %copy-done.28, bf16[128,1024]{1,0:T(8,128)(2,1)} %copy-done.29, bf16[128,1024]{1,0:T(8,128)(2,1)} %collective-permute-done.34.refs_3_, bf16[6,512,256]{2,1,0:T(8,128)(2,1)} %get-tuple-element.216.refs_4_, ...), custom_call_target="tpu_custom_call" | custom-call | flops 2415919104 | bytes 9175040 | tf_op jit(solution)/shard_map/ffn_weight_grads/pallas_call | solution.py:436
  299.5 19.5 %all_to_all.50 = bf16[16,64,128]{2,1,0:T(8,128)(2,1)} all-to-all(bf16[16,64,128]{2,1,0:T(8,128)(2,1)S(1)} %bitcast.320), channel_id=1, replica_groups={{0,2,4,6,8,10,12,14,16,18,20,22,24,26,28,30},{1,3,5,7,9,11,13,15,17,19,..., dimensions={0} | all-to-all | bytes 524288 | tf_op jit(solution)/shard_map/all_to_all | solution.py:973
  322.6 22.9 %attention_backward.2 = (f32[4,128,512]{2,1,0:T(8,128)}, bf16[8,128,512]{2,1,0:T(8,128)(2,1)}) custom-call(s32[1]{0:T(128)} %bitcast.flip_ref, bf16[4,192,512]{2,1,0:T(8,128)(2,1)} %all-to-all-done.3.q_ref.own_ref, bf16[4,64,512]{2,1,0:T(8,128)(2,1)} %get-tuple-element.196.q_aug_ref, f32[4,8,512]{2,1,0:T(8,128)} %get-tuple-element.197.lse_ref, ...), custom_call_target="tpu_custom_call" | custom-call | flops 17179869184 | bytes 4194304 | tf_op jit(solution)/shard_map/attention_backward/pallas_call | solution.py:194
  401.8 4.8 collective-permute-done.48.refs_1_.refs_7_
  413.3 8.0 %ffn_backward.3 = (bf16[6,512,256]{2,1,0:T(8,128)(2,1)}, f32[128,1024]{1,0:T(8,128)}, bf16[128,1024]{1,0:T(8,128)(2,1)}, bf16[128,1024]{1,0:T(8,128)(2,1)}, bf16[128,1024]{1,0:T(8,128)(2,1)}) custom-call(bf16[128,1024]{1,0:T(8,128)(2,1)} %copy-done.10, bf16[128,1024]{1,0:T(8,128)(2,1)} %copy-done.30, bf16[128,1024]{1,0:T(8,128)(2,1)} %copy-done.31, ...), custom_call_target="tpu_custom_call" | custom-call | flops 2415919104 | bytes 10223616 | tf_op jit(solution)/shard_map/ffn_backward/pallas_call | solution.py:382
  424.8 6.7 %ffn_weight_grads.3 = bf16[8,1152,256]{2,1,0:T(8,128)(2,1)} custom-call(bf16[128,1024]{1,0:T(8,128)(2,1)} %copy-done.13, bf16[128,1024]{1,0:T(8,128)(2,1)} %copy-done.26, bf16[128,1024]{1,0:T(8,128)(2,1)} %copy-done.27, bf16[128,1024]{1,0:T(8,128)(2,1)} %collective-permute-done.20.refs_3_, bf16[6,512,256]{2,1,0:T(8,128)(2,1)} %get-tuple-element.244.refs_4_, ...), custom_call_target="tpu_custom_call" | custom-call | flops 2415919104 | bytes 9175040 | tf_op jit(solution)/shard_map/ffn_weight_grads/pallas_call | solution.py:436
  438.4 18.4 %all_to_all.51 = bf16[16,64,128]{2,1,0:T(8,128)(2,1)} all-to-all(bf16[16,64,128]{2,1,0:T(8,128)(2,1)S(1)} %bitcast.321), channel_id=1, replica_groups={{0,2,4,6,8,10,12,14,16,18,20,22,24,26,28,30},{1,3,5,7,9,11,13,15,17,19,..., dimensions={0} | all-to-all | bytes 524288 | tf_op jit(solution)/shard_map/all_to_all | solution.py:973
  460.4 23.0 %attention_backward.3 = (f32[4,128,512]{2,1,0:T(8,128)}, bf16[8,128,512]{2,1,0:T(8,128)(2,1)}) custom-call(s32[1]{0:T(128)} %bitcast.flip_ref, bf16[4,192,512]{2,1,0:T(8,128)(2,1)} %copy-done.17, bf16[4,64,512]{2,1,0:T(8,128)(2,1)} %get-tuple-element.174.q_aug_ref, f32[4,8,512]{2,1,0:T(8,128)} %get-tuple-element.247.lse_ref, ...), custom_call_target="tpu_custom_call" | custom-call | flops 17179869184 | bytes 4194304 | tf_op jit(solution)/shard_map/attention_backward/pallas_call | solution.py:194
  543.5 5.0 finish_gradients.1
  (530 shorter events, 312.0 us)
Async XLA Ops:
  17.3 39.6 %all-gather.5.cloned.1.call-start = ((), (), s32[]{:S(2)}) async-start(), calls=%async_computation.14 | async-start | bytes 2359296 | tf_op jit(solution)/shard_map/all_gather | solution.py:799
  25.6 17.5 %collective-permute-start.2 = (bf16[128,1024]{1,0:T(8,128)(2,1)S(1)}, bf16[128,1024]{1,0:T(8,128)(2,1)S(1)}, u32[]{:S(2)}, u32[]{:S(2)}) collective-permute-start(bf16[128,1024]{1,0:T(8,128)(2,1)S(1)} %multiply_convert_fusion.5), channel_id=1, source_target_pairs={{0,6},{1,7},{2,4},{3,5},{4,2},{5,3},{6,0},{7,1},{8,14},{9,15},{10,... | collective-permute-start | bytes 786440 | tf_op jit(solution)/shard_map/ppermute | solution.py:731
  60.5 24.5 %all-to-all-start.1 = ((bf16[4,192,512]{2,1,0:T(8,128)(2,1)}), bf16[4,192,512]{2,1,0:T(8,128)(2,1)S(1)}, u32[]{:S(2)}, u32[]{:S(2)}) async-start(bf16[4,192,512]{2,1,0:T(8,128)(2,1)} %pad_maximum_fusion.11), calls=%async_computation.1 | async-start | bytes 1572864 | tf_op jit(solution)/shard_map/all_to_all | solution.py:942
  65.4 77.3 %all-gather.9.cloned.1.call-start = ((), (), s32[]{:S(2)}) async-start(), calls=%async_computation.16 | async-start | bytes 5308416 | tf_op jit(solution)/shard_map/all_gather | solution.py:799
  85.9 18.9 %collective-permute-start.14 = (bf16[128,1024]{1,0:T(8,128)(2,1)S(1)}, bf16[128,1024]{1,0:T(8,128)(2,1)S(1)}, u32[]{:S(2)}, u32[]{:S(2)}) collective-permute-start(bf16[128,1024]{1,0:T(8,128)(2,1)S(1)} %slice_select_fusion.1), channel_id=1, source_target_pairs={{0,2},{1,3},{2,0},{3,1},{4,6},{5,7},{6,4},{7,5},{8,10},{9,11},{10,... | collective-permute-start | bytes 786440 | tf_op jit(solution)/shard_map/ppermute | solution.py:729
  104.9 18.4 %all-to-all-start.2 = ((bf16[16,64,128]{2,1,0:T(8,128)(2,1)}), bf16[16,64,128]{2,1,0:T(8,128)(2,1)S(1)}, u32[]{:S(2)}, u32[]{:S(2)}) async-start(bf16[16,64,128]{2,1,0:T(8,128)(2,1)} %bitcast.336), calls=%async_computation.2 | async-start | bytes 524288 | tf_op jit(solution)/shard_map/all_to_all | solution.py:973
  108.9 63.2 %all-gather.7.cloned.1.call-start = ((), (), s32[]{:S(2)}) async-start(), calls=%async_computation.15 | async-start | bytes 2359296 | tf_op jit(solution)/shard_map/all_gather | solution.py:799
  183.5 24.8 %all-to-all-start.3 = ((bf16[4,192,512]{2,1,0:T(8,128)(2,1)}), bf16[4,192,512]{2,1,0:T(8,128)(2,1)}, u32[]{:S(2)}, u32[]{:S(2)}) async-start(bf16[4,192,512]{2,1,0:T(8,128)(2,1)} %pad_maximum_fusion.13), calls=%async_computation.3 | async-start | bytes 1572864 | tf_op jit(solution)/shard_map/all_to_all | solution.py:942
  187.7 79.8 %all-gather.11.cloned.1.call-start = ((), (), s32[]{:S(2)}) async-start(), calls=%async_computation.17 | async-start | bytes 5308416 | tf_op jit(solution)/shard_map/all_gather | solution.py:799
  210.3 18.9 %collective-permute-start.28 = (bf16[128,1024]{1,0:T(8,128)(2,1)S(1)}, bf16[128,1024]{1,0:T(8,128)(2,1)S(1)}, u32[]{:S(2)}, u32[]{:S(2)}) collective-permute-start(bf16[128,1024]{1,0:T(8,128)(2,1)S(1)} %slice_select_fusion), channel_id=1, source_target_pairs={{0,2},{1,3},{2,0},{3,1},{4,6},{5,7},{6,4},{7,5},{8,10},{9,11},{10,... | collective-permute-start | bytes 786440 | tf_op jit(solution)/shard_map/ppermute | solution.py:729
  211.7 17.5 %collective-permute-start.29 = (bf16[128,1024]{1,0:T(8,128)(2,1)S(1)}, bf16[128,1024]{1,0:T(8,128)(2,1)S(1)}, u32[]{:S(2)}, u32[]{:S(2)}) collective-permute-start(bf16[128,1024]{1,0:T(8,128)(2,1)S(1)} %slice_select_fusion), channel_id=1, source_target_pairs={{0,4},{4,0},{8,12},{12,8},{16,20},{20,16},{24,28},{28,24},{1,5},{5... | collective-permute-start | bytes 786440 | tf_op jit(solution)/shard_map/ppermute | solution.py:730
  229.3 20.0 %all-to-all-start.4 = ((bf16[16,64,128]{2,1,0:T(8,128)(2,1)}), bf16[16,64,128]{2,1,0:T(8,128)(2,1)}, u32[]{:S(2)}, u32[]{:S(2)}) async-start(bf16[16,64,128]{2,1,0:T(8,128)(2,1)} %bitcast.337), calls=%async_computation.4 | async-start | bytes 524288 | tf_op jit(solution)/shard_map/all_to_all | solution.py:973
  235.0 161.8 %reduce-scatter.5.cloned.1.call-start = ((), (), s32[]{:S(2)}) async-start(), calls=%async_computation.18 | async-start | bytes 5308416 | tf_op jit(solution)/shard_map/reduce_scatter | solution.py:811
  319.1 26.5 %collective-permute-start.40 = (bf16[128,1280]{1,0:T(8,128)(2,1)S(1)}, bf16[128,1280]{1,0:T(8,128)(2,1)S(1)}, u32[]{:S(2)}, u32[]{:S(2)}) collective-permute-start(bf16[128,1280]{1,0:T(8,128)(2,1)S(1)} %get-tuple-element.411), channel_id=1, source_target_pairs={{0,6},{1,7},{2,4},{3,5},{4,2},{5,3},{6,0},{7,1},{8,14},{9,15},{10,... | collective-permute-start | bytes 983048 | tf_op jit(solution)/shard_map/ppermute | solution.py:731
  319.4 26.2 %collective-permute-start.39 = (bf16[128,1280]{1,0:T(8,128)(2,1)S(1)}, bf16[128,1280]{1,0:T(8,128)(2,1)S(1)}, u32[]{:S(2)}, u32[]{:S(2)}) collective-permute-start(bf16[128,1280]{1,0:T(8,128)(2,1)S(1)} %get-tuple-element.410), channel_id=1, source_target_pairs={{0,4},{4,0},{8,12},{12,8},{16,20},{20,16},{24,28},{28,24},{1,5},{5... | collective-permute-start | bytes 983048 | tf_op jit(solution)/shard_map/ppermute | solution.py:730
  322.0 23.6 %collective-permute-start.38 = (bf16[128,1280]{1,0:T(8,128)(2,1)S(1)}, bf16[128,1280]{1,0:T(8,128)(2,1)S(1)}, u32[]{:S(2)}, u32[]{:S(2)}) collective-permute-start(bf16[128,1280]{1,0:T(8,128)(2,1)S(1)} %get-tuple-element.409), channel_id=1, source_target_pairs={{0,2},{1,3},{2,0},{3,1},{4,6},{5,7},{6,4},{7,5},{8,10},{9,11},{10,... | collective-permute-start | bytes 983048 | tf_op jit(solution)/shard_map/ppermute | solution.py:729
  350.7 24.2 %all-to-all-start.6 = ((bf16[4,192,512]{2,1,0:T(8,128)(2,1)}), bf16[4,192,512]{2,1,0:T(8,128)(2,1)S(1)}, u32[]{:S(2)}, u32[]{:S(2)}) async-start(bf16[4,192,512]{2,1,0:T(8,128)(2,1)} %pad_maximum_fusion.15), calls=%async_computation.6 | async-start | bytes 1572864 | tf_op jit(solution)/shard_map/all_to_all | solution.py:960
  354.2 81.1 %reduce-scatter.7.cloned.1.call-start = ((), (), s32[]{:S(2)}) async-start(), calls=%async_computation.19 | async-start | bytes 2359296 | tf_op jit(solution)/shard_map/reduce_scatter | solution.py:811
  396.8 96.1 %reduce-scatter.9.cloned.1.call-start = ((), (), s32[]{:S(2)}) async-start(), calls=%async_computation.20 | async-start | bytes 5308416 | tf_op jit(solution)/shard_map/reduce_scatter | solution.py:811
  456.9 26.6 %collective-permute-start.56 = (bf16[128,1280]{1,0:T(8,128)(2,1)S(1)}, bf16[128,1280]{1,0:T(8,128)(2,1)S(1)}, u32[]{:S(2)}, u32[]{:S(2)}) collective-permute-start(bf16[128,1280]{1,0:T(8,128)(2,1)S(1)} %get-tuple-element.398), channel_id=1, source_target_pairs={{0,6},{1,7},{2,4},{3,5},{4,2},{5,3},{6,0},{7,1},{8,14},{9,15},{10,... | collective-permute-start | bytes 983048 | tf_op jit(solution)/shard_map/ppermute | solution.py:731
  457.4 26.1 %collective-permute-start.55 = (bf16[128,1280]{1,0:T(8,128)(2,1)S(1)}, bf16[128,1280]{1,0:T(8,128)(2,1)S(1)}, u32[]{:S(2)}, u32[]{:S(2)}) collective-permute-start(bf16[128,1280]{1,0:T(8,128)(2,1)S(1)} %get-tuple-element.397), channel_id=1, source_target_pairs={{0,4},{4,0},{8,12},{12,8},{16,20},{20,16},{24,28},{28,24},{1,5},{5... | collective-permute-start | bytes 983048 | tf_op jit(solution)/shard_map/ppermute | solution.py:730
  459.9 23.7 %collective-permute-start.54 = (bf16[128,1280]{1,0:T(8,128)(2,1)S(1)}, bf16[128,1280]{1,0:T(8,128)(2,1)S(1)}, u32[]{:S(2)}, u32[]{:S(2)}) collective-permute-start(bf16[128,1280]{1,0:T(8,128)(2,1)S(1)} %get-tuple-element.396), channel_id=1, source_target_pairs={{0,2},{1,3},{2,0},{3,1},{4,6},{5,7},{6,4},{7,5},{8,10},{9,11},{10,... | collective-permute-start | bytes 983048 | tf_op jit(solution)/shard_map/ppermute | solution.py:729
  488.6 24.2 %all-to-all-start.8 = ((bf16[4,192,512]{2,1,0:T(8,128)(2,1)}), bf16[4,192,512]{2,1,0:T(8,128)(2,1)S(1)}, u32[]{:S(2)}, u32[]{:S(2)}) async-start(bf16[4,192,512]{2,1,0:T(8,128)(2,1)} %pad_maximum_fusion.16), calls=%async_computation.8 | async-start | bytes 1572864 | tf_op jit(solution)/shard_map/all_to_all | solution.py:960
  492.1 59.5 %reduce-scatter.11.cloned.1.call-start = ((), (), s32[]{:S(2)}) async-start(), calls=%async_computation.21 | async-start | bytes 2359296 | tf_op jit(solution)/shard_map/reduce_scatter | solution.py:811
  (137 other events, 1336.5 us)
Sparse Core Ops, SparseCore 0:
  25.6 29.3 all-gather.4
  85.1 55.7 all-gather.8
  142.8 29.2 all-gather.6
  208.5 57.2 all-gather.10
  296.6 58.9 reduce-scatter.4
  397.0 33.1 reduce-scatter.6
  435.4 57.4 reduce-scatter.8
  517.0 34.6 reduce-scatter.10

commit v6 on v5

--- a/solution.py
+++ b/solution.py
@@ -316,6 +316,68 @@
         put_parts(inner_ref[...], slice(0, D), *part_refs)
 
 
+def ffn_turn_kernel(*refs, unit_rows, down_rows, down_steps):
+    unit_ref, down_ref, grads_ref, hidden_ref = refs[8:12]
+    part_refs, inner_ref, hidden_grad, x_ref, g_ref = refs[12:16], *refs[16:20]
+    join_rows(x_ref, refs[:4])
+    join_rows(g_ref, refs[4:8])
+    step = pl.program_id(0)
+    half = BLOCK // 2
+
+    @pl.when(step < down_steps)
+    def _():
+        total = 0.0
+        for place in range(down_ref.shape[1] // down_rows):
+            matrix = down_ref[:, place * down_rows : (place + 1) * down_rows, :].reshape(-1, BLOCK)
+            lanes = pl.ds(pl.multiple_of((step * FFN_DOWNS + place) * BLOCK, BLOCK), BLOCK)
+            total = total + dot(g_ref[:, lanes], matrix, NT)
+
+        @pl.when(step == 0)
+        def _():
+            hidden_grad[...] = total
+
+        @pl.when(step > 0)
+        def _():
+            hidden_grad[...] += total
+
+    @pl.when(step >= down_steps)
+    def _():
+        count = unit_ref.shape[1] // unit_rows
+        total = 0.0
+        for place in range(count):
+            matrix = unit_ref[:, place * unit_rows : (place + 1) * unit_rows, :].reshape(-1, BLOCK)
+            both = dot(x_ref[...], matrix, NN)
+            gate, upward = both[:, :half], both[:, half:]
+            spot = (step - down_steps) * count + place
+            lanes = pl.ds(pl.multiple_of(spot * half, half), half)
+            above = hidden_grad[:, lanes]
+            sigmoid, silu = silu_parts(gate)
+            hidden_ref[:, lanes] = (silu * upward).astype(LOW)
+            grad_gate = above * upward * (sigmoid * (1.0 + gate * (1.0 - sigmoid)))
+            grads = jnp.concatenate([grad_gate, above * silu], axis=1).astype(LOW)
+            grads_ref[place] = grads
+            total = total + dot(grads, matrix, NT)
+
+        @pl.when(step == down_steps)
+        def _():
+            inner_ref[...] = total
+
+        @pl.when(step > down_steps)
+        def _():
+            inner_ref[...] += total
+
+    @pl.when(step == pl.num_programs(0) - 1)
+    def _():
+        put_parts(inner_ref[...], slice(0, D), *part_refs)
+
+
+def ffn_down_kernel(hidden_ref, down_ref, *out_refs, down_rows):
+    for place in range(down_ref.shape[1] // down_rows):
+        matrix = down_ref[:, place * down_rows : (place + 1) * down_rows, :].reshape(-1, BLOCK)
+        lanes = slice(place * BLOCK, (place + 1) * BLOCK)
+        put_parts(dot(hidden_ref[...], matrix, NN), lanes, *out_refs)
+
+
 FFN_DOWNS = 4
 
 
@@ -396,6 +458,61 @@
         compiler_params=pltpu.CompilerParams(vmem_limit_bytes=VMEM_LIMIT),
         name="ffn_backward",
     )(*rows, packed, packed, both)
+
+
+def ffn_turn(rows, grad_rows, packed, cols_ff, unit_rows, down_rows):
+    tokens, down_steps = 4 * rows[0].shape[0], D // BLOCK // FFN_DOWNS
+    unit_step = lambda i: jnp.maximum(i - down_steps, 0)
+    down_step = lambda i: jnp.minimum(i, down_steps - 1)
+    unit_steps, down_steps, specs = ffn_specs(
+        cols_ff, unit_rows, down_rows, packed.shape[0], unit_step, down_step
+    )
+    parts, part_specs = parts_of(tokens, D, lambda i: (0, 0))
+    results = [
+        jax.ShapeDtypeStruct((2 * cols_ff // BLOCK, tokens, BLOCK), LOW),
+        jax.ShapeDtypeStruct((tokens, cols_ff), LOW),
+        *parts,
+    ]
+    return pl.pallas_call(
+        functools.partial(
+            ffn_turn_kernel, unit_rows=unit_rows, down_rows=down_rows, down_steps=down_steps
+        ),
+        grid=(unit_steps + down_steps,),
+        in_specs=[pl.BlockSpec(rows[0].shape, lambda i: (0, 0))] * 8 + specs,
+        out_specs=[
+            pl.BlockSpec((ffn_units(cols_ff), tokens, BLOCK), lambda i: (unit_step(i), 0, 0)),
+            pl.BlockSpec((tokens, cols_ff), lambda i: (0, 0)),
+            *part_specs,
+        ],
+        out_shape=results,
+        scratch_shapes=[
+            pltpu.VMEM((tokens, D), jnp.float32),
+            pltpu.VMEM((tokens, cols_ff), jnp.float32),
+            pltpu.VMEM((tokens, D), LOW),
+            pltpu.VMEM((tokens, D), LOW),
+        ],
+        cost_estimate=cost(10 * tokens * D * cols_ff, [*rows, *grad_rows, packed], results),
+        compiler_params=pltpu.CompilerParams(vmem_limit_bytes=VMEM_LIMIT),
+        name="ffn_turn",
+    )(*rows, *grad_rows, packed, packed)
+
+
+def ffn_down(hidden, packed, unit_rows, down_rows):
+    tokens, cols_ff = hidden.shape
+    specs = ffn_specs(
+        cols_ff, unit_rows, down_rows, packed.shape[0], lambda i: 0, lambda i: i
+    )[2]
+    results, part_specs = parts_of(tokens, FFN_DOWNS * BLOCK, lambda i: (0, i))
+    return pl.pallas_call(
+        functools.partial(ffn_down_kernel, down_rows=down_rows),
+        grid=(D // BLOCK // FFN_DOWNS,),
+        in_specs=[pl.BlockSpec(hidden.shape, lambda i: (0, 0)), specs[1]],
+        out_specs=part_specs,
+        out_shape=results,
+        cost_estimate=cost(2 * tokens * D * cols_ff, [hidden], results),
+        compiler_params=pltpu.CompilerParams(vmem_limit_bytes=VMEM_LIMIT),
+        name="ffn_down",
+    )(hidden, packed)
 
 
 def ffn_weight_grads_kernel(*refs, unit_rows, down_rows):
@@ -470,12 +587,17 @@
     )(left, right)
 
 
+def gain_column(gain_ref, layer):
+    return jnp.broadcast_to(gain_ref[layer : layer + 1, :], (128, gain_ref.shape[1])).T[:, :1]
+
+
 def take_qkv(room_ref, layer, quarter, weights, gain_ref):
+    gain = gain_column(gain_ref, layer)
     for slot in range(QUARTER_HEADS):
         column = HD * (QUARTERS * slot + quarter)
         for which, weight_ref in enumerate(weights):
             first = (3 * slot + which) * HD
-            part = weight_ref[layer, :, column : column + HD] * gain_ref[layer]
+            part = weight_ref[layer, :, column : column + HD] * gain
             room_ref[:, first : first + HD] = part
 
 
@@ -519,7 +641,7 @@
     taken = 4 * planes * d_rows
     pieces = [(layer, which, part) for layer in range(LAYERS) for which in range(2) for part in range(2)]
     for number, (layer, which, part) in enumerate(pieces):
-        rows = weights[3 + which][layer, :, part * taken : (part + 1) * taken] * gains[1][layer]
+        rows = weights[3 + which][layer, :, part * taken : (part + 1) * taken] * gain_column(gains[1], layer)
         rows_ref[number * w_rows : (number + 1) * w_rows, :] = rows
     placed = dot(rows_ref[...].astype(LOW), unit_places(d_rows, padded, planes), NN)
     for number, (layer, which, part) in enumerate(pieces):
@@ -571,7 +693,7 @@
     for out_ref, weight_ref in zip(outs, weights):
         grad = out_ref[layer]
         gain_grad = gain_grad + jnp.sum(grad * weight_ref[layer], axis=1, keepdims=True)
-        out_ref[layer] = grad * gain_ref[layer]
+        out_ref[layer] = grad * gain_column(gain_ref, layer)
     gain_out_ref[layer : layer + 1, :] = jnp.broadcast_to(gain_grad, (gain_grad.shape[0], 128)).T[:1]
 
 
@@ -596,11 +718,12 @@
     for out_ref, weight_ref in zip(outs, weights):
         grad = out_ref[layer]
         gain_grad = gain_grad + jnp.sum(grad * weight_ref[layer], axis=1, keepdims=True)
-        out_ref[layer] = grad * gain_ref[layer]
+        out_ref[layer] = grad * gain_column(gain_ref, layer)
     gain_out_ref[layer : layer + 1, :] = jnp.broadcast_to(gain_grad, (gain_grad.shape[0], 128)).T[:1]
 
 
 def finish_kernel(place_ref, *refs, unit_end, w_rows, d_rows, padded, planes, with_out):
+    out_lanes = slice(3 * QUARTER_HEADS * HD, 3 * QUARTER_HEADS * HD + BLOCK)
     came_ref, *sums = refs[: 1 + LAYERS]
     out_sums, refs = refs[1 + LAYERS : 2 * LAYERS], refs[2 * LAYERS :]
     weights, gains, outs = refs[:5], refs[5:7], refs[7:]
@@ -618,11 +741,12 @@
             rows = sums[layer][unit_end + block * padded : unit_end + (block + 1) * padded, :]
             outs[6][layer, :, lanes] = rows.astype(jnp.float32)[:d_rows]
             if with_out and layer > 0:
-                rows = out_sums[layer - 1][block * w_rows : (block + 1) * w_rows, :]
+                rows = out_sums[layer - 1][block * w_rows : (block + 1) * w_rows, out_lanes]
                 outs[3][layer, :, lanes] = rows.astype(jnp.float32)
 
 
 def finish_first_kernel(place_ref, came_ref, out_sum_ref, *refs, w_rows, with_out):
+    out_lanes = slice(3 * QUARTER_HEADS * HD, 3 * QUARTER_HEADS * HD + BLOCK)
     weights, gain_ref, have, outs = refs[:3], refs[3], refs[4:9], refs[9:]
     for layer in range(1, LAYERS):
         for have_ref, out_ref in zip(have, outs):
@@ -630,7 +754,7 @@
     put_qkv(came_ref, place_ref, 0, outs[:3], 0, weights, gain_ref, outs[3])
     if with_out:
         for block in range(D // BLOCK):
-            rows = out_sum_ref[block * w_rows : (block + 1) * w_rows, :]
+            rows = out_sum_ref[block * w_rows : (block + 1) * w_rows, out_lanes]
             outs[4][0, :, block * BLOCK : (block + 1) * BLOCK] = rows.astype(jnp.float32)
 
 
@@ -842,7 +966,7 @@
         blocks = whole[:, 3 * quarter_width :].reshape(2 * planes, -1, BLOCK)
         return whole[:, : 3 * quarter_width], from_blocks(blocks, w_rows)
 
-    gains = (gain_attn[:, :, None], gain_ffn[:, :, None])
+    gains = (gain_attn, gain_ffn)
     first_sent = first_parts(
         jnp.reshape(here_lo, (1,)).astype(jnp.int32), (w_query, w_key, w_value), gains[0]
     )
@@ -1037,7 +1161,8 @@
         own, next_part = lax.optimization_barrier((own, next_part))
         packed = gather(next_part).reshape(2 * planes, -1, BLOCK)
         ffn_weights.append(packed)
-        own, out_quarter = lax.optimization_barrier((own, out_quarter))
+        if layer == 0:
+            own, out_quarter = lax.optimization_barrier((own, out_quarter))
         halves = out_quarter.reshape(2, quarter_width // 2, D)
         half = jnp.where(here_core == 0, halves[0], halves[1])
         out_parts = neighbours(half, half, half)
@@ -1063,7 +1188,10 @@
             next_part = attention_part(layer + 1, cut(later_weights)[LAYERS + layer])
             normed_parts, next_part = lax.optimization_barrier((normed_parts, next_part))
             attention_weights.append(attention_matrices(next_part))
-        both, hidden, *parts = ffn_forward(normed_parts, packed, quarter_ff, group_rows, padded)
+        if layer < LAYERS - 1:
+            both, hidden, *parts = ffn_forward(normed_parts, packed, quarter_ff, group_rows, padded)
+        else:
+            both, hidden = None, None
         saved.append(
             (
                 scaled_one, inverse_one, normed, own, sib, queries, q_aug, out, lse, attended,
@@ -1073,7 +1201,7 @@
         if layer < LAYERS - 1:
             stream = middle + fold(*parts)
         else:
-            last_middle, last_parts = middle, parts
+            last_middle = middle
 
     upstream = cotangent
     whole_grads, ffn_sums, qkv_sums = [None] * LAYERS, [None] * LAYERS, [None] * LAYERS
@@ -1089,7 +1217,14 @@
             upstream_parts = beside_parts(upstream.astype(LOW))
         else:
             upstream_parts = last_grad_parts
-        grad_units, *parts = ffn_backward(upstream_parts, packed, both, quarter_ff, group_rows, padded)
+        if layer < LAYERS - 1:
+            grad_units, *parts = ffn_backward(
+                upstream_parts, packed, both, quarter_ff, group_rows, padded
+            )
+        else:
+            grad_units, hidden, *parts = ffn_turn(
+                normed_parts, upstream_parts, packed, quarter_ff, group_rows, padded
+            )
         inner = fold(*parts)
         buffer = ffn_weight_grads(
             normed_parts, grad_units, hidden, upstream_parts, 2 * planes, group_rows, padded
@@ -1104,7 +1239,12 @@
         grad_attended = chip_order(grad_attended.reshape(4, QUARTER_HEADS, HD, tok_rows))
         if spread > 1:
             grad_attended = jnp.repeat(grad_attended, spread, axis=0)
+        if layer == LAYERS - 1:
+            grad_attended, last_hidden = lax.optimization_barrier((grad_attended, hidden))
+            last_parts = ffn_down(last_hidden, packed, group_rows, padded)
         out_grad = my_tiles(over_chips(grad_attended))
+        if layer == LAYERS - 1:
+            out_grad, *last_parts = lax.optimization_barrier((out_grad, *last_parts))
         out_grad, middle_low, attended = lax.optimization_barrier((out_grad, middle_low, attended))
         middle_low, attended = share_for_out(middle_low, attended)
         grad_q, grad_kv = attention_backward(
@@ -1155,10 +1295,6 @@
             upstream = grad_middle + normalize_back(scaled_one, inverse_one, inner)
 
     later_sums = [from_blocks(member[None, :unit_end], group_rows) for member in ffn_sums]
-    out_sums = [member[:, 3 * quarter_width :] for member in qkv_sums]
-    qkv_sums = [member[:, : 3 * quarter_width] for member in qkv_sums]
-    if not split_heads:
-        out_sums = [member[:, :BLOCK] for member in qkv_sums]
     bias_local = lax.dynamic_update_slice(
         jnp.zeros((LAYERS, 2, HEADS), jnp.float32), jnp.stack(bias_parts)[:, :, None], (0, 0, my_head)
     )
@@ -1167,15 +1303,15 @@
     weights = (w_query, w_key, w_value, w_gate, w_up)
     *grads, gain_one, gain_two = finish_gradients(
         quarters ^ (2 * here_y + here_core), came, ffn_sums,
-        out_sums[1:], weights, gains, w_down.shape, unit_end, planes, split_heads,
-    )
-    qkv_sums[0], out_sums[0], gain_two, parts, grads = lax.optimization_barrier(
-        (qkv_sums[0], out_sums[0], gain_two, four_parts(partial), grads)
+        qkv_sums[1:], weights, gains, w_down.shape, unit_end, planes, split_heads,
+    )
+    qkv_sums[0], gain_two, parts, grads = lax.optimization_barrier(
+        (qkv_sums[0], gain_two, four_parts(partial), grads)
     )
     inner = fold(*parts)
     upstream = grad_middle + normalize_back(scaled_one, inverse_one, inner)
     *grads[:3], gain_one, grads[3] = finish_first(
-        2 * quarters + here_lo, cross_back_at_once(qkv_sums[0]), out_sums[0], weights[:3], gains[0],
+        2 * quarters + here_lo, cross_back_at_once(qkv_sums[0][:, : 3 * quarter_width]), qkv_sums[0], weights[:3], gains[0],
         [*grads[:3], gain_one, grads[3]], split_heads,
     )
     if not split_heads:

time: 593 us -> 584 us (0.985)
  blocking collectives: 37.9 us -> 18.4 us
  waiting for transfers between devices: 161 us -> 174 us
  local copies, waits for them, and re-layouts: 33.1 us -> 24.6 us
  starting transfers between devices: 116 us -> 122 us
    all_to_all x2 -> x1, blocking collectives: 37.9 us -> 18.4 us  [over_chips(): lax.all_to_all(value, BOTH, split_axis=0, concat_axis=0, tiled=True, axis...]
    pallas_call x0 -> x2, Pallas kernels: none -> 14.5 us  [the longest x1 10.9 us: ffn_turn(): pl.pallas_call(functools.partial(ffn_turn_kernel, unit_rows=unit_rows, do...]
    all_to_all x2 -> x3, waiting for transfers between devices: 23.8 us -> 33.5 us  [over_chips(): lax.all_to_all(value, BOTH, split_axis=0, concat_axis=0, tiled=True, axis...]
    pallas_call x2 -> x1, Pallas kernels: 15.9 us -> 8 us  [ffn_backward(): pl.pallas_call(functools.partial(ffn_backward_kernel, unit_rows=unit_rows...]
    pallas_call x2 -> x1, Pallas kernels: 14.1 us -> 7.07 us  [ffn_forward(): pl.pallas_call(functools.partial(ffn_forward_kernel, unit_rows=unit_rows,...]
    all_to_all x2 -> x3, starting transfers between devices: 9.74 us -> 15.7 us  [over_chips(): lax.all_to_all(value, BOTH, split_axis=0, concat_axis=0, tiled=True, axis...]
  transfers between devices with their start and end apart: 86 -> 87, of which waited for: 48 -> 47; matrix products, arithmetic and copies ran while one was open for 14% -> 14% of each run, Pallas kernels for 20% -> 21%
where the time goes in v6:
time: 584 us; the launch traced here: 573 us
  waiting for transfers between devices  174 us (30%)
  Pallas kernels  138 us (24%)
  starting transfers between devices  122 us (21%)
  other arithmetic  56.1 us (10%)
  local copies, waits for them, and re-layouts  24.6 us (4%)
  between operations  24.4 us (4%)
  blocking collectives  18.4 us (3%)
  matrix products  15.3 us (3%)
    pallas_call x2, Pallas kernels, attention_backward(): pl.pallas_call(backward_kernel, grid_spec=pltpu.PrefetchScalarGridSpec(nu...  45.8 us
    all_to_all x3, waiting for transfers between devices, over_chips(): lax.all_to_all(value, BOTH, split_axis=0, concat_axis=0, tiled=True, axis...  33.5 us
    ppermute x17, waiting for transfers between devices, neighbours(): lax.ppermute(across_x, 'seq', x_swap)  32.5 us
    pallas_call x2, Pallas kernels, attention_forward(): pl.pallas_call(forward_kernel, grid_spec=pltpu.PrefetchScalarGridSpec(num...  29.1 us
    ppermute x17, waiting for transfers between devices, neighbours(): lax.ppermute(across_both, BOTH, corner_swap)  28.7 us
    ppermute x17, starting transfers between devices, neighbours(): lax.ppermute(across_both, BOTH, corner_swap)  24.9 us
    ppermute x17, starting transfers between devices, neighbours(): lax.ppermute(across_x, 'seq', x_swap)  19.9 us
    all_to_all x2, waiting for transfers between devices, to_heads(): lax.all_to_all(value, 'seq', split_axis=0, concat_axis=0, tiled=True, axi...  19.4 us
  transfers between devices with their start and end apart: 87, of which 47 were waited for; matrix products, arithmetic and copies ran while one was open for 14% of the time, Pallas kernels for 21%

profile of v6, /device:TPU:0, one launch (start us, length us, event | category | flops | bytes accessed | tf_op | source)
XLA Modules:
  0.0 573.0 jit_solution(6488106393821364166)
XLA Ops:
  9.6 5.3 all-to-all-start
  15.9 6.5 %all-to-all-done = bf16[8,32,768]{2,1,0:T(8,128)(2,1)S(1)} async-done(((bf16[8,32,768]{2,1,0:T(8,128)(2,1)}), bf16[8,32,768]{2,1,0:T(8,128)(2,1)S(1)}, u32[]{:S(2)}, u32[]{:S(2)}) %all-to-all-start) | async-done | bytes 393248 | tf_op jit(solution)/shard_map/all_to_all | solution.py:907
  40.8 4.8 later_parts.1
  57.7 5.0 all-to-all-start.1
  87.5 14.6 %attention_forward.2 = (bf16[4,4,64,128]{3,2,1,0:T(8,128)(2,1)}, f32[4,8,512]{2,1,0:T(8,128)}) custom-call(s32[1]{0:T(128)} %bitcast.flip_ref, bf16[4,192,512]{2,1,0:T(8,128)(2,1)} %copy-done.13, bf16[4,64,512]{2,1,0:T(8,128)(2,1)} %get-tuple-element.177.q_aug_ref, bf16[4,192,512]{2,1,0:T(8,128)(2,1)} %copy-done.13, bf16[4,128,512]{2,1,0:T(8,128)(2,1)} %copy-done.66, ...), custom_call_target="tpu_custom_call" | custom-call | flops 8589934592 | bytes 2424832 | tf_op jit(solution)/shard_map/attention_forward/pallas_call | solution.py:170
  108.4 12.2 %all-to-all-done.2 = bf16[16,64,128]{2,1,0:T(8,128)(2,1)S(1)} async-done(((bf16[16,64,128]{2,1,0:T(8,128)(2,1)}), bf16[16,64,128]{2,1,0:T(8,128)(2,1)S(1)}, u32[]{:S(2)}, u32[]{:S(2)}) %all-to-all-start.2) | async-done | bytes 262176 | tf_op jit(solution)/shard_map/all_to_all | solution.py:1097
  139.4 7.1 %ffn_forward.1 = (bf16[6,512,256]{2,1,0:T(8,128)(2,1)}, bf16[512,768]{1,0:T(8,128)(2,1)}, f32[128,1024]{1,0:T(8,128)}, bf16[128,1024]{1,0:T(8,128)(2,1)}, bf16[1...) custom-call(bf16[128,1024]{1,0:T(8,128)(2,1)} %copy-done.10, bf16[128,1024]{1,0:T(8,128)(2,1)} %copy-done.24, ...), custom_call_target="tpu_custom_call" | custom-call | flops 2415919104 | bytes 9437184 | tf_op jit(solution)/shard_map/ffn_forward/pallas_call | solution.py:415
  149.9 6.9 %collective-permute-done.23 = bf16[128,1024]{1,0:T(8,128)(2,1)S(1)} collective-permute-done((bf16[128,1024]{1,0:T(8,128)(2,1)}, bf16[128,1024]{1,0:T(8,128)(2,1)S(1)}, u32[]{:S(2)}, u32[]{:S(2)}) %collective-permute-start.23) | collective-permute-done | bytes 262176 | tf_op jit(solution)/shard_map/ppermute | solution.py:855
  172.2 4.8 collective-permute-done.25
  189.0 16.6 %all-to-all-done.3.q_ref.own_ref = bf16[4,192,512]{2,1,0:T(8,128)(2,1)} async-done(((bf16[4,192,512]{2,1,0:T(8,128)(2,1)}), bf16[4,192,512]{2,1,0:T(8,128)(2,1)}, u32[]{:S(2)}, u32[]{:S(2)}) %all-to-all-start.3) | async-done | bytes 786464 | tf_op jit(solution)/shard_map/all_to_all | solution.py:1066
  211.8 14.5 %attention_forward.3 = (bf16[4,4,64,128]{3,2,1,0:T(8,128)(2,1)}, f32[4,8,512]{2,1,0:T(8,128)}) custom-call(s32[1]{0:T(128)} %bitcast.flip_ref, bf16[4,192,512]{2,1,0:T(8,128)(2,1)} %all-to-all-done.3.q_ref.own_ref, bf16[4,64,512]{2,1,0:T(8,128)(2,1)} %get-tuple-element.198.q_aug_ref, bf16[4,192,512]{2,1,0:T(8,128)(2,1)} %all-to-all-done.3.q_ref.own_ref, ...), custom_call_target="tpu_custom_call" | custom-call | flops 8589934592 | bytes 2424832 | tf_op jit(solution)/shard_map/attention_forward/pallas_call | solution.py:170
  226.3 5.0 all-to-all-start.4
  234.9 10.7 %all-to-all-done.4 = bf16[16,64,128]{2,1,0:T(8,128)(2,1)} async-done(((bf16[16,64,128]{2,1,0:T(8,128)(2,1)}), bf16[16,64,128]{2,1,0:T(8,128)(2,1)}, u32[]{:S(2)}, u32[]{:S(2)}) %all-to-all-start.4) | async-done | bytes 262176 | tf_op jit(solution)/shard_map/all_to_all | solution.py:1097
  264.5 10.9 %ffn_turn.1 = (bf16[6,512,256]{2,1,0:T(8,128)(2,1)}, bf16[512,768]{1,0:T(8,128)(2,1)}, f32[128,1024]{1,0:T(8,128)}, bf16[128,1024]{1,0:T(8,128)(2,1)}, bf16[128,...) custom-call(bf16[128,1024]{1,0:T(8,128)(2,1)} %copy-done.36, bf16[128,1024]{1,0:T(8,128)(2,1)} %copy-done.44, ...), custom_call_target="tpu_custom_call" | custom-call | flops 4026531840 | bytes 10485760 | tf_op jit(solution)/shard_map/ffn_turn/pallas_call | solution.py:476
  278.9 6.8 %ffn_weight_grads.2 = bf16[8,1152,256]{2,1,0:T(8,128)(2,1)} custom-call(bf16[128,1024]{1,0:T(8,128)(2,1)} %copy-done.36, bf16[128,1024]{1,0:T(8,128)(2,1)} %copy-done.44, bf16[128,1024]{1,0:T(8,128)(2,1)} %copy-done.45, bf16[128,1024]{1,0:T(8,128)(2,1)} %collective-permute-done.34.refs_3_, bf16[6,512,256]{2,1,0:T(8,128)(2,1)} %get-tuple-element.216.refs_4_, ...), custom_call_target="tpu_custom_call" | custom-call | flops 2415919104 | bytes 9175040 | tf_op jit(solution)/shard_map/ffn_weight_grads/pallas_call | solution.py:553
  292.6 6.7 %all-to-all-start.5 = ((bf16[16,64,128]{2,1,0:T(8,128)(2,1)}), bf16[16,64,128]{2,1,0:T(8,128)(2,1)S(1)}, u32[]{:S(2)}, u32[]{:S(2)}) async-start(bf16[16,64,128]{2,1,0:T(8,128)(2,1)} %bitcast.72), calls=%async_computation.5 | async-start | bytes 524288 | tf_op jit(solution)/shard_map/all_to_all | solution.py:1097
  302.9 10.6 %all-to-all-done.5 = bf16[16,64,128]{2,1,0:T(8,128)(2,1)S(1)} async-done(((bf16[16,64,128]{2,1,0:T(8,128)(2,1)}), bf16[16,64,128]{2,1,0:T(8,128)(2,1)S(1)}, u32[]{:S(2)}, u32[]{:S(2)}) %all-to-all-start.5) | async-done | bytes 262176 | tf_op jit(solution)/shard_map/all_to_all | solution.py:1097
  317.2 22.9 %attention_backward.2 = (f32[4,128,512]{2,1,0:T(8,128)}, bf16[8,128,512]{2,1,0:T(8,128)(2,1)}) custom-call(s32[1]{0:T(128)} %bitcast.flip_ref, bf16[4,192,512]{2,1,0:T(8,128)(2,1)} %all-to-all-done.3.q_ref.own_ref, bf16[4,64,512]{2,1,0:T(8,128)(2,1)} %get-tuple-element.198.q_aug_ref, f32[4,8,512]{2,1,0:T(8,128)} %get-tuple-element.199.lse_ref, ...), custom_call_target="tpu_custom_call" | custom-call | flops 17179869184 | bytes 4194304 | tf_op jit(solution)/shard_map/attention_backward/pallas_call | solution.py:194
  396.4 4.8 collective-permute-done.48.refs_1_.refs_7_
  407.9 8.0 %ffn_backward.1 = (bf16[6,512,256]{2,1,0:T(8,128)(2,1)}, f32[128,1024]{1,0:T(8,128)}, bf16[128,1024]{1,0:T(8,128)(2,1)}, bf16[128,1024]{1,0:T(8,128)(2,1)}, bf16[128,1024]{1,0:T(8,128)(2,1)}) custom-call(bf16[128,1024]{1,0:T(8,128)(2,1)} %copy-done.7, bf16[128,1024]{1,0:T(8,128)(2,1)} %copy-done.27, bf16[128,1024]{1,0:T(8,128)(2,1)} %copy-done.28, ...), custom_call_target="tpu_custom_call" | custom-call | flops 2415919104 | bytes 10223616 | tf_op jit(solution)/shard_map/ffn_backward/pallas_call | solution.py:444
  419.5 6.8 %ffn_weight_grads.3 = bf16[8,1152,256]{2,1,0:T(8,128)(2,1)} custom-call(bf16[128,1024]{1,0:T(8,128)(2,1)} %copy-done.10, bf16[128,1024]{1,0:T(8,128)(2,1)} %copy-done.24, bf16[128,1024]{1,0:T(8,128)(2,1)} %copy-done.25, bf16[128,1024]{1,0:T(8,128)(2,1)} %collective-permute-done.20.refs_3_, bf16[6,512,256]{2,1,0:T(8,128)(2,1)} %get-tuple-element.251.refs_4_, ...), custom_call_target="tpu_custom_call" | custom-call | flops 2415919104 | bytes 9175040 | tf_op jit(solution)/shard_map/ffn_weight_grads/pallas_call | solution.py:553
  432.3 18.4 %all_to_all.50 = bf16[16,64,128]{2,1,0:T(8,128)(2,1)} all-to-all(bf16[16,64,128]{2,1,0:T(8,128)(2,1)S(1)} %bitcast.321), channel_id=1, replica_groups={{0,2,4,6,8,10,12,14,16,18,20,22,24,26,28,30},{1,3,5,7,9,11,13,15,17,19,..., dimensions={0} | all-to-all | bytes 524288 | tf_op jit(solution)/shard_map/all_to_all | solution.py:1097
  454.4 22.9 %attention_backward.3 = (f32[4,128,512]{2,1,0:T(8,128)}, bf16[8,128,512]{2,1,0:T(8,128)(2,1)}) custom-call(s32[1]{0:T(128)} %bitcast.flip_ref, bf16[4,192,512]{2,1,0:T(8,128)(2,1)} %copy-done.13, bf16[4,64,512]{2,1,0:T(8,128)(2,1)} %get-tuple-element.177.q_aug_ref, f32[4,8,512]{2,1,0:T(8,128)} %get-tuple-element.254.lse_ref, ...), custom_call_target="tpu_custom_call" | custom-call | flops 17179869184 | bytes 4194304 | tf_op jit(solution)/shard_map/attention_backward/pallas_call | solution.py:194
  537.0 5.0 finish_gradients.1
  (523 shorter events, 310.9 us)
Async XLA Ops:
  15.0 39.1 %all-gather.5.cloned.1.call-start = ((), (), s32[]{:S(2)}) async-start(), calls=%async_computation.14 | async-start | bytes 2359296 | tf_op jit(solution)/shard_map/all_gather | solution.py:923
  57.7 24.6 %all-to-all-start.1 = ((bf16[4,192,512]{2,1,0:T(8,128)(2,1)}), bf16[4,192,512]{2,1,0:T(8,128)(2,1)S(1)}, u32[]{:S(2)}, u32[]{:S(2)}) async-start(bf16[4,192,512]{2,1,0:T(8,128)(2,1)} %pad_maximum_fusion.11), calls=%async_computation.1 | async-start | bytes 1572864 | tf_op jit(solution)/shard_map/all_to_all | solution.py:1066
  62.7 76.6 %all-gather.9.cloned.1.call-start = ((), (), s32[]{:S(2)}) async-start(), calls=%async_computation.16 | async-start | bytes 5308416 | tf_op jit(solution)/shard_map/all_gather | solution.py:923
  83.2 18.9 %collective-permute-start.14 = (bf16[128,1024]{1,0:T(8,128)(2,1)S(1)}, bf16[128,1024]{1,0:T(8,128)(2,1)S(1)}, u32[]{:S(2)}, u32[]{:S(2)}) collective-permute-start(bf16[128,1024]{1,0:T(8,128)(2,1)S(1)} %slice_select_fusion.1), channel_id=1, source_target_pairs={{0,2},{1,3},{2,0},{3,1},{4,6},{5,7},{6,4},{7,5},{8,10},{9,11},{10,... | collective-permute-start | bytes 786440 | tf_op jit(solution)/shard_map/ppermute | solution.py:853
  102.1 18.5 %all-to-all-start.2 = ((bf16[16,64,128]{2,1,0:T(8,128)(2,1)}), bf16[16,64,128]{2,1,0:T(8,128)(2,1)S(1)}, u32[]{:S(2)}, u32[]{:S(2)}) async-start(bf16[16,64,128]{2,1,0:T(8,128)(2,1)} %bitcast.337), calls=%async_computation.2 | async-start | bytes 524288 | tf_op jit(solution)/shard_map/all_to_all | solution.py:1097
  106.2 62.6 %all-gather.7.cloned.1.call-start = ((), (), s32[]{:S(2)}) async-start(), calls=%async_computation.15 | async-start | bytes 2359296 | tf_op jit(solution)/shard_map/all_gather | solution.py:923
  180.8 24.8 %all-to-all-start.3 = ((bf16[4,192,512]{2,1,0:T(8,128)(2,1)}), bf16[4,192,512]{2,1,0:T(8,128)(2,1)}, u32[]{:S(2)}, u32[]{:S(2)}) async-start(bf16[4,192,512]{2,1,0:T(8,128)(2,1)} %pad_maximum_fusion.13), calls=%async_computation.3 | async-start | bytes 1572864 | tf_op jit(solution)/shard_map/all_to_all | solution.py:1066
  185.0 79.5 %all-gather.11.cloned.1.call-start = ((), (), s32[]{:S(2)}) async-start(), calls=%async_computation.17 | async-start | bytes 5308416 | tf_op jit(solution)/shard_map/all_gather | solution.py:923
  207.4 18.9 %collective-permute-start.28 = (bf16[128,1024]{1,0:T(8,128)(2,1)S(1)}, bf16[128,1024]{1,0:T(8,128)(2,1)S(1)}, u32[]{:S(2)}, u32[]{:S(2)}) collective-permute-start(bf16[128,1024]{1,0:T(8,128)(2,1)S(1)} %bitcast.341), channel_id=1, source_target_pairs={{0,2},{1,3},{2,0},{3,1},{4,6},{5,7},{6,4},{7,5},{8,10},{9,11},{10,... | collective-permute-start | bytes 786440 | tf_op jit(solution)/shard_map/ppermute | solution.py:853
  208.9 17.4 %collective-permute-start.29 = (bf16[128,1024]{1,0:T(8,128)(2,1)S(1)}, bf16[128,1024]{1,0:T(8,128)(2,1)S(1)}, u32[]{:S(2)}, u32[]{:S(2)}) collective-permute-start(bf16[128,1024]{1,0:T(8,128)(2,1)S(1)} %bitcast.342), channel_id=1, source_target_pairs={{0,4},{4,0},{8,12},{12,8},{16,20},{20,16},{24,28},{28,24},{1,5},{5... | collective-permute-start | bytes 786440 | tf_op jit(solution)/shard_map/ppermute | solution.py:854
  226.3 19.3 %all-to-all-start.4 = ((bf16[16,64,128]{2,1,0:T(8,128)(2,1)}), bf16[16,64,128]{2,1,0:T(8,128)(2,1)}, u32[]{:S(2)}, u32[]{:S(2)}) async-start(bf16[16,64,128]{2,1,0:T(8,128)(2,1)} %bitcast.338), calls=%async_computation.4 | async-start | bytes 524288 | tf_op jit(solution)/shard_map/all_to_all | solution.py:1097
  231.4 160.0 %reduce-scatter.5.cloned.1.call-start = ((), (), s32[]{:S(2)}) async-start(), calls=%async_computation.18 | async-start | bytes 5308416 | tf_op jit(solution)/shard_map/reduce_scatter | solution.py:935
  292.6 21.0 %all-to-all-start.5 = ((bf16[16,64,128]{2,1,0:T(8,128)(2,1)}), bf16[16,64,128]{2,1,0:T(8,128)(2,1)S(1)}, u32[]{:S(2)}, u32[]{:S(2)}) async-start(bf16[16,64,128]{2,1,0:T(8,128)(2,1)} %bitcast.72), calls=%async_computation.5 | async-start | bytes 524288 | tf_op jit(solution)/shard_map/all_to_all | solution.py:1097
  313.7 26.5 %collective-permute-start.40 = (bf16[128,1280]{1,0:T(8,128)(2,1)S(1)}, bf16[128,1280]{1,0:T(8,128)(2,1)S(1)}, u32[]{:S(2)}, u32[]{:S(2)}) collective-permute-start(bf16[128,1280]{1,0:T(8,128)(2,1)S(1)} %get-tuple-element.421), channel_id=1, source_target_pairs={{0,6},{1,7},{2,4},{3,5},{4,2},{5,3},{6,0},{7,1},{8,14},{9,15},{10,... | collective-permute-start | bytes 983048 | tf_op jit(solution)/shard_map/ppermute | solution.py:855
  314.2 26.0 %collective-permute-start.39 = (bf16[128,1280]{1,0:T(8,128)(2,1)S(1)}, bf16[128,1280]{1,0:T(8,128)(2,1)S(1)}, u32[]{:S(2)}, u32[]{:S(2)}) collective-permute-start(bf16[128,1280]{1,0:T(8,128)(2,1)S(1)} %get-tuple-element.420), channel_id=1, source_target_pairs={{0,4},{4,0},{8,12},{12,8},{16,20},{20,16},{24,28},{28,24},{1,5},{5... | collective-permute-start | bytes 983048 | tf_op jit(solution)/shard_map/ppermute | solution.py:854
  316.6 23.6 %collective-permute-start.38 = (bf16[128,1280]{1,0:T(8,128)(2,1)S(1)}, bf16[128,1280]{1,0:T(8,128)(2,1)S(1)}, u32[]{:S(2)}, u32[]{:S(2)}) collective-permute-start(bf16[128,1280]{1,0:T(8,128)(2,1)S(1)} %get-tuple-element.419), channel_id=1, source_target_pairs={{0,2},{1,3},{2,0},{3,1},{4,6},{5,7},{6,4},{7,5},{8,10},{9,11},{10,... | collective-permute-start | bytes 983048 | tf_op jit(solution)/shard_map/ppermute | solution.py:853
  345.3 24.2 %all-to-all-start.6 = ((bf16[4,192,512]{2,1,0:T(8,128)(2,1)}), bf16[4,192,512]{2,1,0:T(8,128)(2,1)S(1)}, u32[]{:S(2)}, u32[]{:S(2)}) async-start(bf16[4,192,512]{2,1,0:T(8,128)(2,1)} %pad_maximum_fusion.15), calls=%async_computation.6 | async-start | bytes 1572864 | tf_op jit(solution)/shard_map/all_to_all | solution.py:1084
  348.8 81.1 %reduce-scatter.7.cloned.1.call-start = ((), (), s32[]{:S(2)}) async-start(), calls=%async_computation.19 | async-start | bytes 2359296 | tf_op jit(solution)/shard_map/reduce_scatter | solution.py:935
  391.4 96.1 %reduce-scatter.9.cloned.1.call-start = ((), (), s32[]{:S(2)}) async-start(), calls=%async_computation.20 | async-start | bytes 5308416 | tf_op jit(solution)/shard_map/reduce_scatter | solution.py:935
  450.9 26.4 %collective-permute-start.56 = (bf16[128,1280]{1,0:T(8,128)(2,1)S(1)}, bf16[128,1280]{1,0:T(8,128)(2,1)S(1)}, u32[]{:S(2)}, u32[]{:S(2)}) collective-permute-start(bf16[128,1280]{1,0:T(8,128)(2,1)S(1)} %get-tuple-element.408), channel_id=1, source_target_pairs={{0,6},{1,7},{2,4},{3,5},{4,2},{5,3},{6,0},{7,1},{8,14},{9,15},{10,... | collective-permute-start | bytes 983048 | tf_op jit(solution)/shard_map/ppermute | solution.py:855
  451.4 25.9 %collective-permute-start.55 = (bf16[128,1280]{1,0:T(8,128)(2,1)S(1)}, bf16[128,1280]{1,0:T(8,128)(2,1)S(1)}, u32[]{:S(2)}, u32[]{:S(2)}) collective-permute-start(bf16[128,1280]{1,0:T(8,128)(2,1)S(1)} %get-tuple-element.407), channel_id=1, source_target_pairs={{0,4},{4,0},{8,12},{12,8},{16,20},{20,16},{24,28},{28,24},{1,5},{5... | collective-permute-start | bytes 983048 | tf_op jit(solution)/shard_map/ppermute | solution.py:854
  453.9 23.5 %collective-permute-start.54 = (bf16[128,1280]{1,0:T(8,128)(2,1)S(1)}, bf16[128,1280]{1,0:T(8,128)(2,1)S(1)}, u32[]{:S(2)}, u32[]{:S(2)}) collective-permute-start(bf16[128,1280]{1,0:T(8,128)(2,1)S(1)} %get-tuple-element.406), channel_id=1, source_target_pairs={{0,2},{1,3},{2,0},{3,1},{4,6},{5,7},{6,4},{7,5},{8,10},{9,11},{10,... | collective-permute-start | bytes 983048 | tf_op jit(solution)/shard_map/ppermute | solution.py:853
  482.4 24.2 %all-to-all-start.8 = ((bf16[4,192,512]{2,1,0:T(8,128)(2,1)}), bf16[4,192,512]{2,1,0:T(8,128)(2,1)S(1)}, u32[]{:S(2)}, u32[]{:S(2)}) async-start(bf16[4,192,512]{2,1,0:T(8,128)(2,1)} %pad_maximum_fusion.16), calls=%async_computation.8 | async-start | bytes 1572864 | tf_op jit(solution)/shard_map/all_to_all | solution.py:1084
  485.9 59.5 %reduce-scatter.11.cloned.1.call-start = ((), (), s32[]{:S(2)}) async-start(), calls=%async_computation.21 | async-start | bytes 2359296 | tf_op jit(solution)/shard_map/reduce_scatter | solution.py:935
  (136 other events, 1157.5 us)
Sparse Core Ops, SparseCore 0:
  23.3 29.3 all-gather.4
  82.4 55.7 all-gather.8
  139.8 28.9 all-gather.6
  205.8 56.5 all-gather.10
  289.0 60.0 reduce-scatter.4
  391.6 33.2 reduce-scatter.6
  430.1 57.4 reduce-scatter.8
  510.7 34.6 reduce-scatter.10

commit v7 on v6

--- a/solution.py
+++ b/solution.py
@@ -47,7 +47,7 @@
 
 def forward_kernel(flip_ref, q_ref, q_aug_ref, own_ref, sib_ref, k_aug_ref, out_ref, lse_ref):
     blocks = own_ref.shape[0]
-    sources = ((own_ref, HD), (sib_ref, 0))
+    sources = ((own_ref, HD), (sib_ref, HD))
     spots = [(half, block) for half in range(2) for block in range(blocks)]
     cols = q_ref.shape[-1]
     q_side = jnp.concatenate([q_ref[0, :HD, :], q_aug_ref[0]], axis=0).T
@@ -94,11 +94,11 @@
 
 def backward_kernel(
     flip_ref, q_ref, q_aug_ref, lse_ref, out_ref, grad_ref, own_ref, sib_ref, k_aug_ref,
-    dq_ref, dkv_ref, dkv_acc,
+    dq_ref, dkv_own_ref, dkv_sib_ref, dkv_acc,
 ):
     step = pl.program_id(0)
     blocks = own_ref.shape[0]
-    sources = ((own_ref, HD), (sib_ref, 0))
+    sources = ((own_ref, HD), (sib_ref, HD))
     cols, key_cols = q_ref.shape[-1], own_ref.shape[-1]
 
     @pl.when(step == 0)
@@ -143,7 +143,8 @@
 
     @pl.when(step == pl.num_programs(0) - 1)
     def _():
-        dkv_ref[...] = dkv_acc[...].astype(LOW)
+        dkv_own_ref[...] = dkv_acc[:blocks].astype(LOW)
+        dkv_sib_ref[...] = dkv_acc[blocks:].astype(LOW)
 
 
 def whole_spec(shape):
@@ -185,11 +186,11 @@
 
 def attention_backward(flip, queries, q_aug, lse, out, grad, own, sib, k_aug):
     tiles, unused, cols = queries.shape
-    dkv_shape = (2 * own.shape[0], 2 * HD, cols)
+    dkv_shape, half_shape = (2 * own.shape[0], 2 * HD, cols), (own.shape[0], 2 * HD, cols)
     pairs = 2 * tiles * own.shape[0] * cols * cols
     results = [
         jax.ShapeDtypeStruct((tiles, 2 * HD, cols), jnp.float32),
-        jax.ShapeDtypeStruct(dkv_shape, LOW),
+        *[jax.ShapeDtypeStruct(half_shape, LOW)] * 2,
     ]
     return pl.pallas_call(
         backward_kernel,
@@ -199,7 +200,7 @@
             in_specs=[tile_spec(3 * HD, cols), tile_spec(HD, cols), tile_spec(8, cols)]
             + [owner_spec(out.shape)] * 2
             + [whole_spec(member.shape) for member in (own, sib, k_aug)],
-            out_specs=[tile_spec(2 * HD, cols), whole_spec(dkv_shape)],
+            out_specs=[tile_spec(2 * HD, cols)] + [whole_spec(half_shape)] * 2,
             scratch_shapes=[pltpu.VMEM(dkv_shape, jnp.float32)],
         ),
         out_shape=results,
@@ -1166,7 +1167,7 @@
         halves = out_quarter.reshape(2, quarter_width // 2, D)
         half = jnp.where(here_core == 0, halves[0], halves[1])
         out_parts = neighbours(half, half, half)
-        sib = lax.ppermute(own[:, HD:], "head", CORE_SWAP)
+        sib = lax.ppermute(own, "head", CORE_SWAP)
         queries = my_tiles(own)
         q_aug = q_augs[layer]
         out, lse = attention_forward(chip_flips, queries, q_aug, own, sib, k_aug)
@@ -1247,7 +1248,7 @@
             out_grad, *last_parts = lax.optimization_barrier((out_grad, *last_parts))
         out_grad, middle_low, attended = lax.optimization_barrier((out_grad, middle_low, attended))
         middle_low, attended = share_for_out(middle_low, attended)
-        grad_q, grad_kv = attention_backward(
+        grad_q, grad_kv, sent_kv = attention_backward(
             chip_flips, queries, q_aug, lse, out, out_grad, own, sib, k_aug
         )
         grad_kv, middle_low, attended = lax.optimization_barrier((grad_kv, middle_low, attended))
@@ -1257,8 +1258,8 @@
             out_blocks = out_weight_grad(attended, middle_low, w_rows)
         same_grad = jnp.sum(grad_q[:, HD : HD + VARIATES] * q_onehots)
         all_grad = jnp.sum(grad_q[:, HD + 16])
-        crossed = lax.ppermute(grad_kv[planes:], "head", CORE_SWAP)
-        grad_kv = (grad_kv[:planes].astype(jnp.float32) + crossed.astype(jnp.float32)).astype(LOW)
+        crossed = lax.ppermute(sent_kv, "head", CORE_SWAP)
+        grad_kv = (grad_kv.astype(jnp.float32) + crossed.astype(jnp.float32)).astype(LOW)
         grad_q = (grad_q[:, :HD] * (1.0 / math.sqrt(HD))).astype(LOW)
         if layer == LAYERS - 1:
             grad_kv, *last_parts = lax.optimization_barrier((grad_kv, *last_parts))

time: 584 us -> 599 us (1.026)
  waiting for transfers between devices: 174 us -> 193 us
    ppermute x17, waiting for transfers between devices: 14.6 us -> 32.1 us  [neighbours(): lax.ppermute(across_y, 'head', Y_SWAP)]
  transfers between devices with their start and end apart: 87 -> 87, of which waited for: 47 -> 53; matrix products, arithmetic and copies ran while one was open for 14% -> 13% of each run, Pallas kernels for 21% -> 21%
where the time goes in v7:
time: 599 us; the launch traced here: 588 us
  waiting for transfers between devices  193 us (32%)
  Pallas kernels  138 us (23%)
  starting transfers between devices  119 us (20%)
  other arithmetic  58.5 us (10%)
  between operations  24.3 us (4%)
  local copies, waits for them, and re-layouts  21.5 us (4%)
  blocking collectives  18 us (3%)
  matrix products  15.2 us (3%)
    pallas_call x2, Pallas kernels, attention_backward(): pl.pallas_call(backward_kernel, grid_spec=pltpu.PrefetchScalarGridSpec(nu...  45.9 us
    ppermute x17, waiting for transfers between devices, neighbours(): lax.ppermute(across_x, 'seq', x_swap)  34.7 us
    all_to_all x3, waiting for transfers between devices, over_chips(): lax.all_to_all(value, BOTH, split_axis=0, concat_axis=0, tiled=True, axis...  33.8 us
    ppermute x17, waiting for transfers between devices, neighbours(): lax.ppermute(across_y, 'head', Y_SWAP)  32.1 us
    ppermute x17, waiting for transfers between devices, neighbours(): lax.ppermute(across_both, BOTH, corner_swap)  30.8 us
    pallas_call x2, Pallas kernels, attention_forward(): pl.pallas_call(forward_kernel, grid_spec=pltpu.PrefetchScalarGridSpec(num...  29.3 us
    ppermute x17, starting transfers between devices, neighbours(): lax.ppermute(across_both, BOTH, corner_swap)  24.2 us
    ppermute x17, starting transfers between devices, neighbours(): lax.ppermute(across_y, 'head', Y_SWAP)  19.1 us
  transfers between devices with their start and end apart: 87, of which 53 were waited for; matrix products, arithmetic and copies ran while one was open for 13% of the time, Pallas kernels for 21%

profile of v7, /device:TPU:0, one launch (start us, length us, event | category | flops | bytes accessed | tf_op | source)
XLA Modules:
  0.0 588.2 jit_solution(2870610546849924819)
XLA Ops:
  9.6 5.3 all-to-all-start
  15.9 6.5 %all-to-all-done = bf16[8,32,768]{2,1,0:T(8,128)(2,1)S(1)} async-done(((bf16[8,32,768]{2,1,0:T(8,128)(2,1)}), bf16[8,32,768]{2,1,0:T(8,128)(2,1)S(1)}, u32[]{:S(2)}, u32[]{:S(2)}) %all-to-all-start) | async-done | bytes 393248 | tf_op jit(solution)/shard_map/all_to_all | solution.py:908
  57.7 5.0 all-to-all-start.1
  87.5 14.6 %attention_forward.2 = (bf16[4,4,64,128]{3,2,1,0:T(8,128)(2,1)}, f32[4,8,512]{2,1,0:T(8,128)}) custom-call(s32[1]{0:T(128)} %bitcast.flip_ref, bf16[4,192,512]{2,1,0:T(8,128)(2,1)} %all-to-all-done.1.q_ref.own_ref, bf16[4,64,512]{2,1,0:T(8,128)(2,1)} %get-tuple-element.179.q_aug_ref, bf16[4,192,512]{2,1,0:T(8,128)(2,1)} %all-to-all-done.1.q_ref.own_ref, ...), custom_call_target="tpu_custom_call" | custom-call | flops 8589934592 | bytes 2686976 | tf_op jit(solution)/shard_map/attention_forward/pallas_call | solution.py:171
  108.5 12.2 %all-to-all-done.2 = bf16[16,64,128]{2,1,0:T(8,128)(2,1)S(1)} async-done(((bf16[16,64,128]{2,1,0:T(8,128)(2,1)}), bf16[16,64,128]{2,1,0:T(8,128)(2,1)S(1)}, u32[]{:S(2)}, u32[]{:S(2)}) %all-to-all-start.2) | async-done | bytes 262176 | tf_op jit(solution)/shard_map/all_to_all | solution.py:1098
  139.5 7.1 %ffn_forward.1 = (bf16[6,512,256]{2,1,0:T(8,128)(2,1)}, bf16[512,768]{1,0:T(8,128)(2,1)}, f32[128,1024]{1,0:T(8,128)}, bf16[128,1024]{1,0:T(8,128)(2,1)}, bf16[1...) custom-call(bf16[128,1024]{1,0:T(8,128)(2,1)} %copy-done.10, bf16[128,1024]{1,0:T(8,128)(2,1)} %copy-done.23, ...), custom_call_target="tpu_custom_call" | custom-call | flops 2415919104 | bytes 9437184 | tf_op jit(solution)/shard_map/ffn_forward/pallas_call | solution.py:416
  150.0 6.9 %collective-permute-done.23 = bf16[128,1024]{1,0:T(8,128)(2,1)S(1)} collective-permute-done((bf16[128,1024]{1,0:T(8,128)(2,1)}, bf16[128,1024]{1,0:T(8,128)(2,1)S(1)}, u32[]{:S(2)}, u32[]{:S(2)}) %collective-permute-start.23) | collective-permute-done | bytes 262176 | tf_op jit(solution)/shard_map/ppermute | solution.py:856
  190.1 15.6 %all-to-all-done.3.q_ref.own_ref = bf16[4,192,512]{2,1,0:T(8,128)(2,1)} async-done(((bf16[4,192,512]{2,1,0:T(8,128)(2,1)}), bf16[4,192,512]{2,1,0:T(8,128)(2,1)}, u32[]{:S(2)}, u32[]{:S(2)}) %all-to-all-start.3) | async-done | bytes 786464 | tf_op jit(solution)/shard_map/all_to_all | solution.py:1067
  210.9 14.6 %attention_forward.3 = (bf16[4,4,64,128]{3,2,1,0:T(8,128)(2,1)}, f32[4,8,512]{2,1,0:T(8,128)}) custom-call(s32[1]{0:T(128)} %bitcast.flip_ref, bf16[4,192,512]{2,1,0:T(8,128)(2,1)} %all-to-all-done.3.q_ref.own_ref, bf16[4,64,512]{2,1,0:T(8,128)(2,1)} %get-tuple-element.200.q_aug_ref, bf16[4,192,512]{2,1,0:T(8,128)(2,1)} %all-to-all-done.3.q_ref.own_ref, ...), custom_call_target="tpu_custom_call" | custom-call | flops 8589934592 | bytes 2686976 | tf_op jit(solution)/shard_map/attention_forward/pallas_call | solution.py:171
  225.6 4.9 all-to-all-start.4
  234.0 10.9 %all-to-all-done.4 = bf16[16,64,128]{2,1,0:T(8,128)(2,1)} async-done(((bf16[16,64,128]{2,1,0:T(8,128)(2,1)}), bf16[16,64,128]{2,1,0:T(8,128)(2,1)}, u32[]{:S(2)}, u32[]{:S(2)}) %all-to-all-start.4) | async-done | bytes 262176 | tf_op jit(solution)/shard_map/all_to_all | solution.py:1098
  253.3 4.8 collective-permute-done.32.refs_1_
  264.6 10.8 %ffn_turn.1 = (bf16[6,512,256]{2,1,0:T(8,128)(2,1)}, bf16[512,768]{1,0:T(8,128)(2,1)}, f32[128,1024]{1,0:T(8,128)}, bf16[128,1024]{1,0:T(8,128)(2,1)}, bf16[128,...) custom-call(bf16[128,1024]{1,0:T(8,128)(2,1)} %copy-done.33, bf16[128,1024]{1,0:T(8,128)(2,1)} %copy-done.41, ...), custom_call_target="tpu_custom_call" | custom-call | flops 4026531840 | bytes 10485760 | tf_op jit(solution)/shard_map/ffn_turn/pallas_call | solution.py:477
  279.0 6.7 %ffn_weight_grads.2 = bf16[8,1152,256]{2,1,0:T(8,128)(2,1)} custom-call(bf16[128,1024]{1,0:T(8,128)(2,1)} %copy-done.33, bf16[128,1024]{1,0:T(8,128)(2,1)} %copy-done.41, bf16[128,1024]{1,0:T(8,128)(2,1)} %copy-done.42, bf16[128,1024]{1,0:T(8,128)(2,1)} %collective-permute-done.34.refs_3_, bf16[6,512,256]{2,1,0:T(8,128)(2,1)} %get-tuple-element.218.refs_4_, ...), custom_call_target="tpu_custom_call" | custom-call | flops 2415919104 | bytes 9175040 | tf_op jit(solution)/shard_map/ffn_weight_grads/pallas_call | solution.py:554
  292.9 6.2 %all-to-all-start.5 = ((bf16[16,64,128]{2,1,0:T(8,128)(2,1)}), bf16[16,64,128]{2,1,0:T(8,128)(2,1)S(1)}, u32[]{:S(2)}, u32[]{:S(2)}) async-start(bf16[16,64,128]{2,1,0:T(8,128)(2,1)} %bitcast.72), calls=%async_computation.5 | async-start | bytes 524288 | tf_op jit(solution)/shard_map/all_to_all | solution.py:1098
  302.7 10.7 %all-to-all-done.5 = bf16[16,64,128]{2,1,0:T(8,128)(2,1)S(1)} async-done(((bf16[16,64,128]{2,1,0:T(8,128)(2,1)}), bf16[16,64,128]{2,1,0:T(8,128)(2,1)S(1)}, u32[]{:S(2)}, u32[]{:S(2)}) %all-to-all-start.5) | async-done | bytes 262176 | tf_op jit(solution)/shard_map/all_to_all | solution.py:1098
  314.1 22.9 %attention_backward.2 = (f32[4,128,512]{2,1,0:T(8,128)}, bf16[4,128,512]{2,1,0:T(8,128)(2,1)}, bf16[4,128,512]{2,1,0:T(8,128)(2,1)}) custom-call(s32[1]{0:T(128)} %bitcast.flip_ref, bf16[4,192,512]{2,1,0:T(8,128)(2,1)} %all-to-all-done.3.q_ref.own_ref, bf16[4,64,512]{2,1,0:T(8,128)(2,1)} %get-tuple-element.200.q_aug_ref, ...), custom_call_target="tpu_custom_call" | custom-call | flops 17179869184 | bytes 4456448 | tf_op jit(solution)/shard_map/attention_backward/pallas_call | solution.py:195
  341.4 6.6 %collective-permute-done.39 = bf16[128,1280]{1,0:T(8,128)(2,1)S(1)} collective-permute-done((bf16[128,1280]{1,0:T(8,128)(2,1)S(1)}, bf16[128,1280]{1,0:T(8,128)(2,1)S(1)}, u32[]{:S(2)}, u32[]{:S(2)}) %collective-permute-start.39) | collective-permute-done | bytes 327712 | tf_op jit(solution)/shard_map/ppermute | solution.py:855
  415.1 8.0 %ffn_backward.1 = (bf16[6,512,256]{2,1,0:T(8,128)(2,1)}, f32[128,1024]{1,0:T(8,128)}, bf16[128,1024]{1,0:T(8,128)(2,1)}, bf16[128,1024]{1,0:T(8,128)(2,1)}, bf16[128,1024]{1,0:T(8,128)(2,1)}) custom-call(bf16[128,1024]{1,0:T(8,128)(2,1)} %copy-done.7, bf16[128,1024]{1,0:T(8,128)(2,1)} %copy-done.26, bf16[128,1024]{1,0:T(8,128)(2,1)} %copy-done.27, ...), custom_call_target="tpu_custom_call" | custom-call | flops 2415919104 | bytes 10223616 | tf_op jit(solution)/shard_map/ffn_backward/pallas_call | solution.py:445
  426.6 6.8 %ffn_weight_grads.3 = bf16[8,1152,256]{2,1,0:T(8,128)(2,1)} custom-call(bf16[128,1024]{1,0:T(8,128)(2,1)} %copy-done.10, bf16[128,1024]{1,0:T(8,128)(2,1)} %copy-done.23, bf16[128,1024]{1,0:T(8,128)(2,1)} %copy-done.24, bf16[128,1024]{1,0:T(8,128)(2,1)} %collective-permute-done.20.refs_3_, bf16[6,512,256]{2,1,0:T(8,128)(2,1)} %get-tuple-element.254.refs_4_, ...), custom_call_target="tpu_custom_call" | custom-call | flops 2415919104 | bytes 9175040 | tf_op jit(solution)/shard_map/ffn_weight_grads/pallas_call | solution.py:554
  439.4 18.0 %all_to_all.50 = bf16[16,64,128]{2,1,0:T(8,128)(2,1)} all-to-all(bf16[16,64,128]{2,1,0:T(8,128)(2,1)S(1)} %bitcast.321), channel_id=1, replica_groups={{0,2,4,6,8,10,12,14,16,18,20,22,24,26,28,30},{1,3,5,7,9,11,13,15,17,19,..., dimensions={0} | all-to-all | bytes 524288 | tf_op jit(solution)/shard_map/all_to_all | solution.py:1098
  460.5 23.0 %attention_backward.3 = (f32[4,128,512]{2,1,0:T(8,128)}, bf16[4,128,512]{2,1,0:T(8,128)(2,1)}, bf16[4,128,512]{2,1,0:T(8,128)(2,1)}) custom-call(s32[1]{0:T(128)} %bitcast.flip_ref, bf16[4,192,512]{2,1,0:T(8,128)(2,1)} %all-to-all-done.1.q_ref.own_ref, bf16[4,64,512]{2,1,0:T(8,128)(2,1)} %get-tuple-element.179.q_aug_ref, ...), custom_call_target="tpu_custom_call" | custom-call | flops 17179869184 | bytes 4456448 | tf_op jit(solution)/shard_map/attention_backward/pallas_call | solution.py:195
  485.4 9.4 %collective-permute-done.54 = bf16[128,1280]{1,0:T(8,128)(2,1)S(1)} collective-permute-done((bf16[128,1280]{1,0:T(8,128)(2,1)S(1)}, bf16[128,1280]{1,0:T(8,128)(2,1)S(1)}, u32[]{:S(2)}, u32[]{:S(2)}) %collective-permute-start.54) | collective-permute-done | bytes 327712 | tf_op jit(solution)/shard_map/ppermute | solution.py:854
  551.5 5.0 finish_gradients.1
  (511 shorter events, 321.2 us)
Async XLA Ops:
  15.0 39.1 %all-gather.5.cloned.1.call-start = ((), (), s32[]{:S(2)}) async-start(), calls=%async_computation.14 | async-start | bytes 2359296 | tf_op jit(solution)/shard_map/all_gather | solution.py:924
  23.3 16.8 %collective-permute-start.2 = (bf16[128,1024]{1,0:T(8,128)(2,1)S(1)}, bf16[128,1024]{1,0:T(8,128)(2,1)S(1)}, u32[]{:S(2)}, u32[]{:S(2)}) collective-permute-start(bf16[128,1024]{1,0:T(8,128)(2,1)S(1)} %multiply_convert_fusion.5), channel_id=1, source_target_pairs={{0,6},{1,7},{2,4},{3,5},{4,2},{5,3},{6,0},{7,1},{8,14},{9,15},{10,... | collective-permute-start | bytes 786440 | tf_op jit(solution)/shard_map/ppermute | solution.py:856
  57.7 24.7 %all-to-all-start.1 = ((bf16[4,192,512]{2,1,0:T(8,128)(2,1)}), bf16[4,192,512]{2,1,0:T(8,128)(2,1)}, u32[]{:S(2)}, u32[]{:S(2)}) async-start(bf16[4,192,512]{2,1,0:T(8,128)(2,1)} %pad_maximum_fusion.11), calls=%async_computation.1 | async-start | bytes 1572864 | tf_op jit(solution)/shard_map/all_to_all | solution.py:1067
  62.7 76.7 %all-gather.9.cloned.1.call-start = ((), (), s32[]{:S(2)}) async-start(), calls=%async_computation.16 | async-start | bytes 5308416 | tf_op jit(solution)/shard_map/all_gather | solution.py:924
  83.0 19.1 %collective-permute-start.14 = (bf16[128,1024]{1,0:T(8,128)(2,1)S(1)}, bf16[128,1024]{1,0:T(8,128)(2,1)S(1)}, u32[]{:S(2)}, u32[]{:S(2)}) collective-permute-start(bf16[128,1024]{1,0:T(8,128)(2,1)S(1)} %slice_select_fusion.1), channel_id=1, source_target_pairs={{0,2},{1,3},{2,0},{3,1},{4,6},{5,7},{6,4},{7,5},{8,10},{9,11},{10,... | collective-permute-start | bytes 786440 | tf_op jit(solution)/shard_map/ppermute | solution.py:854
  85.0 17.2 %collective-permute-start.15 = (bf16[128,1024]{1,0:T(8,128)(2,1)S(1)}, bf16[128,1024]{1,0:T(8,128)(2,1)S(1)}, u32[]{:S(2)}, u32[]{:S(2)}) collective-permute-start(bf16[128,1024]{1,0:T(8,128)(2,1)S(1)} %slice_select_fusion.1), channel_id=1, source_target_pairs={{0,4},{4,0},{8,12},{12,8},{16,20},{20,16},{24,28},{28,24},{1,5},{5... | collective-permute-start | bytes 786440 | tf_op jit(solution)/shard_map/ppermute | solution.py:855
  85.3 16.9 %collective-permute-start.16 = (bf16[128,1024]{1,0:T(8,128)(2,1)S(1)}, bf16[128,1024]{1,0:T(8,128)(2,1)S(1)}, u32[]{:S(2)}, u32[]{:S(2)}) collective-permute-start(bf16[128,1024]{1,0:T(8,128)(2,1)S(1)} %slice_select_fusion.1), channel_id=1, source_target_pairs={{0,6},{1,7},{2,4},{3,5},{4,2},{5,3},{6,0},{7,1},{8,14},{9,15},{10,... | collective-permute-start | bytes 786440 | tf_op jit(solution)/shard_map/ppermute | solution.py:856
  102.2 18.4 %all-to-all-start.2 = ((bf16[16,64,128]{2,1,0:T(8,128)(2,1)}), bf16[16,64,128]{2,1,0:T(8,128)(2,1)S(1)}, u32[]{:S(2)}, u32[]{:S(2)}) async-start(bf16[16,64,128]{2,1,0:T(8,128)(2,1)} %bitcast.337), calls=%async_computation.2 | async-start | bytes 524288 | tf_op jit(solution)/shard_map/all_to_all | solution.py:1098
  106.3 62.8 %all-gather.7.cloned.1.call-start = ((), (), s32[]{:S(2)}) async-start(), calls=%async_computation.15 | async-start | bytes 2359296 | tf_op jit(solution)/shard_map/all_gather | solution.py:924
  180.9 24.8 %all-to-all-start.3 = ((bf16[4,192,512]{2,1,0:T(8,128)(2,1)}), bf16[4,192,512]{2,1,0:T(8,128)(2,1)}, u32[]{:S(2)}, u32[]{:S(2)}) async-start(bf16[4,192,512]{2,1,0:T(8,128)(2,1)} %pad_maximum_fusion.13), calls=%async_computation.3 | async-start | bytes 1572864 | tf_op jit(solution)/shard_map/all_to_all | solution.py:1067
  185.2 79.4 %all-gather.11.cloned.1.call-start = ((), (), s32[]{:S(2)}) async-start(), calls=%async_computation.17 | async-start | bytes 5308416 | tf_op jit(solution)/shard_map/all_gather | solution.py:924
  206.4 19.1 %collective-permute-start.28 = (bf16[128,1024]{1,0:T(8,128)(2,1)S(1)}, bf16[128,1024]{1,0:T(8,128)(2,1)S(1)}, u32[]{:S(2)}, u32[]{:S(2)}) collective-permute-start(bf16[128,1024]{1,0:T(8,128)(2,1)S(1)} %bitcast.341), channel_id=1, source_target_pairs={{0,2},{1,3},{2,0},{3,1},{4,6},{5,7},{6,4},{7,5},{8,10},{9,11},{10,... | collective-permute-start | bytes 786440 | tf_op jit(solution)/shard_map/ppermute | solution.py:854
  208.0 17.6 %collective-permute-start.29 = (bf16[128,1024]{1,0:T(8,128)(2,1)S(1)}, bf16[128,1024]{1,0:T(8,128)(2,1)S(1)}, u32[]{:S(2)}, u32[]{:S(2)}) collective-permute-start(bf16[128,1024]{1,0:T(8,128)(2,1)S(1)} %bitcast.342), channel_id=1, source_target_pairs={{0,4},{4,0},{8,12},{12,8},{16,20},{20,16},{24,28},{28,24},{1,5},{5... | collective-permute-start | bytes 786440 | tf_op jit(solution)/shard_map/ppermute | solution.py:855
  225.6 19.3 %all-to-all-start.4 = ((bf16[16,64,128]{2,1,0:T(8,128)(2,1)}), bf16[16,64,128]{2,1,0:T(8,128)(2,1)}, u32[]{:S(2)}, u32[]{:S(2)}) async-start(bf16[16,64,128]{2,1,0:T(8,128)(2,1)} %bitcast.338), calls=%async_computation.4 | async-start | bytes 524288 | tf_op jit(solution)/shard_map/all_to_all | solution.py:1098
  230.5 167.4 %reduce-scatter.5.cloned.1.call-start = ((), (), s32[]{:S(2)}) async-start(), calls=%async_computation.18 | async-start | bytes 5308416 | tf_op jit(solution)/shard_map/reduce_scatter | solution.py:936
  292.9 20.5 %all-to-all-start.5 = ((bf16[16,64,128]{2,1,0:T(8,128)(2,1)}), bf16[16,64,128]{2,1,0:T(8,128)(2,1)S(1)}, u32[]{:S(2)}, u32[]{:S(2)}) async-start(bf16[16,64,128]{2,1,0:T(8,128)(2,1)} %bitcast.72), calls=%async_computation.5 | async-start | bytes 524288 | tf_op jit(solution)/shard_map/all_to_all | solution.py:1098
  313.5 27.8 %collective-permute-start.40 = (bf16[128,1280]{1,0:T(8,128)(2,1)S(1)}, bf16[128,1280]{1,0:T(8,128)(2,1)S(1)}, u32[]{:S(2)}, u32[]{:S(2)}) collective-permute-start(bf16[128,1280]{1,0:T(8,128)(2,1)S(1)} %get-tuple-element.425), channel_id=1, source_target_pairs={{0,6},{1,7},{2,4},{3,5},{4,2},{5,3},{6,0},{7,1},{8,14},{9,15},{10,... | collective-permute-start | bytes 983048 | tf_op jit(solution)/shard_map/ppermute | solution.py:856
  353.6 23.4 %all-to-all-start.6 = ((bf16[4,192,512]{2,1,0:T(8,128)(2,1)}), bf16[4,192,512]{2,1,0:T(8,128)(2,1)S(1)}, u32[]{:S(2)}, u32[]{:S(2)}) async-start(bf16[4,192,512]{2,1,0:T(8,128)(2,1)} %pad_maximum_fusion.15), calls=%async_computation.6 | async-start | bytes 1572864 | tf_op jit(solution)/shard_map/all_to_all | solution.py:1085
  357.1 79.9 %reduce-scatter.7.cloned.1.call-start = ((), (), s32[]{:S(2)}) async-start(), calls=%async_computation.19 | async-start | bytes 2359296 | tf_op jit(solution)/shard_map/reduce_scatter | solution.py:936
  397.9 103.9 %reduce-scatter.9.cloned.1.call-start = ((), (), s32[]{:S(2)}) async-start(), calls=%async_computation.20 | async-start | bytes 5308416 | tf_op jit(solution)/shard_map/reduce_scatter | solution.py:936
  457.5 27.8 %collective-permute-start.56 = (bf16[128,1280]{1,0:T(8,128)(2,1)S(1)}, bf16[128,1280]{1,0:T(8,128)(2,1)S(1)}, u32[]{:S(2)}, u32[]{:S(2)}) collective-permute-start(bf16[128,1280]{1,0:T(8,128)(2,1)S(1)} %get-tuple-element.412), channel_id=1, source_target_pairs={{0,6},{1,7},{2,4},{3,5},{4,2},{5,3},{6,0},{7,1},{8,14},{9,15},{10,... | collective-permute-start | bytes 983048 | tf_op jit(solution)/shard_map/ppermute | solution.py:856
  458.0 27.2 %collective-permute-start.55 = (bf16[128,1280]{1,0:T(8,128)(2,1)S(1)}, bf16[128,1280]{1,0:T(8,128)(2,1)S(1)}, u32[]{:S(2)}, u32[]{:S(2)}) collective-permute-start(bf16[128,1280]{1,0:T(8,128)(2,1)S(1)} %get-tuple-element.411), channel_id=1, source_target_pairs={{0,4},{4,0},{8,12},{12,8},{16,20},{20,16},{24,28},{28,24},{1,5},{5... | collective-permute-start | bytes 983048 | tf_op jit(solution)/shard_map/ppermute | solution.py:855
  497.7 23.7 %all-to-all-start.8 = ((bf16[4,192,512]{2,1,0:T(8,128)(2,1)}), bf16[4,192,512]{2,1,0:T(8,128)(2,1)S(1)}, u32[]{:S(2)}, u32[]{:S(2)}) async-start(bf16[4,192,512]{2,1,0:T(8,128)(2,1)} %pad_maximum_fusion.16), calls=%async_computation.8 | async-start | bytes 1572864 | tf_op jit(solution)/shard_map/all_to_all | solution.py:1085
  501.2 59.4 %reduce-scatter.11.cloned.1.call-start = ((), (), s32[]{:S(2)}) async-start(), calls=%async_computation.21 | async-start | bytes 2359296 | tf_op jit(solution)/shard_map/reduce_scatter | solution.py:936
  (132 other events, 1167.2 us)
Sparse Core Ops, SparseCore 0:
  23.3 29.3 all-gather.4
  82.5 55.7 all-gather.8
  139.9 29.0 all-gather.6
  205.9 56.5 all-gather.10
  289.2 59.5 reduce-scatter.4
  398.0 34.0 reduce-scatter.6
  437.2 56.9 reduce-scatter.8
  525.7 34.9 reduce-scatter.10
